TPU v7x, 32 devices: a whole 2x2x4 slice. The times are simulated.
32 devices in a mesh: layer: 4 (over y, x), row: 2 (over core), col: 4 (over z).
Axes of the slice: x: 2, y: 2, z: 4, core: 2. Of those that a mesh axis runs over, the one named last changes fastest.
Arguments:
- partial_top: float32 [4, 4096, 4096], P('layer', 'row', 'col'), as said below
- partial_mid: float32 [4, 3072, 3072], P('layer', 'row', 'col'), may hold values from -6 to 6
- partial_low: float32 [4, 2048, 2048], P('layer', 'row', 'col'), may hold values from -6 to 6
- pattern_top: int32 [4, 32, 32], P('layer', 'row', 'col'), may hold values 0 or 1
- pattern_mid: int32 [4, 24, 24], P('layer', 'row', 'col'), may hold values 0 or 1
- pattern_low: int32 [4, 16, 16], P('layer', 'row', 'col'), may hold values 0 or 1
- pivots: int32 [4096], P('row'), may hold values from 0 to 4095, as said below
Outputs:
- top_factor: float32 [4096, 4096], P('row', 'col')
- mid_sums: float32 [4, 3072, 3072], P('layer', 'row', 'col')
- low_sums: float32 [4, 2048, 2048], P('layer', 'row', 'col')
Inputs may be any that keep to these rules, and one draw needn't show every extreme that they name: `pivots`: each aligned block of 128 positions holds a permutation of the same 128 row numbers. `partial_top`: each column has one larger positive entry, at row pivots[column].
All inputs are finite; a program needn't handle non-finite values. No bound on the sum of `pattern_top` or of `pattern_mid` or of `pattern_low` on one device may be relied on, other than what follows from the above.
Results may differ from a plain program's by a relative error of at most 0.0017.
Values may be sent and summed in bfloat16 or wider, within the bound.
No kernel may reach another device: no remote copies, remote signals or barrier semaphores. Data moves between devices by JAX's collectives and lax.ppermute only.
A program may use at most 128 MiB of HBM per device.

v0:
```python
import jax
import jax.numpy as jnp
from jax import lax
from jax.sharding import PartitionSpec as P

PANEL = 128
BLK = 128


def swapped(value, axis, apart):
    return lax.ppermute(value, axis, [(i, i ^ 1 << apart) for i in range(lax.axis_size(axis))])


def spread(value, axis, source):
    kept = jnp.where(lax.axis_index(axis) == source, value, 0).astype(value.dtype)
    return lax.psum(kept, axis)


def split_factors(packed):
    order = packed.shape[0]
    lower_unit = jnp.tril(packed, -1) + jnp.eye(order, dtype=packed.dtype)
    upper_part = jnp.triu(packed)
    return (lower_unit, upper_part)


def highest_dot(left, right):
    return jnp.dot(left, right, precision=lax.Precision.HIGHEST)


def invert_lower_leaf(lower):
    order = lower.shape[0]
    positions = lax.broadcasted_iota(jnp.int32, (order,), 0)

    def substitute(step, current):
        row = lax.dynamic_index_in_dim(lower, step, 0, keepdims=False)
        row = jnp.where(positions < step, row, jnp.zeros_like(row))
        unit = (positions == step).astype(lower.dtype)
        fresh = unit - highest_dot(row, current)
        return lax.dynamic_update_index_in_dim(current, fresh, step, 0)

    return lax.fori_loop(0, order, substitute, jnp.zeros_like(lower))


def invert_upper_leaf(upper):
    order = upper.shape[0]
    positions = lax.broadcasted_iota(jnp.int32, (order,), 0)

    def substitute(count, current):
        step = order - 1 - count
        row = lax.dynamic_index_in_dim(upper, step, 0, keepdims=False)
        pivot_value = lax.dynamic_index_in_dim(row, step, 0, keepdims=False)
        row = jnp.where(positions > step, row, jnp.zeros_like(row))
        unit = (positions == step).astype(upper.dtype)
        fresh = (unit - highest_dot(row, current)) / pivot_value
        return lax.dynamic_update_index_in_dim(current, fresh, step, 0)

    return lax.fori_loop(0, order, substitute, jnp.zeros_like(upper))


def invert_lower(lower):
    order = lower.shape[0]
    return invert_lower_leaf(lower)


def invert_upper(upper):
    order = upper.shape[0]
    return invert_upper_leaf(upper)


def factor_leaf(matrix):
    order = matrix.shape[0]
    positions = lax.broadcasted_iota(jnp.int32, (order,), 0)

    def eliminate(step, current):
        pivot_col = lax.dynamic_index_in_dim(current, step, 1, keepdims=False)
        pivot_row = lax.dynamic_index_in_dim(current, step, 0, keepdims=False)
        pivot_value = lax.dynamic_index_in_dim(pivot_row, step, 0, keepdims=False)
        below = positions > step
        multipliers = jnp.where(below, pivot_col / pivot_value, jnp.zeros_like(pivot_col))
        right_row = jnp.where(below, pivot_row, jnp.zeros_like(pivot_row))
        current = current - multipliers[:, None] * right_row[None, :]
        target = below[:, None] & (positions[None, :] == step)
        return jnp.where(target, multipliers[:, None], current)

    return lax.fori_loop(0, order - 1, eliminate, matrix)


def factor_block(matrix):
    order = matrix.shape[0]
    return factor_leaf(matrix)


def expand_kept(pattern, row_start, col_start):
    block_rows, block_cols = pattern.shape
    block_row = row_start + lax.broadcasted_iota(jnp.int32, (block_rows, block_cols), 0)
    block_col = col_start + lax.broadcasted_iota(jnp.int32, (block_rows, block_cols), 1)
    kept = (pattern == 1) | (block_row == block_col)
    kept = jnp.broadcast_to(kept[:, None, :, None], (block_rows, BLK, block_cols, BLK))
    return kept.reshape(block_rows * BLK, block_cols * BLK)


def local_part(partial_value, pattern):
    first_row = lax.axis_index("row") * pattern.shape[1]
    first_col = lax.axis_index("col") * pattern.shape[2]
    kept = expand_kept(pattern[0], first_row, first_col)
    return jnp.where(kept, partial_value[0], jnp.float32(0.0))


def lower_solve(upper_part, panel_cols):
    return highest_dot(panel_cols, invert_upper(upper_part))


def upper_solve(lower_unit, panel_rows):
    return highest_dot(invert_lower(lower_unit), panel_rows)


def on_device(partial_top, partial_mid, partial_low, pattern_top, pattern_mid, pattern_low, pivots):
    own_mid = local_part(partial_mid, pattern_mid)
    own_low = local_part(partial_low, pattern_low)
    other_mid, other_low = swapped((own_mid, own_low), "layer", 0)
    mid_total = own_mid + other_mid
    low_total = own_low + other_low
    mid_total = mid_total + swapped(mid_total, "layer", 1)
    row_count = partial_top.shape[1]
    col_count = partial_top.shape[2]
    row_start = lax.axis_index("row") * row_count
    col_start = lax.axis_index("col") * col_count
    own_top = local_part(partial_top, pattern_top)
    own_top = jnp.take(own_top, pivots - row_start, axis=0)
    summed = lax.psum(own_top, "layer")
    panel_cols = summed[:, :PANEL]
    panel_rows = summed[:PANEL, :]
    corner = spread(panel_rows[:, :PANEL], ("row", "col"), 0)
    packed = factor_block(corner)
    lower_unit, upper_part = split_factors(packed)
    wide_cols = spread(panel_cols, "col", 0)
    wide_rows = spread(panel_rows, "row", 0)
    lower_panel = lower_solve(upper_part, wide_cols)
    upper_panel = upper_solve(lower_unit, wide_rows)
    lower_low = lower_panel.astype(jnp.bfloat16)
    upper_low = upper_panel.astype(jnp.bfloat16)
    product = jnp.dot(lower_low, upper_low, preferred_element_type=jnp.float32)
    trailing = summed - product
    global_row = row_start + lax.broadcasted_iota(jnp.int32, (row_count, col_count), 0)
    global_col = col_start + lax.broadcasted_iota(jnp.int32, (row_count, col_count), 1)
    empty = jnp.zeros((row_count, col_count), jnp.float32)
    corner_full = empty.at[:PANEL, :PANEL].set(packed)
    upper_full = empty.at[:PANEL, :].set(upper_panel)
    lower_full = empty.at[:, :PANEL].set(lower_panel)
    top_factor = jnp.where(
        (global_row < PANEL) & (global_col < PANEL),
        corner_full,
        jnp.where(
            global_row < PANEL, upper_full, jnp.where(global_col < PANEL, lower_full, trailing)
        ),
    )
    return (top_factor, mid_total[None], low_total[None])


def solution(mesh):
    placed = (
        P("layer", "row", "col"),
        P("layer", "row", "col"),
        P("layer", "row", "col"),
        P("layer", "row", "col"),
        P("layer", "row", "col"),
        P("layer", "row", "col"),
        P("row"),
    )
    return jax.shard_map(
        on_device,
        mesh=mesh,
        in_specs=placed,
        out_specs=(P("row", "col"), P("layer", "row", "col"), P("layer", "row", "col")),
        check_vma=False,
    )
```

profile of v0, /device:TPU:0, one launch (start us, length us, event | category | flops | bytes accessed | tf_op | source)
XLA Modules:
  0.0 816.2 jit_solution(773519335536688664)
XLA Ops:
  8.6 0.8 bitcast_or_fusion
  10.1 9.1 %bitcast_select_fusion.2 = f32[2048,1024]{1,0:T(8,128)} fusion(f32[1,2048,1024]{2,1,0:T(8,128)} %param.19, pred[256,8,8,128]{3,2,1,0:T(8,128)(4,1)S(1)} %bitcast.117), kind=kLoop, calls=%fused_computation.36 | loop fusion | flops 2097152 | bytes 18874368 | tf_op jit(solution)/shard_map/jit(_where)/select_n | solution.py:106
  19.2 15.2 %gather_fusion = f32[2048,1024]{1,0:T(8,128)} fusion(f32[2048,1024]{1,0:T(8,128)} %bitcast_select_fusion.2, s32[2048]{0:T(1024)S(1)} %fusion.32), kind=kCustom, calls=%fused_computation | custom fusion | bytes 16785408 | tf_op jit(solution)/shard_map/jit(_take)/gather | solution.py:129
  34.4 5.9 broadcast_select_fusion
  41.7 5.4 bitcast_select_fusion.3
  47.1 2.9 collective-permute-start
  50.6 2.0 bitcast_select_fusion.4
  53.4 278.7 %all-reduce.8.cloned.1.call-done = f32[2048,1024]{1,0:T(8,128)} async-done(((f32[2048,1024]{1,0:T(8,128)}), f32[2048,1024]{1,0:T(8,128)}) %all-reduce.8.cloned.1.call-update) | async-done | bytes 8388624 | tf_op jit(solution)/shard_map/psum | solution.py:130
  332.1 1.5 slice_select_fusion.2
  333.7 1.9 slice_select_fusion.1
  335.7 3.4 add_bitcast_fusion.1
  339.0 6.6 add.250
  345.6 1.5 collective-permute-start.1
  347.1 2.3 slice_select_fusion
  349.4 38.8 %all-reduce.10.cloned.1.call-done = f32[128,128]{1,0:T(8,128)} async-done(((f32[128,128]{1,0:T(8,128)}), f32[128,128]{1,0:T(8,128)}) %all-reduce.10.cloned.1.call-update) | async-done | bytes 65552 | tf_op jit(solution)/shard_map/psum | solution.py:16
  388.2 0.9 copy.21
  389.1 191.4 %while.54 = (s32[]{:T(128)}, f32[128,128]{0,1:T(8,128)S(1)}, s32[]{:T(128)}, s32[]{:T(128)}, s32[]{:T(128)}) while((s32[]{:T(128)}, f32[128,128]{0,1:T(8,128)S(1)}, s32[]{:T(128)}, s32[]{:T(128)}, s32[]{:T(128)}) %tuple.138), condition=%wide.region_3.4_spmd.clone.clone, body=%wide.region_2.3_spmd.clone.clone.sunk | while | flops 66435 | bytes 268381 | solution.py:85
  580.7 184.9 %while.56 = (s32[]{:T(128)}, f32[128,128]{1,0:T(8,128)S(1)}, f32[128,128]{1,0:T(8,128)S(1)}, s32[]{:T(128)}, s32[]{:T(128)}, /*index=5*/s32[]{:T(128)}, s32[]{:T(128)}) while((s32[]{:T(128)}, f32[128,128]{1,0:T(8,128)S(1)}, f32[128,128]{1,0:T(8,128)S(1)}, s32[]{:T(128)}, s32[]{:T(128)}, /*index=5*/s32[]{:T(128)}, ...), condition=%wide.region_10.11_spmd.clone.clone, body=%wide.region_9.10_spmd.clone.clone.sunk | while | flops 197383 | bytes 69279 | solution.py:57
  581.3 0.8 fusion.58
  582.8 0.8 fusion.58
  584.2 0.8 fusion.58
  585.7 0.8 fusion.58
  590.0 0.8 fusion.58
  591.5 0.8 fusion.58
  592.9 0.8 fusion.58
  594.3 0.8 fusion.58
  600.1 0.8 fusion.58
  765.6 26.2 %while.55 = (s32[]{:T(128)}, f32[128,128]{1,0:T(8,128)S(1)}, f32[128,128]{1,0:T(8,128)S(1)}, s32[]{:T(128)}, s32[]{:T(128)}) while((s32[]{:T(128)}, f32[128,128]{1,0:T(8,128)S(1)}, f32[128,128]{1,0:T(8,128)S(1)}, s32[]{:T(128)}, s32[]{:T(128)}) %tuple.144), condition=%wide.region_5.6_spmd.clone.clone, body=%wide.region_4.5_spmd.clone.clone.sunk | while | flops 197250 | bytes 69185 | solution.py:41
  791.9 1.6 fusion.35
  793.5 2.8 broadcast_select_fusion.1
  796.4 6.7 select_select_fusion
  803.1 6.6 add_bitcast_fusion
  (1435 shorter events, 387.5 us)
Async XLA Ops:
  7.2 325.0 %all-reduce.8.cloned.1.call-start = ((), (), s32[]{:S(2)}) async-start(), calls=%async_computation | async-start | bytes 16777216 | tf_op jit(solution)/shard_map/psum | solution.py:130
  40.3 0.7 copy-start
  40.4 347.8 %all-reduce.10.cloned.1.call-start = ((), (), s32[]{:S(2)}) async-start(), calls=%async_computation.1 | async-start | bytes 131072 | tf_op jit(solution)/shard_map/psum | solution.py:16
  41.7 8.4 %copy-start.1 = (s32[1,8,4]{1,2,0:T(4,128)S(1)}, s32[1,8,4]{1,2,0:T(4,128)}, u32[]{:S(2)}) copy-start(s32[1,8,4]{1,2,0:T(4,128)} %param.24) | copy-start | bytes 388
  47.1 291.9 %collective-permute-start = (f32[1536,768]{1,0:T(8,128)}, f32[1536,768]{1,0:T(8,128)}, u32[]{:S(2)}, u32[]{:S(2)}) collective-permute-start(f32[1536,768]{1,0:T(8,128)} %bitcast_select_fusion.3), channel_id=1, source_target_pairs={{0,8},{8,0},{16,24},{24,16},{1,9},{9,1},{17,25},{25,17},{2,10},{10... | collective-permute-start | bytes 14155784 | tf_op jit(solution)/shard_map/ppermute | solution.py:11
  52.6 283.1 %collective-permute-start.2 = (f32[1024,512]{1,0:T(8,128)S(1)}, f32[1024,512]{1,0:T(8,128)}, u32[]{:S(2)}, u32[]{:S(2)}) collective-permute-start(f32[1024,512]{1,0:T(8,128)S(1)} %bitcast_select_fusion.4), channel_id=1, source_target_pairs={{0,8},{8,0},{16,24},{24,16},{1,9},{9,1},{17,25},{25,17},{2,10},{10... | collective-permute-start | bytes 6291464 | tf_op jit(solution)/shard_map/ppermute | solution.py:11
  333.6 458.2 %all-reduce.12.cloned.1.call-start = ((), (), s32[]{:S(2)}) async-start(), calls=%async_computation.2 | async-start | bytes 1048576 | tf_op jit(solution)/shard_map/psum | solution.py:16
  335.6 457.9 %all-reduce.14.cloned.1.call-start = ((), (), s32[]{:S(2)}) async-start(), calls=%async_computation.3 | async-start | bytes 2097152 | tf_op jit(solution)/shard_map/psum | solution.py:16
  345.6 457.5 %collective-permute-start.1 = (f32[1536,768]{1,0:T(8,128)}, f32[1536,768]{1,0:T(8,128)}, u32[]{:S(2)}, u32[]{:S(2)}) collective-permute-start(f32[1536,768]{1,0:T(8,128)} %add.250), channel_id=1, source_target_pairs={{0,16},{8,24},{16,0},{24,8},{1,17},{9,25},{17,1},{25,9},{2,18},{10... | collective-permute-start | bytes 14155784 | tf_op jit(solution)/shard_map/ppermute | solution.py:11
Sparse Core Ops, SparseCore 0:
  40.5 291.6 all-reduce.7
  334.5 53.5 all-reduce.9
  390.5 17.8 all-reduce.11
  411.3 53.0 all-reduce.13
where the time goes:
time: 820 us; the launch traced here: 816 us
  waiting for transfers between devices  318 us (39%)
  local copies, waits for them, and re-layouts  196 us (24%)
  other arithmetic  142 us (17%)
  matrix products  128 us (16%)
  between operations  13.9 us (2%)
  loops' own time  13.4 us (2%)
    psum x1, waiting for transfers between devices, on_device(): summed = lax.psum(own_top, 'layer')  279 us
    dot_general x258, matrix products, highest_dot(): return jnp.dot(left, right, precision=lax.Precision.HIGHEST)  121 us
    dynamic_slice x128, local copies, waits for them, and re-layouts, substitute(): pivot_value = lax.dynamic_index_in_dim(row, step, 0, keepdims=False)  79.6 us
    dynamic_slice x127, local copies, waits for them, and re-layouts, eliminate(): pivot_value = lax.dynamic_index_in_dim(pivot_row, step, 0, keepdims=False)  78.9 us
    broadcast_in_dim x127, other arithmetic, eliminate(): return jnp.where(target, multipliers[:, None], current)  78.5 us
    psum x3, waiting for transfers between devices, spread(): return lax.psum(kept, axis)  38.8 us
    select_n x3, other arithmetic, local_part(): return jnp.where(kept, partial_value[0], jnp.float32(0.0))  16.5 us
  transfers between devices with their start and end apart: 7, of which 2 were waited for; matrix products, arithmetic and copies ran while one was open for 52% of the time, Pallas kernels for 0%

commit v1 on v0

v1 whole, which is shorter than its diff:
```python
import jax
import jax.numpy as jnp
from jax import lax
from jax.experimental import pallas as pl
from jax.experimental.pallas import tpu as pltpu
from jax.sharding import PartitionSpec as P

PANEL = 128
BLK = 128
EXTRA = 16
HIGHEST = lax.Precision.HIGHEST
VMEM_LIMIT = 48 * 1024 * 1024

SMEM_SPEC = pl.BlockSpec(memory_space=pltpu.SMEM)
VMEM_SPEC = pl.BlockSpec(memory_space=pltpu.VMEM)


def params():
    return pltpu.CompilerParams(vmem_limit_bytes=VMEM_LIMIT)


def cost(nbytes, flops=0):
    return pl.CostEstimate(flops=int(flops), bytes_accessed=int(nbytes), transcendentals=0)


def swapped(value, bit):
    count = lax.axis_size("layer")
    return lax.ppermute(value, "layer", [(i, i ^ (1 << bit)) for i in range(count)])


def broadcast_from_first(value, axis):
    count = lax.axis_size(axis)
    own = lax.axis_index(axis)
    span = count // 2
    while span >= 1:
        got = lax.ppermute(value, axis, [(i, i + span) for i in range(0, count, 2 * span)])
        value = jnp.where(own % (2 * span) == span, got, value)
        span //= 2
    return value


def exponents(largest):
    return jnp.floor(jnp.log2(jnp.maximum(largest, 1e-30))) - 14.0


def coded(value, inverse):
    scaled = jnp.round(value * inverse)
    scaled = jnp.minimum(jnp.maximum(scaled, -32767.0), 32767.0)
    return scaled.astype(jnp.int32).astype(jnp.int16)


def scales(code_ref, rows, cols):
    held = code_ref[pl.ds(rows, EXTRA), cols].astype(jnp.int32).astype(jnp.float32)
    return jnp.exp2(held[0:1])


def decoded(code_ref, row, scale, cols):
    return code_ref[pl.ds(row, BLK), cols].astype(jnp.int32).astype(jnp.float32) * scale


def encode_columns(load, out_ref, rows, cols):
    largest = jnp.zeros((1, BLK), jnp.float32)
    for i in range(rows // BLK):
        largest = jnp.maximum(largest, jnp.max(jnp.abs(load(i)), axis=0, keepdims=True))
    power = exponents(largest)
    inverse = jnp.exp2(-power)
    for i in range(rows // BLK):
        out_ref[pl.ds(i * BLK, BLK), cols] = coded(load(i), inverse)
    held = jnp.broadcast_to(power, (EXTRA, BLK))
    out_ref[pl.ds(rows, EXTRA), cols] = held.astype(jnp.int32).astype(jnp.int16)


def masked_load(place, pattern_ref, x_ref, rows, block_col, col):
    def load(i):
        block_row = place[0] * (rows // BLK) + i
        kept = (pattern_ref[block_row, block_col] == 1) | (place[1] + block_row == place[2] + block_col)
        value = x_ref[0, pl.ds(i * BLK, BLK), col]
        return jnp.where(kept, value, 0.0)

    return load


def encode_partial(partial, pattern, place, rows, first_block, blocks, received=None):
    width = partial.shape[2]

    def kernel(place_ref, pattern_ref, x_ref, *refs):
        out_ref = refs[-1]

        @pl.loop(0, blocks)
        def _(j):
            col_in = pl.ds(pl.multiple_of((j + first_block) * BLK, BLK), BLK)
            col_out = pl.ds(pl.multiple_of(j * BLK, BLK), BLK)
            load = masked_load(place_ref, pattern_ref, x_ref, rows, j + first_block, col_in)
            if received is not None:
                scale = scales(refs[0], rows, col_out)
                own = load
                load = lambda i: own(i) + decoded(refs[0], i * BLK, scale, col_out)
            encode_columns(load, out_ref, rows, col_out)

    if first_block == 0 and blocks * BLK < width:
        width = blocks * BLK
    shape = (rows + EXTRA, blocks * BLK)
    extra = [] if received is None else [received]
    return pl.pallas_call(
        kernel,
        grid_spec=pltpu.PrefetchScalarGridSpec(
            num_scalar_prefetch=2,
            grid=(1,),
            in_specs=[pl.BlockSpec((1, rows, width), lambda g, place_ref, pattern_ref: (0, place_ref[0], 0))]
            + [VMEM_SPEC] * len(extra),
            out_specs=VMEM_SPEC,
        ),
        out_shape=jax.ShapeDtypeStruct(shape, jnp.int16),
        compiler_params=params(),
        cost_estimate=cost(rows * width * 4 + rows * blocks * BLK * 2 * (1 + len(extra))),
    )(place, pattern, partial, *extra)


def merge(first, second):
    rows = first.shape[0] - EXTRA

    def kernel(a_ref, b_ref, out_ref):
        @pl.loop(0, first.shape[1] // BLK)
        def _(j):
            cols = pl.ds(pl.multiple_of(j * BLK, BLK), BLK)
            a_scale = scales(a_ref, rows, cols)
            b_scale = scales(b_ref, rows, cols)
            load = lambda i: decoded(a_ref, i * BLK, a_scale, cols) + decoded(b_ref, i * BLK, b_scale, cols)
            encode_columns(load, out_ref, rows, cols)

    return pl.pallas_call(
        kernel,
        in_specs=[VMEM_SPEC] * 2,
        out_specs=VMEM_SPEC,
        out_shape=jax.ShapeDtypeStruct(first.shape, jnp.int16),
        compiler_params=params(),
        cost_estimate=cost(first.size * 6),
    )(first, second)


def low_total(partial, pattern, place, received):
    _, rows, width = partial.shape

    def kernel(place_ref, pattern_ref, x_ref, code_ref, out_ref):
        @pl.loop(0, width // BLK)
        def _(j):
            cols = pl.ds(pl.multiple_of(j * BLK, BLK), BLK)
            scale = scales(code_ref, rows, cols)
            load = masked_load(place_ref, pattern_ref, x_ref, rows, j, cols)
            for i in range(rows // BLK):
                out_ref[0, pl.ds(i * BLK, BLK), cols] = load(i) + decoded(code_ref, i * BLK, scale, cols)

    return pl.pallas_call(
        kernel,
        in_specs=[SMEM_SPEC, SMEM_SPEC, VMEM_SPEC, VMEM_SPEC],
        out_specs=VMEM_SPEC,
        out_shape=jax.ShapeDtypeStruct(partial.shape, jnp.float32),
        compiler_params=params(),
        cost_estimate=cost(partial.size * 10),
    )(place, pattern, partial, received)


def mid_total(owner, own, received):
    rows, width = own.shape[0] - EXTRA, own.shape[1]

    def kernel(owner_ref, own_ref, got_ref, out_ref):
        def write(code_ref):
            @pl.loop(0, width // BLK)
            def _(j):
                cols = pl.ds(pl.multiple_of(j * BLK, BLK), BLK)
                scale = scales(code_ref, rows, cols)
                for i in range(rows // BLK):
                    out_ref[0, pl.ds(i * BLK, BLK), cols] = decoded(code_ref, i * BLK, scale, cols)

        is_own = pl.program_id(0) == owner_ref[0]
        pl.when(is_own)(lambda: write(own_ref))
        pl.when(jnp.logical_not(is_own))(lambda: write(got_ref))

    return pl.pallas_call(
        kernel,
        grid=(2,),
        in_specs=[SMEM_SPEC, VMEM_SPEC, VMEM_SPEC],
        out_specs=pl.BlockSpec((1, rows, width), lambda g: (0, g, 0)),
        out_shape=jax.ShapeDtypeStruct((1, 2 * rows, width), jnp.float32),
        compiler_params=params(),
        cost_estimate=cost(own.size * 12),
    )(owner, own, received)


def factor(corner):
    order = corner.shape[0]

    def kernel(a_ref, packed_ref, lower_ref, upper_ref, direct, direct_unit, turned, turned_unit):
        lane = lax.broadcasted_iota(jnp.int32, (order, order), 1)
        sub = lax.broadcasted_iota(jnp.int32, (order, order), 0)
        lane_row = lax.broadcasted_iota(jnp.int32, (1, order), 1)
        sub_col = lax.broadcasted_iota(jnp.int32, (order, 1), 0)
        unit = (lane == sub).astype(jnp.float32)
        direct[...] = a_ref[...]
        direct_unit[...] = unit
        turned[...] = a_ref[...].T
        turned_unit[...] = unit

        @pl.loop(0, order - 1)
        def _(k):
            for held, held_unit in ((direct, direct_unit), (turned, turned_unit)):
                left = held[...]
                row_left = held[pl.ds(k, 1), :]
                row_right = held_unit[pl.ds(k, 1), :]
                col = jnp.sum(jnp.where(lane == k, left, 0.0), axis=1, keepdims=True)
                pivot = jnp.sum(jnp.where(lane_row == k, row_left, 0.0), axis=1, keepdims=True)
                below = sub_col > k
                multipliers = jnp.where(below, col / pivot, 0.0)
                fresh = left - multipliers * jnp.where(lane_row > k, row_left, 0.0)
                held[...] = jnp.where((lane == k) & below, multipliers, fresh)
                held_unit[...] = held_unit[...] - multipliers * row_right

        packed_ref[...] = direct[...]
        lower_ref[...] = direct_unit[...]
        pivots = jnp.sum(jnp.where(lane == sub, turned[...], 0.0), axis=1, keepdims=True)
        upper_ref[...] = (turned_unit[...] / pivots).T

    shape = jax.ShapeDtypeStruct((order, order), jnp.float32)
    return pl.pallas_call(
        kernel,
        in_specs=[VMEM_SPEC],
        out_specs=[VMEM_SPEC] * 3,
        out_shape=[shape] * 3,
        scratch_shapes=[pltpu.VMEM((order, order), jnp.float32)] * 4,
        compiler_params=params(),
        cost_estimate=cost(order * order * 16, 2e9),
    )(corner)


def exact_dot(left, right):
    return jnp.dot(left, right, precision=HIGHEST, preferred_element_type=jnp.float32)


def low_dot(left, right):
    return jnp.dot(left, right, preferred_element_type=jnp.float32)


def permuted_codes(order_block, codes, scale):
    codes = codes.astype(jnp.int32)
    high = (codes >> 8).astype(jnp.float32).astype(jnp.bfloat16)
    low = (codes & 255).astype(jnp.float32).astype(jnp.bfloat16)
    return (low_dot(order_block, high) * 256.0 + low_dot(order_block, low)) * scale


def lower_panel(flags, order, own, received, upper_inverse):
    rows = own.shape[0] - EXTRA

    def kernel(flag_ref, order_ref, own_ref, got_ref, inverse_ref, slab_ref, low_ref):
        cols = pl.ds(0, PANEL)
        own_scale = scales(own_ref, rows, cols)
        got_scale = scales(got_ref, rows, cols)
        first_col = flag_ref[3] == 0

        @pl.loop(0, rows // BLK)
        def _(i):
            row = pl.multiple_of(i * BLK, BLK)
            summed = decoded(own_ref, row, own_scale, cols) + decoded(got_ref, row, got_scale, cols)
            summed = exact_dot(order_ref[pl.ds(row, BLK), :].astype(jnp.float32), summed)
            panel = exact_dot(summed, inverse_ref[...])
            low_ref[pl.ds(row, BLK), :] = panel.astype(jnp.bfloat16)
            slab_ref[pl.ds(row, BLK), :] = jnp.where(first_col, panel, summed)

    return pl.pallas_call(
        kernel,
        in_specs=[SMEM_SPEC] + [VMEM_SPEC] * 4,
        out_specs=[VMEM_SPEC] * 2,
        out_shape=[
            jax.ShapeDtypeStruct((rows, PANEL), jnp.float32),
            jax.ShapeDtypeStruct((rows, PANEL), jnp.bfloat16),
        ],
        compiler_params=params(),
        cost_estimate=cost(rows * PANEL * 14, rows * PANEL * PANEL * 24),
    )(flags, order, own, received, upper_inverse)


def upper_panel(flags, order, slab, own, received, lower_inverse):
    rows, rest = own.shape[0] - EXTRA, own.shape[1]
    width = rest + PANEL

    def kernel(flag_ref, order_ref, slab_ref, own_ref, own_scale, got_ref, got_scale, inverse_ref, up_ref, low_ref):
        first = exact_dot(inverse_ref[...], slab_ref[...])
        up_ref[:, :PANEL] = first
        low_ref[:, :PANEL] = first.astype(jnp.bfloat16)

        def write(code_ref, scale_ref):
            scale = jnp.exp2(scale_ref[...].astype(jnp.int32).astype(jnp.float32)[0:1])
            value = permuted_codes(order_ref[...], code_ref[...], scale)
            value = exact_dot(inverse_ref[...], value)
            up_ref[:, PANEL:] = value
            low_ref[:, PANEL:] = value.astype(jnp.bfloat16)

        pl.when(flag_ref[0] == 0)(lambda: write(own_ref, own_scale))
        pl.when(flag_ref[0] == 1)(lambda: write(got_ref, got_scale))

    first_block = lambda g: (0, 0)
    code_spec = pl.BlockSpec((BLK, rest), first_block)
    scale_spec = pl.BlockSpec((EXTRA, rest), lambda g: (rows // EXTRA, 0))
    square = pl.BlockSpec((BLK, BLK), first_block)
    return pl.pallas_call(
        kernel,
        grid=(1,),
        in_specs=[SMEM_SPEC, square, square, code_spec, scale_spec, code_spec, scale_spec, square],
        out_specs=[pl.BlockSpec((BLK, width), first_block)] * 2,
        out_shape=[
            jax.ShapeDtypeStruct((PANEL, width), jnp.float32),
            jax.ShapeDtypeStruct((PANEL, width), jnp.bfloat16),
        ],
        compiler_params=params(),
        cost_estimate=cost(BLK * width * 10, BLK * BLK * width * 16),
    )(flags, order, slab, own, own, received, received, lower_inverse)


def top_total(flags, order, codes, slab, lower_low, upper_low, upper, packed):
    total_rows = slab.shape[0]
    rows, rest = codes[0].shape[0] - EXTRA, codes[0].shape[1]
    width = rest + PANEL
    part_blocks = rows // BLK

    def kernel(flag_ref, order_ref, own_a, got_a, own_b, got_b, slab_ref, low_ref, up_low_ref, up_ref, packed_ref, out_ref):
        i = pl.program_id(0)
        part = i // part_blocks
        row = pl.multiple_of((i % part_blocks) * BLK, BLK)
        first_row = (flag_ref[2] == 0) & (i == 0)
        first_col = flag_ref[3] == 0
        rest_cols = pl.ds(0, rest)

        @pl.when(jnp.logical_not(first_row))
        def _():
            low = low_ref[...]

            def write(code_ref):
                scale = scales(code_ref, rows, rest_cols)
                value = permuted_codes(order_ref[...], code_ref[pl.ds(row, BLK), :], scale)
                out_ref[:, PANEL:] = value - low_dot(low, up_low_ref[:, PANEL:])

            owned_a = part == flag_ref[0]
            owned_b = part == 2 + flag_ref[1]
            pl.when(owned_a)(lambda: write(own_a))
            pl.when((part < 2) & jnp.logical_not(owned_a))(lambda: write(got_a))
            pl.when(owned_b)(lambda: write(own_b))
            pl.when((part >= 2) & jnp.logical_not(owned_b))(lambda: write(got_b))
            product = low_dot(low, up_low_ref[:, :PANEL])
            out_ref[:, :PANEL] = jnp.where(first_col, slab_ref[...], slab_ref[...] - product)

        @pl.when(first_row)
        def _():
            out_ref[:, PANEL:] = up_ref[:, PANEL:]
            out_ref[:, :PANEL] = jnp.where(first_col, packed_ref[...], up_ref[:, :PANEL])

    square = pl.BlockSpec((BLK, BLK), lambda i: (i, 0))
    return pl.pallas_call(
        kernel,
        grid=(total_rows // BLK,),
        in_specs=[SMEM_SPEC, square] + [VMEM_SPEC] * 4 + [square, square] + [VMEM_SPEC] * 3,
        out_specs=pl.BlockSpec((BLK, width), lambda i: (i, 0)),
        out_shape=jax.ShapeDtypeStruct((total_rows, width), jnp.float32),
        compiler_params=params(),
        cost_estimate=cost(total_rows * width * 6, total_rows * width * BLK * 6),
    )(flags, order, *codes, slab, lower_low, upper_low, upper, packed)


def reduced(partial, pattern, first_place, own_place, rows, first_block, blocks, first_bit, bits):
    sent = encode_partial(partial, pattern, first_place, rows, first_block, blocks)
    own = encode_partial(partial, pattern, own_place, rows, first_block, blocks, swapped(sent, first_bit))
    for bit in bits:
        if bit != first_bit:
            own = merge(own, swapped(own, bit))
    return own, swapped(own, first_bit)


def on_device(partial_top, partial_mid, partial_low, pattern_top, pattern_mid, pattern_low, pivots):
    layer, row, col = (lax.axis_index(name) for name in ("layer", "row", "col"))
    bits = range(lax.axis_size("layer").bit_length() - 1)
    low_bit, high_bit = layer & 1, (layer >> 1) & 1
    flags = jnp.stack([low_bit, high_bit, row, col]).astype(jnp.int32)
    order = ((pivots % BLK)[:, None] == jnp.arange(BLK, dtype=jnp.int32)[None, :]).astype(jnp.bfloat16)

    def place(part, pattern):
        first_row, first_col = row * pattern.shape[1], col * pattern.shape[2]
        return jnp.stack([jnp.asarray(part, jnp.int32), first_row, first_col]).astype(jnp.int32)

    corner = exact_dot(order[:BLK].astype(jnp.float32), partial_top[0, :BLK, :BLK])
    for bit in bits:
        corner = corner + swapped(corner, bit)
    corner = broadcast_from_first(broadcast_from_first(corner, "row"), "col")

    mid_rows = partial_mid.shape[1] // 2
    mid_blocks = partial_mid.shape[2] // BLK
    mid_own, mid_got = reduced(
        partial_mid, pattern_mid[0], place(1 - high_bit, pattern_mid), place(high_bit, pattern_mid),
        mid_rows, 0, mid_blocks, 1, bits[:2],
    )

    top_rows = partial_top.shape[1]
    top_blocks = partial_top.shape[2] // BLK
    pattern = pattern_top[0]
    slab_own = encode_partial(partial_top, pattern, place(0, pattern_top), top_rows, 0, 1)
    for bit in bits[:-1]:
        slab_own = merge(slab_own, swapped(slab_own, bit))
    slab_got = swapped(slab_own, bits[-1])

    part_rows = top_rows // 4
    a_own, a_got = reduced(
        partial_top, pattern, place(1 - low_bit, pattern_top), place(low_bit, pattern_top),
        part_rows, 1, top_blocks - 1, 0, bits,
    )
    b_own, b_got = reduced(
        partial_top, pattern, place(3 - high_bit, pattern_top), place(2 + high_bit, pattern_top),
        part_rows, 1, top_blocks - 1, 1, bits,
    )

    low_rows = partial_low.shape[1]
    low_place = place(0, pattern_low)
    low_sent = encode_partial(partial_low, pattern_low[0], low_place, low_rows, 0, partial_low.shape[2] // BLK)
    low_sums = low_total(partial_low, pattern_low[0], low_place, swapped(low_sent, 0))

    packed, lower_inverse, upper_inverse = factor(corner)
    slab, lower_low = lower_panel(flags, order, slab_own, slab_got, upper_inverse)
    lower_low = broadcast_from_first(lower_low, "col")
    upper, upper_low = upper_panel(flags, order, slab, a_own, a_got, lower_inverse)
    upper_low = broadcast_from_first(upper_low, "row")
    top_factor = top_total(flags, order, (a_own, a_got, b_own, b_got), slab, lower_low, upper_low, upper, packed)
    mid_sums = mid_total(high_bit[None].astype(jnp.int32), mid_own, mid_got)
    return top_factor, mid_sums, low_sums


def solution(mesh):
    placed = (
        P("layer", "row", "col"),
        P("layer", "row", "col"),
        P("layer", "row", "col"),
        P("layer", "row", "col"),
        P("layer", "row", "col"),
        P("layer", "row", "col"),
        P("row"),
    )
    return jax.shard_map(
        on_device,
        mesh=mesh,
        in_specs=placed,
        out_specs=(P("row", "col"), P("layer", "row", "col"), P("layer", "row", "col")),
        check_vma=False,
    )
```

time: 820 us -> 208 us (0.25)
  waiting for transfers between devices: 318 us -> 89.5 us
  local copies, waits for them, and re-layouts: 196 us -> 5.4 us
  other arithmetic: 142 us -> 3.07 us
  matrix products: 128 us -> 1.02 us
  Pallas kernels: 0 us -> 74.9 us
  starting transfers between devices: 4.75 us -> 31.3 us
  loops' own time: 13.4 us -> 0 us
  between operations: 13.9 us -> 0.83 us
    psum x4 -> x0, waiting for transfers between devices: 318 us -> none  [the longest x1 279 us: on_device(): summed = lax.psum(own_top, 'layer')]
    dynamic_slice x255 -> x0, local copies, waits for them, and re-layouts: 159 us -> none  [the longest x128 79.6 us: substitute(): pivot_value = lax.dynamic_index_in_dim(row, step, 0, keepdims=False)]
    dot_general x259 -> x1, matrix products: 128 us -> 1.02 us  [exact_dot(): jnp.dot(left, right, precision=HIGHEST, preferred_element_type=jnp.float32)]
    ppermute x3 -> x20, waiting for transfers between devices: 0.01 us -> 89.5 us  [the longest x14 86.2 us: swapped(): lax.ppermute(value, 'layer', [(i, i ^ 1 << bit) for i in range(count)])]
    broadcast_in_dim x129 -> x0, other arithmetic: 88.5 us -> none  [the longest x127 78.5 us: eliminate(): return jnp.where(target, multipliers[:, None], current)]
    pallas_call x0 -> x18, Pallas kernels: none -> 74.9 us  [the longest x8 24.9 us: encode_partial(): pl.pallas_call(kernel, grid_spec=pltpu.PrefetchScalarGridSpec(num_scalar_...]
    select_n x134 -> x7, other arithmetic: 41.6 us -> 1.93 us  [the longest x6 1.23 us: broadcast_from_first(): value = jnp.where(own % (2 * span) == span, got, value)]
    ppermute x3 -> x20, starting transfers between devices: 4.58 us -> 31.3 us  [the longest x14 16.3 us: swapped(): lax.ppermute(value, 'layer', [(i, i ^ 1 << bit) for i in range(count)])]
  transfers between devices with their start and end apart: 7 -> 20, of which waited for: 2 -> 8; matrix products, arithmetic and copies ran while one was open for 52% -> 1% of each run, Pallas kernels for 0% -> 35%
where the time goes in v1:
time: 208 us; the launch traced here: 206 us
  waiting for transfers between devices  89.5 us (43%)
  Pallas kernels  74.9 us (36%)
  starting transfers between devices  31.3 us (15%)
  local copies, waits for them, and re-layouts  5.4 us (3%)
  other arithmetic  3.07 us (1%)
    ppermute x14, waiting for transfers between devices, swapped(): lax.ppermute(value, 'layer', [(i, i ^ 1 << bit) for i in range(count)])  86.2 us
    pallas_call x8, Pallas kernels, encode_partial(): pl.pallas_call(kernel, grid_spec=pltpu.PrefetchScalarGridSpec(num_scalar_...  24.9 us
    ppermute x14, starting transfers between devices, swapped(): lax.ppermute(value, 'layer', [(i, i ^ 1 << bit) for i in range(count)])  16.3 us
    pallas_call x1, Pallas kernels, factor(): pl.pallas_call(kernel, in_specs=[VMEM_SPEC], out_specs=[VMEM_SPEC] * 3, o...  15.3 us
    ppermute x6, starting transfers between devices, broadcast_from_first(): lax.ppermute(value, axis, [(i, i + span) for i in range(0, count, 2 * spa...  15 us
    pallas_call x1, Pallas kernels, top_total(): pl.pallas_call(kernel, grid=(total_rows // BLK,), in_specs=[SMEM_SPEC, sq...  13 us
    pallas_call x1, Pallas kernels, lower_panel(): pl.pallas_call(kernel, in_specs=[SMEM_SPEC] + [VMEM_SPEC] * 4, out_specs=...  8.53 us
    pallas_call x4, Pallas kernels, merge(): pl.pallas_call(kernel, in_specs=[VMEM_SPEC] * 2, out_specs=VMEM_SPEC, out...  6.83 us
  transfers between devices with their start and end apart: 20, of which 8 were waited for; matrix products, arithmetic and copies ran while one was open for 1% of the time, Pallas kernels for 35%

profile of v1, /device:TPU:0, one launch (start us, length us, event | category | flops | bytes accessed | tf_op | source)
XLA Modules:
  0.0 206.0 jit_solution(14183444771713707111)
XLA Ops:
  2.8 3.0 %collective-permute-start.8 = (f32[128,128]{1,0:T(8,128)S(1)}, f32[128,128]{1,0:T(8,128)S(1)}, u32[]{:S(2)}, u32[]{:S(2)}) collective-permute-start(f32[128,128]{1,0:T(8,128)S(1)} %fusion), channel_id=1, source_target_pairs={{0,8},{8,0},{16,24},{24,16},{1,9},{9,1},{17,25},{25,17},{2,10},{10... | collective-permute-start | bytes 196616 | tf_op jit(solution)/shard_map/ppermute | solution.py:28
  6.6 3.9 %shard_map.94 = s16[528,896]{1,0:T(8,128)(2,1)} custom-call(s32[3]{0:T(128)S(1)} %add_add_fusion.1.place_ref, s32[16,8]{1,0:T(8,128)S(1)} %copy.11.pattern_ref, f32[1,2048,1024]{2,1,0:T(8,128)} %x_ref.13), custom_call_target="tpu_custom_call" | custom-call | bytes 3014656 | tf_op jit(solution)/shard_map/pallas_call | solution.py:104
  10.7 2.1 %shard_map.100.a_ref = s16[2064,128]{1,0:T(8,128)(2,1)S(1)} custom-call(s32[3]{0:T(128)S(1)} %fusion.6.place_ref, s32[16,8]{1,0:T(8,128)S(1)} %copy.11.pattern_ref, f32[1,2048,1024]{2,1,0:T(8,128)} %x_ref.13), custom_call_target="tpu_custom_call" | custom-call | bytes 1572864 | tf_op jit(solution)/shard_map/pallas_call | solution.py:104
  12.8 2.1 %collective-permute-start.6 = (s16[2064,128]{1,0:T(8,128)(2,1)S(1)}, s16[2064,128]{1,0:T(8,128)(2,1)S(1)}, u32[]{:S(2)}, u32[]{:S(2)}) collective-permute-start(s16[2064,128]{1,0:T(8,128)(2,1)S(1)} %shard_map.100.a_ref), channel_id=1, source_target_pairs={{0,8},{8,0},{16,24},{24,16},{1,9},{9,1},{17,25},{25,17},{2,10},{10... | collective-permute-start | bytes 1585160 | tf_op jit(solution)/shard_map/ppermute | solution.py:28
  14.9 1.6 collective-permute-start.9
  16.6 3.9 %shard_map.97 = s16[528,896]{1,0:T(8,128)(2,1)} custom-call(s32[3]{0:T(128)S(1)} %add_add_fusion.3.place_ref, s32[16,8]{1,0:T(8,128)S(1)} %copy.11.pattern_ref, f32[1,2048,1024]{2,1,0:T(8,128)} %x_ref.13), custom_call_target="tpu_custom_call" | custom-call | bytes 3014656 | tf_op jit(solution)/shard_map/pallas_call | solution.py:104
  22.5 2.3 %copy-done = f32[1,1536,768]{2,1,0:T(8,128)S(1)} copy-done((f32[1,1536,768]{2,1,0:T(8,128)S(1)}, f32[1,1536,768]{2,1,0:T(8,128)}, u32[]{:S(2)}) %copy-start) | copy-done | bytes 4718616
  24.8 2.4 %shard_map.106 = s16[784,768]{1,0:T(8,128)(2,1)} custom-call(s32[3]{0:T(128)S(1)} %add_add_fusion.5.place_ref, s32[12,6]{1,0:T(8,128)S(1)} %bitcast.20, f32[1,1536,768]{2,1,0:T(8,128)S(1)} %copy-done), custom_call_target="tpu_custom_call" | custom-call | bytes 3538944 | tf_op jit(solution)/shard_map/pallas_call | solution.py:104
  27.2 1.5 collective-permute-start.16
  28.8 4.5 %collective-permute-start.11 = (f32[128,128]{1,0:T(8,128)S(1)}, f32[128,128]{1,0:T(8,128)S(1)}, u32[]{:S(2)}, u32[]{:S(2)}) collective-permute-start(f32[128,128]{1,0:T(8,128)S(1)} %broadcast_select_fusion.3), channel_id=1, source_target_pairs={{0,2},{4,6},{8,10},{12,14},{16,18},{20,22},{24,26},{28,30}} | collective-permute-start | bytes 196616 | tf_op jit(solution)/shard_map/ppermute | solution.py:36
  33.4 2.2 %collective-permute-done.11 = f32[128,128]{1,0:T(8,128)S(1)} collective-permute-done((f32[128,128]{1,0:T(8,128)S(1)}, f32[128,128]{1,0:T(8,128)S(1)}, u32[]{:S(2)}, u32[]{:S(2)}) %collective-permute-start.11) | collective-permute-done | bytes 65568 | tf_op jit(solution)/shard_map/ppermute | solution.py:36
  36.9 7.7 %collective-permute-done.6.b_ref = s16[2064,128]{1,0:T(8,128)(2,1)S(1)} collective-permute-done((s16[2064,128]{1,0:T(8,128)(2,1)S(1)}, s16[2064,128]{1,0:T(8,128)(2,1)S(1)}, u32[]{:S(2)}, u32[]{:S(2)}) %collective-permute-start.6) | collective-permute-done | bytes 528416 | tf_op jit(solution)/shard_map/ppermute | solution.py:28
  45.2 1.6 collective-permute-start.7
  46.9 4.0 %shard_map.95.a_ref = s16[528,896]{1,0:T(8,128)(2,1)} custom-call(s32[3]{0:T(128)S(1)} %add_add_fusion.place_ref, s32[16,8]{1,0:T(8,128)S(1)} %copy.11.pattern_ref, f32[1,2048,1024]{2,1,0:T(8,128)} %x_ref.13, s16[528,896]{1,0:T(8,128)(2,1)S(1)} %collective-permute-done.refs_0_), custom_call_target="tpu_custom_call" | custom-call | bytes 3932160 | tf_op jit(solution)/shard_map/pallas_call | solution.py:104
  51.4 15.3 %shard_map.102 = (f32[128,128]{1,0:T(8,128)S(1)}, f32[128,128]{1,0:T(8,128)S(1)}, f32[128,128]{1,0:T(8,128)S(1)}) custom-call(f32[128,128]{1,0:T(8,128)S(1)} %broadcast_select_fusion.5.a_ref), custom_call_target="tpu_custom_call" | custom-call | flops 2000000000 | bytes 262144 | tf_op jit(solution)/shard_map/pallas_call | solution.py:224
  66.7 15.1 %collective-permute-done.7.got_ref = s16[2064,128]{1,0:T(8,128)(2,1)S(1)} collective-permute-done((s16[2064,128]{1,0:T(8,128)(2,1)S(1)}, s16[2064,128]{1,0:T(8,128)(2,1)S(1)}, u32[]{:S(2)}, u32[]{:S(2)}) %collective-permute-start.7) | collective-permute-done | bytes 528416 | tf_op jit(solution)/shard_map/ppermute | solution.py:28
  81.7 8.5 %shard_map.103 = (f32[2048,128]{1,0:T(8,128)S(1)}, bf16[2048,128]{1,0:T(8,128)(2,1)}) custom-call(s32[4]{0:T(128)S(1)} %pad_add_fusion.2.flag_ref, bf16[2048,128]{1,0:T(8,128)(2,1)S(1)} %get-tuple-element.18.order_ref, s16[2064,128]{1,0:T(8,128)(2,1)S(1)} %shard_map.101.own_ref, s16[2064,128]{1,0:T(8,128)(2,1)S(1)} %collective-permute-done.7.got_ref, ...), custom_call_target="tpu_custom_call" | custom-call | flops 805306368 | bytes 3670016 | tf_op jit(solution)/shard_map/pallas_call | solution.py:268
  90.3 5.3 %collective-permute-start.13 = (bf16[2048,128]{1,0:T(8,128)(2,1)}, bf16[2048,128]{1,0:T(8,128)(2,1)}, u32[]{:S(2)}, u32[]{:S(2)}) collective-permute-start(bf16[2048,128]{1,0:T(8,128)(2,1)} %get-tuple-element.12), channel_id=1, source_target_pairs={{0,2},{4,6},{8,10},{12,14},{16,18},{20,22},{24,26},{28,30}} | collective-permute-start | bytes 1572872 | tf_op jit(solution)/shard_map/ppermute | solution.py:36
  95.6 3.9 %shard_map.107.a_ref = s16[784,768]{1,0:T(8,128)(2,1)S(1)} custom-call(s32[3]{0:T(128)S(1)} %add_add_fusion.4.place_ref, s32[12,6]{1,0:T(8,128)S(1)} %bitcast.21, f32[1,1536,768]{2,1,0:T(8,128)} %x_ref.15, s16[784,768]{1,0:T(8,128)(2,1)} %collective-permute-done.16.refs_0_), custom_call_target="tpu_custom_call" | custom-call | bytes 4718592 | tf_op jit(solution)/shard_map/pallas_call | solution.py:104
  100.3 3.4 %shard_map.98.a_ref = s16[528,896]{1,0:T(8,128)(2,1)S(1)} custom-call(s32[3]{0:T(128)S(1)} %add_add_fusion.2.place_ref, s32[16,8]{1,0:T(8,128)S(1)} %copy.11.pattern_ref, f32[1,2048,1024]{2,1,0:T(8,128)} %x_ref.13, s16[528,896]{1,0:T(8,128)(2,1)} %collective-permute-done.3.refs_0_), custom_call_target="tpu_custom_call" | custom-call | bytes 3932160 | tf_op jit(solution)/shard_map/pallas_call | solution.py:104
  103.6 1.6 collective-permute-start.4
  107.2 2.5 %shard_map.96.own_ref.own_scale.own_a = s16[528,896]{1,0:T(8,128)(2,1)S(1)} custom-call(s16[528,896]{1,0:T(8,128)(2,1)} %shard_map.95.a_ref, s16[528,896]{1,0:T(8,128)(2,1)} %collective-permute-done.1.b_ref), custom_call_target="tpu_custom_call" | custom-call | bytes 2838528 | tf_op jit(solution)/shard_map/pallas_call | solution.py:131
  109.7 1.5 collective-permute-start.2
  113.7 15.4 %collective-permute-done.17.b_ref = s16[784,768]{1,0:T(8,128)(2,1)} collective-permute-done((s16[784,768]{1,0:T(8,128)(2,1)S(1)}, s16[784,768]{1,0:T(8,128)(2,1)}, u32[]{:S(2)}, u32[]{:S(2)}) %collective-permute-start.17) | collective-permute-done | bytes 1204256 | tf_op jit(solution)/shard_map/ppermute | solution.py:28
  129.1 2.7 %shard_map.108.own_ref = s16[784,768]{1,0:T(8,128)(2,1)S(1)} custom-call(s16[784,768]{1,0:T(8,128)(2,1)S(1)} %shard_map.107.a_ref, s16[784,768]{1,0:T(8,128)(2,1)} %collective-permute-done.17.b_ref), custom_call_target="tpu_custom_call" | custom-call | bytes 3612672 | tf_op jit(solution)/shard_map/pallas_call | solution.py:131
  132.4 16.9 %collective-permute-done.4.b_ref = s16[528,896]{1,0:T(8,128)(2,1)S(1)} collective-permute-done((s16[528,896]{1,0:T(8,128)(2,1)S(1)}, s16[528,896]{1,0:T(8,128)(2,1)S(1)}, u32[]{:S(2)}, u32[]{:S(2)}) %collective-permute-start.4) | collective-permute-done | bytes 946208 | tf_op jit(solution)/shard_map/ppermute | solution.py:28
  153.0 19.1 %collective-permute-done.19.code_ref = s16[1040,512]{1,0:T(8,128)(2,1)S(1)} collective-permute-done((s16[1040,512]{1,0:T(8,128)(2,1)S(1)}, s16[1040,512]{1,0:T(8,128)(2,1)S(1)}, u32[]{:S(2)}, u32[]{:S(2)}) %collective-permute-start.19) | collective-permute-done | bytes 1064992 | tf_op jit(solution)/shard_map/ppermute | solution.py:28
  172.1 2.4 %shard_map.111 = f32[1,1024,512]{2,1,0:T(8,128)} custom-call(s32[3]{0:T(128)S(1)} %fusion.7.place_ref, s32[8,4]{1,0:T(8,128)S(1)} %copy.18.pattern_ref, f32[1,1024,512]{2,1,0:T(8,128)S(1)} %copy-done.1, s16[1040,512]{1,0:T(8,128)(2,1)S(1)} %collective-permute-done.19.code_ref), custom_call_target="tpu_custom_call" | custom-call | bytes 5242880 | tf_op jit(solution)/shard_map/pallas_call | solution.py:153
  174.5 12.1 %collective-permute-done.2.got_ref.got_scale.got_a = s16[528,896]{1,0:T(8,128)(2,1)S(1)} collective-permute-done((s16[528,896]{1,0:T(8,128)(2,1)S(1)}, s16[528,896]{1,0:T(8,128)(2,1)S(1)}, u32[]{:S(2)}, u32[]{:S(2)}) %collective-permute-start.2) | collective-permute-done | bytes 946208 | tf_op jit(solution)/shard_map/ppermute | solution.py:28
  186.5 1.6 shard_map.104
  190.6 13.0 %shard_map.105 = f32[2048,1024]{1,0:T(8,128)} custom-call(s32[4]{0:T(128)S(1)} %pad_add_fusion.2.flag_ref, bf16[2048,128]{1,0:T(8,128)(2,1)S(1)} %get-tuple-element.18.order_ref, s16[528,896]{1,0:T(8,128)(2,1)S(1)} %shard_map.96.own_ref.own_scale.own_a, s16[528,896]{1,0:T(8,128)(2,1)S(1)} %collective-permute-done.2.got_ref.got_scale.got_a, ...), custom_call_target="tpu_custom_call" | custom-call | flops 1610612736 | bytes 12582912 | tf_op jit(solution)/shard_map/pallas_call | solution.py:356
  203.6 2.4 %shard_map.109 = f32[1,1536,768]{2,1,0:T(8,128)} custom-call(s32[1]{0:T(128)} %bitcast.1.owner_ref, s16[784,768]{1,0:T(8,128)(2,1)S(1)} %shard_map.108.own_ref, s16[784,768]{1,0:T(8,128)(2,1)S(1)} %collective-permute-done.18.got_ref), custom_call_target="tpu_custom_call" | custom-call | bytes 7225344 | tf_op jit(solution)/shard_map/pallas_call | solution.py:179
  (63 shorter events, 19.8 us)
Async XLA Ops:
  2.8 12.1 %collective-permute-start.8 = (f32[128,128]{1,0:T(8,128)S(1)}, f32[128,128]{1,0:T(8,128)S(1)}, u32[]{:S(2)}, u32[]{:S(2)}) collective-permute-start(f32[128,128]{1,0:T(8,128)S(1)} %fusion), channel_id=1, source_target_pairs={{0,8},{8,0},{16,24},{24,16},{1,9},{9,1},{17,25},{25,17},{2,10},{10... | collective-permute-start | bytes 196616 | tf_op jit(solution)/shard_map/ppermute | solution.py:28
  10.6 36.3 %collective-permute-start = (s16[528,896]{1,0:T(8,128)(2,1)}, s16[528,896]{1,0:T(8,128)(2,1)S(1)}, u32[]{:S(2)}, u32[]{:S(2)}) collective-permute-start(s16[528,896]{1,0:T(8,128)(2,1)} %shard_map.94), channel_id=1, source_target_pairs={{0,8},{8,0},{16,24},{24,16},{1,9},{9,1},{17,25},{25,17},{2,10},{10... | collective-permute-start | bytes 2838536 | tf_op jit(solution)/shard_map/ppermute | solution.py:28
  12.8 31.7 %collective-permute-start.6 = (s16[2064,128]{1,0:T(8,128)(2,1)S(1)}, s16[2064,128]{1,0:T(8,128)(2,1)S(1)}, u32[]{:S(2)}, u32[]{:S(2)}) collective-permute-start(s16[2064,128]{1,0:T(8,128)(2,1)S(1)} %shard_map.100.a_ref), channel_id=1, source_target_pairs={{0,8},{8,0},{16,24},{24,16},{1,9},{9,1},{17,25},{25,17},{2,10},{10... | collective-permute-start | bytes 1585160 | tf_op jit(solution)/shard_map/ppermute | solution.py:28
  14.9 6.2 %collective-permute-start.9 = (f32[128,128]{1,0:T(8,128)S(1)}, f32[128,128]{1,0:T(8,128)S(1)}, u32[]{:S(2)}, u32[]{:S(2)}) collective-permute-start(f32[128,128]{1,0:T(8,128)S(1)} %add.33), channel_id=1, source_target_pairs={{0,16},{8,24},{16,0},{24,8},{1,17},{9,25},{17,1},{25,9},{2,18},{10... | collective-permute-start | bytes 196616 | tf_op jit(solution)/shard_map/ppermute | solution.py:28
  16.6 4.5 %copy-start.5 = (s32[1,12,6]{1,0,2:T(1,128)S(1)}, s32[1,12,6]{1,0,2:T(1,128)}, u32[]{:S(2)}) copy-start(s32[1,12,6]{1,0,2:T(1,128)} %param.11) | copy-start | bytes 868
  20.5 79.8 %collective-permute-start.3 = (s16[528,896]{1,0:T(8,128)(2,1)}, s16[528,896]{1,0:T(8,128)(2,1)}, u32[]{:S(2)}, u32[]{:S(2)}) collective-permute-start(s16[528,896]{1,0:T(8,128)(2,1)} %shard_map.97), channel_id=1, source_target_pairs={{0,16},{8,24},{16,0},{24,8},{1,17},{9,25},{17,1},{25,9},{2,18},{10... | collective-permute-start | bytes 2838536 | tf_op jit(solution)/shard_map/ppermute | solution.py:28
  21.1 7.6 %collective-permute-start.10 = (f32[128,128]{1,0:T(8,128)S(1)}, f32[128,128]{1,0:T(8,128)S(1)}, u32[]{:S(2)}, u32[]{:S(2)}) collective-permute-start(f32[128,128]{1,0:T(8,128)S(1)} %add.34), channel_id=1, source_target_pairs={{0,4},{1,5},{2,6},{3,7},{8,12},{9,13},{10,14},{11,15},{16,20},{17,... | collective-permute-start | bytes 196616 | tf_op jit(solution)/shard_map/ppermute | solution.py:36
  22.5 2.3 %copy-start = (f32[1,1536,768]{2,1,0:T(8,128)S(1)}, f32[1,1536,768]{2,1,0:T(8,128)}, u32[]{:S(2)}) copy-start(f32[1,1536,768]{2,1,0:T(8,128)} %x_ref.15) | copy-start | bytes 14155780
  27.2 68.4 %collective-permute-start.16 = (s16[784,768]{1,0:T(8,128)(2,1)}, s16[784,768]{1,0:T(8,128)(2,1)}, u32[]{:S(2)}, u32[]{:S(2)}) collective-permute-start(s16[784,768]{1,0:T(8,128)(2,1)} %shard_map.106), channel_id=1, source_target_pairs={{0,16},{8,24},{16,0},{24,8},{1,17},{9,25},{17,1},{25,9},{2,18},{10... | collective-permute-start | bytes 3612680 | tf_op jit(solution)/shard_map/ppermute | solution.py:28
  28.8 6.8 %collective-permute-start.11 = (f32[128,128]{1,0:T(8,128)S(1)}, f32[128,128]{1,0:T(8,128)S(1)}, u32[]{:S(2)}, u32[]{:S(2)}) collective-permute-start(f32[128,128]{1,0:T(8,128)S(1)} %broadcast_select_fusion.3), channel_id=1, source_target_pairs={{0,2},{4,6},{8,10},{12,14},{16,18},{20,22},{24,26},{28,30}} | collective-permute-start | bytes 196616 | tf_op jit(solution)/shard_map/ppermute | solution.py:36
  35.6 15.8 %collective-permute-start.12 = (f32[128,128]{1,0:T(8,128)S(1)}, f32[128,128]{1,0:T(8,128)S(1)}, u32[]{:S(2)}, u32[]{:S(2)}) collective-permute-start(f32[128,128]{1,0:T(8,128)S(1)} %broadcast_select_fusion.4), channel_id=1, source_target_pairs={{0,1},{2,3},{4,5},{6,7},{8,9},{10,11},{12,13},{14,15},{16,17},{18,... | collective-permute-start | bytes 196616 | tf_op jit(solution)/shard_map/ppermute | solution.py:36
  45.2 36.6 %collective-permute-start.7 = (s16[2064,128]{1,0:T(8,128)(2,1)S(1)}, s16[2064,128]{1,0:T(8,128)(2,1)S(1)}, u32[]{:S(2)}, u32[]{:S(2)}) collective-permute-start(s16[2064,128]{1,0:T(8,128)(2,1)S(1)} %shard_map.101.own_ref), channel_id=1, source_target_pairs={{0,16},{8,24},{16,0},{24,8},{1,17},{9,25},{17,1},{25,9},{2,18},{10... | collective-permute-start | bytes 1585160 | tf_op jit(solution)/shard_map/ppermute | solution.py:28
  50.9 56.4 %collective-permute-start.1 = (s16[528,896]{1,0:T(8,128)(2,1)}, s16[528,896]{1,0:T(8,128)(2,1)}, u32[]{:S(2)}, u32[]{:S(2)}) collective-permute-start(s16[528,896]{1,0:T(8,128)(2,1)} %shard_map.95.a_ref), channel_id=1, source_target_pairs={{0,16},{8,24},{16,0},{24,8},{1,17},{9,25},{17,1},{25,9},{2,18},{10... | collective-permute-start | bytes 2838536 | tf_op jit(solution)/shard_map/ppermute | solution.py:28
  90.3 96.3 %copy-start.2 = (f32[2048,128]{1,0:T(8,128)}, f32[2048,128]{1,0:T(8,128)S(1)}, u32[]{:S(2)}) copy-start(f32[2048,128]{1,0:T(8,128)S(1)} %get-tuple-element.11.slab_ref) | copy-start | bytes 3145732
  90.3 21.0 %collective-permute-start.13 = (bf16[2048,128]{1,0:T(8,128)(2,1)}, bf16[2048,128]{1,0:T(8,128)(2,1)}, u32[]{:S(2)}, u32[]{:S(2)}) collective-permute-start(bf16[2048,128]{1,0:T(8,128)(2,1)} %get-tuple-element.12), channel_id=1, source_target_pairs={{0,2},{4,6},{8,10},{12,14},{16,18},{20,22},{24,26},{28,30}} | collective-permute-start | bytes 1572872 | tf_op jit(solution)/shard_map/ppermute | solution.py:36
  95.6 4.5 %copy-start.6 = (s32[1,8,4]{1,2,0:T(4,128)S(1)}, s32[1,8,4]{1,2,0:T(4,128)}, u32[]{:S(2)}) copy-start(s32[1,8,4]{1,2,0:T(4,128)} %param.12) | copy-start | bytes 388
  99.5 29.6 %collective-permute-start.17 = (s16[784,768]{1,0:T(8,128)(2,1)S(1)}, s16[784,768]{1,0:T(8,128)(2,1)}, u32[]{:S(2)}, u32[]{:S(2)}) collective-permute-start(s16[784,768]{1,0:T(8,128)(2,1)S(1)} %shard_map.107.a_ref), channel_id=1, source_target_pairs={{0,8},{8,0},{16,24},{24,16},{1,9},{9,1},{17,25},{25,17},{2,10},{10... | collective-permute-start | bytes 3612680 | tf_op jit(solution)/shard_map/ppermute | solution.py:28
  100.3 5.0 %copy-start.1 = (f32[1,1024,512]{2,1,0:T(8,128)S(1)}, f32[1,1024,512]{2,1,0:T(8,128)}, u32[]{:S(2)}) copy-start(f32[1,1024,512]{2,1,0:T(8,128)} %x_ref.17) | copy-start | bytes 6291460
  103.6 45.6 %collective-permute-start.4 = (s16[528,896]{1,0:T(8,128)(2,1)S(1)}, s16[528,896]{1,0:T(8,128)(2,1)S(1)}, u32[]{:S(2)}, u32[]{:S(2)}) collective-permute-start(s16[528,896]{1,0:T(8,128)(2,1)S(1)} %shard_map.98.a_ref), channel_id=1, source_target_pairs={{0,8},{8,0},{16,24},{24,16},{1,9},{9,1},{17,25},{25,17},{2,10},{10... | collective-permute-start | bytes 2838536 | tf_op jit(solution)/shard_map/ppermute | solution.py:28
  106.6 65.5 %collective-permute-start.19 = (s16[1040,512]{1,0:T(8,128)(2,1)S(1)}, s16[1040,512]{1,0:T(8,128)(2,1)S(1)}, u32[]{:S(2)}, u32[]{:S(2)}) collective-permute-start(s16[1040,512]{1,0:T(8,128)(2,1)S(1)} %shard_map.110), channel_id=1, source_target_pairs={{0,8},{8,0},{16,24},{24,16},{1,9},{9,1},{17,25},{25,17},{2,10},{10... | collective-permute-start | bytes 3194888 | tf_op jit(solution)/shard_map/ppermute | solution.py:28
  109.7 76.8 %collective-permute-start.2 = (s16[528,896]{1,0:T(8,128)(2,1)S(1)}, s16[528,896]{1,0:T(8,128)(2,1)S(1)}, u32[]{:S(2)}, u32[]{:S(2)}) collective-permute-start(s16[528,896]{1,0:T(8,128)(2,1)S(1)} %shard_map.96.own_ref.own_scale.own_a), channel_id=1, source_target_pairs={{0,8},{8,0},{16,24},{24,16},{1,9},{9,1},{17,25},{25,17},{2,10},{10... | collective-permute-start | bytes 2838536 | tf_op jit(solution)/shard_map/ppermute | solution.py:28
  112.4 77.1 %collective-permute-start.14 = (bf16[2048,128]{1,0:T(8,128)(2,1)S(1)}, bf16[2048,128]{1,0:T(8,128)(2,1)S(1)}, u32[]{:S(2)}, u32[]{:S(2)}) collective-permute-start(bf16[2048,128]{1,0:T(8,128)(2,1)S(1)} %broadcast_select_fusion), channel_id=1, source_target_pairs={{0,1},{2,3},{4,5},{6,7},{8,9},{10,11},{12,13},{14,15},{16,17},{18,... | collective-permute-start | bytes 1572872 | tf_op jit(solution)/shard_map/ppermute | solution.py:36
  131.8 71.8 %collective-permute-start.18 = (s16[784,768]{1,0:T(8,128)(2,1)S(1)}, s16[784,768]{1,0:T(8,128)(2,1)S(1)}, u32[]{:S(2)}, u32[]{:S(2)}) collective-permute-start(s16[784,768]{1,0:T(8,128)(2,1)S(1)} %shard_map.108.own_ref), channel_id=1, source_target_pairs={{0,16},{8,24},{16,0},{24,8},{1,17},{9,25},{17,1},{25,9},{2,18},{10... | collective-permute-start | bytes 3612680 | tf_op jit(solution)/shard_map/ppermute | solution.py:28
  149.3 0.9 copy-start.3
  150.2 1.2 copy-start.4
  152.4 38.2 %collective-permute-start.5 = (s16[528,896]{1,0:T(8,128)(2,1)S(1)}, s16[528,896]{1,0:T(8,128)(2,1)S(1)}, u32[]{:S(2)}, u32[]{:S(2)}) collective-permute-start(s16[528,896]{1,0:T(8,128)(2,1)S(1)} %shard_map.99.own_b), channel_id=1, source_target_pairs={{0,16},{8,24},{16,0},{24,8},{1,17},{9,25},{17,1},{25,9},{2,18},{10... | collective-permute-start | bytes 2838536 | tf_op jit(solution)/shard_map/ppermute | solution.py:28
  188.1 2.4 %collective-permute-start.15 = (bf16[128,1024]{1,0:T(8,128)(2,1)S(1)}, bf16[128,1024]{1,0:T(8,128)(2,1)S(1)}, u32[]{:S(2)}, u32[]{:S(2)}) collective-permute-start(bf16[128,1024]{1,0:T(8,128)(2,1)S(1)} %get-tuple-element.14), channel_id=1, source_target_pairs={{0,4},{1,5},{2,6},{3,7},{8,12},{9,13},{10,14},{11,15},{16,20},{17,... | collective-permute-start | bytes 786440 | tf_op jit(solution)/shard_map/ppermute | solution.py:36

commit v2 on v1

v2 whole, which is shorter than its diff:
```python
import jax
import jax.numpy as jnp
from jax import lax
from jax.experimental import pallas as pl
from jax.experimental.pallas import tpu as pltpu
from jax.sharding import PartitionSpec as P

PANEL = 128
BLK = 128
EXTRA = 16
HIGHEST = lax.Precision.HIGHEST
VMEM_LIMIT = 48 * 1024 * 1024

SMEM_SPEC = pl.BlockSpec(memory_space=pltpu.SMEM)
VMEM_SPEC = pl.BlockSpec(memory_space=pltpu.VMEM)


def swapped(value, bit):
    count = lax.axis_size("layer")
    return lax.ppermute(value, "layer", [(i, i ^ (1 << bit)) for i in range(count)])


def broadcast_from_first(value, axis):
    count = lax.axis_size(axis)
    own = lax.axis_index(axis)
    span = count // 2
    while span >= 1:
        got = lax.ppermute(value, axis, [(i, i + span) for i in range(0, count, 2 * span)])
        value = jnp.where(own % (2 * span) == span, got, value)
        span //= 2
    return value


def exponents(largest):
    return jnp.floor(jnp.log2(jnp.maximum(largest, 1e-30))) - 14.0


def coded(value, inverse):
    scaled = jnp.round(value * inverse)
    scaled = jnp.minimum(jnp.maximum(scaled, -32767.0), 32767.0)
    return scaled.astype(jnp.int32).astype(jnp.int16)


def scales(code_ref, rows, cols):
    held = code_ref[pl.ds(rows, EXTRA), cols].astype(jnp.int32).astype(jnp.float32)
    return jnp.exp2(held[0:1])


def decoded(code_ref, row, scale, cols):
    return code_ref[pl.ds(row, BLK), cols].astype(jnp.int32).astype(jnp.float32) * scale


def run(kernel, after, operands, specs, out_specs, out_shape, nbytes, flops=0, grid=(1,), scalars=(), scratch=(), aliases=None):
    taken = len(scalars) + len(operands)
    after = [] if after is None else [after]

    def body(*refs):
        kernel(*refs[:taken], *refs[taken + len(after):])

    return pl.pallas_call(
        body,
        grid_spec=pltpu.PrefetchScalarGridSpec(
            num_scalar_prefetch=len(scalars),
            grid=grid,
            in_specs=list(specs) + [pl.BlockSpec(memory_space=pl.ANY)] * len(after),
            out_specs=out_specs,
            scratch_shapes=list(scratch),
        ),
        out_shape=out_shape,
        input_output_aliases=aliases or {},
        compiler_params=pltpu.CompilerParams(vmem_limit_bytes=VMEM_LIMIT),
        cost_estimate=pl.CostEstimate(flops=0, bytes_accessed=1024, transcendentals=0),
    )(*scalars, *operands, *after)


def encode_all(load, out_ref, value_ref, scale_ref, rows, blocks):
    @pl.loop(0, blocks)
    def _(j):
        cols = pl.ds(pl.multiple_of(j * BLK, BLK), BLK)
        fetch = load(j)
        largest = jnp.zeros((1, BLK), jnp.float32)
        for i in range(rows // BLK):
            value = fetch(i)
            value_ref[pl.ds(i * BLK, BLK), cols] = value
            largest = jnp.maximum(largest, jnp.max(jnp.abs(value), axis=0, keepdims=True))
        scale_ref[0:1, cols] = largest

    power = exponents(scale_ref[0:1, :])
    scale_ref[0:1, :] = jnp.exp2(-power)
    held = jnp.broadcast_to(power, (EXTRA, blocks * BLK))
    out_ref[pl.ds(rows, EXTRA), :] = held.astype(jnp.int32).astype(jnp.int16)

    @pl.loop(0, blocks)
    def _(j):
        cols = pl.ds(pl.multiple_of(j * BLK, BLK), BLK)
        inverse = scale_ref[0:1, cols]
        for i in range(rows // BLK):
            here = pl.ds(i * BLK, BLK)
            out_ref[here, cols] = coded(value_ref[here, cols], inverse)


def message_scratch(rows, blocks):
    return [pltpu.VMEM((rows, blocks * BLK), jnp.float32), pltpu.VMEM((8, blocks * BLK), jnp.float32)]


def masked_load(place, pattern_ref, x_ref, rows, block_col):
    col = pl.ds(pl.multiple_of(block_col * BLK, BLK), BLK)

    def load(i):
        block_row = place[0] * (rows // BLK) + i
        kept = (pattern_ref[block_row, block_col] == 1) | (place[1] + block_row == place[2] + block_col)
        value = x_ref[0, pl.ds(i * BLK, BLK), col]
        return jnp.where(kept, value, 0.0)

    return load


def encode_partial(after, partial, pattern, place, rows, first_block, blocks, received=None):
    width = partial.shape[2] if first_block > 0 else blocks * BLK
    extra = [] if received is None else [received]

    def kernel(place_ref, pattern_ref, x_ref, *refs):
        out_ref, value_ref, scale_ref = refs[-3:]

        def load(j):
            own = masked_load(place_ref, pattern_ref, x_ref, rows, j + first_block)
            if received is None:
                return own
            cols = pl.ds(pl.multiple_of(j * BLK, BLK), BLK)
            scale = scales(refs[0], rows, cols)
            return lambda i: own(i) + decoded(refs[0], i * BLK, scale, cols)

        encode_all(load, out_ref, value_ref, scale_ref, rows, blocks)

    return run(
        kernel, after, [partial] + extra,
        [pl.BlockSpec((1, rows, width), lambda g, place_ref, pattern_ref: (0, place_ref[0], 0))]
        + [VMEM_SPEC] * len(extra),
        VMEM_SPEC, jax.ShapeDtypeStruct((rows + EXTRA, blocks * BLK), jnp.int16),
        rows * width * 4 + rows * blocks * BLK * 2 * (1 + len(extra)),
        scalars=(place, pattern), scratch=message_scratch(rows, blocks),
    )


def merge(after, first, second):
    rows, blocks = first.shape[0] - EXTRA, first.shape[1] // BLK

    def kernel(a_ref, b_ref, out_ref, value_ref, scale_ref):
        def load(j):
            cols = pl.ds(pl.multiple_of(j * BLK, BLK), BLK)
            a_scale = scales(a_ref, rows, cols)
            b_scale = scales(b_ref, rows, cols)
            return lambda i: decoded(a_ref, i * BLK, a_scale, cols) + decoded(b_ref, i * BLK, b_scale, cols)

        encode_all(load, out_ref, value_ref, scale_ref, rows, blocks)

    return run(
        kernel, after, [first, second], [VMEM_SPEC] * 2, VMEM_SPEC,
        jax.ShapeDtypeStruct(first.shape, jnp.int16), first.size * 6, scratch=message_scratch(rows, blocks),
    )


def low_total(after, partial, pattern, place, received):
    _, total_rows, width = partial.shape
    rows = total_rows // len(received)

    def kernel(place_ref, pattern_ref, x_ref, *refs):
        out_ref = refs[-1]

        @pl.loop(0, width // BLK)
        def _(j):
            cols = pl.ds(pl.multiple_of(j * BLK, BLK), BLK)
            load = masked_load(place_ref, pattern_ref, x_ref, total_rows, j)
            for part, code_ref in enumerate(refs[:-1]):
                scale = scales(code_ref, rows, cols)
                for i in range(rows // BLK):
                    block = part * (rows // BLK) + i
                    out_ref[0, pl.ds(block * BLK, BLK), cols] = load(block) + decoded(code_ref, i * BLK, scale, cols)

    return run(
        kernel, after, [partial, *received], [VMEM_SPEC] * (1 + len(received)), VMEM_SPEC,
        jax.ShapeDtypeStruct(partial.shape, jnp.float32), partial.size * 10, scalars=(place, pattern),
    )


def mid_half(after, owner, code, base=None):
    rows, width = code.shape[0] - EXTRA, code.shape[1]
    extra = [] if base is None else [base]

    def kernel(owner_ref, code_ref, *refs):
        @pl.loop(0, width // BLK)
        def _(j):
            cols = pl.ds(pl.multiple_of(j * BLK, BLK), BLK)
            scale = scales(code_ref, rows, cols)
            for i in range(rows // BLK):
                refs[-1][0, pl.ds(i * BLK, BLK), cols] = decoded(code_ref, i * BLK, scale, cols)

    return run(
        kernel, after, [code] + extra, [VMEM_SPEC] + [pl.BlockSpec(memory_space=pl.ANY)] * len(extra),
        pl.BlockSpec((1, rows, width), lambda g, owner_ref: (0, owner_ref[0], 0)),
        jax.ShapeDtypeStruct((1, 2 * rows, width), jnp.float32), code.size * 6, scalars=(owner,),
        aliases={2: 0} if extra else None,
    )


def factor(after, corner):
    order = corner.shape[0]

    def kernel(a_ref, packed_ref, lower_ref, upper_ref, direct, direct_unit, turned, turned_unit):
        lane = lax.broadcasted_iota(jnp.int32, (order, order), 1)
        sub = lax.broadcasted_iota(jnp.int32, (order, order), 0)
        lane_row = lax.broadcasted_iota(jnp.int32, (1, order), 1)
        sub_col = lax.broadcasted_iota(jnp.int32, (order, 1), 0)
        unit = (lane == sub).astype(jnp.float32)
        direct[...] = a_ref[...]
        direct_unit[...] = unit
        turned[...] = a_ref[...].T
        turned_unit[...] = unit

        @pl.loop(0, order - 1)
        def _(k):
            for held, held_unit in ((direct, direct_unit), (turned, turned_unit)):
                left = held[...]
                row_left = held[pl.ds(k, 1), :]
                row_right = held_unit[pl.ds(k, 1), :]
                col = jnp.sum(jnp.where(lane == k, left, 0.0), axis=1, keepdims=True)
                pivot = jnp.sum(jnp.where(lane_row == k, row_left, 0.0), axis=1, keepdims=True)
                below = sub_col > k
                multipliers = jnp.where(below, col / pivot, 0.0)
                fresh = left - multipliers * jnp.where(lane_row > k, row_left, 0.0)
                held[...] = jnp.where((lane == k) & below, multipliers, fresh)
                held_unit[...] = held_unit[...] - multipliers * row_right

        packed_ref[...] = direct[...]
        lower_ref[...] = direct_unit[...]
        pivots = jnp.sum(jnp.where(lane == sub, turned[...], 0.0), axis=1, keepdims=True)
        upper_ref[...] = (turned_unit[...] / pivots).T

    shape = jax.ShapeDtypeStruct((order, order), jnp.float32)
    return run(
        kernel, after, [corner], [VMEM_SPEC], [VMEM_SPEC] * 3, [shape] * 3, order * order * 16, 2e9,
        scratch=[pltpu.VMEM((order, order), jnp.float32)] * 4,
    )


def exact_dot(left, right):
    return jnp.dot(left, right, precision=HIGHEST, preferred_element_type=jnp.float32)


def low_dot(left, right):
    return jnp.dot(left, right, preferred_element_type=jnp.float32)


def permuted_codes(order_block, codes, scale):
    codes = codes.astype(jnp.int32)
    high = (codes >> 8).astype(jnp.float32).astype(jnp.bfloat16)
    low = (codes & 255).astype(jnp.float32).astype(jnp.bfloat16)
    return (low_dot(order_block, high) * 256.0 + low_dot(order_block, low)) * scale


def lower_panel(after, flags, order, own, received, upper_inverse):
    rows = own.shape[0] - EXTRA

    def kernel(flag_ref, order_ref, own_ref, got_ref, inverse_ref, slab_ref, low_ref):
        cols = pl.ds(0, PANEL)
        own_scale = scales(own_ref, rows, cols)
        got_scale = scales(got_ref, rows, cols)
        first_col = flag_ref[3] == 0

        @pl.loop(0, rows // BLK, unroll=4)
        def _(i):
            here = pl.ds(pl.multiple_of(i * BLK, BLK), BLK)
            order_block = order_ref[here, :]
            slab_ref[here, :] = permuted_codes(order_block, own_ref[here, :], own_scale) + permuted_codes(
                order_block, got_ref[here, :], got_scale
            )

        panel = exact_dot(slab_ref[...], inverse_ref[...])
        low_ref[...] = panel.astype(jnp.bfloat16)

        @pl.when(first_col)
        def _():
            slab_ref[...] = panel

    return run(
        kernel, after, [flags, order, own, received, upper_inverse], [SMEM_SPEC] + [VMEM_SPEC] * 4, [VMEM_SPEC] * 2,
        [jax.ShapeDtypeStruct((rows, PANEL), jnp.float32), jax.ShapeDtypeStruct((rows, PANEL), jnp.bfloat16)],
        rows * PANEL * 14, rows * PANEL * PANEL * 20,
    )


def upper_panel(after, flags, order, slab, own, received, lower_inverse):
    rows, rest = own.shape[0] - EXTRA, own.shape[1]
    width = rest + PANEL

    def kernel(flag_ref, order_ref, slab_ref, own_ref, own_scale, got_ref, got_scale, inverse_ref, up_ref, low_ref):
        first = exact_dot(inverse_ref[...], slab_ref[...])
        up_ref[:, :PANEL] = first
        low_ref[:, :PANEL] = first.astype(jnp.bfloat16)

        def write(code_ref, scale_ref):
            scale = jnp.exp2(scale_ref[...].astype(jnp.int32).astype(jnp.float32)[0:1])
            value = permuted_codes(order_ref[...], code_ref[...], scale)
            value = exact_dot(inverse_ref[...], value)
            up_ref[:, PANEL:] = value
            low_ref[:, PANEL:] = value.astype(jnp.bfloat16)

        pl.when(flag_ref[0] == 0)(lambda: write(own_ref, own_scale))
        pl.when(flag_ref[0] == 1)(lambda: write(got_ref, got_scale))

    first_block = lambda g: (0, 0)
    code_spec = pl.BlockSpec((BLK, rest), first_block)
    scale_spec = pl.BlockSpec((EXTRA, rest), lambda g: (rows // EXTRA, 0))
    square = pl.BlockSpec((BLK, BLK), first_block)
    return run(
        kernel, after, [flags, order, slab, own, own, received, received, lower_inverse],
        [SMEM_SPEC, square, square, code_spec, scale_spec, code_spec, scale_spec, square],
        [pl.BlockSpec((BLK, width), first_block)] * 2,
        [jax.ShapeDtypeStruct((PANEL, width), jnp.float32), jax.ShapeDtypeStruct((PANEL, width), jnp.bfloat16)],
        BLK * width * 10, BLK * BLK * width * 16,
    )


def top_total(after, flags, order, codes, slab, lower_low, upper_low, upper, packed):
    total_rows = slab.shape[0]
    rows, rest = codes[0].shape[0] - EXTRA, codes[0].shape[1]
    width = rest + PANEL
    part_blocks = rows // BLK

    def kernel(flag_ref, order_ref, own_a, got_a, own_b, got_b, slab_ref, low_ref, up_low_ref, up_ref, packed_ref, out_ref):
        i = pl.program_id(0)
        part = i // part_blocks
        row = pl.multiple_of((i % part_blocks) * BLK, BLK)
        first_row = (flag_ref[2] == 0) & (i == 0)
        first_col = flag_ref[3] == 0
        rest_cols = pl.ds(0, rest)

        @pl.when(jnp.logical_not(first_row))
        def _():
            low = low_ref[...]

            def write(code_ref):
                scale = scales(code_ref, rows, rest_cols)
                value = permuted_codes(order_ref[...], code_ref[pl.ds(row, BLK), :], scale)
                out_ref[:, PANEL:] = value - low_dot(low, up_low_ref[:, PANEL:])

            owned_a = part == flag_ref[0]
            owned_b = part == 2 + flag_ref[1]
            pl.when(owned_a)(lambda: write(own_a))
            pl.when((part < 2) & jnp.logical_not(owned_a))(lambda: write(got_a))
            pl.when(owned_b)(lambda: write(own_b))
            pl.when((part >= 2) & jnp.logical_not(owned_b))(lambda: write(got_b))
            product = low_dot(low, up_low_ref[:, :PANEL])
            out_ref[:, :PANEL] = jnp.where(first_col, slab_ref[...], slab_ref[...] - product)

        @pl.when(first_row)
        def _():
            out_ref[:, PANEL:] = up_ref[:, PANEL:]
            out_ref[:, :PANEL] = jnp.where(first_col, packed_ref[...], up_ref[:, :PANEL])

    square = pl.BlockSpec((BLK, BLK), lambda i: (i, 0))
    return run(
        kernel, after, [flags, order, *codes, slab, lower_low, upper_low, upper, packed],
        [SMEM_SPEC, square] + [VMEM_SPEC] * 4 + [square, square] + [VMEM_SPEC] * 3,
        pl.BlockSpec((BLK, width), lambda i: (i, 0)),
        jax.ShapeDtypeStruct((total_rows, width), jnp.float32),
        total_rows * width * 6, total_rows * width * BLK * 6, grid=(total_rows // BLK,),
    )


def on_device(partial_top, partial_mid, partial_low, pattern_top, pattern_mid, pattern_low, pivots):
    layer, row, col = (lax.axis_index(name) for name in ("layer", "row", "col"))
    bits = list(range(lax.axis_size("layer").bit_length() - 1))
    low_bit, high_bit = layer & 1, (layer >> 1) & 1
    flags = jnp.stack([low_bit, high_bit, row, col]).astype(jnp.int32)
    order = ((pivots % BLK)[:, None] == jnp.arange(BLK, dtype=jnp.int32)[None, :]).astype(jnp.bfloat16)

    def sender(partial, pattern, rows, first_block, blocks):
        corner_block = [row * pattern.shape[1], col * pattern.shape[2]]

        def encode(after, part, received=None):
            place = jnp.stack([jnp.asarray(part, jnp.int32), *corner_block]).astype(jnp.int32)
            return encode_partial(after, partial, pattern[0], place, rows, first_block, blocks, received)

        return encode

    def exchanged(after, own, some):
        for bit in some:
            own = after = merge(after, own, swapped(own, bit))
        return own

    top_rows, top_blocks = partial_top.shape[1], partial_top.shape[2] // BLK
    mid_blocks, low_blocks = partial_mid.shape[2] // BLK, partial_low.shape[2] // BLK
    low_rows = partial_low.shape[1]
    encode_mid = sender(partial_mid, pattern_mid, partial_mid.shape[1] // 2, 0, mid_blocks)
    encode_slab = sender(partial_top, pattern_top, top_rows, 0, 1)
    encode_top = sender(partial_top, pattern_top, top_rows // 4, 1, top_blocks - 1)
    encode_low = sender(partial_low, pattern_low, low_rows // 2, 0, low_blocks)

    mid_sent = encode_mid(None, 1 - high_bit)
    mid_got = swapped(mid_sent, 1)
    slab = last = encode_slab(mid_sent, 0)
    slab_got = swapped(slab, 0)

    corner = exact_dot(order[:BLK].astype(jnp.float32), partial_top[0, :BLK, :BLK])
    for bit in bits:
        corner = corner + swapped(corner, bit)
    corner = broadcast_from_first(broadcast_from_first(corner, "row"), "col")

    last = encode_top(last, 1 - low_bit)
    a_got = swapped(last, 0)
    last = encode_top(last, 3 - high_bit)
    b_got = swapped(last, 1)
    slab = last = merge(last, slab, slab_got)
    slab = exchanged(last, slab, bits[1:-1])
    slab_got = swapped(slab, bits[-1])
    mid = last = encode_mid(last, high_bit, mid_got)
    mid_got = swapped(mid, 0)
    a = last = encode_top(last, low_bit, a_got)
    a_got = swapped(a, 1)
    packed, lower_inverse, upper_inverse = factor(last, corner)
    b = last = encode_top(packed, 2 + high_bit, b_got)
    b_got = swapped(b, 0)
    last = low_first = encode_low(last, 0)
    low_first = swapped(low_first, 0)
    panel, lower_low = lower_panel(last, flags, order, slab, slab_got, upper_inverse)
    lower_low = broadcast_from_first(lower_low, "col")
    b = last = merge(panel, b, b_got)
    b = last = exchanged(last, b, bits[2:])
    b_got = swapped(b, 1)
    a = last = merge(last, a, a_got)
    a = last = exchanged(last, a, bits[2:])
    a_got = swapped(a, 0)
    mid = last = merge(last, mid, mid_got)
    mid_got = swapped(mid, 1)
    last = low_second = encode_low(last, 1)
    low_second = swapped(low_second, 0)
    mid_sums = mid_half(last, high_bit[None].astype(jnp.int32), mid)
    upper, upper_low = upper_panel(mid_sums, flags, order, panel, a, a_got, lower_inverse)
    upper_low = broadcast_from_first(upper_low, "row")
    top_factor = top_total(None, flags, order, (a, a_got, b, b_got), panel, lower_low, upper_low, upper, packed)
    low_place = jnp.stack([jnp.int32(0), row * pattern_low.shape[1], col * pattern_low.shape[2]]).astype(jnp.int32)
    low_sums = low_total(top_factor, partial_low, pattern_low[0], low_place, [low_first, low_second])
    mid_sums = mid_half(top_factor, (1 - high_bit)[None].astype(jnp.int32), mid_got, mid_sums)
    return top_factor, mid_sums, low_sums


def solution(mesh):
    placed = (
        P("layer", "row", "col"),
        P("layer", "row", "col"),
        P("layer", "row", "col"),
        P("layer", "row", "col"),
        P("layer", "row", "col"),
        P("layer", "row", "col"),
        P("row"),
    )
    return jax.shard_map(
        on_device,
        mesh=mesh,
        in_specs=placed,
        out_specs=(P("row", "col"), P("layer", "row", "col"), P("layer", "row", "col")),
        check_vma=False,
    )
```

time: 208 us -> 203 us (0.976)
  waiting for transfers between devices: 89.5 us -> 82.3 us
  starting transfers between devices: 31.3 us -> 34.5 us
  Pallas kernels: 74.9 us -> 72.2 us
    ppermute x14 -> x15, waiting for transfers between devices: 86.2 us -> 78.7 us  [swapped(): lax.ppermute(value, 'layer', [(i, i ^ 1 << bit) for i in range(count)])]
    pallas_call x18 -> x20, Pallas kernels: 74.9 us -> 72.2 us  [run(): pl.pallas_call(body, grid_spec=pltpu.PrefetchScalarGridSpec(num_scalar_pr...]
    ppermute x6, starting transfers between devices: 15 us -> 17.7 us  [broadcast_from_first(): lax.ppermute(value, axis, [(i, i + span) for i in range(0, count, 2 * spa...]
    unnamed x14 -> x20, local copies, waits for them, and re-layouts: 4.47 us -> 6.12 us
    ppermute x14 -> x15, starting transfers between devices: 16.3 us -> 16.8 us  [swapped(): lax.ppermute(value, 'layer', [(i, i ^ 1 << bit) for i in range(count)])]
  transfers between devices with their start and end apart: 20 -> 21, of which waited for: 8 -> 8; matrix products, arithmetic and copies ran while one was open for 1% -> 1% of each run, Pallas kernels for 35% -> 35%
where the time goes in v2:
time: 203 us; the launch traced here: 202 us
  waiting for transfers between devices  82.3 us (41%)
  Pallas kernels  72.2 us (36%)
  starting transfers between devices  34.5 us (17%)
  local copies, waits for them, and re-layouts  7.04 us (3%)
  other arithmetic  3.64 us (2%)
    ppermute x15, waiting for transfers between devices, swapped(): lax.ppermute(value, 'layer', [(i, i ^ 1 << bit) for i in range(count)])  78.7 us
    pallas_call x20, Pallas kernels, run(): pl.pallas_call(body, grid_spec=pltpu.PrefetchScalarGridSpec(num_scalar_pr...  72.2 us
    ppermute x6, starting transfers between devices, broadcast_from_first(): lax.ppermute(value, axis, [(i, i + span) for i in range(0, count, 2 * spa...  17.7 us
    ppermute x15, starting transfers between devices, swapped(): lax.ppermute(value, 'layer', [(i, i ^ 1 << bit) for i in range(count)])  16.8 us
    unnamed x20, local copies, waits for them, and re-layouts  6.12 us
  transfers between devices with their start and end apart: 21, of which 8 were waited for; matrix products, arithmetic and copies ran while one was open for 1% of the time, Pallas kernels for 35%

profile of v2, /device:TPU:0, one launch (start us, length us, event | category | flops | bytes accessed | tf_op | source)
XLA Modules:
  0.0 201.6 jit_solution(15495427310357670168)
XLA Ops:
  3.5 3.0 %collective-permute-start.5 = (f32[128,128]{1,0:T(8,128)S(1)}, f32[128,128]{1,0:T(8,128)}, u32[]{:S(2)}, u32[]{:S(2)}) collective-permute-start(f32[128,128]{1,0:T(8,128)S(1)} %fusion), channel_id=1, source_target_pairs={{0,8},{8,0},{16,24},{24,16},{1,9},{9,1},{17,25},{25,17},{2,10},{10... | collective-permute-start | bytes 196616 | tf_op jit(solution)/shard_map/ppermute | solution.py:20
  7.3 2.3 %copy-done.1 = f32[1,1536,768]{2,1,0:T(8,128)S(1)} copy-done((f32[1,1536,768]{2,1,0:T(8,128)S(1)}, f32[1,1536,768]{2,1,0:T(8,128)}, u32[]{:S(2)}) %copy-start.1) | copy-done | bytes 4718616
  11.2 1.6 collective-permute-start.1
  12.9 2.1 %shard_map.95.refs_3_.refs_0_ = s16[2064,128]{1,0:T(8,128)(2,1)S(1)} custom-call(s32[3]{0:T(128)S(1)} %fusion.6.refs_0_, s32[16,8]{1,0:T(8,128)S(1)} %copy.16.refs_1_, f32[1,2048,1024]{2,1,0:T(8,128)} %refs_2_.16, s16[784,768]{1,0:T(8,128)(2,1)S(1)} %shard_map.94.refs_3_), custom_call_target="tpu_custom_call" | custom-call | bytes 1024 | tf_op jit(solution)/shard_map/pallas_call | solution.py:60
  15.7 3.8 %shard_map.96.refs_3_ = s16[528,896]{1,0:T(8,128)(2,1)} custom-call(s32[3]{0:T(128)S(1)} %add_add_fusion.1.refs_0_, s32[16,8]{1,0:T(8,128)S(1)} %copy.16.refs_1_, f32[1,2048,1024]{2,1,0:T(8,128)} %refs_2_.16, s16[2064,128]{1,0:T(8,128)(2,1)S(1)} %shard_map.95.refs_3_.refs_0_), custom_call_target="tpu_custom_call" | custom-call | bytes 1024 | tf_op jit(solution)/shard_map/pallas_call | solution.py:60
  22.5 3.8 %shard_map.97.refs_2_ = s16[528,896]{1,0:T(8,128)(2,1)} custom-call(s32[3]{0:T(128)S(1)} %add_add_fusion.4.refs_0_, s32[16,8]{1,0:T(8,128)S(1)} %copy.16.refs_1_, f32[1,2048,1024]{2,1,0:T(8,128)} %refs_2_.16, s16[528,896]{1,0:T(8,128)(2,1)} %shard_map.96.refs_3_), custom_call_target="tpu_custom_call" | custom-call | bytes 1024 | tf_op jit(solution)/shard_map/pallas_call | solution.py:60
  26.4 1.5 collective-permute-start.4
  27.9 14.2 %collective-permute-done.6 = f32[128,128]{1,0:T(8,128)S(1)} collective-permute-done((f32[128,128]{1,0:T(8,128)S(1)}, f32[128,128]{1,0:T(8,128)S(1)}, u32[]{:S(2)}, u32[]{:S(2)}) %collective-permute-start.6) | collective-permute-done | bytes 65568 | tf_op jit(solution)/shard_map/ppermute | solution.py:20
  42.1 1.9 collective-permute-start.7
  44.4 4.5 %collective-permute-start.8 = (f32[128,128]{1,0:T(8,128)S(1)}, f32[128,128]{1,0:T(8,128)S(1)}, u32[]{:S(2)}, u32[]{:S(2)}) collective-permute-start(f32[128,128]{1,0:T(8,128)S(1)} %broadcast_select_fusion.3), channel_id=1, source_target_pairs={{0,2},{4,6},{8,10},{12,14},{16,18},{20,22},{24,26},{28,30}} | collective-permute-start | bytes 196616 | tf_op jit(solution)/shard_map/ppermute | solution.py:28
  49.0 2.2 %collective-permute-done.8 = f32[128,128]{1,0:T(8,128)S(1)} collective-permute-done((f32[128,128]{1,0:T(8,128)S(1)}, f32[128,128]{1,0:T(8,128)S(1)}, u32[]{:S(2)}, u32[]{:S(2)}) %collective-permute-start.8) | collective-permute-done | bytes 65568 | tf_op jit(solution)/shard_map/ppermute | solution.py:28
  53.8 1.5 collective-permute-start.11
  57.7 3.2 %shard_map.99.refs_4_.refs_0_ = s16[784,768]{1,0:T(8,128)(2,1)S(1)} custom-call(s32[3]{0:T(128)S(1)} %add_add_fusion.3.refs_0_, s32[12,6]{1,0:T(8,128)S(1)} %bitcast.21, f32[1,1536,768]{2,1,0:T(8,128)} %refs_2_.14, s16[784,768]{1,0:T(8,128)(2,1)S(1)} %copy-done.5, s16[2064,128]{1,0:T(8,128)(2,1)} %shard_map.98.refs_4_.refs_2_), custom_call_target="tpu_custom_call" | custom-call | bytes 1024 | tf_op jit(solution)/shard_map/pallas_call | solution.py:60
  60.9 4.2 %shard_map.100.refs_1_.refs_0_ = s16[528,896]{1,0:T(8,128)(2,1)} custom-call(s32[3]{0:T(128)S(1)} %add_add_fusion.refs_0_, s32[16,8]{1,0:T(8,128)S(1)} %copy.16.refs_1_, f32[1,2048,1024]{2,1,0:T(8,128)} %refs_2_.16, s16[528,896]{1,0:T(8,128)(2,1)} %collective-permute-done.refs_3_, s16[784,768]{1,0:T(8,128)(2,1)S(1)} %shard_map.99.refs_4_.refs_0_), custom_call_target="tpu_custom_call" | custom-call | bytes 1024 | tf_op jit(solution)/shard_map/pallas_call | solution.py:60
  65.1 15.3 %shard_map.101 = (f32[128,128]{1,0:T(8,128)S(1)}, f32[128,128]{1,0:T(8,128)S(1)}, f32[128,128]{1,0:T(8,128)S(1)}) custom-call(f32[128,128]{1,0:T(8,128)S(1)} %broadcast_select_fusion.5.refs_0_, s16[528,896]{1,0:T(8,128)(2,1)} %shard_map.100.refs_1_.refs_0_), custom_call_target="tpu_custom_call" | custom-call | bytes 1024 | tf_op jit(solution)/shard_map/pallas_call | solution.py:60
  81.0 4.2 %shard_map.102.refs_3_.refs_0_ = s16[528,896]{1,0:T(8,128)(2,1)} custom-call(s32[3]{0:T(128)S(1)} %add_add_fusion.5.refs_0_, s32[16,8]{1,0:T(8,128)S(1)} %copy.16.refs_1_, f32[1,2048,1024]{2,1,0:T(8,128)} %refs_2_.16, s16[528,896]{1,0:T(8,128)(2,1)} %collective-permute-done.4.refs_3_, f32[128,128]{1,0:T(8,128)S(1)} %get-tuple-element.10.refs_4_.refs_10_), custom_call_target="tpu_custom_call" | custom-call | bytes 1024 | tf_op jit(solution)/shard_map/pallas_call | solution.py:60
  86.5 1.5 collective-permute-start.16
  90.1 3.5 %shard_map.104 = (f32[2048,128]{1,0:T(8,128)S(1)}, bf16[2048,128]{1,0:T(8,128)(2,1)S(1)}) custom-call(s32[4]{0:T(128)S(1)} %pad_add_fusion.2.refs_0_, bf16[2048,128]{1,0:T(8,128)(2,1)S(1)} %copy-done.3, s16[2064,128]{1,0:T(8,128)(2,1)} %shard_map.98.refs_4_.refs_2_, s16[2064,128]{1,0:T(8,128)(2,1)} %collective-permute-done.11.refs_3_, ...), custom_call_target="tpu_custom_call" | custom-call | bytes 1024 | tf_op jit(solution)/shard_map/pallas_call | solution.py:60
  93.7 5.0 %collective-permute-start.14 = (bf16[2048,128]{1,0:T(8,128)(2,1)S(1)}, bf16[2048,128]{1,0:T(8,128)(2,1)S(1)}, u32[]{:S(2)}, u32[]{:S(2)}) collective-permute-start(bf16[2048,128]{1,0:T(8,128)(2,1)S(1)} %get-tuple-element.13), channel_id=1, source_target_pairs={{0,2},{4,6},{8,10},{12,14},{16,18},{20,22},{24,26},{28,30}} | collective-permute-start | bytes 1572872 | tf_op jit(solution)/shard_map/ppermute | solution.py:28
  98.7 10.7 %collective-permute-done.10.refs_1_ = s16[528,896]{1,0:T(8,128)(2,1)} collective-permute-done((s16[528,896]{1,0:T(8,128)(2,1)}, s16[528,896]{1,0:T(8,128)(2,1)}, u32[]{:S(2)}, u32[]{:S(2)}) %collective-permute-start.10) | collective-permute-done | bytes 946208 | tf_op jit(solution)/shard_map/ppermute | solution.py:20
  109.4 2.3 %shard_map.105.refs_2_.refs_4_ = s16[528,896]{1,0:T(8,128)(2,1)S(1)} custom-call(s16[528,896]{1,0:T(8,128)(2,1)} %shard_map.102.refs_3_.refs_0_, s16[528,896]{1,0:T(8,128)(2,1)} %collective-permute-done.10.refs_1_, f32[2048,128]{1,0:T(8,128)S(1)} %get-tuple-element.12.refs_2_.refs_6_), custom_call_target="tpu_custom_call" | custom-call | bytes 1024 | tf_op jit(solution)/shard_map/pallas_call | solution.py:60
  111.7 2.3 %shard_map.106.refs_2_.refs_3_.refs_4_ = s16[528,896]{1,0:T(8,128)(2,1)S(1)} custom-call(s16[528,896]{1,0:T(8,128)(2,1)} %shard_map.100.refs_1_.refs_0_, s16[528,896]{1,0:T(8,128)(2,1)} %collective-permute-done.3.refs_1_, s16[528,896]{1,0:T(8,128)(2,1)S(1)} %shard_map.105.refs_2_.refs_4_), custom_call_target="tpu_custom_call" | custom-call | bytes 1024 | tf_op jit(solution)/shard_map/pallas_call | solution.py:60
  114.7 3.6 %collective-permute-start.15 = (bf16[2048,128]{1,0:T(8,128)(2,1)S(1)}, bf16[2048,128]{1,0:T(8,128)(2,1)S(1)}, u32[]{:S(2)}, u32[]{:S(2)}) collective-permute-start(bf16[2048,128]{1,0:T(8,128)(2,1)S(1)} %broadcast_select_fusion), channel_id=1, source_target_pairs={{0,1},{2,3},{4,5},{6,7},{8,9},{10,11},{12,13},{14,15},{16,17},{18,... | collective-permute-start | bytes 1572872 | tf_op jit(solution)/shard_map/ppermute | solution.py:28
  118.4 16.8 %collective-permute-done.16.refs_1_ = s16[784,768]{1,0:T(8,128)(2,1)} collective-permute-done((s16[784,768]{1,0:T(8,128)(2,1)S(1)}, s16[784,768]{1,0:T(8,128)(2,1)}, u32[]{:S(2)}, u32[]{:S(2)}) %collective-permute-start.16) | collective-permute-done | bytes 1204256 | tf_op jit(solution)/shard_map/ppermute | solution.py:20
  135.2 2.4 %shard_map.107.refs_3_.refs_1_ = s16[784,768]{1,0:T(8,128)(2,1)S(1)} custom-call(s16[784,768]{1,0:T(8,128)(2,1)S(1)} %shard_map.99.refs_4_.refs_0_, s16[784,768]{1,0:T(8,128)(2,1)} %collective-permute-done.16.refs_1_, s16[528,896]{1,0:T(8,128)(2,1)S(1)} %shard_map.106.refs_2_.refs_3_.refs_4_), custom_call_target="tpu_custom_call" | custom-call | bytes 1024 | tf_op jit(solution)/shard_map/pallas_call | solution.py:60
  141.3 1.7 shard_map.109.refs_8_.refs_2_
  143.0 12.4 %collective-permute-done.12.refs_5_.refs_6_.refs_3_ = s16[528,896]{1,0:T(8,128)(2,1)S(1)} collective-permute-done((s16[528,896]{1,0:T(8,128)(2,1)S(1)}, s16[528,896]{1,0:T(8,128)(2,1)S(1)}, u32[]{:S(2)}, u32[]{:S(2)}) %collective-permute-start.12) | collective-permute-done | bytes 946208 | tf_op jit(solution)/shard_map/ppermute | solution.py:20
  155.9 1.6 shard_map.110
  160.0 24.6 %collective-permute-done.13.refs_5_ = s16[528,896]{1,0:T(8,128)(2,1)S(1)} collective-permute-done((s16[528,896]{1,0:T(8,128)(2,1)S(1)}, s16[528,896]{1,0:T(8,128)(2,1)S(1)}, u32[]{:S(2)}, u32[]{:S(2)}) %collective-permute-start.13) | collective-permute-done | bytes 946208 | tf_op jit(solution)/shard_map/ppermute | solution.py:20
  184.6 13.0 %shard_map.111.refs_3_.refs_5_ = f32[2048,1024]{1,0:T(8,128)} custom-call(s32[4]{0:T(128)S(1)} %pad_add_fusion.2.refs_0_, bf16[2048,128]{1,0:T(8,128)(2,1)S(1)} %copy-done.3, s16[528,896]{1,0:T(8,128)(2,1)S(1)} %shard_map.106.refs_2_.refs_3_.refs_4_, s16[528,896]{1,0:T(8,128)(2,1)S(1)} %collective-permute-done.12.refs_5_.refs_6_.refs_3_, ...), custom_call_target="tpu_custom_call" | custom-call | bytes 1024 | tf_op jit(solution)/shard_map/pallas_call | solution.py:60
  197.6 2.3 %shard_map.113 = f32[1,1024,512]{2,1,0:T(8,128)} custom-call(s32[3]{0:T(128)S(1)} %fusion.7.refs_0_, s32[8,4]{1,0:T(8,128)S(1)} %copy.18.refs_1_, f32[1,1024,512]{2,1,0:T(8,128)S(1)} %copy-done, s16[528,512]{1,0:T(8,128)(2,1)S(1)} %collective-permute-done.19.refs_3_, s16[528,512]{1,0:T(8,128)(2,1)S(1)} %collective-permute-done.20.refs_4_, ...), custom_call_target="tpu_custom_call" | custom-call | bytes 1024 | tf_op jit(solution)/shard_map/pallas_call | solution.py:60
  199.9 1.7 shard_map.112
  (74 shorter events, 25.9 us)
Async XLA Ops:
  3.5 17.5 %collective-permute-start.5 = (f32[128,128]{1,0:T(8,128)S(1)}, f32[128,128]{1,0:T(8,128)}, u32[]{:S(2)}, u32[]{:S(2)}) collective-permute-start(f32[128,128]{1,0:T(8,128)S(1)} %fusion), channel_id=1, source_target_pairs={{0,8},{8,0},{16,24},{24,16},{1,9},{9,1},{17,25},{25,17},{2,10},{10... | collective-permute-start | bytes 196616 | tf_op jit(solution)/shard_map/ppermute | solution.py:20
  7.3 2.3 %copy-start.1 = (f32[1,1536,768]{2,1,0:T(8,128)S(1)}, f32[1,1536,768]{2,1,0:T(8,128)}, u32[]{:S(2)}) copy-start(f32[1,1536,768]{2,1,0:T(8,128)} %refs_2_.14) | copy-start | bytes 14155780
  9.7 3.1 %copy-start.8 = (s32[1,16,8]{1,2,0:T(8,128)S(1)}, s32[1,16,8]{1,2,0:T(8,128)}, u32[]{:S(2)}) copy-start(s32[1,16,8]{1,2,0:T(8,128)} %param.10) | copy-start | bytes 1540
  11.2 44.2 %collective-permute-start.1 = (s16[784,768]{1,0:T(8,128)(2,1)S(1)}, s16[784,768]{1,0:T(8,128)(2,1)S(1)}, u32[]{:S(2)}, u32[]{:S(2)}) collective-permute-start(s16[784,768]{1,0:T(8,128)(2,1)S(1)} %shard_map.94.refs_3_), channel_id=1, source_target_pairs={{0,16},{8,24},{16,0},{24,8},{1,17},{9,25},{17,1},{25,9},{2,18},{10... | collective-permute-start | bytes 3612680 | tf_op jit(solution)/shard_map/ppermute | solution.py:20
  15.0 37.5 %collective-permute-start.2 = (s16[2064,128]{1,0:T(8,128)(2,1)S(1)}, s16[2064,128]{1,0:T(8,128)(2,1)S(1)}, u32[]{:S(2)}, u32[]{:S(2)}) collective-permute-start(s16[2064,128]{1,0:T(8,128)(2,1)S(1)} %shard_map.95.refs_3_.refs_0_), channel_id=1, source_target_pairs={{0,8},{8,0},{16,24},{24,16},{1,9},{9,1},{17,25},{25,17},{2,10},{10... | collective-permute-start | bytes 1585160 | tf_op jit(solution)/shard_map/ppermute | solution.py:20
  19.5 41.4 %collective-permute-start = (s16[528,896]{1,0:T(8,128)(2,1)}, s16[528,896]{1,0:T(8,128)(2,1)}, u32[]{:S(2)}, u32[]{:S(2)}) collective-permute-start(s16[528,896]{1,0:T(8,128)(2,1)} %shard_map.96.refs_3_), channel_id=1, source_target_pairs={{0,8},{8,0},{16,24},{24,16},{1,9},{9,1},{17,25},{25,17},{2,10},{10... | collective-permute-start | bytes 2838536 | tf_op jit(solution)/shard_map/ppermute | solution.py:20
  21.9 20.2 %collective-permute-start.6 = (f32[128,128]{1,0:T(8,128)S(1)}, f32[128,128]{1,0:T(8,128)S(1)}, u32[]{:S(2)}, u32[]{:S(2)}) collective-permute-start(f32[128,128]{1,0:T(8,128)S(1)} %add.33), channel_id=1, source_target_pairs={{0,16},{8,24},{16,0},{24,8},{1,17},{9,25},{17,1},{25,9},{2,18},{10... | collective-permute-start | bytes 196616 | tf_op jit(solution)/shard_map/ppermute | solution.py:20
  26.4 54.7 %collective-permute-start.4 = (s16[528,896]{1,0:T(8,128)(2,1)}, s16[528,896]{1,0:T(8,128)(2,1)}, u32[]{:S(2)}, u32[]{:S(2)}) collective-permute-start(s16[528,896]{1,0:T(8,128)(2,1)} %shard_map.97.refs_2_), channel_id=1, source_target_pairs={{0,16},{8,24},{16,0},{24,8},{1,17},{9,25},{17,1},{25,9},{2,18},{10... | collective-permute-start | bytes 2838536 | tf_op jit(solution)/shard_map/ppermute | solution.py:20
  42.1 2.3 %collective-permute-start.7 = (f32[128,128]{1,0:T(8,128)S(1)}, f32[128,128]{1,0:T(8,128)}, u32[]{:S(2)}, u32[]{:S(2)}) collective-permute-start(f32[128,128]{1,0:T(8,128)S(1)} %add.34), channel_id=1, source_target_pairs={{0,4},{1,5},{2,6},{3,7},{8,12},{9,13},{10,14},{11,15},{16,20},{17,... | collective-permute-start | bytes 196616 | tf_op jit(solution)/shard_map/ppermute | solution.py:28
  44.4 6.8 %collective-permute-start.8 = (f32[128,128]{1,0:T(8,128)S(1)}, f32[128,128]{1,0:T(8,128)S(1)}, u32[]{:S(2)}, u32[]{:S(2)}) collective-permute-start(f32[128,128]{1,0:T(8,128)S(1)} %broadcast_select_fusion.3), channel_id=1, source_target_pairs={{0,2},{4,6},{8,10},{12,14},{16,18},{20,22},{24,26},{28,30}} | collective-permute-start | bytes 196616 | tf_op jit(solution)/shard_map/ppermute | solution.py:28
  51.2 4.2 %collective-permute-start.9 = (f32[128,128]{1,0:T(8,128)S(1)}, f32[128,128]{1,0:T(8,128)S(1)}, u32[]{:S(2)}, u32[]{:S(2)}) collective-permute-start(f32[128,128]{1,0:T(8,128)S(1)} %broadcast_select_fusion.4), channel_id=1, source_target_pairs={{0,1},{2,3},{4,5},{6,7},{8,9},{10,11},{12,13},{14,15},{16,17},{18,... | collective-permute-start | bytes 196616 | tf_op jit(solution)/shard_map/ppermute | solution.py:28
  53.8 35.4 %collective-permute-start.11 = (s16[2064,128]{1,0:T(8,128)(2,1)}, s16[2064,128]{1,0:T(8,128)(2,1)}, u32[]{:S(2)}, u32[]{:S(2)}) collective-permute-start(s16[2064,128]{1,0:T(8,128)(2,1)} %shard_map.98.refs_4_.refs_2_), channel_id=1, source_target_pairs={{0,16},{8,24},{16,0},{24,8},{1,17},{9,25},{17,1},{25,9},{2,18},{10... | collective-permute-start | bytes 1585160 | tf_op jit(solution)/shard_map/ppermute | solution.py:20
  55.4 1.0 copy-start.4
  56.4 1.3 copy-start.5
  80.4 0.6 copy-start.6
  81.0 7.0 %copy-start.9 = (s32[1,8,4]{1,2,0:T(4,128)S(1)}, s32[1,8,4]{1,2,0:T(4,128)}, u32[]{:S(2)}) copy-start(s32[1,8,4]{1,2,0:T(4,128)} %param.12) | copy-start | bytes 388
  81.0 7.2 %copy-start = (f32[1,1024,512]{2,1,0:T(8,128)S(1)}, f32[1,1024,512]{2,1,0:T(8,128)}, u32[]{:S(2)}) copy-start(f32[1,1024,512]{2,1,0:T(8,128)} %refs_2_.19) | copy-start | bytes 6291460
  85.3 24.1 %collective-permute-start.10 = (s16[528,896]{1,0:T(8,128)(2,1)}, s16[528,896]{1,0:T(8,128)(2,1)}, u32[]{:S(2)}, u32[]{:S(2)}) collective-permute-start(s16[528,896]{1,0:T(8,128)(2,1)} %shard_map.102.refs_3_.refs_0_), channel_id=1, source_target_pairs={{0,8},{8,0},{16,24},{24,16},{1,9},{9,1},{17,25},{25,17},{2,10},{10... | collective-permute-start | bytes 2838536 | tf_op jit(solution)/shard_map/ppermute | solution.py:20
  85.8 25.9 %collective-permute-start.3 = (s16[528,896]{1,0:T(8,128)(2,1)}, s16[528,896]{1,0:T(8,128)(2,1)}, u32[]{:S(2)}, u32[]{:S(2)}) collective-permute-start(s16[528,896]{1,0:T(8,128)(2,1)} %shard_map.100.refs_1_.refs_0_), channel_id=1, source_target_pairs={{0,16},{8,24},{16,0},{24,8},{1,17},{9,25},{17,1},{25,9},{2,18},{10... | collective-permute-start | bytes 2838536 | tf_op jit(solution)/shard_map/ppermute | solution.py:20
  86.5 48.7 %collective-permute-start.16 = (s16[784,768]{1,0:T(8,128)(2,1)S(1)}, s16[784,768]{1,0:T(8,128)(2,1)}, u32[]{:S(2)}, u32[]{:S(2)}) collective-permute-start(s16[784,768]{1,0:T(8,128)(2,1)S(1)} %shard_map.99.refs_4_.refs_0_), channel_id=1, source_target_pairs={{0,8},{8,0},{16,24},{24,16},{1,9},{9,1},{17,25},{25,17},{2,10},{10... | collective-permute-start | bytes 3612680 | tf_op jit(solution)/shard_map/ppermute | solution.py:20
  88.2 1.1 copy-start.3
  89.3 0.8 copy-start.7
  93.7 62.3 %copy-start.2 = (f32[2048,128]{1,0:T(8,128)}, f32[2048,128]{1,0:T(8,128)S(1)}, u32[]{:S(2)}) copy-start(f32[2048,128]{1,0:T(8,128)S(1)} %get-tuple-element.12.refs_2_.refs_6_) | copy-start | bytes 3145732
  93.7 21.0 %collective-permute-start.14 = (bf16[2048,128]{1,0:T(8,128)(2,1)S(1)}, bf16[2048,128]{1,0:T(8,128)(2,1)S(1)}, u32[]{:S(2)}, u32[]{:S(2)}) collective-permute-start(bf16[2048,128]{1,0:T(8,128)(2,1)S(1)} %get-tuple-element.13), channel_id=1, source_target_pairs={{0,2},{4,6},{8,10},{12,14},{16,18},{20,22},{24,26},{28,30}} | collective-permute-start | bytes 1572872 | tf_op jit(solution)/shard_map/ppermute | solution.py:28
  114.1 41.3 %collective-permute-start.12 = (s16[528,896]{1,0:T(8,128)(2,1)S(1)}, s16[528,896]{1,0:T(8,128)(2,1)S(1)}, u32[]{:S(2)}, u32[]{:S(2)}) collective-permute-start(s16[528,896]{1,0:T(8,128)(2,1)S(1)} %shard_map.106.refs_2_.refs_3_.refs_4_), channel_id=1, source_target_pairs={{0,8},{8,0},{16,24},{24,16},{1,9},{9,1},{17,25},{25,17},{2,10},{10... | collective-permute-start | bytes 2838536 | tf_op jit(solution)/shard_map/ppermute | solution.py:20
  114.7 42.8 %collective-permute-start.15 = (bf16[2048,128]{1,0:T(8,128)(2,1)S(1)}, bf16[2048,128]{1,0:T(8,128)(2,1)S(1)}, u32[]{:S(2)}, u32[]{:S(2)}) collective-permute-start(bf16[2048,128]{1,0:T(8,128)(2,1)S(1)} %broadcast_select_fusion), channel_id=1, source_target_pairs={{0,1},{2,3},{4,5},{6,7},{8,9},{10,11},{12,13},{14,15},{16,17},{18,... | collective-permute-start | bytes 1572872 | tf_op jit(solution)/shard_map/ppermute | solution.py:28
  137.6 62.4 %collective-permute-start.18 = (s16[784,768]{1,0:T(8,128)(2,1)S(1)}, s16[784,768]{1,0:T(8,128)(2,1)S(1)}, u32[]{:S(2)}, u32[]{:S(2)}) collective-permute-start(s16[784,768]{1,0:T(8,128)(2,1)S(1)} %shard_map.107.refs_3_.refs_1_), channel_id=1, source_target_pairs={{0,16},{8,24},{16,0},{24,8},{1,17},{9,25},{17,1},{25,9},{2,18},{10... | collective-permute-start | bytes 3612680 | tf_op jit(solution)/shard_map/ppermute | solution.py:20
  138.4 46.2 %collective-permute-start.13 = (s16[528,896]{1,0:T(8,128)(2,1)S(1)}, s16[528,896]{1,0:T(8,128)(2,1)S(1)}, u32[]{:S(2)}, u32[]{:S(2)}) collective-permute-start(s16[528,896]{1,0:T(8,128)(2,1)S(1)} %shard_map.105.refs_2_.refs_4_), channel_id=1, source_target_pairs={{0,16},{8,24},{16,0},{24,8},{1,17},{9,25},{17,1},{25,9},{2,18},{10... | collective-permute-start | bytes 2838536 | tf_op jit(solution)/shard_map/ppermute | solution.py:20
  139.7 57.8 %collective-permute-start.19 = (s16[528,512]{1,0:T(8,128)(2,1)S(1)}, s16[528,512]{1,0:T(8,128)(2,1)S(1)}, u32[]{:S(2)}, u32[]{:S(2)}) collective-permute-start(s16[528,512]{1,0:T(8,128)(2,1)S(1)} %shard_map.103.refs_5_), channel_id=1, source_target_pairs={{0,8},{8,0},{16,24},{24,16},{1,9},{9,1},{17,25},{25,17},{2,10},{10... | collective-permute-start | bytes 1622024 | tf_op jit(solution)/shard_map/ppermute | solution.py:20
  155.4 42.2 %collective-permute-start.20 = (s16[528,512]{1,0:T(8,128)(2,1)S(1)}, s16[528,512]{1,0:T(8,128)(2,1)S(1)}, u32[]{:S(2)}, u32[]{:S(2)}) collective-permute-start(s16[528,512]{1,0:T(8,128)(2,1)S(1)} %shard_map.108.refs_2_), channel_id=1, source_target_pairs={{0,8},{8,0},{16,24},{24,16},{1,9},{9,1},{17,25},{25,17},{2,10},{10... | collective-permute-start | bytes 1622024 | tf_op jit(solution)/shard_map/ppermute | solution.py:20
  157.5 2.4 %collective-permute-start.17 = (bf16[128,1024]{1,0:T(8,128)(2,1)S(1)}, bf16[128,1024]{1,0:T(8,128)(2,1)S(1)}, u32[]{:S(2)}, u32[]{:S(2)}) collective-permute-start(bf16[128,1024]{1,0:T(8,128)(2,1)S(1)} %get-tuple-element.15), channel_id=1, source_target_pairs={{0,4},{1,5},{2,6},{3,7},{8,12},{9,13},{10,14},{11,15},{16,20},{17,... | collective-permute-start | bytes 786440 | tf_op jit(solution)/shard_map/ppermute | solution.py:28

commit v3 on v2

--- a/solution.py
+++ b/solution.py
@@ -17,18 +17,22 @@
 
 def swapped(value, bit):
     count = lax.axis_size("layer")
-    return lax.ppermute(value, "layer", [(i, i ^ (1 << bit)) for i in range(count)])
-
-
-def broadcast_from_first(value, axis):
+    pairs = [(i, i ^ (1 << bit)) for i in range(count)]
+    return jax.tree.map(lambda piece: lax.ppermute(piece, "layer", pairs), value)
+
+
+def broadcast_stages(value, axis):
     count = lax.axis_size(axis)
     own = lax.axis_index(axis)
     span = count // 2
+    stages = []
     while span >= 1:
         got = lax.ppermute(value, axis, [(i, i + span) for i in range(0, count, 2 * span)])
-        value = jnp.where(own % (2 * span) == span, got, value)
+        takes = own % (2 * span) == span
+        value = jnp.where(takes, got, value)
+        stages.append(value)
         span //= 2
-    return value
+    return stages
 
 
 def exponents(largest):
@@ -52,7 +56,6 @@
 
 def run(kernel, after, operands, specs, out_specs, out_shape, nbytes, flops=0, grid=(1,), scalars=(), scratch=(), aliases=None):
     taken = len(scalars) + len(operands)
-    after = [] if after is None else [after]
 
     def body(*refs):
         kernel(*refs[:taken], *refs[taken + len(after):])
@@ -73,30 +76,49 @@
     )(*scalars, *operands, *after)
 
 
-def encode_all(load, out_ref, value_ref, scale_ref, rows, blocks):
-    @pl.loop(0, blocks)
-    def _(j):
-        cols = pl.ds(pl.multiple_of(j * BLK, BLK), BLK)
-        fetch = load(j)
-        largest = jnp.zeros((1, BLK), jnp.float32)
-        for i in range(rows // BLK):
-            value = fetch(i)
-            value_ref[pl.ds(i * BLK, BLK), cols] = value
-            largest = jnp.maximum(largest, jnp.max(jnp.abs(value), axis=0, keepdims=True))
-        scale_ref[0:1, cols] = largest
-
-    power = exponents(scale_ref[0:1, :])
-    scale_ref[0:1, :] = jnp.exp2(-power)
-    held = jnp.broadcast_to(power, (EXTRA, blocks * BLK))
-    out_ref[pl.ds(rows, EXTRA), :] = held.astype(jnp.int32).astype(jnp.int16)
-
-    @pl.loop(0, blocks)
-    def _(j):
-        cols = pl.ds(pl.multiple_of(j * BLK, BLK), BLK)
-        inverse = scale_ref[0:1, cols]
-        for i in range(rows // BLK):
-            here = pl.ds(i * BLK, BLK)
-            out_ref[here, cols] = coded(value_ref[here, cols], inverse)
+def spans(pieces):
+    first, result = 0, []
+    for piece in pieces:
+        blocks = piece.shape[1] // BLK
+        result.append((piece, first, blocks))
+        first += blocks
+    return result
+
+
+def encode_all(segments, out_refs, value_ref, scale_ref, rows):
+    for first, blocks, load in segments:
+
+        @pl.loop(0, blocks)
+        def _(j):
+            cols = pl.ds(pl.multiple_of((j + first) * BLK, BLK), BLK)
+            fetch = load(j)
+            largest = jnp.zeros((1, BLK), jnp.float32)
+            for i in range(rows // BLK):
+                value = fetch(i)
+                value_ref[pl.ds(i * BLK, BLK), cols] = value
+                largest = jnp.maximum(largest, jnp.max(jnp.abs(value), axis=0, keepdims=True))
+            scale_ref[0:1, cols] = largest
+
+    for out_ref, first, blocks in spans(out_refs):
+        width = pl.ds(first * BLK, blocks * BLK)
+        power = exponents(scale_ref[0:1, width])
+        scale_ref[0:1, width] = jnp.exp2(-power)
+        held = jnp.broadcast_to(power, (EXTRA, blocks * BLK))
+        out_ref[pl.ds(rows, EXTRA), :] = held.astype(jnp.int32).astype(jnp.int16)
+
+        @pl.loop(0, blocks)
+        def _(j):
+            source = pl.ds(pl.multiple_of((j + first) * BLK, BLK), BLK)
+            cols = pl.ds(pl.multiple_of(j * BLK, BLK), BLK)
+            inverse = scale_ref[0:1, source]
+            for i in range(rows // BLK):
+                here = pl.ds(i * BLK, BLK)
+                out_ref[here, cols] = coded(value_ref[here, source], inverse)
+
+
+def message_shapes(rows, blocks, pieces):
+    counts = [blocks] if pieces == 1 else [blocks // 2, blocks - blocks // 2]
+    return [jax.ShapeDtypeStruct((rows + EXTRA, count * BLK), jnp.int16) for count in counts]
 
 
 def message_scratch(rows, blocks):
@@ -115,91 +137,107 @@
     return load
 
 
-def encode_partial(after, partial, pattern, place, rows, first_block, blocks, received=None):
+def encode_partial(after, partial, pattern, place, rows, first_block, blocks, received=(), pieces=1):
     width = partial.shape[2] if first_block > 0 else blocks * BLK
-    extra = [] if received is None else [received]
 
     def kernel(place_ref, pattern_ref, x_ref, *refs):
-        out_ref, value_ref, scale_ref = refs[-3:]
-
-        def load(j):
-            own = masked_load(place_ref, pattern_ref, x_ref, rows, j + first_block)
-            if received is None:
-                return own
-            cols = pl.ds(pl.multiple_of(j * BLK, BLK), BLK)
-            scale = scales(refs[0], rows, cols)
-            return lambda i: own(i) + decoded(refs[0], i * BLK, scale, cols)
-
-        encode_all(load, out_ref, value_ref, scale_ref, rows, blocks)
-
-    return run(
-        kernel, after, [partial] + extra,
+        got_refs, out_refs, (value_ref, scale_ref) = refs[:len(received)], refs[len(received):-2], refs[-2:]
+
+        def segment(code_ref, first):
+            def load(j):
+                own = masked_load(place_ref, pattern_ref, x_ref, rows, j + first + first_block)
+                if code_ref is None:
+                    return own
+                cols = pl.ds(pl.multiple_of(j * BLK, BLK), BLK)
+                scale = scales(code_ref, rows, cols)
+                return lambda i: own(i) + decoded(code_ref, i * BLK, scale, cols)
+
+            return load
+
+        segments = [(first, count, segment(code_ref, first)) for code_ref, first, count in spans(got_refs)]
+        encode_all(segments or [(0, blocks, segment(None, 0))], out_refs, value_ref, scale_ref, rows)
+
+    shapes = message_shapes(rows, blocks, pieces)
+    return run(
+        kernel, after, [partial, *received],
         [pl.BlockSpec((1, rows, width), lambda g, place_ref, pattern_ref: (0, place_ref[0], 0))]
-        + [VMEM_SPEC] * len(extra),
-        VMEM_SPEC, jax.ShapeDtypeStruct((rows + EXTRA, blocks * BLK), jnp.int16),
-        rows * width * 4 + rows * blocks * BLK * 2 * (1 + len(extra)),
+        + [VMEM_SPEC] * len(received),
+        [VMEM_SPEC] * len(shapes), shapes, rows * width * 4 + rows * blocks * BLK * 2 * (1 + len(received)),
         scalars=(place, pattern), scratch=message_scratch(rows, blocks),
     )
 
 
 def merge(after, first, second):
-    rows, blocks = first.shape[0] - EXTRA, first.shape[1] // BLK
-
-    def kernel(a_ref, b_ref, out_ref, value_ref, scale_ref):
-        def load(j):
-            cols = pl.ds(pl.multiple_of(j * BLK, BLK), BLK)
-            a_scale = scales(a_ref, rows, cols)
-            b_scale = scales(b_ref, rows, cols)
-            return lambda i: decoded(a_ref, i * BLK, a_scale, cols) + decoded(b_ref, i * BLK, b_scale, cols)
-
-        encode_all(load, out_ref, value_ref, scale_ref, rows, blocks)
-
-    return run(
-        kernel, after, [first, second], [VMEM_SPEC] * 2, VMEM_SPEC,
-        jax.ShapeDtypeStruct(first.shape, jnp.int16), first.size * 6, scratch=message_scratch(rows, blocks),
+    rows, blocks = first[0].shape[0] - EXTRA, sum(piece.shape[1] for piece in first) // BLK
+
+    def kernel(*refs):
+        count = len(first)
+        out_refs, (value_ref, scale_ref) = refs[2 * count:-2], refs[-2:]
+
+        def segment(a_ref, b_ref):
+            def load(j):
+                cols = pl.ds(pl.multiple_of(j * BLK, BLK), BLK)
+                a_scale = scales(a_ref, rows, cols)
+                b_scale = scales(b_ref, rows, cols)
+                return lambda i: decoded(a_ref, i * BLK, a_scale, cols) + decoded(b_ref, i * BLK, b_scale, cols)
+
+            return load
+
+        segments = [
+            (start, blocks, segment(a_ref, b_ref))
+            for (a_ref, start, blocks), b_ref in zip(spans(refs[:count]), refs[count:2 * count])
+        ]
+        encode_all(segments, out_refs, value_ref, scale_ref, rows)
+
+    return run(
+        kernel, after, [*first, *second], [VMEM_SPEC] * (2 * len(first)), [VMEM_SPEC] * len(first),
+        [jax.ShapeDtypeStruct(piece.shape, jnp.int16) for piece in first],
+        rows * blocks * BLK * 6, scratch=message_scratch(rows, blocks),
     )
 
 
 def low_total(after, partial, pattern, place, received):
-    _, total_rows, width = partial.shape
-    rows = total_rows // len(received)
+    _, rows, width = partial.shape
 
     def kernel(place_ref, pattern_ref, x_ref, *refs):
-        out_ref = refs[-1]
-
-        @pl.loop(0, width // BLK)
-        def _(j):
-            cols = pl.ds(pl.multiple_of(j * BLK, BLK), BLK)
-            load = masked_load(place_ref, pattern_ref, x_ref, total_rows, j)
-            for part, code_ref in enumerate(refs[:-1]):
+        for code_ref, first, blocks in spans(refs[:-1]):
+
+            @pl.loop(0, blocks)
+            def _(j):
+                cols = pl.ds(pl.multiple_of(j * BLK, BLK), BLK)
+                target = pl.ds(pl.multiple_of((j + first) * BLK, BLK), BLK)
+                scale = scales(code_ref, rows, cols)
+                load = masked_load(place_ref, pattern_ref, x_ref, rows, j + first)
+                for i in range(rows // BLK):
+                    refs[-1][0, pl.ds(i * BLK, BLK), target] = load(i) + decoded(code_ref, i * BLK, scale, cols)
+
+    return run(
+        kernel, after, [partial, *received], [VMEM_SPEC] * (1 + len(received)), VMEM_SPEC,
+        jax.ShapeDtypeStruct(partial.shape, jnp.float32), partial.size * 10, scalars=(place, pattern),
+    )
+
+
+def mid_half(after, owner, code, base=None):
+    rows, width = code[0].shape[0] - EXTRA, sum(piece.shape[1] for piece in code)
+    extra = [] if base is None else [base]
+
+    def kernel(owner_ref, *refs):
+        for code_ref, first, blocks in spans(refs[:len(code)]):
+
+            @pl.loop(0, blocks)
+            def _(j):
+                cols = pl.ds(pl.multiple_of(j * BLK, BLK), BLK)
+                target = pl.ds(pl.multiple_of((j + first) * BLK, BLK), BLK)
                 scale = scales(code_ref, rows, cols)
                 for i in range(rows // BLK):
-                    block = part * (rows // BLK) + i
-                    out_ref[0, pl.ds(block * BLK, BLK), cols] = load(block) + decoded(code_ref, i * BLK, scale, cols)
-
-    return run(
-        kernel, after, [partial, *received], [VMEM_SPEC] * (1 + len(received)), VMEM_SPEC,
-        jax.ShapeDtypeStruct(partial.shape, jnp.float32), partial.size * 10, scalars=(place, pattern),
-    )
-
-
-def mid_half(after, owner, code, base=None):
-    rows, width = code.shape[0] - EXTRA, code.shape[1]
-    extra = [] if base is None else [base]
-
-    def kernel(owner_ref, code_ref, *refs):
-        @pl.loop(0, width // BLK)
-        def _(j):
-            cols = pl.ds(pl.multiple_of(j * BLK, BLK), BLK)
-            scale = scales(code_ref, rows, cols)
-            for i in range(rows // BLK):
-                refs[-1][0, pl.ds(i * BLK, BLK), cols] = decoded(code_ref, i * BLK, scale, cols)
-
-    return run(
-        kernel, after, [code] + extra, [VMEM_SPEC] + [pl.BlockSpec(memory_space=pl.ANY)] * len(extra),
+                    refs[-1][0, pl.ds(i * BLK, BLK), target] = decoded(code_ref, i * BLK, scale, cols)
+
+    return run(
+        kernel, after, [*code] + extra,
+        [VMEM_SPEC] * len(code) + [pl.BlockSpec(memory_space=pl.ANY)] * len(extra),
         pl.BlockSpec((1, rows, width), lambda g, owner_ref: (0, owner_ref[0], 0)),
-        jax.ShapeDtypeStruct((1, 2 * rows, width), jnp.float32), code.size * 6, scalars=(owner,),
-        aliases={2: 0} if extra else None,
+        jax.ShapeDtypeStruct((1, 2 * rows, width), jnp.float32), rows * width * 6, scalars=(owner,),
+        aliases={1 + len(code): 0} if extra else None,
     )
 
 
@@ -305,8 +343,8 @@
             up_ref[:, PANEL:] = value
             low_ref[:, PANEL:] = value.astype(jnp.bfloat16)
 
-        pl.when(flag_ref[0] == 0)(lambda: write(own_ref, own_scale))
-        pl.when(flag_ref[0] == 1)(lambda: write(got_ref, got_scale))
+        pl.when(flag_ref[1] == 0)(lambda: write(own_ref, own_scale))
+        pl.when(flag_ref[1] == 1)(lambda: write(got_ref, got_scale))
 
     first_block = lambda g: (0, 0)
     code_spec = pl.BlockSpec((BLK, rest), first_block)
@@ -344,12 +382,12 @@
                 value = permuted_codes(order_ref[...], code_ref[pl.ds(row, BLK), :], scale)
                 out_ref[:, PANEL:] = value - low_dot(low, up_low_ref[:, PANEL:])
 
-            owned_a = part == flag_ref[0]
-            owned_b = part == 2 + flag_ref[1]
+            owned_b = part == flag_ref[1]
+            owned_a = part == 2 + flag_ref[0]
+            pl.when(owned_b)(lambda: write(own_b))
+            pl.when((part < 2) & jnp.logical_not(owned_b))(lambda: write(got_b))
             pl.when(owned_a)(lambda: write(own_a))
-            pl.when((part < 2) & jnp.logical_not(owned_a))(lambda: write(got_a))
-            pl.when(owned_b)(lambda: write(own_b))
-            pl.when((part >= 2) & jnp.logical_not(owned_b))(lambda: write(got_b))
+            pl.when((part >= 2) & jnp.logical_not(owned_a))(lambda: write(got_a))
             product = low_dot(low, up_low_ref[:, :PANEL])
             out_ref[:, :PANEL] = jnp.where(first_col, slab_ref[...], slab_ref[...] - product)
 
@@ -378,15 +416,16 @@
     def sender(partial, pattern, rows, first_block, blocks):
         corner_block = [row * pattern.shape[1], col * pattern.shape[2]]
 
-        def encode(after, part, received=None):
+        def encode(after, part, received=(), pieces=1):
             place = jnp.stack([jnp.asarray(part, jnp.int32), *corner_block]).astype(jnp.int32)
-            return encode_partial(after, partial, pattern[0], place, rows, first_block, blocks, received)
+            return encode_partial(after, partial, pattern[0], place, rows, first_block, blocks, received, pieces)
 
         return encode
 
-    def exchanged(after, own, some):
+    def exchanged(after, own, got, some):
+        own = merge(after, own, got)
         for bit in some:
-            own = after = merge(after, own, swapped(own, bit))
+            own = merge([], own, swapped(own, bit))
         return own
 
     top_rows, top_blocks = partial_top.shape[1], partial_top.shape[2] // BLK
@@ -395,53 +434,53 @@
     encode_mid = sender(partial_mid, pattern_mid, partial_mid.shape[1] // 2, 0, mid_blocks)
     encode_slab = sender(partial_top, pattern_top, top_rows, 0, 1)
     encode_top = sender(partial_top, pattern_top, top_rows // 4, 1, top_blocks - 1)
-    encode_low = sender(partial_low, pattern_low, low_rows // 2, 0, low_blocks)
-
-    mid_sent = encode_mid(None, 1 - high_bit)
+    encode_low = sender(partial_low, pattern_low, low_rows, 0, low_blocks)
+
+
+    corner = exact_dot(order[:BLK].astype(jnp.float32), partial_top[0, :BLK, :BLK])
+    count = lax.axis_size("layer")
+    beside = [lax.ppermute(corner, "layer", [(i, i ^ apart) for i in range(count)]) for apart in (1, 2, 3)]
+
+    slab = encode_slab([corner], 0)
+    slab_got = swapped(slab, 0)
+    corner = (corner + beside[0]) + (beside[1] + beside[2])
+    for bit in bits[2:]:
+        corner = corner + swapped(corner, bit)
+    corner_row = broadcast_stages(corner, "row")
+    corner_col = broadcast_stages(corner_row[-1], "col")
+
+    mid_sent = encode_mid([*[*slab]], 1 - high_bit, (), 1)
     mid_got = swapped(mid_sent, 1)
-    slab = last = encode_slab(mid_sent, 0)
-    slab_got = swapped(slab, 0)
-
-    corner = exact_dot(order[:BLK].astype(jnp.float32), partial_top[0, :BLK, :BLK])
-    for bit in bits:
-        corner = corner + swapped(corner, bit)
-    corner = broadcast_from_first(broadcast_from_first(corner, "row"), "col")
-
-    last = encode_top(last, 1 - low_bit)
-    a_got = swapped(last, 0)
-    last = encode_top(last, 3 - high_bit)
-    b_got = swapped(last, 1)
-    slab = last = merge(last, slab, slab_got)
-    slab = exchanged(last, slab, bits[1:-1])
+    a_sent = encode_top([*mid_sent, corner_row[-1]], 3 - low_bit)
+    a_got = swapped(a_sent, 0)
+    b_sent = encode_top([*a_sent, corner_col[0]], 1 - high_bit)
+    b_got = swapped(b_sent, 1)
+    slab = exchanged([*b_sent, corner_col[-1]], slab, slab_got, bits[1:-1])
     slab_got = swapped(slab, bits[-1])
-    mid = last = encode_mid(last, high_bit, mid_got)
+    mid = encode_mid([*slab], high_bit, mid_got, 1)
     mid_got = swapped(mid, 0)
-    a = last = encode_top(last, low_bit, a_got)
+    packed, lower_inverse, upper_inverse = factor([*mid, *a_got], corner_col[-1])
+    b = encode_top([*[packed]], high_bit, b_got)
+    b_got = swapped(b, 0)
+    a = encode_top([*b], 2 + low_bit, a_got)
     a_got = swapped(a, 1)
-    packed, lower_inverse, upper_inverse = factor(last, corner)
-    b = last = encode_top(packed, 2 + high_bit, b_got)
-    b_got = swapped(b, 0)
-    last = low_first = encode_low(last, 0)
-    low_first = swapped(low_first, 0)
-    panel, lower_low = lower_panel(last, flags, order, slab, slab_got, upper_inverse)
-    lower_low = broadcast_from_first(lower_low, "col")
-    b = last = merge(panel, b, b_got)
-    b = last = exchanged(last, b, bits[2:])
+    panel, lower_low = lower_panel([*a, *mid_got], flags, order, *slab, *slab_got, upper_inverse)
+    lower_low = broadcast_stages(lower_low, "col")[-1]
+    mid = merge([*[panel]], mid, mid_got)
+    mid_got = swapped(mid, 1)
+    a = exchanged([*mid], a, a_got, bits[2:])
+    a_got = swapped(a, 0)
+    b = exchanged([*a], b, b_got, bits[2:])
     b_got = swapped(b, 1)
-    a = last = merge(last, a, a_got)
-    a = last = exchanged(last, a, bits[2:])
-    a_got = swapped(a, 0)
-    mid = last = merge(last, mid, mid_got)
-    mid_got = swapped(mid, 1)
-    last = low_second = encode_low(last, 1)
-    low_second = swapped(low_second, 0)
-    mid_sums = mid_half(last, high_bit[None].astype(jnp.int32), mid)
-    upper, upper_low = upper_panel(mid_sums, flags, order, panel, a, a_got, lower_inverse)
-    upper_low = broadcast_from_first(upper_low, "row")
-    top_factor = top_total(None, flags, order, (a, a_got, b, b_got), panel, lower_low, upper_low, upper, packed)
+    mid_sums = mid_half([*b], high_bit[None].astype(jnp.int32), mid)
+    low = encode_low([*[mid_sums]], 0, (), 2)
+    low_got = swapped(low, 0)
+    upper, upper_low = upper_panel([*low], flags, order, panel, *b, *b_got, lower_inverse)
+    upper_low = broadcast_stages(upper_low, "row")[-1]
+    top_factor = top_total([*[upper]], flags, order, (*a, *a_got, *b, *b_got), panel, lower_low, upper_low, upper, packed)
     low_place = jnp.stack([jnp.int32(0), row * pattern_low.shape[1], col * pattern_low.shape[2]]).astype(jnp.int32)
-    low_sums = low_total(top_factor, partial_low, pattern_low[0], low_place, [low_first, low_second])
-    mid_sums = mid_half(top_factor, (1 - high_bit)[None].astype(jnp.int32), mid_got, mid_sums)
+    low_sums = low_total([*[top_factor]], partial_low, pattern_low[0], low_place, low_got)
+    mid_sums = mid_half([top_factor], (1 - high_bit)[None].astype(jnp.int32), mid_got, mid_sums)
     return top_factor, mid_sums, low_sums
 
 

time: 203 us -> 156 us (0.77)
  waiting for transfers between devices: 82.3 us -> 39.9 us
  Pallas kernels: 72.2 us -> 68.9 us
    ppermute x21 -> x22, waiting for transfers between devices: 82.3 us -> 39.9 us  [the longest x13 37.3 us: swapped(): lax.ppermute(piece, 'layer', pairs)]
    pallas_call x20 -> x19, Pallas kernels: 72.2 us -> 68.9 us  [run(): pl.pallas_call(body, grid_spec=pltpu.PrefetchScalarGridSpec(num_scalar_pr...]
    unnamed x20 -> x30, local copies, waits for them, and re-layouts: 6.12 us -> 4.4 us
    ppermute x21 -> x22, starting transfers between devices: 34.5 us -> 32.8 us  [the longest x6 15.7 us: broadcast_stages(): lax.ppermute(value, axis, [(i, i + span) for i in range(0, count, 2 * spa...]
  transfers between devices with their start and end apart: 21 -> 22, of which waited for: 8 -> 9; matrix products, arithmetic and copies ran while one was open for 1% -> 3% of each run, Pallas kernels for 35% -> 43%
where the time goes in v3:
time: 156 us; the launch traced here: 154 us
  Pallas kernels  68.9 us (44%)
  waiting for transfers between devices  39.9 us (26%)
  starting transfers between devices  32.8 us (21%)
  local copies, waits for them, and re-layouts  5.33 us (3%)
  other arithmetic  4.78 us (3%)
    pallas_call x19, Pallas kernels, run(): pl.pallas_call(body, grid_spec=pltpu.PrefetchScalarGridSpec(num_scalar_pr...  68.9 us
    ppermute x13, waiting for transfers between devices, swapped(): lax.ppermute(piece, 'layer', pairs)  37.3 us
    ppermute x6, starting transfers between devices, broadcast_stages(): lax.ppermute(value, axis, [(i, i + span) for i in range(0, count, 2 * spa...  15.7 us
    ppermute x13, starting transfers between devices, swapped(): lax.ppermute(piece, 'layer', pairs)  12.5 us
    ppermute x3, starting transfers between devices, on_device(): lax.ppermute(corner, 'layer', [(i, i ^ apart) for i in range(count)])  4.6 us
    unnamed x30, local copies, waits for them, and re-layouts  4.4 us
  transfers between devices with their start and end apart: 22, of which 9 were waited for; matrix products, arithmetic and copies ran while one was open for 3% of the time, Pallas kernels for 43%

profile of v3, /device:TPU:0, one launch (start us, length us, event | category | flops | bytes accessed | tf_op | source)
XLA Modules:
  0.0 153.8 jit_solution(5395113334462539372)
XLA Ops:
  2.9 4.0 %collective-permute-start.2 = (f32[128,128]{1,0:T(8,128)S(1)}, f32[128,128]{1,0:T(8,128)}, u32[]{:S(2)}, u32[]{:S(2)}) collective-permute-start(f32[128,128]{1,0:T(8,128)S(1)} %fusion.refs_3_), channel_id=1, source_target_pairs={{0,24},{8,16},{16,8},{24,0},{1,25},{9,17},{17,9},{25,1},{2,26},{10... | collective-permute-start | bytes 196616 | tf_op jit(solution)/shard_map/ppermute | solution.py:442
  8.3 2.1 %shard_map.94.refs_3_.refs_0_ = s16[2064,128]{1,0:T(8,128)(2,1)S(1)} custom-call(s32[3]{0:T(128)S(1)} %fusion.6.refs_0_, s32[16,8]{1,0:T(8,128)S(1)} %copy.17.refs_1_, f32[1,2048,1024]{2,1,0:T(8,128)} %refs_2_.15, f32[128,128]{1,0:T(8,128)S(1)} %fusion.refs_3_), custom_call_target="tpu_custom_call" | custom-call | bytes 1024 | tf_op jit(solution)/shard_map/pallas_call | solution.py:63
  10.4 2.0 %collective-permute-start.9 = (s16[2064,128]{1,0:T(8,128)(2,1)S(1)}, s16[2064,128]{1,0:T(8,128)(2,1)}, u32[]{:S(2)}, u32[]{:S(2)}) collective-permute-start(s16[2064,128]{1,0:T(8,128)(2,1)S(1)} %shard_map.94.refs_3_.refs_0_), channel_id=1, source_target_pairs={{0,8},{8,0},{16,24},{24,16},{1,9},{9,1},{17,25},{25,17},{2,10},{10... | collective-permute-start | bytes 1585160 | tf_op jit(solution)/shard_map/ppermute | solution.py:21
  12.6 3.1 %shard_map.95.refs_3_ = s16[784,768]{1,0:T(8,128)(2,1)S(1)} custom-call(s32[3]{0:T(128)S(1)} %add_add_fusion.3.refs_0_, s32[12,6]{1,0:T(8,128)S(1)} %bitcast.19, f32[1,1536,768]{2,1,0:T(8,128)} %refs_2_.13, s16[2064,128]{1,0:T(8,128)(2,1)S(1)} %shard_map.94.refs_3_.refs_0_), custom_call_target="tpu_custom_call" | custom-call | bytes 1024 | tf_op jit(solution)/shard_map/pallas_call | solution.py:63
  15.7 1.6 %collective-permute-start.8 = (s16[784,768]{1,0:T(8,128)(2,1)S(1)}, s16[784,768]{1,0:T(8,128)(2,1)S(1)}, u32[]{:S(2)}, u32[]{:S(2)}) collective-permute-start(s16[784,768]{1,0:T(8,128)(2,1)S(1)} %shard_map.95.refs_3_), channel_id=1, source_target_pairs={{0,16},{8,24},{16,0},{24,8},{1,17},{9,25},{17,1},{25,9},{2,18},{10... | collective-permute-start | bytes 3612680 | tf_op jit(solution)/shard_map/ppermute | solution.py:21
  20.4 4.5 %collective-permute-start.5 = (f32[128,128]{1,0:T(8,128)S(1)}, f32[128,128]{1,0:T(8,128)S(1)}, u32[]{:S(2)}, u32[]{:S(2)}) collective-permute-start(f32[128,128]{1,0:T(8,128)S(1)} %broadcast_select_fusion.5.refs_4_), channel_id=1, source_target_pairs={{0,2},{4,6},{8,10},{12,14},{16,18},{20,22},{24,26},{28,30}} | collective-permute-start | bytes 196616 | tf_op jit(solution)/shard_map/ppermute | solution.py:30
  25.0 1.8 %collective-permute-done.5 = f32[128,128]{1,0:T(8,128)S(1)} collective-permute-done((f32[128,128]{1,0:T(8,128)S(1)}, f32[128,128]{1,0:T(8,128)S(1)}, u32[]{:S(2)}, u32[]{:S(2)}) %collective-permute-start.5) | collective-permute-done | bytes 65568 | tf_op jit(solution)/shard_map/ppermute | solution.py:30
  28.2 3.8 %shard_map.96.refs_3_ = s16[528,896]{1,0:T(8,128)(2,1)} custom-call(s32[3]{0:T(128)S(1)} %add_add_fusion.2.refs_0_, s32[16,8]{1,0:T(8,128)S(1)} %copy.17.refs_1_, f32[1,2048,1024]{2,1,0:T(8,128)} %refs_2_.15, s16[784,768]{1,0:T(8,128)(2,1)S(1)} %shard_map.95.refs_3_, f32[128,128]{1,0:T(8,128)S(1)} %broadcast_select_fusion.5.refs_4_), custom_call_target="tpu_custom_call" | custom-call | bytes 1024 | tf_op jit(solution)/shard_map/pallas_call | solution.py:63
  32.6 3.8 %shard_map.97.refs_2_ = s16[528,896]{1,0:T(8,128)(2,1)} custom-call(s32[3]{0:T(128)S(1)} %add_add_fusion.5.refs_0_, s32[16,8]{1,0:T(8,128)S(1)} %copy.17.refs_1_, f32[1,2048,1024]{2,1,0:T(8,128)} %refs_2_.15, s16[528,896]{1,0:T(8,128)(2,1)} %shard_map.96.refs_3_, f32[128,128]{1,0:T(8,128)S(1)} %broadcast_select_fusion.4.refs_4_), custom_call_target="tpu_custom_call" | custom-call | bytes 1024 | tf_op jit(solution)/shard_map/pallas_call | solution.py:63
  37.0 1.5 shard_map.98.refs_4_.refs_2_
  38.5 6.7 %collective-permute-done.8.refs_3_ = s16[784,768]{1,0:T(8,128)(2,1)S(1)} collective-permute-done((s16[784,768]{1,0:T(8,128)(2,1)S(1)}, s16[784,768]{1,0:T(8,128)(2,1)S(1)}, u32[]{:S(2)}, u32[]{:S(2)}) %collective-permute-start.8) | collective-permute-done | bytes 1204256 | tf_op jit(solution)/shard_map/ppermute | solution.py:21
  47.5 3.2 %shard_map.99.refs_1_.refs_0_ = s16[784,768]{1,0:T(8,128)(2,1)S(1)} custom-call(s32[3]{0:T(128)S(1)} %add_add_fusion.6.refs_0_, s32[12,6]{1,0:T(8,128)S(1)} %bitcast.20, f32[1,1536,768]{2,1,0:T(8,128)} %refs_2_.13, s16[784,768]{1,0:T(8,128)(2,1)S(1)} %copy-done.10, s16[2064,128]{1,0:T(8,128)(2,1)S(1)} %shard_map.98.refs_4_.refs_2_), custom_call_target="tpu_custom_call" | custom-call | bytes 1024 | tf_op jit(solution)/shard_map/pallas_call | solution.py:63
  51.0 1.9 %collective-permute-start.12 = (s16[2064,128]{1,0:T(8,128)(2,1)}, s16[2064,128]{1,0:T(8,128)(2,1)S(1)}, u32[]{:S(2)}, u32[]{:S(2)}) collective-permute-start(s16[2064,128]{1,0:T(8,128)(2,1)} %copy-done.7), channel_id=1, source_target_pairs={{0,16},{8,24},{16,0},{24,8},{1,17},{9,25},{17,1},{25,9},{2,18},{10... | collective-permute-start | bytes 1585160 | tf_op jit(solution)/shard_map/ppermute | solution.py:21
  53.0 3.3 %collective-permute-done.4.refs_2_.refs_3_ = s16[528,896]{1,0:T(8,128)(2,1)} collective-permute-done((s16[528,896]{1,0:T(8,128)(2,1)}, s16[528,896]{1,0:T(8,128)(2,1)}, u32[]{:S(2)}, u32[]{:S(2)}) %collective-permute-start.4) | collective-permute-done | bytes 946208 | tf_op jit(solution)/shard_map/ppermute | solution.py:21
  56.3 15.3 %shard_map.100 = (f32[128,128]{1,0:T(8,128)S(1)}, f32[128,128]{1,0:T(8,128)S(1)}, f32[128,128]{1,0:T(8,128)S(1)}) custom-call(f32[128,128]{1,0:T(8,128)S(1)} %broadcast_select_fusion.3.refs_3_.refs_0_, s16[784,768]{1,0:T(8,128)(2,1)S(1)} %shard_map.99.refs_1_.refs_0_, s16[528,896]{1,0:T(8,128)(2,1)} %collective-permute-done.4.refs_2_.refs_3_), custom_call_target="tpu_custom_call" | custom-call | bytes 1024 | tf_op jit(solution)/shard_map/pallas_call | solution.py:63
  71.6 3.3 %shard_map.101.refs_4_.refs_0_ = s16[528,896]{1,0:T(8,128)(2,1)S(1)} custom-call(s32[3]{0:T(128)S(1)} %add_add_fusion.4.refs_0_, s32[16,8]{1,0:T(8,128)S(1)} %copy.17.refs_1_, f32[1,2048,1024]{2,1,0:T(8,128)} %refs_2_.15, s16[528,896]{1,0:T(8,128)(2,1)} %collective-permute-done.6.refs_3_, f32[128,128]{1,0:T(8,128)S(1)} %get-tuple-element.12.refs_4_.refs_10_), custom_call_target="tpu_custom_call" | custom-call | bytes 1024 | tf_op jit(solution)/shard_map/pallas_call | solution.py:63
  74.9 3.3 %shard_map.102.refs_5_.refs_0_ = s16[528,896]{1,0:T(8,128)(2,1)S(1)} custom-call(s32[3]{0:T(128)S(1)} %add_add_fusion.1.refs_0_, s32[16,8]{1,0:T(8,128)S(1)} %copy.17.refs_1_, f32[1,2048,1024]{2,1,0:T(8,128)} %refs_2_.15, s16[528,896]{1,0:T(8,128)(2,1)} %collective-permute-done.4.refs_2_.refs_3_, s16[528,896]{1,0:T(8,128)(2,1)S(1)} %shard_map.101.refs_4_.refs_0_), custom_call_target="tpu_custom_call" | custom-call | bytes 1024 | tf_op jit(solution)/shard_map/pallas_call | solution.py:63
  79.3 2.6 %collective-permute-done.11.refs_6_.refs_1_ = s16[784,768]{1,0:T(8,128)(2,1)S(1)} collective-permute-done((s16[784,768]{1,0:T(8,128)(2,1)S(1)}, s16[784,768]{1,0:T(8,128)(2,1)S(1)}, u32[]{:S(2)}, u32[]{:S(2)}) %collective-permute-start.11) | collective-permute-done | bytes 1204256 | tf_op jit(solution)/shard_map/ppermute | solution.py:21
  82.0 2.9 %shard_map.103 = (f32[2048,128]{1,0:T(8,128)S(1)}, bf16[2048,128]{1,0:T(8,128)(2,1)S(1)}) custom-call(s32[4]{0:T(128)S(1)} %pad_add_fusion.2.refs_0_, bf16[2048,128]{1,0:T(8,128)(2,1)S(1)} %get-tuple-element.22.refs_1_, s16[2064,128]{1,0:T(8,128)(2,1)S(1)} %copy-done.8, s16[2064,128]{1,0:T(8,128)(2,1)S(1)} %collective-permute-done.12.refs_3_, ...), custom_call_target="tpu_custom_call" | custom-call | bytes 1024 | tf_op jit(solution)/shard_map/pallas_call | solution.py:63
  84.9 5.2 %collective-permute-start.16 = (bf16[2048,128]{1,0:T(8,128)(2,1)S(1)}, bf16[2048,128]{1,0:T(8,128)(2,1)S(1)}, u32[]{:S(2)}, u32[]{:S(2)}) collective-permute-start(bf16[2048,128]{1,0:T(8,128)(2,1)S(1)} %get-tuple-element.15), channel_id=1, source_target_pairs={{0,2},{4,6},{8,10},{12,14},{16,18},{20,22},{24,26},{28,30}} | collective-permute-start | bytes 1572872 | tf_op jit(solution)/shard_map/ppermute | solution.py:30
  92.4 5.7 %collective-permute-done.10.refs_1_ = s16[528,896]{1,0:T(8,128)(2,1)S(1)} collective-permute-done((s16[528,896]{1,0:T(8,128)(2,1)S(1)}, s16[528,896]{1,0:T(8,128)(2,1)S(1)}, u32[]{:S(2)}, u32[]{:S(2)}) %collective-permute-start.10) | collective-permute-done | bytes 946208 | tf_op jit(solution)/shard_map/ppermute | solution.py:21
  99.0 1.7 %collective-permute-done.14.refs_1_ = s16[528,896]{1,0:T(8,128)(2,1)S(1)} collective-permute-done((s16[528,896]{1,0:T(8,128)(2,1)S(1)}, s16[528,896]{1,0:T(8,128)(2,1)S(1)}, u32[]{:S(2)}, u32[]{:S(2)}) %collective-permute-start.14) | collective-permute-done | bytes 946208 | tf_op jit(solution)/shard_map/ppermute | solution.py:21
  103.0 2.1 %collective-permute-start.17 = (bf16[2048,128]{1,0:T(8,128)(2,1)}, bf16[2048,128]{1,0:T(8,128)(2,1)}, u32[]{:S(2)}, u32[]{:S(2)}) collective-permute-start(bf16[2048,128]{1,0:T(8,128)(2,1)} %broadcast_select_fusion), channel_id=1, source_target_pairs={{0,1},{2,3},{4,5},{6,7},{8,9},{10,11},{12,13},{14,15},{16,17},{18,... | collective-permute-start | bytes 1572872 | tf_op jit(solution)/shard_map/ppermute | solution.py:30
  105.1 1.5 collective-permute-start.19
  107.3 1.7 %shard_map.107.refs_3_.refs_2_ = f32[1,1536,768]{2,1,0:T(8,128)} custom-call(s32[1]{0:T(128)} %bitcast.1.refs_0_, s16[784,768]{1,0:T(8,128)(2,1)S(1)} %shard_map.104.refs_2_.refs_1_, s16[528,896]{1,0:T(8,128)(2,1)S(1)} %shard_map.106.refs_2_.refs_3_.refs_4_), custom_call_target="tpu_custom_call" | custom-call | bytes 1024 | tf_op jit(solution)/shard_map/pallas_call | solution.py:63
  111.1 1.6 %collective-permute-start.20 = (s16[1040,256]{1,0:T(8,128)(2,1)S(1)}, s16[1040,256]{1,0:T(8,128)(2,1)S(1)}, u32[]{:S(2)}, u32[]{:S(2)}) collective-permute-start(s16[1040,256]{1,0:T(8,128)(2,1)S(1)} %get-tuple-element.17.refs_8_), channel_id=1, source_target_pairs={{0,8},{8,0},{16,24},{24,16},{1,9},{9,1},{17,25},{25,17},{2,10},{10... | collective-permute-start | bytes 1597448 | tf_op jit(solution)/shard_map/ppermute | solution.py:21
  112.6 13.0 %collective-permute-done.15.refs_5_.refs_6_ = s16[528,896]{1,0:T(8,128)(2,1)} collective-permute-done((s16[528,896]{1,0:T(8,128)(2,1)S(1)}, s16[528,896]{1,0:T(8,128)(2,1)}, u32[]{:S(2)}, u32[]{:S(2)}) %collective-permute-start.15) | collective-permute-done | bytes 946208 | tf_op jit(solution)/shard_map/ppermute | solution.py:21
  126.2 2.0 %shard_map.109 = (f32[128,1024]{1,0:T(8,128)S(1)}, bf16[128,1024]{1,0:T(8,128)(2,1)S(1)}) custom-call(s32[4]{0:T(128)S(1)} %pad_add_fusion.2.refs_0_, bf16[2048,128]{1,0:T(8,128)(2,1)S(1)} %copy-done.4, f32[2048,128]{1,0:T(8,128)S(1)} %copy-done.1, s16[528,896]{1,0:T(8,128)(2,1)S(1)} %shard_map.106.refs_2_.refs_3_.refs_4_, ...), custom_call_target="tpu_custom_call" | custom-call | bytes 1024 | tf_op jit(solution)/shard_map/pallas_call | solution.py:63
  130.7 13.7 %shard_map.110.refs_3_.refs_5_ = f32[2048,1024]{1,0:T(8,128)} custom-call(s32[4]{0:T(128)S(1)} %pad_add_fusion.2.refs_0_, bf16[2048,128]{1,0:T(8,128)(2,1)S(1)} %copy-done.4, s16[528,896]{1,0:T(8,128)(2,1)S(1)} %shard_map.105.refs_2_, s16[528,896]{1,0:T(8,128)(2,1)} %collective-permute-done.13.refs_3_, ...), custom_call_target="tpu_custom_call" | custom-call | bytes 1024 | tf_op jit(solution)/shard_map/pallas_call | solution.py:63
  144.3 4.3 %collective-permute-done.19.refs_1_ = s16[784,768]{1,0:T(8,128)(2,1)} collective-permute-done((s16[784,768]{1,0:T(8,128)(2,1)S(1)}, s16[784,768]{1,0:T(8,128)(2,1)}, u32[]{:S(2)}, u32[]{:S(2)}) %collective-permute-start.19) | collective-permute-done | bytes 1204256 | tf_op jit(solution)/shard_map/ppermute | solution.py:21
  148.6 2.9 %shard_map.111 = f32[1,1536,768]{2,1,0:T(8,128)} custom-call(s32[1]{0:T(128)} %bitcast.9.refs_0_, s16[784,768]{1,0:T(8,128)(2,1)} %collective-permute-done.19.refs_1_, f32[1,1536,768]{2,1,0:T(8,128)} %shard_map.107.refs_3_.refs_2_, f32[2048,1024]{1,0:T(8,128)} %shard_map.110.refs_3_.refs_5_), custom_call_target="tpu_custom_call", output_to_operand_aliasing={{}: (2, {})} | custom-call | bytes 1024 | tf_op jit(solution)/shard_map/pallas_call | solution.py:63
  151.5 2.3 %shard_map.112 = f32[1,1024,512]{2,1,0:T(8,128)} custom-call(s32[3]{0:T(128)S(1)} %fusion.7.refs_0_, s32[8,4]{1,0:T(8,128)S(1)} %copy.18.refs_1_, f32[1,1024,512]{2,1,0:T(8,128)S(1)} %copy-done.2, s16[1040,256]{1,0:T(8,128)(2,1)S(1)} %collective-permute-done.20.refs_3_, s16[1040,256]{1,0:T(8,128)(2,1)S(1)} %collective-permute-done.21.refs_4_, ...), custom_call_target="tpu_custom_call" | custom-call | bytes 1024 | tf_op jit(solution)/shard_map/pallas_call | solution.py:63
  (83 shorter events, 24.6 us)
Async XLA Ops:
  1.8 80.2 %copy-start.3 = (bf16[2048,128]{1,0:T(8,128)(2,1)}, bf16[2048,128]{1,0:T(8,128)(2,1)S(1)}, u32[]{:S(2)}) copy-start(bf16[2048,128]{1,0:T(8,128)(2,1)S(1)} %get-tuple-element.22.refs_1_) | copy-start | bytes 1572868
  2.9 14.4 %collective-permute-start.2 = (f32[128,128]{1,0:T(8,128)S(1)}, f32[128,128]{1,0:T(8,128)}, u32[]{:S(2)}, u32[]{:S(2)}) collective-permute-start(f32[128,128]{1,0:T(8,128)S(1)} %fusion.refs_3_), channel_id=1, source_target_pairs={{0,24},{8,16},{16,8},{24,0},{1,25},{9,17},{17,9},{25,1},{2,26},{10... | collective-permute-start | bytes 196616 | tf_op jit(solution)/shard_map/ppermute | solution.py:442
  6.8 10.4 %collective-permute-start.1 = (f32[128,128]{1,0:T(8,128)S(1)}, f32[128,128]{1,0:T(8,128)}, u32[]{:S(2)}, u32[]{:S(2)}) collective-permute-start(f32[128,128]{1,0:T(8,128)S(1)} %fusion.refs_3_), channel_id=1, source_target_pairs={{0,16},{8,24},{16,0},{24,8},{1,17},{9,25},{17,1},{25,9},{2,18},{10... | collective-permute-start | bytes 196616 | tf_op jit(solution)/shard_map/ppermute | solution.py:442
  7.4 9.9 %collective-permute-start = (f32[128,128]{1,0:T(8,128)S(1)}, f32[128,128]{1,0:T(8,128)}, u32[]{:S(2)}, u32[]{:S(2)}) collective-permute-start(f32[128,128]{1,0:T(8,128)S(1)} %fusion.refs_3_), channel_id=1, source_target_pairs={{0,8},{8,0},{16,24},{24,16},{1,9},{9,1},{17,25},{25,17},{2,10},{10... | collective-permute-start | bytes 196616 | tf_op jit(solution)/shard_map/ppermute | solution.py:442
  8.3 4.1 %copy-start.13 = (s32[1,12,6]{1,0,2:T(1,128)S(1)}, s32[1,12,6]{1,0,2:T(1,128)}, u32[]{:S(2)}) copy-start(s32[1,12,6]{1,0,2:T(1,128)} %param.11) | copy-start | bytes 868
  10.4 26.5 %collective-permute-start.9 = (s16[2064,128]{1,0:T(8,128)(2,1)S(1)}, s16[2064,128]{1,0:T(8,128)(2,1)}, u32[]{:S(2)}, u32[]{:S(2)}) collective-permute-start(s16[2064,128]{1,0:T(8,128)(2,1)S(1)} %shard_map.94.refs_3_.refs_0_), channel_id=1, source_target_pairs={{0,8},{8,0},{16,24},{24,16},{1,9},{9,1},{17,25},{25,17},{2,10},{10... | collective-permute-start | bytes 1585160 | tf_op jit(solution)/shard_map/ppermute | solution.py:21
  15.7 29.5 %collective-permute-start.8 = (s16[784,768]{1,0:T(8,128)(2,1)S(1)}, s16[784,768]{1,0:T(8,128)(2,1)S(1)}, u32[]{:S(2)}, u32[]{:S(2)}) collective-permute-start(s16[784,768]{1,0:T(8,128)(2,1)S(1)} %shard_map.95.refs_3_), channel_id=1, source_target_pairs={{0,16},{8,24},{16,0},{24,8},{1,17},{9,25},{17,1},{25,9},{2,18},{10... | collective-permute-start | bytes 3612680 | tf_op jit(solution)/shard_map/ppermute | solution.py:21
  18.2 2.2 %collective-permute-start.3 = (f32[128,128]{1,0:T(8,128)S(1)}, f32[128,128]{1,0:T(8,128)S(1)}, u32[]{:S(2)}, u32[]{:S(2)}) collective-permute-start(f32[128,128]{1,0:T(8,128)S(1)} %add_add_fusion), channel_id=1, source_target_pairs={{0,4},{1,5},{2,6},{3,7},{8,12},{9,13},{10,14},{11,15},{16,20},{17,... | collective-permute-start | bytes 196616 | tf_op jit(solution)/shard_map/ppermute | solution.py:30
  20.4 6.4 %collective-permute-start.5 = (f32[128,128]{1,0:T(8,128)S(1)}, f32[128,128]{1,0:T(8,128)S(1)}, u32[]{:S(2)}, u32[]{:S(2)}) collective-permute-start(f32[128,128]{1,0:T(8,128)S(1)} %broadcast_select_fusion.5.refs_4_), channel_id=1, source_target_pairs={{0,2},{4,6},{8,10},{12,14},{16,18},{20,22},{24,26},{28,30}} | collective-permute-start | bytes 196616 | tf_op jit(solution)/shard_map/ppermute | solution.py:30
  26.8 10.1 %collective-permute-start.7 = (f32[128,128]{1,0:T(8,128)S(1)}, f32[128,128]{1,0:T(8,128)S(1)}, u32[]{:S(2)}, u32[]{:S(2)}) collective-permute-start(f32[128,128]{1,0:T(8,128)S(1)} %broadcast_select_fusion.4.refs_4_), channel_id=1, source_target_pairs={{0,1},{2,3},{4,5},{6,7},{8,9},{10,11},{12,13},{14,15},{16,17},{18,... | collective-permute-start | bytes 196616 | tf_op jit(solution)/shard_map/ppermute | solution.py:30
  32.0 24.2 %collective-permute-start.4 = (s16[528,896]{1,0:T(8,128)(2,1)}, s16[528,896]{1,0:T(8,128)(2,1)}, u32[]{:S(2)}, u32[]{:S(2)}) collective-permute-start(s16[528,896]{1,0:T(8,128)(2,1)} %shard_map.96.refs_3_), channel_id=1, source_target_pairs={{0,8},{8,0},{16,24},{24,16},{1,9},{9,1},{17,25},{25,17},{2,10},{10... | collective-permute-start | bytes 2838536 | tf_op jit(solution)/shard_map/ppermute | solution.py:21
  36.4 35.1 %collective-permute-start.6 = (s16[528,896]{1,0:T(8,128)(2,1)}, s16[528,896]{1,0:T(8,128)(2,1)}, u32[]{:S(2)}, u32[]{:S(2)}) collective-permute-start(s16[528,896]{1,0:T(8,128)(2,1)} %shard_map.97.refs_2_), channel_id=1, source_target_pairs={{0,16},{8,24},{16,0},{24,8},{1,17},{9,25},{17,1},{25,9},{2,18},{10... | collective-permute-start | bytes 2838536 | tf_op jit(solution)/shard_map/ppermute | solution.py:21
  38.5 6.7 %copy-start.7 = (s16[2064,128]{1,0:T(8,128)(2,1)}, s16[2064,128]{1,0:T(8,128)(2,1)S(1)}, u32[]{:S(2)}) copy-start(s16[2064,128]{1,0:T(8,128)(2,1)S(1)} %shard_map.98.refs_4_.refs_2_) | copy-start | bytes 1585156
  50.7 31.3 %collective-permute-start.11 = (s16[784,768]{1,0:T(8,128)(2,1)S(1)}, s16[784,768]{1,0:T(8,128)(2,1)S(1)}, u32[]{:S(2)}, u32[]{:S(2)}) collective-permute-start(s16[784,768]{1,0:T(8,128)(2,1)S(1)} %shard_map.99.refs_1_.refs_0_), channel_id=1, source_target_pairs={{0,8},{8,0},{16,24},{24,16},{1,9},{9,1},{17,25},{25,17},{2,10},{10... | collective-permute-start | bytes 3612680 | tf_op jit(solution)/shard_map/ppermute | solution.py:21
  51.0 28.4 %collective-permute-start.12 = (s16[2064,128]{1,0:T(8,128)(2,1)}, s16[2064,128]{1,0:T(8,128)(2,1)S(1)}, u32[]{:S(2)}, u32[]{:S(2)}) collective-permute-start(s16[2064,128]{1,0:T(8,128)(2,1)} %copy-done.7), channel_id=1, source_target_pairs={{0,16},{8,24},{16,0},{24,8},{1,17},{9,25},{17,1},{25,9},{2,18},{10... | collective-permute-start | bytes 1585160 | tf_op jit(solution)/shard_map/ppermute | solution.py:21
  74.9 7.1 %copy-start.8 = (s16[2064,128]{1,0:T(8,128)(2,1)S(1)}, s16[2064,128]{1,0:T(8,128)(2,1)}, u32[]{:S(2)}) copy-start(s16[2064,128]{1,0:T(8,128)(2,1)} %copy-done.7) | copy-start | bytes 1585156
  78.2 20.0 %collective-permute-start.10 = (s16[528,896]{1,0:T(8,128)(2,1)S(1)}, s16[528,896]{1,0:T(8,128)(2,1)S(1)}, u32[]{:S(2)}, u32[]{:S(2)}) collective-permute-start(s16[528,896]{1,0:T(8,128)(2,1)S(1)} %shard_map.102.refs_5_.refs_0_), channel_id=1, source_target_pairs={{0,16},{8,24},{16,0},{24,8},{1,17},{9,25},{17,1},{25,9},{2,18},{10... | collective-permute-start | bytes 2838536 | tf_op jit(solution)/shard_map/ppermute | solution.py:21
  78.7 22.0 %collective-permute-start.14 = (s16[528,896]{1,0:T(8,128)(2,1)S(1)}, s16[528,896]{1,0:T(8,128)(2,1)S(1)}, u32[]{:S(2)}, u32[]{:S(2)}) collective-permute-start(s16[528,896]{1,0:T(8,128)(2,1)S(1)} %shard_map.101.refs_4_.refs_0_), channel_id=1, source_target_pairs={{0,8},{8,0},{16,24},{24,16},{1,9},{9,1},{17,25},{25,17},{2,10},{10... | collective-permute-start | bytes 2838536 | tf_op jit(solution)/shard_map/ppermute | solution.py:21
  82.0 8.1 %copy-start.5 = (s16[784,768]{1,0:T(8,128)(2,1)}, s16[784,768]{1,0:T(8,128)(2,1)S(1)}, u32[]{:S(2)}) copy-start(s16[784,768]{1,0:T(8,128)(2,1)S(1)} %collective-permute-done.11.refs_6_.refs_1_) | copy-start | bytes 3612676
  84.8 7.6 %copy-start = (f32[2048,128]{1,0:T(8,128)}, f32[2048,128]{1,0:T(8,128)S(1)}, u32[]{:S(2)}) copy-start(f32[2048,128]{1,0:T(8,128)S(1)} %get-tuple-element.14.refs_2_.refs_6_) | copy-start | bytes 3145732
  84.9 17.3 %collective-permute-start.16 = (bf16[2048,128]{1,0:T(8,128)(2,1)S(1)}, bf16[2048,128]{1,0:T(8,128)(2,1)S(1)}, u32[]{:S(2)}, u32[]{:S(2)}) collective-permute-start(bf16[2048,128]{1,0:T(8,128)(2,1)S(1)} %get-tuple-element.15), channel_id=1, source_target_pairs={{0,2},{4,6},{8,10},{12,14},{16,18},{20,22},{24,26},{28,30}} | collective-permute-start | bytes 1572872 | tf_op jit(solution)/shard_map/ppermute | solution.py:30
  99.0 8.2 %copy-start.14 = (s32[1,8,4]{1,2,0:T(4,128)S(1)}, s32[1,8,4]{1,2,0:T(4,128)}, u32[]{:S(2)}) copy-start(s32[1,8,4]{1,2,0:T(4,128)} %param.12) | copy-start | bytes 388
  101.6 24.1 %collective-permute-start.15 = (s16[528,896]{1,0:T(8,128)(2,1)S(1)}, s16[528,896]{1,0:T(8,128)(2,1)}, u32[]{:S(2)}, u32[]{:S(2)}) collective-permute-start(s16[528,896]{1,0:T(8,128)(2,1)S(1)} %shard_map.106.refs_2_.refs_3_.refs_4_), channel_id=1, source_target_pairs={{0,16},{8,24},{16,0},{24,8},{1,17},{9,25},{17,1},{25,9},{2,18},{10... | collective-permute-start | bytes 2838536 | tf_op jit(solution)/shard_map/ppermute | solution.py:21
  103.0 25.2 %collective-permute-start.17 = (bf16[2048,128]{1,0:T(8,128)(2,1)}, bf16[2048,128]{1,0:T(8,128)(2,1)}, u32[]{:S(2)}, u32[]{:S(2)}) collective-permute-start(bf16[2048,128]{1,0:T(8,128)(2,1)} %broadcast_select_fusion), channel_id=1, source_target_pairs={{0,1},{2,3},{4,5},{6,7},{8,9},{10,11},{12,13},{14,15},{16,17},{18,... | collective-permute-start | bytes 1572872 | tf_op jit(solution)/shard_map/ppermute | solution.py:30
  105.1 43.5 %collective-permute-start.19 = (s16[784,768]{1,0:T(8,128)(2,1)S(1)}, s16[784,768]{1,0:T(8,128)(2,1)}, u32[]{:S(2)}, u32[]{:S(2)}) collective-permute-start(s16[784,768]{1,0:T(8,128)(2,1)S(1)} %shard_map.104.refs_2_.refs_1_), channel_id=1, source_target_pairs={{0,16},{8,24},{16,0},{24,8},{1,17},{9,25},{17,1},{25,9},{2,18},{10... | collective-permute-start | bytes 3612680 | tf_op jit(solution)/shard_map/ppermute | solution.py:21
  106.6 24.0 %collective-permute-start.13 = (s16[528,896]{1,0:T(8,128)(2,1)S(1)}, s16[528,896]{1,0:T(8,128)(2,1)}, u32[]{:S(2)}, u32[]{:S(2)}) collective-permute-start(s16[528,896]{1,0:T(8,128)(2,1)S(1)} %shard_map.105.refs_2_), channel_id=1, source_target_pairs={{0,8},{8,0},{16,24},{24,16},{1,9},{9,1},{17,25},{25,17},{2,10},{10... | collective-permute-start | bytes 2838536 | tf_op jit(solution)/shard_map/ppermute | solution.py:21
  109.8 16.4 %copy-start.1 = (f32[2048,128]{1,0:T(8,128)S(1)}, f32[2048,128]{1,0:T(8,128)}, u32[]{:S(2)}) copy-start(f32[2048,128]{1,0:T(8,128)} %copy-done) | copy-start | bytes 3145732
  109.8 16.4 %copy-start.4 = (bf16[2048,128]{1,0:T(8,128)(2,1)S(1)}, bf16[2048,128]{1,0:T(8,128)(2,1)}, u32[]{:S(2)}) copy-start(bf16[2048,128]{1,0:T(8,128)(2,1)} %copy-done.3) | copy-start | bytes 1572868
  109.8 16.4 %copy-start.12 = (f32[128,128]{1,0:T(8,128)S(1)}, f32[128,128]{1,0:T(8,128)}, u32[]{:S(2)}) copy-start(f32[128,128]{1,0:T(8,128)} %copy-done.11) | copy-start | bytes 196612
  111.1 40.4 %collective-permute-start.20 = (s16[1040,256]{1,0:T(8,128)(2,1)S(1)}, s16[1040,256]{1,0:T(8,128)(2,1)S(1)}, u32[]{:S(2)}, u32[]{:S(2)}) collective-permute-start(s16[1040,256]{1,0:T(8,128)(2,1)S(1)} %get-tuple-element.17.refs_8_), channel_id=1, source_target_pairs={{0,8},{8,0},{16,24},{24,16},{1,9},{9,1},{17,25},{25,17},{2,10},{10... | collective-permute-start | bytes 1597448 | tf_op jit(solution)/shard_map/ppermute | solution.py:21
  125.6 25.9 %collective-permute-start.21 = (s16[1040,256]{1,0:T(8,128)(2,1)S(1)}, s16[1040,256]{1,0:T(8,128)(2,1)S(1)}, u32[]{:S(2)}, u32[]{:S(2)}) collective-permute-start(s16[1040,256]{1,0:T(8,128)(2,1)S(1)} %get-tuple-element.18.refs_9_), channel_id=1, source_target_pairs={{0,8},{8,0},{16,24},{24,16},{1,9},{9,1},{17,25},{25,17},{2,10},{10... | collective-permute-start | bytes 1597448 | tf_op jit(solution)/shard_map/ppermute | solution.py:21
  128.2 2.4 %collective-permute-start.18 = (bf16[128,1024]{1,0:T(8,128)(2,1)S(1)}, bf16[128,1024]{1,0:T(8,128)(2,1)S(1)}, u32[]{:S(2)}, u32[]{:S(2)}) collective-permute-start(bf16[128,1024]{1,0:T(8,128)(2,1)S(1)} %get-tuple-element.19), channel_id=1, source_target_pairs={{0,4},{1,5},{2,6},{3,7},{8,12},{9,13},{10,14},{11,15},{16,20},{17,... | collective-permute-start | bytes 786440 | tf_op jit(solution)/shard_map/ppermute | solution.py:30
  (5 other events, 9.3 us)

commit v4 on v3

--- a/solution.py
+++ b/solution.py
@@ -167,7 +167,7 @@
     )
 
 
-def merge(after, first, second):
+def merge(after, first, second, pieces=1):
     rows, blocks = first[0].shape[0] - EXTRA, sum(piece.shape[1] for piece in first) // BLK
 
     def kernel(*refs):
@@ -189,55 +189,62 @@
         ]
         encode_all(segments, out_refs, value_ref, scale_ref, rows)
 
-    return run(
-        kernel, after, [*first, *second], [VMEM_SPEC] * (2 * len(first)), [VMEM_SPEC] * len(first),
-        [jax.ShapeDtypeStruct(piece.shape, jnp.int16) for piece in first],
+    shapes = message_shapes(rows, blocks, pieces)
+    return run(
+        kernel, after, [*first, *second], [VMEM_SPEC] * (2 * len(first)), [VMEM_SPEC] * len(shapes), shapes,
         rows * blocks * BLK * 6, scratch=message_scratch(rows, blocks),
     )
 
 
-def low_total(after, partial, pattern, place, received):
-    _, rows, width = partial.shape
-
-    def kernel(place_ref, pattern_ref, x_ref, *refs):
-        for code_ref, first, blocks in spans(refs[:-1]):
-
-            @pl.loop(0, blocks)
-            def _(j):
-                cols = pl.ds(pl.multiple_of(j * BLK, BLK), BLK)
-                target = pl.ds(pl.multiple_of((j + first) * BLK, BLK), BLK)
-                scale = scales(code_ref, rows, cols)
-                load = masked_load(place_ref, pattern_ref, x_ref, rows, j + first)
-                for i in range(rows // BLK):
-                    refs[-1][0, pl.ds(i * BLK, BLK), target] = load(i) + decoded(code_ref, i * BLK, scale, cols)
-
-    return run(
-        kernel, after, [partial, *received], [VMEM_SPEC] * (1 + len(received)), VMEM_SPEC,
-        jax.ShapeDtypeStruct(partial.shape, jnp.float32), partial.size * 10, scalars=(place, pattern),
-    )
-
-
-def mid_half(after, owner, code, base=None):
-    rows, width = code[0].shape[0] - EXTRA, sum(piece.shape[1] for piece in code)
-    extra = [] if base is None else [base]
-
-    def kernel(owner_ref, *refs):
-        for code_ref, first, blocks in spans(refs[:len(code)]):
-
-            @pl.loop(0, blocks)
-            def _(j):
-                cols = pl.ds(pl.multiple_of(j * BLK, BLK), BLK)
-                target = pl.ds(pl.multiple_of((j + first) * BLK, BLK), BLK)
-                scale = scales(code_ref, rows, cols)
-                for i in range(rows // BLK):
-                    refs[-1][0, pl.ds(i * BLK, BLK), target] = decoded(code_ref, i * BLK, scale, cols)
-
-    return run(
-        kernel, after, [*code] + extra,
-        [VMEM_SPEC] * len(code) + [pl.BlockSpec(memory_space=pl.ANY)] * len(extra),
-        pl.BlockSpec((1, rows, width), lambda g, owner_ref: (0, owner_ref[0], 0)),
-        jax.ShapeDtypeStruct((1, 2 * rows, width), jnp.float32), rows * width * 6, scalars=(owner,),
-        aliases={1 + len(code): 0} if extra else None,
+def piece_total(after, part, code, first, base, level=None):
+    rows, blocks = code.shape[0] - EXTRA, code.shape[1] // BLK
+    partial, pattern, place, shape = level
+    inputs, specs = [code], [pl.BlockSpec((rows + EXTRA, BLK), lambda j, *_: (0, j))]
+    if partial is not None:
+        inputs.append(partial)
+        specs.append(pl.BlockSpec((1, rows, BLK), lambda j, *_: (0, 0, first + j)))
+    if base is not None:
+        inputs.append(base)
+        specs.append(pl.BlockSpec(memory_space=pl.ANY))
+
+    def kernel(part_ref, place_ref, pattern_ref, code_ref, *refs):
+        out_ref, token_ref = refs[-2:]
+        token_ref[...] = jnp.zeros_like(token_ref)
+        cols = pl.ds(0, BLK)
+        scale = scales(code_ref, rows, cols)
+        block_col = first + pl.program_id(0)
+        for i in range(rows // BLK):
+            here = pl.ds(i * BLK, BLK)
+            value = decoded(code_ref, i * BLK, scale, cols)
+            if partial is not None:
+                kept = (pattern_ref[i, block_col] == 1) | (place_ref[1] + i == place_ref[2] + block_col)
+                value = jnp.where(kept, refs[0][0, here, cols], 0.0) + value
+            out_ref[0, here, cols] = value
+
+    return run(
+        kernel, after, inputs, specs,
+        [pl.BlockSpec((1, rows, BLK), lambda j, part_ref, *_: (0, part_ref[0], first + j)),
+         pl.BlockSpec((8, BLK), lambda j, *_: (0, 0))],
+        [jax.ShapeDtypeStruct(shape, jnp.float32), jax.ShapeDtypeStruct((8, BLK), jnp.float32)],
+        rows * blocks * BLK * 6, grid=(blocks,), scalars=(part, place, pattern),
+        aliases=None if base is None else {2 + len(inputs): 0},
+    )
+
+
+def corner_rows(after, pivots, partial):
+    lines = pivots.reshape(-1, BLK)
+
+    def kernel(pivot_ref, x_ref, out_ref):
+        source = pivot_ref[0:1, :] % BLK
+        turned = (lax.broadcasted_iota(jnp.int32, (BLK, BLK), 0) == source).astype(jnp.float32)
+        out_ref[...] = lax.dot_general(
+            turned, x_ref[0], (((0,), (0,)), ((), ())), precision=HIGHEST, preferred_element_type=jnp.float32
+        )
+
+    return run(
+        kernel, after, [lines, partial],
+        [pl.BlockSpec((8, BLK), lambda g: (0, 0)), pl.BlockSpec((1, BLK, BLK), lambda g: (0, 0, 0))],
+        pl.BlockSpec((BLK, BLK), lambda g: (0, 0)), jax.ShapeDtypeStruct((BLK, BLK), jnp.float32), BLK * BLK * 8,
     )
 
 
@@ -436,51 +443,56 @@
     encode_top = sender(partial_top, pattern_top, top_rows // 4, 1, top_blocks - 1)
     encode_low = sender(partial_low, pattern_low, low_rows, 0, low_blocks)
 
-
-    corner = exact_dot(order[:BLK].astype(jnp.float32), partial_top[0, :BLK, :BLK])
+    part_of = lambda value: jnp.asarray(value, jnp.int32)[None]
+    no_place = jnp.zeros((3,), jnp.int32)
+    mid_level = (None, pattern_mid[0], no_place, partial_mid.shape)
+    low_place = jnp.stack([jnp.int32(0), row * pattern_low.shape[1], col * pattern_low.shape[2]]).astype(jnp.int32)
+    low_level = (partial_low, pattern_low[0], low_place, partial_low.shape)
     count = lax.axis_size("layer")
+    slab = encode_slab([], 0)
+    slab_got = swapped(slab, 0)
+    corner = corner_rows([*slab], pivots, partial_top)
     beside = [lax.ppermute(corner, "layer", [(i, i ^ apart) for i in range(count)]) for apart in (1, 2, 3)]
-
-    slab = encode_slab([corner], 0)
-    slab_got = swapped(slab, 0)
+    corner_own = corner
     corner = (corner + beside[0]) + (beside[1] + beside[2])
     for bit in bits[2:]:
         corner = corner + swapped(corner, bit)
     corner_row = broadcast_stages(corner, "row")
     corner_col = broadcast_stages(corner_row[-1], "col")
-
-    mid_sent = encode_mid([*[*slab]], 1 - high_bit, (), 1)
+    corner_all = corner_col[-1]
+    mid_sent = encode_mid([*[corner_own]], 1 - high_bit, (), 1)
     mid_got = swapped(mid_sent, 1)
-    a_sent = encode_top([*mid_sent, corner_row[-1]], 3 - low_bit)
+    a_sent = encode_top([*mid_sent, corner_row[-1], *slab_got], 3 - low_bit)
     a_got = swapped(a_sent, 0)
     b_sent = encode_top([*a_sent, corner_col[0]], 1 - high_bit)
     b_got = swapped(b_sent, 1)
     slab = exchanged([*b_sent, corner_col[-1]], slab, slab_got, bits[1:-1])
     slab_got = swapped(slab, bits[-1])
-    mid = encode_mid([*slab], high_bit, mid_got, 1)
+    mid = encode_mid([*slab, *mid_got], high_bit, mid_got, 1)
     mid_got = swapped(mid, 0)
-    packed, lower_inverse, upper_inverse = factor([*mid, *a_got], corner_col[-1])
+    packed, lower_inverse, upper_inverse = factor([*mid], corner_all)
     b = encode_top([*[packed]], high_bit, b_got)
     b_got = swapped(b, 0)
     a = encode_top([*b], 2 + low_bit, a_got)
     a_got = swapped(a, 1)
     panel, lower_low = lower_panel([*a, *mid_got], flags, order, *slab, *slab_got, upper_inverse)
-    lower_low = broadcast_stages(lower_low, "col")[-1]
-    mid = merge([*[panel]], mid, mid_got)
+    lower_stages = broadcast_stages(lower_low, "col")
+    lower_low = lower_stages[-1]
+    low = encode_low([*[panel]], 0, (), 2)
+    low_got = swapped(low, 0)
+    mid = merge([*low], mid, mid_got, 1)
     mid_got = swapped(mid, 1)
     a = exchanged([*mid], a, a_got, bits[2:])
     a_got = swapped(a, 0)
     b = exchanged([*a], b, b_got, bits[2:])
     b_got = swapped(b, 1)
-    mid_sums = mid_half([*b], high_bit[None].astype(jnp.int32), mid)
-    low = encode_low([*[mid_sums]], 0, (), 2)
-    low_got = swapped(low, 0)
-    upper, upper_low = upper_panel([*low], flags, order, panel, *b, *b_got, lower_inverse)
+    upper, upper_low = upper_panel([*b, *a_got], flags, order, panel, *b, *b_got, lower_inverse)
     upper_low = broadcast_stages(upper_low, "row")[-1]
-    top_factor = top_total([*[upper]], flags, order, (*a, *a_got, *b, *b_got), panel, lower_low, upper_low, upper, packed)
-    low_place = jnp.stack([jnp.int32(0), row * pattern_low.shape[1], col * pattern_low.shape[2]]).astype(jnp.int32)
-    low_sums = low_total([*[top_factor]], partial_low, pattern_low[0], low_place, low_got)
-    mid_sums = mid_half([top_factor], (1 - high_bit)[None].astype(jnp.int32), mid_got, mid_sums)
+    mid_sums, token = piece_total([*[upper]], part_of(high_bit), mid[0], 0, None, mid_level)
+    top_factor = top_total([*[token]], flags, order, (*a, *a_got, *b, *b_got), panel, lower_low, upper_low, upper, packed)
+    low_sums, token = piece_total([*[top_factor]], part_of(0), low_got[0], 0, None, low_level)
+    low_sums, token = piece_total([*[token]], part_of(0), low_got[1], low_got[0].shape[1] // BLK, low_sums, low_level)
+    mid_sums, token = piece_total([*[token]], part_of(1 - high_bit), mid_got[0], 0, mid_sums, mid_level)
     return top_factor, mid_sums, low_sums
 
 

time: 156 us -> 156 us (level)
  waiting for transfers between devices: 39.9 us -> 31.1 us
  Pallas kernels: 68.9 us -> 76.8 us
  local copies, waits for them, and re-layouts: 5.33 us -> 8.59 us
  other arithmetic: 4.78 us -> 3.18 us
    ppermute x13, waiting for transfers between devices: 37.3 us -> 28.5 us  [swapped(): lax.ppermute(piece, 'layer', pairs)]
    pallas_call x19 -> x21, Pallas kernels: 68.9 us -> 76.8 us  [run(): pl.pallas_call(body, grid_spec=pltpu.PrefetchScalarGridSpec(num_scalar_pr...]
    unnamed x30 -> x28, local copies, waits for them, and re-layouts: 4.4 us -> 7.66 us
  transfers between devices with their start and end apart: 22 -> 22, of which waited for: 9 -> 6; matrix products, arithmetic and copies ran while one was open for 3% -> 2% of each run, Pallas kernels for 43% -> 45%
where the time goes in v4:
time: 156 us; the launch traced here: 155 us
  Pallas kernels  76.8 us (49%)
  starting transfers between devices  34 us (22%)
  waiting for transfers between devices  31.1 us (20%)
  local copies, waits for them, and re-layouts  8.59 us (6%)
  other arithmetic  3.18 us (2%)
    pallas_call x21, Pallas kernels, run(): pl.pallas_call(body, grid_spec=pltpu.PrefetchScalarGridSpec(num_scalar_pr...  76.8 us
    ppermute x13, waiting for transfers between devices, swapped(): lax.ppermute(piece, 'layer', pairs)  28.5 us
    ppermute x6, starting transfers between devices, broadcast_stages(): lax.ppermute(value, axis, [(i, i + span) for i in range(0, count, 2 * spa...  16 us
    ppermute x13, starting transfers between devices, swapped(): lax.ppermute(piece, 'layer', pairs)  13.4 us
    unnamed x28, local copies, waits for them, and re-layouts  7.66 us
    ppermute x3, starting transfers between devices, on_device(): lax.ppermute(corner, 'layer', [(i, i ^ apart) for i in range(count)])  4.6 us
  transfers between devices with their start and end apart: 22, of which 6 were waited for; matrix products, arithmetic and copies ran while one was open for 2% of the time, Pallas kernels for 45%

profile of v4, /device:TPU:0, one launch (start us, length us, event | category | flops | bytes accessed | tf_op | source)
XLA Modules:
  0.0 154.6 jit_solution(15815087657399768102)
XLA Ops:
  1.5 2.1 %shard_map.94.refs_2_.refs_0_ = s16[2064,128]{1,0:T(8,128)(2,1)S(1)} custom-call(s32[3]{0:T(128)S(1)} %fusion.2.refs_0_, s32[16,8]{1,0:T(8,128)S(1)} %copy.18.refs_1_, f32[1,2048,1024]{2,1,0:T(8,128)} %refs_2_.14), custom_call_target="tpu_custom_call" | custom-call | bytes 1024 | tf_op jit(solution)/shard_map/pallas_call | solution.py:63
  4.7 4.0 %collective-permute-start.2 = (f32[128,128]{1,0:T(8,128)S(1)}, f32[128,128]{1,0:T(8,128)}, u32[]{:S(2)}, u32[]{:S(2)}) collective-permute-start(f32[128,128]{1,0:T(8,128)S(1)} %shard_map.95.refs_3_), channel_id=1, source_target_pairs={{0,24},{8,16},{16,8},{24,0},{1,25},{9,17},{17,9},{25,1},{2,26},{10... | collective-permute-start | bytes 196616 | tf_op jit(solution)/shard_map/ppermute | solution.py:455
  9.3 1.9 %collective-permute-start.4 = (s16[2064,128]{1,0:T(8,128)(2,1)S(1)}, s16[2064,128]{1,0:T(8,128)(2,1)S(1)}, u32[]{:S(2)}, u32[]{:S(2)}) collective-permute-start(s16[2064,128]{1,0:T(8,128)(2,1)S(1)} %shard_map.94.refs_2_.refs_0_), channel_id=1, source_target_pairs={{0,8},{8,0},{16,24},{24,16},{1,9},{9,1},{17,25},{25,17},{2,10},{10... | collective-permute-start | bytes 1585160 | tf_op jit(solution)/shard_map/ppermute | solution.py:21
  11.4 2.3 %copy-done = f32[1,1536,768]{2,1,0:T(8,128)S(1)} copy-done((f32[1,1536,768]{2,1,0:T(8,128)S(1)}, f32[1,1536,768]{2,1,0:T(8,128)}, u32[]{:S(2)}) %copy-start) | copy-done | bytes 4718616
  15.2 1.6 %collective-permute-start.9 = (s16[784,768]{1,0:T(8,128)(2,1)S(1)}, s16[784,768]{1,0:T(8,128)(2,1)S(1)}, u32[]{:S(2)}, u32[]{:S(2)}) collective-permute-start(s16[784,768]{1,0:T(8,128)(2,1)S(1)} %shard_map.96.refs_3_), channel_id=1, source_target_pairs={{0,16},{8,24},{16,0},{24,8},{1,17},{9,25},{17,1},{25,9},{2,18},{10... | collective-permute-start | bytes 3612680 | tf_op jit(solution)/shard_map/ppermute | solution.py:21
  19.9 4.5 %collective-permute-start.6 = (f32[128,128]{1,0:T(8,128)S(1)}, f32[128,128]{1,0:T(8,128)S(1)}, u32[]{:S(2)}, u32[]{:S(2)}) collective-permute-start(f32[128,128]{1,0:T(8,128)S(1)} %broadcast_select_fusion.5.refs_4_), channel_id=1, source_target_pairs={{0,2},{4,6},{8,10},{12,14},{16,18},{20,22},{24,26},{28,30}} | collective-permute-start | bytes 196616 | tf_op jit(solution)/shard_map/ppermute | solution.py:30
  24.5 1.8 %collective-permute-done.6 = f32[128,128]{1,0:T(8,128)S(1)} collective-permute-done((f32[128,128]{1,0:T(8,128)S(1)}, f32[128,128]{1,0:T(8,128)S(1)}, u32[]{:S(2)}, u32[]{:S(2)}) %collective-permute-start.6) | collective-permute-done | bytes 65568 | tf_op jit(solution)/shard_map/ppermute | solution.py:30
  27.7 3.8 %shard_map.97.refs_3_ = s16[528,896]{1,0:T(8,128)(2,1)} custom-call(s32[3]{0:T(128)S(1)} %add_add_fusion.2.refs_0_, s32[16,8]{1,0:T(8,128)S(1)} %copy.18.refs_1_, f32[1,2048,1024]{2,1,0:T(8,128)} %refs_2_.14, s16[784,768]{1,0:T(8,128)(2,1)S(1)} %shard_map.96.refs_3_, f32[128,128]{1,0:T(8,128)S(1)} %broadcast_select_fusion.5.refs_4_, ...), custom_call_target="tpu_custom_call" | custom-call | bytes 1024 | tf_op jit(solution)/shard_map/pallas_call | solution.py:63
  32.1 3.8 %shard_map.98.refs_2_ = s16[528,896]{1,0:T(8,128)(2,1)} custom-call(s32[3]{0:T(128)S(1)} %add_add_fusion.5.refs_0_, s32[16,8]{1,0:T(8,128)S(1)} %copy.18.refs_1_, f32[1,2048,1024]{2,1,0:T(8,128)} %refs_2_.14, s16[528,896]{1,0:T(8,128)(2,1)} %shard_map.97.refs_3_, f32[128,128]{1,0:T(8,128)S(1)} %broadcast_select_fusion.4.refs_4_), custom_call_target="tpu_custom_call" | custom-call | bytes 1024 | tf_op jit(solution)/shard_map/pallas_call | solution.py:63
  36.9 7.8 %collective-permute-done.9.refs_3_.refs_5_ = s16[784,768]{1,0:T(8,128)(2,1)S(1)} collective-permute-done((s16[784,768]{1,0:T(8,128)(2,1)S(1)}, s16[784,768]{1,0:T(8,128)(2,1)S(1)}, u32[]{:S(2)}, u32[]{:S(2)}) %collective-permute-start.9) | collective-permute-done | bytes 1204256 | tf_op jit(solution)/shard_map/ppermute | solution.py:21
  47.0 3.2 %shard_map.100.refs_1_.refs_0_ = s16[784,768]{1,0:T(8,128)(2,1)S(1)} custom-call(s32[3]{0:T(128)S(1)} %add_add_fusion.6.refs_0_, s32[12,6]{1,0:T(8,128)S(1)} %bitcast.18, f32[1,1536,768]{2,1,0:T(8,128)} %refs_2_.12, s16[784,768]{1,0:T(8,128)(2,1)S(1)} %copy-done.8, s16[2064,128]{1,0:T(8,128)(2,1)S(1)} %shard_map.99.refs_4_.refs_2_, s16[784,768]{1,0:T(8,128)(2,1)S(1)} %copy-done.8), custom_call_target="tpu_custom_call" | custom-call | bytes 1024 | tf_op jit(solution)/shard_map/pallas_call | solution.py:63
  51.3 2.0 %collective-permute-start.12 = (s16[2064,128]{1,0:T(8,128)(2,1)}, s16[2064,128]{1,0:T(8,128)(2,1)S(1)}, u32[]{:S(2)}, u32[]{:S(2)}) collective-permute-start(s16[2064,128]{1,0:T(8,128)(2,1)} %copy-done.9), channel_id=1, source_target_pairs={{0,16},{8,24},{16,0},{24,8},{1,17},{9,25},{17,1},{25,9},{2,18},{10... | collective-permute-start | bytes 1585160 | tf_op jit(solution)/shard_map/ppermute | solution.py:21
  53.4 15.3 %shard_map.101 = (f32[128,128]{1,0:T(8,128)S(1)}, f32[128,128]{1,0:T(8,128)S(1)}, f32[128,128]{1,0:T(8,128)S(1)}) custom-call(f32[128,128]{1,0:T(8,128)S(1)} %broadcast_select_fusion.3.refs_3_.refs_0_, s16[784,768]{1,0:T(8,128)(2,1)S(1)} %shard_map.100.refs_1_.refs_0_), custom_call_target="tpu_custom_call" | custom-call | bytes 1024 | tf_op jit(solution)/shard_map/pallas_call | solution.py:63
  68.7 4.2 %shard_map.102.refs_4_.refs_0_ = s16[528,896]{1,0:T(8,128)(2,1)} custom-call(s32[3]{0:T(128)S(1)} %add_add_fusion.4.refs_0_, s32[16,8]{1,0:T(8,128)S(1)} %copy.18.refs_1_, f32[1,2048,1024]{2,1,0:T(8,128)} %refs_2_.14, s16[528,896]{1,0:T(8,128)(2,1)} %collective-permute-done.7.refs_3_, f32[128,128]{1,0:T(8,128)S(1)} %get-tuple-element.19.refs_4_.refs_10_), custom_call_target="tpu_custom_call" | custom-call | bytes 1024 | tf_op jit(solution)/shard_map/pallas_call | solution.py:63
  72.9 1.5 collective-permute-start.14
  74.4 4.2 %shard_map.103.refs_5_.refs_0_ = s16[528,896]{1,0:T(8,128)(2,1)} custom-call(s32[3]{0:T(128)S(1)} %add_add_fusion.1.refs_0_, s32[16,8]{1,0:T(8,128)S(1)} %copy.18.refs_1_, f32[1,2048,1024]{2,1,0:T(8,128)} %refs_2_.14, s16[528,896]{1,0:T(8,128)(2,1)} %collective-permute-done.5.refs_3_, s16[528,896]{1,0:T(8,128)(2,1)} %shard_map.102.refs_4_.refs_0_), custom_call_target="tpu_custom_call" | custom-call | bytes 1024 | tf_op jit(solution)/shard_map/pallas_call | solution.py:63
  79.5 2.1 %collective-permute-done.11.refs_6_.refs_1_ = s16[784,768]{1,0:T(8,128)(2,1)} collective-permute-done((s16[784,768]{1,0:T(8,128)(2,1)S(1)}, s16[784,768]{1,0:T(8,128)(2,1)}, u32[]{:S(2)}, u32[]{:S(2)}) %collective-permute-start.11) | collective-permute-done | bytes 1204256 | tf_op jit(solution)/shard_map/ppermute | solution.py:21
  81.6 3.7 %shard_map.104 = (f32[2048,128]{1,0:T(8,128)S(1)}, bf16[2048,128]{1,0:T(8,128)(2,1)}) custom-call(s32[4]{0:T(128)S(1)} %pad_add_fusion.2.refs_0_, bf16[2048,128]{1,0:T(8,128)(2,1)S(1)} %fusion.refs_1_, s16[2064,128]{1,0:T(8,128)(2,1)S(1)} %copy-done.10, s16[2064,128]{1,0:T(8,128)(2,1)S(1)} %collective-permute-done.12.refs_3_, ...), custom_call_target="tpu_custom_call" | custom-call | bytes 1024 | tf_op jit(solution)/shard_map/pallas_call | solution.py:63
  86.2 5.9 %collective-permute-start.16 = (bf16[2048,128]{1,0:T(8,128)(2,1)}, bf16[2048,128]{1,0:T(8,128)(2,1)}, u32[]{:S(2)}, u32[]{:S(2)}) collective-permute-start(bf16[2048,128]{1,0:T(8,128)(2,1)} %get-tuple-element.24), channel_id=1, source_target_pairs={{0,2},{4,6},{8,10},{12,14},{16,18},{20,22},{24,26},{28,30}} | collective-permute-start | bytes 1572872 | tf_op jit(solution)/shard_map/ppermute | solution.py:30
  94.9 2.4 %shard_map.106.refs_2_.refs_3_ = s16[784,768]{1,0:T(8,128)(2,1)S(1)} custom-call(s16[784,768]{1,0:T(8,128)(2,1)S(1)} %shard_map.100.refs_1_.refs_0_, s16[784,768]{1,0:T(8,128)(2,1)} %collective-permute-done.11.refs_6_.refs_1_, s16[1040,256]{1,0:T(8,128)(2,1)S(1)} %get-tuple-element.22.refs_2_, s16[1040,256]{1,0:T(8,128)(2,1)S(1)} %get-tuple-element.23.refs_3_), custom_call_target="tpu_custom_call" | custom-call | bytes 1024 | tf_op jit(solution)/shard_map/pallas_call | solution.py:63
  97.3 2.3 %shard_map.107.refs_2_ = s16[528,896]{1,0:T(8,128)(2,1)S(1)} custom-call(s16[528,896]{1,0:T(8,128)(2,1)} %shard_map.103.refs_5_.refs_0_, s16[528,896]{1,0:T(8,128)(2,1)} %collective-permute-done.10.refs_1_, s16[784,768]{1,0:T(8,128)(2,1)S(1)} %shard_map.106.refs_2_.refs_3_), custom_call_target="tpu_custom_call" | custom-call | bytes 1024 | tf_op jit(solution)/shard_map/pallas_call | solution.py:63
  101.3 2.3 %shard_map.108.refs_3_.refs_4_.refs_8_ = s16[528,896]{1,0:T(8,128)(2,1)S(1)} custom-call(s16[528,896]{1,0:T(8,128)(2,1)} %shard_map.102.refs_4_.refs_0_, s16[528,896]{1,0:T(8,128)(2,1)} %collective-permute-done.14.refs_1_, s16[528,896]{1,0:T(8,128)(2,1)S(1)} %shard_map.107.refs_2_), custom_call_target="tpu_custom_call" | custom-call | bytes 1024 | tf_op jit(solution)/shard_map/pallas_call | solution.py:63
  105.3 1.7 %collective-permute-start.17 = (bf16[2048,128]{1,0:T(8,128)(2,1)S(1)}, bf16[2048,128]{1,0:T(8,128)(2,1)S(1)}, u32[]{:S(2)}, u32[]{:S(2)}) collective-permute-start(bf16[2048,128]{1,0:T(8,128)(2,1)S(1)} %broadcast_select_fusion), channel_id=1, source_target_pairs={{0,1},{2,3},{4,5},{6,7},{8,9},{10,11},{12,13},{14,15},{16,17},{18,... | collective-permute-start | bytes 1572872 | tf_op jit(solution)/shard_map/ppermute | solution.py:30
  107.0 1.6 %collective-permute-start.19 = (s16[784,768]{1,0:T(8,128)(2,1)S(1)}, s16[784,768]{1,0:T(8,128)(2,1)S(1)}, u32[]{:S(2)}, u32[]{:S(2)}) collective-permute-start(s16[784,768]{1,0:T(8,128)(2,1)S(1)} %shard_map.106.refs_2_.refs_3_), channel_id=1, source_target_pairs={{0,16},{8,24},{16,0},{24,8},{1,17},{9,25},{17,1},{25,9},{2,18},{10... | collective-permute-start | bytes 3612680 | tf_op jit(solution)/shard_map/ppermute | solution.py:21
  108.6 1.5 collective-permute-start.21
  110.1 17.5 %collective-permute-done.15.refs_5_.refs_6_ = s16[528,896]{1,0:T(8,128)(2,1)S(1)} collective-permute-done((s16[528,896]{1,0:T(8,128)(2,1)S(1)}, s16[528,896]{1,0:T(8,128)(2,1)S(1)}, u32[]{:S(2)}, u32[]{:S(2)}) %collective-permute-start.15) | collective-permute-done | bytes 946208 | tf_op jit(solution)/shard_map/ppermute | solution.py:21
  128.1 1.6 %shard_map.109 = (f32[128,1024]{1,0:T(8,128)S(1)}, bf16[128,1024]{1,0:T(8,128)(2,1)S(1)}) custom-call(s32[4]{0:T(128)S(1)} %pad_add_fusion.2.refs_0_, bf16[2048,128]{1,0:T(8,128)(2,1)S(1)} %copy-done.6, f32[2048,128]{1,0:T(8,128)S(1)} %copy-done.4, s16[528,896]{1,0:T(8,128)(2,1)S(1)} %shard_map.108.refs_3_.refs_4_.refs_8_, ...), custom_call_target="tpu_custom_call" | custom-call | bytes 1024 | tf_op jit(solution)/shard_map/pallas_call | solution.py:63
  131.1 3.3 %shard_map.110 = (f32[1,1536,768]{2,1,0:T(8,128)}, f32[8,128]{1,0:T(8,128)S(1)}) custom-call(s32[1]{0:T(128)} %bitcast.1.refs_0_, s32[3]{0:T(128)S(1)} %broadcast_3_refs_1_.2.refs_1_, s32[12,6]{1,0:T(8,128)S(1)} %bitcast.19, s16[784,768]{1,0:T(8,128)(2,1)S(1)} %shard_map.106.refs_2_.refs_3_, f32[128,1024]{1,0:T(8,128)S(1)} %get-tuple-element.27.refs_4_.refs_9_), custom_call_target="tpu_custom_call" | custom-call | bytes 1024 | tf_op jit(solution)/shard_map/pallas_call | solution.py:63
  134.5 12.9 %shard_map.111.refs_5_ = f32[2048,1024]{1,0:T(8,128)} custom-call(s32[4]{0:T(128)S(1)} %pad_add_fusion.2.refs_0_, bf16[2048,128]{1,0:T(8,128)(2,1)S(1)} %copy-done.6, s16[528,896]{1,0:T(8,128)(2,1)S(1)} %shard_map.107.refs_2_, s16[528,896]{1,0:T(8,128)(2,1)S(1)} %collective-permute-done.13.refs_9_.refs_3_, ...), custom_call_target="tpu_custom_call" | custom-call | bytes 1024 | tf_op jit(solution)/shard_map/pallas_call | solution.py:63
  147.5 1.9 %shard_map.112 = (f32[1,1024,512]{2,1,0:T(8,128)}, f32[8,128]{1,0:T(8,128)S(1)}) custom-call(s32[1]{0:T(128)} %constant.70.clone.1.refs_0_, s32[3]{0:T(128)S(1)} %fusion.3.refs_0_.refs_1_, s32[8,4]{1,0:T(8,128)S(1)} %copy.19.refs_1_.refs_2_, s16[1040,256]{1,0:T(8,128)(2,1)S(1)} %collective-permute-done.21.refs_3_, f32[1,1024,512]{2,1,0:T(8,128)S(1)} %copy-done.1, ...), custom_call_target="tpu_custom_call" | custom-call | bytes 1024 | tf_op jit(solution)/shard_map/pallas_call | solution.py:63
  149.4 1.9 %shard_map.113 = (f32[1,1024,512]{2,1,0:T(8,128)}, f32[8,128]{1,0:T(8,128)S(1)}) custom-call(s32[1]{0:T(128)} %constant.70.clone.1.refs_0_, s32[3]{0:T(128)S(1)} %fusion.3.refs_0_.refs_1_, s32[8,4]{1,0:T(8,128)S(1)} %copy.19.refs_1_.refs_2_, s16[1040,256]{1,0:T(8,128)(2,1)S(1)} %collective-permute-done.20.refs_3_, ...), custom_call_target="tpu_custom_call", output_to_operand_aliasing={{0}: (5, {})} | custom-call | bytes 1024 | tf_op jit(solution)/shard_map/pallas_call | solution.py:63
  151.3 3.3 %shard_map.114 = (f32[1,1536,768]{2,1,0:T(8,128)}, f32[8,128]{1,0:T(8,128)}) custom-call(s32[1]{0:T(128)} %bitcast.9.refs_0_, s32[3]{0:T(128)S(1)} %broadcast_3_refs_1_.2.refs_1_, s32[12,6]{1,0:T(8,128)S(1)} %bitcast.20, s16[784,768]{1,0:T(8,128)(2,1)S(1)} %collective-permute-done.19.refs_3_, ...), custom_call_target="tpu_custom_call", output_to_operand_aliasing={{0}: (4, {})} | custom-call | bytes 1024 | tf_op jit(solution)/shard_map/pallas_call | solution.py:63
  (83 shorter events, 23.7 us)
Async XLA Ops:
  1.5 2.1 %copy-start.11 = (s32[2048]{0:T(1024)S(1)}, s32[2048]{0:T(1024)}, u32[]{:S(2)}) copy-start(s32[2048]{0:T(1024)} %param.13) | copy-start | bytes 24580
  3.6 7.6 %copy-start.12 = (s32[1,12,6]{1,0,2:T(1,128)S(1)}, s32[1,12,6]{1,0,2:T(1,128)}, u32[]{:S(2)}) copy-start(s32[1,12,6]{1,0,2:T(1,128)} %param.11) | copy-start | bytes 868
  4.7 12.1 %collective-permute-start.2 = (f32[128,128]{1,0:T(8,128)S(1)}, f32[128,128]{1,0:T(8,128)}, u32[]{:S(2)}, u32[]{:S(2)}) collective-permute-start(f32[128,128]{1,0:T(8,128)S(1)} %shard_map.95.refs_3_), channel_id=1, source_target_pairs={{0,24},{8,16},{16,8},{24,0},{1,25},{9,17},{17,9},{25,1},{2,26},{10... | collective-permute-start | bytes 196616 | tf_op jit(solution)/shard_map/ppermute | solution.py:455
  8.7 8.1 %collective-permute-start.1 = (f32[128,128]{1,0:T(8,128)S(1)}, f32[128,128]{1,0:T(8,128)}, u32[]{:S(2)}, u32[]{:S(2)}) collective-permute-start(f32[128,128]{1,0:T(8,128)S(1)} %shard_map.95.refs_3_), channel_id=1, source_target_pairs={{0,16},{8,24},{16,0},{24,8},{1,17},{9,25},{17,1},{25,9},{2,18},{10... | collective-permute-start | bytes 196616 | tf_op jit(solution)/shard_map/ppermute | solution.py:455
  9.2 7.6 %collective-permute-start = (f32[128,128]{1,0:T(8,128)S(1)}, f32[128,128]{1,0:T(8,128)}, u32[]{:S(2)}, u32[]{:S(2)}) collective-permute-start(f32[128,128]{1,0:T(8,128)S(1)} %shard_map.95.refs_3_), channel_id=1, source_target_pairs={{0,8},{8,0},{16,24},{24,16},{1,9},{9,1},{17,25},{25,17},{2,10},{10... | collective-permute-start | bytes 196616 | tf_op jit(solution)/shard_map/ppermute | solution.py:455
  9.3 18.4 %collective-permute-start.4 = (s16[2064,128]{1,0:T(8,128)(2,1)S(1)}, s16[2064,128]{1,0:T(8,128)(2,1)S(1)}, u32[]{:S(2)}, u32[]{:S(2)}) collective-permute-start(s16[2064,128]{1,0:T(8,128)(2,1)S(1)} %shard_map.94.refs_2_.refs_0_), channel_id=1, source_target_pairs={{0,8},{8,0},{16,24},{24,16},{1,9},{9,1},{17,25},{25,17},{2,10},{10... | collective-permute-start | bytes 1585160 | tf_op jit(solution)/shard_map/ppermute | solution.py:21
  11.4 2.3 %copy-start = (f32[1,1536,768]{2,1,0:T(8,128)S(1)}, f32[1,1536,768]{2,1,0:T(8,128)}, u32[]{:S(2)}) copy-start(f32[1,1536,768]{2,1,0:T(8,128)} %refs_2_.12) | copy-start | bytes 14155780
  15.2 29.5 %collective-permute-start.9 = (s16[784,768]{1,0:T(8,128)(2,1)S(1)}, s16[784,768]{1,0:T(8,128)(2,1)S(1)}, u32[]{:S(2)}, u32[]{:S(2)}) collective-permute-start(s16[784,768]{1,0:T(8,128)(2,1)S(1)} %shard_map.96.refs_3_), channel_id=1, source_target_pairs={{0,16},{8,24},{16,0},{24,8},{1,17},{9,25},{17,1},{25,9},{2,18},{10... | collective-permute-start | bytes 3612680 | tf_op jit(solution)/shard_map/ppermute | solution.py:21
  17.7 2.2 %collective-permute-start.3 = (f32[128,128]{1,0:T(8,128)S(1)}, f32[128,128]{1,0:T(8,128)S(1)}, u32[]{:S(2)}, u32[]{:S(2)}) collective-permute-start(f32[128,128]{1,0:T(8,128)S(1)} %add_add_fusion), channel_id=1, source_target_pairs={{0,4},{1,5},{2,6},{3,7},{8,12},{9,13},{10,14},{11,15},{16,20},{17,... | collective-permute-start | bytes 196616 | tf_op jit(solution)/shard_map/ppermute | solution.py:30
  19.9 6.4 %collective-permute-start.6 = (f32[128,128]{1,0:T(8,128)S(1)}, f32[128,128]{1,0:T(8,128)S(1)}, u32[]{:S(2)}, u32[]{:S(2)}) collective-permute-start(f32[128,128]{1,0:T(8,128)S(1)} %broadcast_select_fusion.5.refs_4_), channel_id=1, source_target_pairs={{0,2},{4,6},{8,10},{12,14},{16,18},{20,22},{24,26},{28,30}} | collective-permute-start | bytes 196616 | tf_op jit(solution)/shard_map/ppermute | solution.py:30
  26.3 10.1 %collective-permute-start.8 = (f32[128,128]{1,0:T(8,128)S(1)}, f32[128,128]{1,0:T(8,128)S(1)}, u32[]{:S(2)}, u32[]{:S(2)}) collective-permute-start(f32[128,128]{1,0:T(8,128)S(1)} %broadcast_select_fusion.4.refs_4_), channel_id=1, source_target_pairs={{0,1},{2,3},{4,5},{6,7},{8,9},{10,11},{12,13},{14,15},{16,17},{18,... | collective-permute-start | bytes 196616 | tf_op jit(solution)/shard_map/ppermute | solution.py:30
  31.6 42.8 %collective-permute-start.5 = (s16[528,896]{1,0:T(8,128)(2,1)}, s16[528,896]{1,0:T(8,128)(2,1)}, u32[]{:S(2)}, u32[]{:S(2)}) collective-permute-start(s16[528,896]{1,0:T(8,128)(2,1)} %shard_map.97.refs_3_), channel_id=1, source_target_pairs={{0,8},{8,0},{16,24},{24,16},{1,9},{9,1},{17,25},{25,17},{2,10},{10... | collective-permute-start | bytes 2838536 | tf_op jit(solution)/shard_map/ppermute | solution.py:21
  35.9 32.7 %collective-permute-start.7 = (s16[528,896]{1,0:T(8,128)(2,1)}, s16[528,896]{1,0:T(8,128)(2,1)}, u32[]{:S(2)}, u32[]{:S(2)}) collective-permute-start(s16[528,896]{1,0:T(8,128)(2,1)} %shard_map.98.refs_2_), channel_id=1, source_target_pairs={{0,16},{8,24},{16,0},{24,8},{1,17},{9,25},{17,1},{25,9},{2,18},{10... | collective-permute-start | bytes 2838536 | tf_op jit(solution)/shard_map/ppermute | solution.py:21
  45.7 1.3 copy-start.8
  51.0 30.6 %collective-permute-start.11 = (s16[784,768]{1,0:T(8,128)(2,1)S(1)}, s16[784,768]{1,0:T(8,128)(2,1)}, u32[]{:S(2)}, u32[]{:S(2)}) collective-permute-start(s16[784,768]{1,0:T(8,128)(2,1)S(1)} %shard_map.100.refs_1_.refs_0_), channel_id=1, source_target_pairs={{0,8},{8,0},{16,24},{24,16},{1,9},{9,1},{17,25},{25,17},{2,10},{10... | collective-permute-start | bytes 3612680 | tf_op jit(solution)/shard_map/ppermute | solution.py:21
  51.3 28.1 %collective-permute-start.12 = (s16[2064,128]{1,0:T(8,128)(2,1)}, s16[2064,128]{1,0:T(8,128)(2,1)S(1)}, u32[]{:S(2)}, u32[]{:S(2)}) collective-permute-start(s16[2064,128]{1,0:T(8,128)(2,1)} %copy-done.9), channel_id=1, source_target_pairs={{0,16},{8,24},{16,0},{24,8},{1,17},{9,25},{17,1},{25,9},{2,18},{10... | collective-permute-start | bytes 1585160 | tf_op jit(solution)/shard_map/ppermute | solution.py:21
  72.9 8.7 %copy-start.10 = (s16[2064,128]{1,0:T(8,128)(2,1)S(1)}, s16[2064,128]{1,0:T(8,128)(2,1)}, u32[]{:S(2)}) copy-start(s16[2064,128]{1,0:T(8,128)(2,1)} %copy-done.9) | copy-start | bytes 1585156
  72.9 28.4 %collective-permute-start.14 = (s16[528,896]{1,0:T(8,128)(2,1)}, s16[528,896]{1,0:T(8,128)(2,1)}, u32[]{:S(2)}, u32[]{:S(2)}) collective-permute-start(s16[528,896]{1,0:T(8,128)(2,1)} %shard_map.102.refs_4_.refs_0_), channel_id=1, source_target_pairs={{0,8},{8,0},{16,24},{24,16},{1,9},{9,1},{17,25},{25,17},{2,10},{10... | collective-permute-start | bytes 2838536 | tf_op jit(solution)/shard_map/ppermute | solution.py:21
  78.6 13.6 %copy-start.13 = (s32[1,8,4]{1,2,0:T(4,128)S(1)}, s32[1,8,4]{1,2,0:T(4,128)}, u32[]{:S(2)}) copy-start(s32[1,8,4]{1,2,0:T(4,128)} %param.12) | copy-start | bytes 388
  78.6 13.7 %copy-start.1 = (f32[1,1024,512]{2,1,0:T(8,128)S(1)}, f32[1,1024,512]{2,1,0:T(8,128)}, u32[]{:S(2)}) copy-start(f32[1,1024,512]{2,1,0:T(8,128)} %refs_4_.3) | copy-start | bytes 6291460
  78.6 18.7 %collective-permute-start.10 = (s16[528,896]{1,0:T(8,128)(2,1)}, s16[528,896]{1,0:T(8,128)(2,1)}, u32[]{:S(2)}, u32[]{:S(2)}) collective-permute-start(s16[528,896]{1,0:T(8,128)(2,1)} %shard_map.103.refs_5_.refs_0_), channel_id=1, source_target_pairs={{0,16},{8,24},{16,0},{24,8},{1,17},{9,25},{17,1},{25,9},{2,18},{10... | collective-permute-start | bytes 2838536 | tf_op jit(solution)/shard_map/ppermute | solution.py:21
  79.4 5.8 %copy-start.5 = (bf16[2048,128]{1,0:T(8,128)(2,1)}, bf16[2048,128]{1,0:T(8,128)(2,1)S(1)}, u32[]{:S(2)}) copy-start(bf16[2048,128]{1,0:T(8,128)(2,1)S(1)} %fusion.refs_1_) | copy-start | bytes 1572868
  86.2 18.0 %collective-permute-start.16 = (bf16[2048,128]{1,0:T(8,128)(2,1)}, bf16[2048,128]{1,0:T(8,128)(2,1)}, u32[]{:S(2)}, u32[]{:S(2)}) collective-permute-start(bf16[2048,128]{1,0:T(8,128)(2,1)} %get-tuple-element.24), channel_id=1, source_target_pairs={{0,2},{4,6},{8,10},{12,14},{16,18},{20,22},{24,26},{28,30}} | collective-permute-start | bytes 1572872 | tf_op jit(solution)/shard_map/ppermute | solution.py:30
  99.6 28.5 %copy-start.4 = (f32[2048,128]{1,0:T(8,128)S(1)}, f32[2048,128]{1,0:T(8,128)}, u32[]{:S(2)}) copy-start(f32[2048,128]{1,0:T(8,128)} %copy-done.2) | copy-start | bytes 3145732
  99.6 28.5 %copy-start.6 = (bf16[2048,128]{1,0:T(8,128)(2,1)S(1)}, bf16[2048,128]{1,0:T(8,128)(2,1)}, u32[]{:S(2)}) copy-start(bf16[2048,128]{1,0:T(8,128)(2,1)} %copy-done.5) | copy-start | bytes 1572868
  99.7 28.5 %collective-permute-start.13 = (s16[528,896]{1,0:T(8,128)(2,1)S(1)}, s16[528,896]{1,0:T(8,128)(2,1)S(1)}, u32[]{:S(2)}, u32[]{:S(2)}) collective-permute-start(s16[528,896]{1,0:T(8,128)(2,1)S(1)} %shard_map.107.refs_2_), channel_id=1, source_target_pairs={{0,8},{8,0},{16,24},{24,16},{1,9},{9,1},{17,25},{25,17},{2,10},{10... | collective-permute-start | bytes 2838536 | tf_op jit(solution)/shard_map/ppermute | solution.py:21
  103.6 24.0 %collective-permute-start.15 = (s16[528,896]{1,0:T(8,128)(2,1)S(1)}, s16[528,896]{1,0:T(8,128)(2,1)S(1)}, u32[]{:S(2)}, u32[]{:S(2)}) collective-permute-start(s16[528,896]{1,0:T(8,128)(2,1)S(1)} %shard_map.108.refs_3_.refs_4_.refs_8_), channel_id=1, source_target_pairs={{0,16},{8,24},{16,0},{24,8},{1,17},{9,25},{17,1},{25,9},{2,18},{10... | collective-permute-start | bytes 2838536 | tf_op jit(solution)/shard_map/ppermute | solution.py:21
  105.3 29.1 %collective-permute-start.17 = (bf16[2048,128]{1,0:T(8,128)(2,1)S(1)}, bf16[2048,128]{1,0:T(8,128)(2,1)S(1)}, u32[]{:S(2)}, u32[]{:S(2)}) collective-permute-start(bf16[2048,128]{1,0:T(8,128)(2,1)S(1)} %broadcast_select_fusion), channel_id=1, source_target_pairs={{0,1},{2,3},{4,5},{6,7},{8,9},{10,11},{12,13},{14,15},{16,17},{18,... | collective-permute-start | bytes 1572872 | tf_op jit(solution)/shard_map/ppermute | solution.py:30
  107.0 44.3 %collective-permute-start.19 = (s16[784,768]{1,0:T(8,128)(2,1)S(1)}, s16[784,768]{1,0:T(8,128)(2,1)S(1)}, u32[]{:S(2)}, u32[]{:S(2)}) collective-permute-start(s16[784,768]{1,0:T(8,128)(2,1)S(1)} %shard_map.106.refs_2_.refs_3_), channel_id=1, source_target_pairs={{0,16},{8,24},{16,0},{24,8},{1,17},{9,25},{17,1},{25,9},{2,18},{10... | collective-permute-start | bytes 3612680 | tf_op jit(solution)/shard_map/ppermute | solution.py:21
  108.6 38.9 %collective-permute-start.21 = (s16[1040,256]{1,0:T(8,128)(2,1)S(1)}, s16[1040,256]{1,0:T(8,128)(2,1)S(1)}, u32[]{:S(2)}, u32[]{:S(2)}) collective-permute-start(s16[1040,256]{1,0:T(8,128)(2,1)S(1)} %get-tuple-element.22.refs_2_), channel_id=1, source_target_pairs={{0,8},{8,0},{16,24},{24,16},{1,9},{9,1},{17,25},{25,17},{2,10},{10... | collective-permute-start | bytes 1597448 | tf_op jit(solution)/shard_map/ppermute | solution.py:21
  127.6 21.8 %collective-permute-start.20 = (s16[1040,256]{1,0:T(8,128)(2,1)S(1)}, s16[1040,256]{1,0:T(8,128)(2,1)S(1)}, u32[]{:S(2)}, u32[]{:S(2)}) collective-permute-start(s16[1040,256]{1,0:T(8,128)(2,1)S(1)} %get-tuple-element.23.refs_3_), channel_id=1, source_target_pairs={{0,8},{8,0},{16,24},{24,16},{1,9},{9,1},{17,25},{25,17},{2,10},{10... | collective-permute-start | bytes 1597448 | tf_op jit(solution)/shard_map/ppermute | solution.py:21
  129.7 4.7 %collective-permute-start.18 = (bf16[128,1024]{1,0:T(8,128)(2,1)S(1)}, bf16[128,1024]{1,0:T(8,128)(2,1)S(1)}, u32[]{:S(2)}, u32[]{:S(2)}) collective-permute-start(bf16[128,1024]{1,0:T(8,128)(2,1)S(1)} %get-tuple-element.26), channel_id=1, source_target_pairs={{0,4},{1,5},{2,6},{3,7},{8,12},{9,13},{10,14},{11,15},{16,20},{17,... | collective-permute-start | bytes 786440 | tf_op jit(solution)/shard_map/ppermute | solution.py:30
  (4 other events, 4.0 us)

commit v5 on v3

--- a/solution.py
+++ b/solution.py
@@ -167,7 +167,7 @@
     )
 
 
-def merge(after, first, second):
+def merge(after, first, second, pieces=1):
     rows, blocks = first[0].shape[0] - EXTRA, sum(piece.shape[1] for piece in first) // BLK
 
     def kernel(*refs):
@@ -189,9 +189,9 @@
         ]
         encode_all(segments, out_refs, value_ref, scale_ref, rows)
 
-    return run(
-        kernel, after, [*first, *second], [VMEM_SPEC] * (2 * len(first)), [VMEM_SPEC] * len(first),
-        [jax.ShapeDtypeStruct(piece.shape, jnp.int16) for piece in first],
+    shapes = message_shapes(rows, blocks, pieces)
+    return run(
+        kernel, after, [*first, *second], [VMEM_SPEC] * (2 * len(first)), [VMEM_SPEC] * len(shapes), shapes,
         rows * blocks * BLK * 6, scratch=message_scratch(rows, blocks),
     )
 
@@ -239,6 +239,31 @@
         jax.ShapeDtypeStruct((1, 2 * rows, width), jnp.float32), rows * width * 6, scalars=(owner,),
         aliases={1 + len(code): 0} if extra else None,
     )
+
+
+def corner_rows(after, pivots, partial):
+    lines = pivots.reshape(-1, BLK)
+
+    def kernel(pivot_ref, x_ref, out_ref):
+        source = pivot_ref[0:1, :] % BLK
+        turned = (lax.broadcasted_iota(jnp.int32, (BLK, BLK), 0) == source).astype(jnp.float32)
+        out_ref[...] = lax.dot_general(
+            turned, x_ref[0], (((0,), (0,)), ((), ())), precision=HIGHEST, preferred_element_type=jnp.float32
+        )
+
+    return run(
+        kernel, after, [lines, partial],
+        [pl.BlockSpec((8, BLK), lambda g: (0, 0)), pl.BlockSpec((1, BLK, BLK), lambda g: (0, 0, 0))],
+        pl.BlockSpec((BLK, BLK), lambda g: (0, 0)), jax.ShapeDtypeStruct((BLK, BLK), jnp.float32), BLK * BLK * 8,
+    )
+
+
+def corner_sum(after, parts):
+    def kernel(a_ref, b_ref, c_ref, d_ref, out_ref):
+        out_ref[...] = (a_ref[...] + b_ref[...]) + (c_ref[...] + d_ref[...])
+
+    shape = jax.ShapeDtypeStruct((BLK, BLK), jnp.float32)
+    return run(kernel, after, parts, [VMEM_SPEC] * 4, VMEM_SPEC, shape, BLK * BLK * 20)
 
 
 def factor(after, corner):
@@ -436,46 +461,46 @@
     encode_top = sender(partial_top, pattern_top, top_rows // 4, 1, top_blocks - 1)
     encode_low = sender(partial_low, pattern_low, low_rows, 0, low_blocks)
 
-
-    corner = exact_dot(order[:BLK].astype(jnp.float32), partial_top[0, :BLK, :BLK])
     count = lax.axis_size("layer")
+    corner = corner_rows([], pivots, partial_top)
     beside = [lax.ppermute(corner, "layer", [(i, i ^ apart) for i in range(count)]) for apart in (1, 2, 3)]
-
-    slab = encode_slab([corner], 0)
+    slab = encode_slab([*[corner]], 0)
     slab_got = swapped(slab, 0)
-    corner = (corner + beside[0]) + (beside[1] + beside[2])
+    mid_sent = encode_mid([*slab, *beside], 1 - high_bit, (), 1)
+    mid_got = swapped(mid_sent, 1)
+    a_sent = encode_top([*mid_sent], 3 - low_bit)
+    a_got = swapped(a_sent, 0)
+    summed = corner_sum([*a_sent], [corner, *beside])
+    corner = summed
     for bit in bits[2:]:
         corner = corner + swapped(corner, bit)
     corner_row = broadcast_stages(corner, "row")
     corner_col = broadcast_stages(corner_row[-1], "col")
-
-    mid_sent = encode_mid([*[*slab]], 1 - high_bit, (), 1)
-    mid_got = swapped(mid_sent, 1)
-    a_sent = encode_top([*mid_sent, corner_row[-1]], 3 - low_bit)
-    a_got = swapped(a_sent, 0)
-    b_sent = encode_top([*a_sent, corner_col[0]], 1 - high_bit)
+    corner_all = corner_col[-1]
+    b_sent = encode_top([*[summed]], 1 - high_bit)
     b_got = swapped(b_sent, 1)
-    slab = exchanged([*b_sent, corner_col[-1]], slab, slab_got, bits[1:-1])
+    slab = exchanged([*b_sent, corner_row[-1]], slab, slab_got, bits[1:-1])
     slab_got = swapped(slab, bits[-1])
-    mid = encode_mid([*slab], high_bit, mid_got, 1)
+    mid = encode_mid([*slab, corner_col[0]], high_bit, mid_got, 2)
     mid_got = swapped(mid, 0)
-    packed, lower_inverse, upper_inverse = factor([*mid, *a_got], corner_col[-1])
+    packed, lower_inverse, upper_inverse = factor([*mid], corner_all)
     b = encode_top([*[packed]], high_bit, b_got)
     b_got = swapped(b, 0)
     a = encode_top([*b], 2 + low_bit, a_got)
     a_got = swapped(a, 1)
     panel, lower_low = lower_panel([*a, *mid_got], flags, order, *slab, *slab_got, upper_inverse)
-    lower_low = broadcast_stages(lower_low, "col")[-1]
-    mid = merge([*[panel]], mid, mid_got)
+    lower_stages = broadcast_stages(lower_low, "col")
+    lower_low = lower_stages[-1]
+    mid = merge([*[panel]], mid, mid_got, 1)
     mid_got = swapped(mid, 1)
     a = exchanged([*mid], a, a_got, bits[2:])
     a_got = swapped(a, 0)
     b = exchanged([*a], b, b_got, bits[2:])
     b_got = swapped(b, 1)
     mid_sums = mid_half([*b], high_bit[None].astype(jnp.int32), mid)
-    low = encode_low([*[mid_sums]], 0, (), 2)
+    low = encode_low([*[mid_sums]], 0, (), 1)
     low_got = swapped(low, 0)
-    upper, upper_low = upper_panel([*low], flags, order, panel, *b, *b_got, lower_inverse)
+    upper, upper_low = upper_panel([*low, *a_got], flags, order, panel, *b, *b_got, lower_inverse)
     upper_low = broadcast_stages(upper_low, "row")[-1]
     top_factor = top_total([*[upper]], flags, order, (*a, *a_got, *b, *b_got), panel, lower_low, upper_low, upper, packed)
     low_place = jnp.stack([jnp.int32(0), row * pattern_low.shape[1], col * pattern_low.shape[2]]).astype(jnp.int32)

time: 156 us -> 150 us (0.962)
  waiting for transfers between devices: 39.9 us -> 35.9 us
  starting transfers between devices: 32.8 us -> 36.4 us
  local copies, waits for them, and re-layouts: 5.33 us -> 1.77 us
    ppermute x13, waiting for transfers between devices: 37.3 us -> 34 us  [swapped(): lax.ppermute(piece, 'layer', pairs)]
    unnamed x30 -> x24, local copies, waits for them, and re-layouts: 4.4 us -> 1.52 us
    ppermute x6, starting transfers between devices: 15.7 us -> 17.5 us  [broadcast_stages(): lax.ppermute(value, axis, [(i, i + span) for i in range(0, count, 2 * spa...]
    ppermute x13, starting transfers between devices: 12.5 us -> 14.3 us  [swapped(): lax.ppermute(piece, 'layer', pairs)]
    pallas_call x19 -> x21, Pallas kernels: 68.9 us -> 69.6 us  [run(): pl.pallas_call(body, grid_spec=pltpu.PrefetchScalarGridSpec(num_scalar_pr...]
  transfers between devices with their start and end apart: 22 -> 22, of which waited for: 9 -> 8; matrix products, arithmetic and copies ran while one was open for 3% -> 3% of each run, Pallas kernels for 43% -> 44%
where the time goes in v5:
time: 150 us; the launch traced here: 149 us
  Pallas kernels  69.6 us (46%)
  starting transfers between devices  36.4 us (24%)
  waiting for transfers between devices  35.9 us (24%)
  other arithmetic  4.25 us (3%)
  local copies, waits for them, and re-layouts  1.77 us (1%)
    pallas_call x21, Pallas kernels, run(): pl.pallas_call(body, grid_spec=pltpu.PrefetchScalarGridSpec(num_scalar_pr...  69.6 us
    ppermute x13, waiting for transfers between devices, swapped(): lax.ppermute(piece, 'layer', pairs)  34 us
    ppermute x6, starting transfers between devices, broadcast_stages(): lax.ppermute(value, axis, [(i, i + span) for i in range(0, count, 2 * spa...  17.5 us
    ppermute x13, starting transfers between devices, swapped(): lax.ppermute(piece, 'layer', pairs)  14.3 us
    ppermute x3, starting transfers between devices, on_device(): lax.ppermute(corner, 'layer', [(i, i ^ apart) for i in range(count)])  4.6 us
  transfers between devices with their start and end apart: 22, of which 8 were waited for; matrix products, arithmetic and copies ran while one was open for 3% of the time, Pallas kernels for 44%

profile of v5, /device:TPU:0, one launch (start us, length us, event | category | flops | bytes accessed | tf_op | source)
XLA Modules:
  0.0 148.9 jit_solution(7564623484420599604)
XLA Ops:
  2.5 4.0 %collective-permute-start.2 = (f32[128,128]{1,0:T(8,128)S(1)}, f32[128,128]{1,0:T(8,128)S(1)}, u32[]{:S(2)}, u32[]{:S(2)}) collective-permute-start(f32[128,128]{1,0:T(8,128)S(1)} %shard_map.94.refs_3_.refs_0_), channel_id=1, source_target_pairs={{0,24},{8,16},{16,8},{24,0},{1,25},{9,17},{17,9},{25,1},{2,26},{10... | collective-permute-start | bytes 196616 | tf_op jit(solution)/shard_map/ppermute | solution.py:466
  7.2 2.1 %shard_map.95.refs_3_.refs_0_ = s16[2064,128]{1,0:T(8,128)(2,1)S(1)} custom-call(s32[3]{0:T(128)S(1)} %fusion.2.refs_0_, s32[16,8]{1,0:T(8,128)S(1)} %copy.17.refs_1_, f32[1,2048,1024]{2,1,0:T(8,128)} %refs_2_.15, f32[128,128]{1,0:T(8,128)S(1)} %shard_map.94.refs_3_.refs_0_), custom_call_target="tpu_custom_call" | custom-call | bytes 1024 | tf_op jit(solution)/shard_map/pallas_call | solution.py:63
  9.3 2.0 %collective-permute-start.9 = (s16[2064,128]{1,0:T(8,128)(2,1)S(1)}, s16[2064,128]{1,0:T(8,128)(2,1)S(1)}, u32[]{:S(2)}, u32[]{:S(2)}) collective-permute-start(s16[2064,128]{1,0:T(8,128)(2,1)S(1)} %shard_map.95.refs_3_.refs_0_), channel_id=1, source_target_pairs={{0,8},{8,0},{16,24},{24,16},{1,9},{9,1},{17,25},{25,17},{2,10},{10... | collective-permute-start | bytes 1585160 | tf_op jit(solution)/shard_map/ppermute | solution.py:21
  12.2 3.1 %shard_map.96.refs_3_ = s16[784,768]{1,0:T(8,128)(2,1)S(1)} custom-call(s32[3]{0:T(128)S(1)} %add_add_fusion.2.refs_0_, s32[12,6]{1,0:T(8,128)S(1)} %bitcast.17, f32[1,1536,768]{2,1,0:T(8,128)} %refs_2_.13, s16[2064,128]{1,0:T(8,128)(2,1)S(1)} %shard_map.95.refs_3_.refs_0_, f32[128,128]{1,0:T(8,128)S(1)} %collective-permute-done.refs_4_.refs_1_, ...), custom_call_target="tpu_custom_call" | custom-call | bytes 1024 | tf_op jit(solution)/shard_map/pallas_call | solution.py:63
  15.3 1.6 %collective-permute-start.8 = (s16[784,768]{1,0:T(8,128)(2,1)S(1)}, s16[784,768]{1,0:T(8,128)(2,1)}, u32[]{:S(2)}, u32[]{:S(2)}) collective-permute-start(s16[784,768]{1,0:T(8,128)(2,1)S(1)} %shard_map.96.refs_3_), channel_id=1, source_target_pairs={{0,16},{8,24},{16,0},{24,8},{1,17},{9,25},{17,1},{25,9},{2,18},{10... | collective-permute-start | bytes 3612680 | tf_op jit(solution)/shard_map/ppermute | solution.py:21
  17.6 2.9 %shard_map.97.refs_4_ = s16[528,896]{1,0:T(8,128)(2,1)S(1)} custom-call(s32[3]{0:T(128)S(1)} %add_add_fusion.1.refs_0_, s32[16,8]{1,0:T(8,128)S(1)} %copy.17.refs_1_, f32[1,2048,1024]{2,1,0:T(8,128)} %refs_2_.15, s16[784,768]{1,0:T(8,128)(2,1)S(1)} %shard_map.96.refs_3_), custom_call_target="tpu_custom_call" | custom-call | bytes 1024 | tf_op jit(solution)/shard_map/pallas_call | solution.py:63
  22.5 3.8 %shard_map.99.refs_2_ = s16[528,896]{1,0:T(8,128)(2,1)} custom-call(s32[3]{0:T(128)S(1)} %copy-done.7, s32[16,8]{1,0:T(8,128)S(1)} %copy.17.refs_1_, f32[1,2048,1024]{2,1,0:T(8,128)} %refs_2_.15, f32[128,128]{1,0:T(8,128)S(1)} %shard_map.98.refs_3_), custom_call_target="tpu_custom_call" | custom-call | bytes 1024 | tf_op jit(solution)/shard_map/pallas_call | solution.py:63
  26.5 4.9 %collective-permute-start.6 = (f32[128,128]{1,0:T(8,128)S(1)}, f32[128,128]{1,0:T(8,128)S(1)}, u32[]{:S(2)}, u32[]{:S(2)}) collective-permute-start(f32[128,128]{1,0:T(8,128)S(1)} %broadcast_select_fusion.3.refs_3_), channel_id=1, source_target_pairs={{0,2},{4,6},{8,10},{12,14},{16,18},{20,22},{24,26},{28,30}} | collective-permute-start | bytes 196616 | tf_op jit(solution)/shard_map/ppermute | solution.py:30
  31.5 1.9 %collective-permute-done.6 = f32[128,128]{1,0:T(8,128)S(1)} collective-permute-done((f32[128,128]{1,0:T(8,128)S(1)}, f32[128,128]{1,0:T(8,128)S(1)}, u32[]{:S(2)}, u32[]{:S(2)}) %collective-permute-start.6) | collective-permute-done | bytes 65568 | tf_op jit(solution)/shard_map/ppermute | solution.py:30
  35.3 1.6 %collective-permute-start.13 = (s16[2064,128]{1,0:T(8,128)(2,1)S(1)}, s16[2064,128]{1,0:T(8,128)(2,1)S(1)}, u32[]{:S(2)}, u32[]{:S(2)}) collective-permute-start(s16[2064,128]{1,0:T(8,128)(2,1)S(1)} %shard_map.100.refs_4_.refs_2_), channel_id=1, source_target_pairs={{0,16},{8,24},{16,0},{24,8},{1,17},{9,25},{17,1},{25,9},{2,18},{10... | collective-permute-start | bytes 1585160 | tf_op jit(solution)/shard_map/ppermute | solution.py:21
  36.9 8.0 %collective-permute-done.8.refs_3_ = s16[784,768]{1,0:T(8,128)(2,1)} collective-permute-done((s16[784,768]{1,0:T(8,128)(2,1)S(1)}, s16[784,768]{1,0:T(8,128)(2,1)}, u32[]{:S(2)}, u32[]{:S(2)}) %collective-permute-start.8) | collective-permute-done | bytes 1204256 | tf_op jit(solution)/shard_map/ppermute | solution.py:21
  44.9 3.6 %shard_map.101 = (s16[784,384]{1,0:T(8,128)(2,1)S(1)}, s16[784,384]{1,0:T(8,128)(2,1)S(1)}) custom-call(s32[3]{0:T(128)S(1)} %add_add_fusion.5.refs_0_, s32[12,6]{1,0:T(8,128)S(1)} %bitcast.18, f32[1,1536,768]{2,1,0:T(8,128)} %refs_2_.13, s16[784,768]{1,0:T(8,128)(2,1)} %collective-permute-done.8.refs_3_, s16[2064,128]{1,0:T(8,128)(2,1)S(1)} %shard_map.100.refs_4_.refs_2_, ...), custom_call_target="tpu_custom_call" | custom-call | bytes 1024 | tf_op jit(solution)/shard_map/pallas_call | solution.py:63
  48.7 1.9 %collective-permute-start.12 = (s16[784,384]{1,0:T(8,128)(2,1)S(1)}, s16[784,384]{1,0:T(8,128)(2,1)S(1)}, u32[]{:S(2)}, u32[]{:S(2)}) collective-permute-start(s16[784,384]{1,0:T(8,128)(2,1)S(1)} %get-tuple-element.13.refs_2_.refs_1_), channel_id=1, source_target_pairs={{0,8},{8,0},{16,24},{24,16},{1,9},{9,1},{17,25},{25,17},{2,10},{10... | collective-permute-start | bytes 1806344 | tf_op jit(solution)/shard_map/ppermute | solution.py:21
  50.6 15.3 %shard_map.102 = (f32[128,128]{1,0:T(8,128)S(1)}, f32[128,128]{1,0:T(8,128)S(1)}, f32[128,128]{1,0:T(8,128)S(1)}) custom-call(f32[128,128]{1,0:T(8,128)S(1)} %broadcast_select_fusion.5.refs_0_, s16[784,384]{1,0:T(8,128)(2,1)S(1)} %get-tuple-element.12.refs_1_.refs_0_, s16[784,384]{1,0:T(8,128)(2,1)S(1)} %get-tuple-element.13.refs_2_.refs_1_), custom_call_target="tpu_custom_call" | custom-call | bytes 1024 | tf_op jit(solution)/shard_map/pallas_call | solution.py:63
  65.9 3.3 %shard_map.103.refs_4_.refs_0_ = s16[528,896]{1,0:T(8,128)(2,1)S(1)} custom-call(s32[3]{0:T(128)S(1)} %add_add_fusion.3.refs_0_, s32[16,8]{1,0:T(8,128)S(1)} %copy.17.refs_1_, f32[1,2048,1024]{2,1,0:T(8,128)} %refs_2_.15, s16[528,896]{1,0:T(8,128)(2,1)} %collective-permute-done.4.refs_3_, f32[128,128]{1,0:T(8,128)S(1)} %get-tuple-element.14.refs_4_.refs_10_), custom_call_target="tpu_custom_call" | custom-call | bytes 1024 | tf_op jit(solution)/shard_map/pallas_call | solution.py:63
  69.4 3.3 %shard_map.104.refs_5_.refs_0_ = s16[528,896]{1,0:T(8,128)(2,1)S(1)} custom-call(s32[3]{0:T(128)S(1)} %add_add_fusion.refs_0_, s32[16,8]{1,0:T(8,128)S(1)} %copy.17.refs_1_, f32[1,2048,1024]{2,1,0:T(8,128)} %refs_2_.15, s16[528,896]{1,0:T(8,128)(2,1)} %collective-permute-done.3.refs_3_, s16[528,896]{1,0:T(8,128)(2,1)S(1)} %shard_map.103.refs_4_.refs_0_), custom_call_target="tpu_custom_call" | custom-call | bytes 1024 | tf_op jit(solution)/shard_map/pallas_call | solution.py:63
  72.7 2.0 %collective-permute-start.10 = (s16[528,896]{1,0:T(8,128)(2,1)S(1)}, s16[528,896]{1,0:T(8,128)(2,1)S(1)}, u32[]{:S(2)}, u32[]{:S(2)}) collective-permute-start(s16[528,896]{1,0:T(8,128)(2,1)S(1)} %shard_map.104.refs_5_.refs_0_), channel_id=1, source_target_pairs={{0,16},{8,24},{16,0},{24,8},{1,17},{9,25},{17,1},{25,9},{2,18},{10... | collective-permute-start | bytes 2838536 | tf_op jit(solution)/shard_map/ppermute | solution.py:21
  76.4 1.6 %collective-permute-done.12.refs_7_.refs_3_ = s16[784,384]{1,0:T(8,128)(2,1)S(1)} collective-permute-done((s16[784,384]{1,0:T(8,128)(2,1)S(1)}, s16[784,384]{1,0:T(8,128)(2,1)S(1)}, u32[]{:S(2)}, u32[]{:S(2)}) %collective-permute-start.12) | collective-permute-done | bytes 602144 | tf_op jit(solution)/shard_map/ppermute | solution.py:21
  78.0 2.8 %shard_map.105 = (f32[2048,128]{1,0:T(8,128)S(1)}, bf16[2048,128]{1,0:T(8,128)(2,1)S(1)}) custom-call(s32[4]{0:T(128)S(1)} %pad_add_fusion.2.refs_0_, bf16[2048,128]{1,0:T(8,128)(2,1)S(1)} %fusion.refs_1_, s16[2064,128]{1,0:T(8,128)(2,1)S(1)} %shard_map.100.refs_4_.refs_2_, s16[2064,128]{1,0:T(8,128)(2,1)S(1)} %collective-permute-done.13.refs_3_, ...), custom_call_target="tpu_custom_call" | custom-call | bytes 1024 | tf_op jit(solution)/shard_map/pallas_call | solution.py:63
  80.8 4.4 %collective-permute-start.17 = (bf16[2048,128]{1,0:T(8,128)(2,1)S(1)}, bf16[2048,128]{1,0:T(8,128)(2,1)S(1)}, u32[]{:S(2)}, u32[]{:S(2)}) collective-permute-start(bf16[2048,128]{1,0:T(8,128)(2,1)S(1)} %get-tuple-element.17), channel_id=1, source_target_pairs={{0,2},{4,6},{8,10},{12,14},{16,18},{20,22},{24,26},{28,30}} | collective-permute-start | bytes 1572872 | tf_op jit(solution)/shard_map/ppermute | solution.py:30
  86.3 8.0 %collective-permute-done.10.refs_1_ = s16[528,896]{1,0:T(8,128)(2,1)S(1)} collective-permute-done((s16[528,896]{1,0:T(8,128)(2,1)S(1)}, s16[528,896]{1,0:T(8,128)(2,1)S(1)}, u32[]{:S(2)}, u32[]{:S(2)}) %collective-permute-start.10) | collective-permute-done | bytes 946208 | tf_op jit(solution)/shard_map/ppermute | solution.py:21
  94.3 1.8 %shard_map.107.refs_2_ = s16[528,896]{1,0:T(8,128)(2,1)} custom-call(s16[528,896]{1,0:T(8,128)(2,1)S(1)} %shard_map.104.refs_5_.refs_0_, s16[528,896]{1,0:T(8,128)(2,1)S(1)} %collective-permute-done.10.refs_1_, s16[784,768]{1,0:T(8,128)(2,1)S(1)} %shard_map.106.refs_2_.refs_1_), custom_call_target="tpu_custom_call" | custom-call | bytes 1024 | tf_op jit(solution)/shard_map/pallas_call | solution.py:63
  97.4 1.7 %collective-permute-start.16 = (s16[528,896]{1,0:T(8,128)(2,1)S(1)}, s16[528,896]{1,0:T(8,128)(2,1)}, u32[]{:S(2)}, u32[]{:S(2)}) collective-permute-start(s16[528,896]{1,0:T(8,128)(2,1)S(1)} %shard_map.108.refs_2_.refs_3_.refs_4_), channel_id=1, source_target_pairs={{0,16},{8,24},{16,0},{24,8},{1,17},{9,25},{17,1},{25,9},{2,18},{10... | collective-permute-start | bytes 2838536 | tf_op jit(solution)/shard_map/ppermute | solution.py:21
  100.0 4.3 %collective-permute-start.18 = (bf16[2048,128]{1,0:T(8,128)(2,1)}, bf16[2048,128]{1,0:T(8,128)(2,1)}, u32[]{:S(2)}, u32[]{:S(2)}) collective-permute-start(bf16[2048,128]{1,0:T(8,128)(2,1)} %broadcast_select_fusion), channel_id=1, source_target_pairs={{0,1},{2,3},{4,5},{6,7},{8,9},{10,11},{12,13},{14,15},{16,17},{18,... | collective-permute-start | bytes 1572872 | tf_op jit(solution)/shard_map/ppermute | solution.py:30
  104.9 1.7 %shard_map.109.refs_3_.refs_2_ = f32[1,1536,768]{2,1,0:T(8,128)} custom-call(s32[1]{0:T(128)} %bitcast.1.refs_0_, s16[784,768]{1,0:T(8,128)(2,1)S(1)} %shard_map.106.refs_2_.refs_1_, s16[528,896]{1,0:T(8,128)(2,1)S(1)} %shard_map.108.refs_2_.refs_3_.refs_4_), custom_call_target="tpu_custom_call" | custom-call | bytes 1024 | tf_op jit(solution)/shard_map/pallas_call | solution.py:63
  108.7 1.6 %collective-permute-start.21 = (s16[1040,512]{1,0:T(8,128)(2,1)S(1)}, s16[1040,512]{1,0:T(8,128)(2,1)S(1)}, u32[]{:S(2)}, u32[]{:S(2)}) collective-permute-start(s16[1040,512]{1,0:T(8,128)(2,1)S(1)} %shard_map.110.refs_8_), channel_id=1, source_target_pairs={{0,8},{8,0},{16,24},{24,16},{1,9},{9,1},{17,25},{25,17},{2,10},{10... | collective-permute-start | bytes 3194888 | tf_op jit(solution)/shard_map/ppermute | solution.py:21
  110.3 10.1 %collective-permute-done.14.refs_9_.refs_3_ = s16[528,896]{1,0:T(8,128)(2,1)} collective-permute-done((s16[528,896]{1,0:T(8,128)(2,1)}, s16[528,896]{1,0:T(8,128)(2,1)}, u32[]{:S(2)}, u32[]{:S(2)}) %collective-permute-start.14) | collective-permute-done | bytes 946208 | tf_op jit(solution)/shard_map/ppermute | solution.py:21
  121.5 2.0 %shard_map.111 = (f32[128,1024]{1,0:T(8,128)S(1)}, bf16[128,1024]{1,0:T(8,128)(2,1)S(1)}) custom-call(s32[4]{0:T(128)S(1)} %pad_add_fusion.2.refs_0_, bf16[2048,128]{1,0:T(8,128)(2,1)S(1)} %copy-done.3, f32[2048,128]{1,0:T(8,128)S(1)} %get-tuple-element.16.refs_4_.refs_2_.refs_6_, s16[528,896]{1,0:T(8,128)(2,1)S(1)} %shard_map.108.refs_2_.refs_3_.refs_4_, ...), custom_call_target="tpu_custom_call" | custom-call | bytes 1024 | tf_op jit(solution)/shard_map/pallas_call | solution.py:63
  126.0 13.9 %shard_map.112.refs_3_.refs_4_ = f32[2048,1024]{1,0:T(8,128)} custom-call(s32[4]{0:T(128)S(1)} %pad_add_fusion.2.refs_0_, bf16[2048,128]{1,0:T(8,128)(2,1)S(1)} %copy-done.3, s16[528,896]{1,0:T(8,128)(2,1)} %shard_map.107.refs_2_, s16[528,896]{1,0:T(8,128)(2,1)} %collective-permute-done.14.refs_9_.refs_3_, ...), custom_call_target="tpu_custom_call" | custom-call | bytes 1024 | tf_op jit(solution)/shard_map/pallas_call | solution.py:63
  139.9 3.7 %collective-permute-done.20.refs_1_ = s16[784,768]{1,0:T(8,128)(2,1)} collective-permute-done((s16[784,768]{1,0:T(8,128)(2,1)S(1)}, s16[784,768]{1,0:T(8,128)(2,1)}, u32[]{:S(2)}, u32[]{:S(2)}) %collective-permute-start.20) | collective-permute-done | bytes 1204256 | tf_op jit(solution)/shard_map/ppermute | solution.py:21
  143.6 2.9 %shard_map.113 = f32[1,1536,768]{2,1,0:T(8,128)} custom-call(s32[1]{0:T(128)} %bitcast.9.refs_0_, s16[784,768]{1,0:T(8,128)(2,1)} %collective-permute-done.20.refs_1_, f32[1,1536,768]{2,1,0:T(8,128)} %shard_map.109.refs_3_.refs_2_, f32[2048,1024]{1,0:T(8,128)} %shard_map.112.refs_3_.refs_4_), custom_call_target="tpu_custom_call", output_to_operand_aliasing={{}: (2, {})} | custom-call | bytes 1024 | tf_op jit(solution)/shard_map/pallas_call | solution.py:63
  146.6 2.4 %shard_map.114 = f32[1,1024,512]{2,1,0:T(8,128)} custom-call(s32[3]{0:T(128)S(1)} %fusion.3.refs_0_, s32[8,4]{1,0:T(8,128)S(1)} %copy.18.refs_1_, f32[1,1024,512]{2,1,0:T(8,128)S(1)} %copy-done.1, s16[1040,512]{1,0:T(8,128)(2,1)S(1)} %collective-permute-done.21.refs_3_, f32[2048,1024]{1,0:T(8,128)} %shard_map.112.refs_3_.refs_4_), custom_call_target="tpu_custom_call" | custom-call | bytes 1024 | tf_op jit(solution)/shard_map/pallas_call | solution.py:63
  (77 shorter events, 19.9 us)
Async XLA Ops:
  1.3 5.7 %copy-start.9 = (s32[1,16,8]{1,2,0:T(8,128)S(1)}, s32[1,16,8]{1,2,0:T(8,128)}, u32[]{:S(2)}) copy-start(s32[1,16,8]{1,2,0:T(8,128)} %param.10) | copy-start | bytes 1540
  2.5 9.7 %collective-permute-start.2 = (f32[128,128]{1,0:T(8,128)S(1)}, f32[128,128]{1,0:T(8,128)S(1)}, u32[]{:S(2)}, u32[]{:S(2)}) collective-permute-start(f32[128,128]{1,0:T(8,128)S(1)} %shard_map.94.refs_3_.refs_0_), channel_id=1, source_target_pairs={{0,24},{8,16},{16,8},{24,0},{1,25},{9,17},{17,9},{25,1},{2,26},{10... | collective-permute-start | bytes 196616 | tf_op jit(solution)/shard_map/ppermute | solution.py:466
  6.4 5.7 %collective-permute-start.1 = (f32[128,128]{1,0:T(8,128)S(1)}, f32[128,128]{1,0:T(8,128)S(1)}, u32[]{:S(2)}, u32[]{:S(2)}) collective-permute-start(f32[128,128]{1,0:T(8,128)S(1)} %shard_map.94.refs_3_.refs_0_), channel_id=1, source_target_pairs={{0,16},{8,24},{16,0},{24,8},{1,17},{9,25},{17,1},{25,9},{2,18},{10... | collective-permute-start | bytes 196616 | tf_op jit(solution)/shard_map/ppermute | solution.py:466
  6.9 5.2 %collective-permute-start = (f32[128,128]{1,0:T(8,128)S(1)}, f32[128,128]{1,0:T(8,128)S(1)}, u32[]{:S(2)}, u32[]{:S(2)}) collective-permute-start(f32[128,128]{1,0:T(8,128)S(1)} %shard_map.94.refs_3_.refs_0_), channel_id=1, source_target_pairs={{0,8},{8,0},{16,24},{24,16},{1,9},{9,1},{17,25},{25,17},{2,10},{10... | collective-permute-start | bytes 196616 | tf_op jit(solution)/shard_map/ppermute | solution.py:466
  7.2 4.8 %copy-start.10 = (s32[1,12,6]{1,0,2:T(1,128)S(1)}, s32[1,12,6]{1,0,2:T(1,128)}, u32[]{:S(2)}) copy-start(s32[1,12,6]{1,0,2:T(1,128)} %param.11) | copy-start | bytes 868
  9.3 25.5 %collective-permute-start.9 = (s16[2064,128]{1,0:T(8,128)(2,1)S(1)}, s16[2064,128]{1,0:T(8,128)(2,1)S(1)}, u32[]{:S(2)}, u32[]{:S(2)}) collective-permute-start(s16[2064,128]{1,0:T(8,128)(2,1)S(1)} %shard_map.95.refs_3_.refs_0_), channel_id=1, source_target_pairs={{0,8},{8,0},{16,24},{24,16},{1,9},{9,1},{17,25},{25,17},{2,10},{10... | collective-permute-start | bytes 1585160 | tf_op jit(solution)/shard_map/ppermute | solution.py:21
  12.1 4.9 %copy-start.6 = (s32[2048]{0:T(1024)S(1)}, s32[2048]{0:T(1024)}, u32[]{:S(2)}) copy-start(s32[2048]{0:T(1024)} %param.13) | copy-start | bytes 24580
  15.3 29.6 %collective-permute-start.8 = (s16[784,768]{1,0:T(8,128)(2,1)S(1)}, s16[784,768]{1,0:T(8,128)(2,1)}, u32[]{:S(2)}, u32[]{:S(2)}) collective-permute-start(s16[784,768]{1,0:T(8,128)(2,1)S(1)} %shard_map.96.refs_3_), channel_id=1, source_target_pairs={{0,16},{8,24},{16,0},{24,8},{1,17},{9,25},{17,1},{25,9},{2,18},{10... | collective-permute-start | bytes 3612680 | tf_op jit(solution)/shard_map/ppermute | solution.py:21
  17.6 4.8 %copy-start.7 = (s32[3]{0:T(128)S(1)}, s32[3]{0:T(128)}, u32[]{:S(2)}) copy-start(s32[3]{0:T(128)} %add_add_fusion.4.refs_0_) | copy-start | bytes 40
  20.6 48.8 %collective-permute-start.3 = (s16[528,896]{1,0:T(8,128)(2,1)S(1)}, s16[528,896]{1,0:T(8,128)(2,1)}, u32[]{:S(2)}, u32[]{:S(2)}) collective-permute-start(s16[528,896]{1,0:T(8,128)(2,1)S(1)} %shard_map.97.refs_4_), channel_id=1, source_target_pairs={{0,8},{8,0},{16,24},{24,16},{1,9},{9,1},{17,25},{25,17},{2,10},{10... | collective-permute-start | bytes 2838536 | tf_op jit(solution)/shard_map/ppermute | solution.py:21
  21.2 5.3 %collective-permute-start.5 = (f32[128,128]{1,0:T(8,128)S(1)}, f32[128,128]{1,0:T(8,128)S(1)}, u32[]{:S(2)}, u32[]{:S(2)}) collective-permute-start(f32[128,128]{1,0:T(8,128)S(1)} %shard_map.98.refs_3_), channel_id=1, source_target_pairs={{0,4},{1,5},{2,6},{3,7},{8,12},{9,13},{10,14},{11,15},{16,20},{17,... | collective-permute-start | bytes 196616 | tf_op jit(solution)/shard_map/ppermute | solution.py:30
  26.3 39.5 %collective-permute-start.4 = (s16[528,896]{1,0:T(8,128)(2,1)}, s16[528,896]{1,0:T(8,128)(2,1)}, u32[]{:S(2)}, u32[]{:S(2)}) collective-permute-start(s16[528,896]{1,0:T(8,128)(2,1)} %shard_map.99.refs_2_), channel_id=1, source_target_pairs={{0,16},{8,24},{16,0},{24,8},{1,17},{9,25},{17,1},{25,9},{2,18},{10... | collective-permute-start | bytes 2838536 | tf_op jit(solution)/shard_map/ppermute | solution.py:21
  26.5 6.9 %collective-permute-start.6 = (f32[128,128]{1,0:T(8,128)S(1)}, f32[128,128]{1,0:T(8,128)S(1)}, u32[]{:S(2)}, u32[]{:S(2)}) collective-permute-start(f32[128,128]{1,0:T(8,128)S(1)} %broadcast_select_fusion.3.refs_3_), channel_id=1, source_target_pairs={{0,2},{4,6},{8,10},{12,14},{16,18},{20,22},{24,26},{28,30}} | collective-permute-start | bytes 196616 | tf_op jit(solution)/shard_map/ppermute | solution.py:30
  33.4 15.2 %collective-permute-start.7 = (f32[128,128]{1,0:T(8,128)S(1)}, f32[128,128]{1,0:T(8,128)S(1)}, u32[]{:S(2)}, u32[]{:S(2)}) collective-permute-start(f32[128,128]{1,0:T(8,128)S(1)} %broadcast_select_fusion.4.refs_5_), channel_id=1, source_target_pairs={{0,1},{2,3},{4,5},{6,7},{8,9},{10,11},{12,13},{14,15},{16,17},{18,... | collective-permute-start | bytes 196616 | tf_op jit(solution)/shard_map/ppermute | solution.py:30
  35.3 41.1 %collective-permute-start.13 = (s16[2064,128]{1,0:T(8,128)(2,1)S(1)}, s16[2064,128]{1,0:T(8,128)(2,1)S(1)}, u32[]{:S(2)}, u32[]{:S(2)}) collective-permute-start(s16[2064,128]{1,0:T(8,128)(2,1)S(1)} %shard_map.100.refs_4_.refs_2_), channel_id=1, source_target_pairs={{0,16},{8,24},{16,0},{24,8},{1,17},{9,25},{17,1},{25,9},{2,18},{10... | collective-permute-start | bytes 1585160 | tf_op jit(solution)/shard_map/ppermute | solution.py:21
  48.5 27.9 %collective-permute-start.11 = (s16[784,384]{1,0:T(8,128)(2,1)S(1)}, s16[784,384]{1,0:T(8,128)(2,1)S(1)}, u32[]{:S(2)}, u32[]{:S(2)}) collective-permute-start(s16[784,384]{1,0:T(8,128)(2,1)S(1)} %get-tuple-element.12.refs_1_.refs_0_), channel_id=1, source_target_pairs={{0,8},{8,0},{16,24},{24,16},{1,9},{9,1},{17,25},{25,17},{2,10},{10... | collective-permute-start | bytes 1806344 | tf_op jit(solution)/shard_map/ppermute | solution.py:21
  48.7 29.3 %collective-permute-start.12 = (s16[784,384]{1,0:T(8,128)(2,1)S(1)}, s16[784,384]{1,0:T(8,128)(2,1)S(1)}, u32[]{:S(2)}, u32[]{:S(2)}) collective-permute-start(s16[784,384]{1,0:T(8,128)(2,1)S(1)} %get-tuple-element.13.refs_2_.refs_1_), channel_id=1, source_target_pairs={{0,8},{8,0},{16,24},{24,16},{1,9},{9,1},{17,25},{25,17},{2,10},{10... | collective-permute-start | bytes 1806344 | tf_op jit(solution)/shard_map/ppermute | solution.py:21
  69.2 5.5 %copy-start.8 = (s32[2048]{0:T(1024)S(1)}, s32[2048]{0:T(1024)}, u32[]{:S(2)}) copy-start(s32[2048]{0:T(1024)} %add_select_fusion) | copy-start | bytes 24580
  69.2 27.4 %collective-permute-start.15 = (s16[528,896]{1,0:T(8,128)(2,1)S(1)}, s16[528,896]{1,0:T(8,128)(2,1)S(1)}, u32[]{:S(2)}, u32[]{:S(2)}) collective-permute-start(s16[528,896]{1,0:T(8,128)(2,1)S(1)} %shard_map.103.refs_4_.refs_0_), channel_id=1, source_target_pairs={{0,8},{8,0},{16,24},{24,16},{1,9},{9,1},{17,25},{25,17},{2,10},{10... | collective-permute-start | bytes 2838536 | tf_op jit(solution)/shard_map/ppermute | solution.py:21
  72.7 21.7 %collective-permute-start.10 = (s16[528,896]{1,0:T(8,128)(2,1)S(1)}, s16[528,896]{1,0:T(8,128)(2,1)S(1)}, u32[]{:S(2)}, u32[]{:S(2)}) collective-permute-start(s16[528,896]{1,0:T(8,128)(2,1)S(1)} %shard_map.104.refs_5_.refs_0_), channel_id=1, source_target_pairs={{0,16},{8,24},{16,0},{24,8},{1,17},{9,25},{17,1},{25,9},{2,18},{10... | collective-permute-start | bytes 2838536 | tf_op jit(solution)/shard_map/ppermute | solution.py:21
  75.0 10.3 %copy-start.2 = (bf16[2048,128]{1,0:T(8,128)(2,1)}, bf16[2048,128]{1,0:T(8,128)(2,1)S(1)}, u32[]{:S(2)}) copy-start(bf16[2048,128]{1,0:T(8,128)(2,1)S(1)} %fusion.refs_1_) | copy-start | bytes 1572868
  80.8 40.7 %copy-start = (f32[2048,128]{1,0:T(8,128)}, f32[2048,128]{1,0:T(8,128)S(1)}, u32[]{:S(2)}) copy-start(f32[2048,128]{1,0:T(8,128)S(1)} %get-tuple-element.16.refs_4_.refs_2_.refs_6_) | copy-start | bytes 3145732
  80.8 18.3 %collective-permute-start.17 = (bf16[2048,128]{1,0:T(8,128)(2,1)S(1)}, bf16[2048,128]{1,0:T(8,128)(2,1)S(1)}, u32[]{:S(2)}, u32[]{:S(2)}) collective-permute-start(bf16[2048,128]{1,0:T(8,128)(2,1)S(1)} %get-tuple-element.17), channel_id=1, source_target_pairs={{0,2},{4,6},{8,10},{12,14},{16,18},{20,22},{24,26},{28,30}} | collective-permute-start | bytes 1572872 | tf_op jit(solution)/shard_map/ppermute | solution.py:30
  96.1 8.6 %copy-start.11 = (s32[1,8,4]{1,2,0:T(4,128)S(1)}, s32[1,8,4]{1,2,0:T(4,128)}, u32[]{:S(2)}) copy-start(s32[1,8,4]{1,2,0:T(4,128)} %param.12) | copy-start | bytes 388
  96.1 24.2 %collective-permute-start.14 = (s16[528,896]{1,0:T(8,128)(2,1)}, s16[528,896]{1,0:T(8,128)(2,1)}, u32[]{:S(2)}, u32[]{:S(2)}) collective-permute-start(s16[528,896]{1,0:T(8,128)(2,1)} %shard_map.107.refs_2_), channel_id=1, source_target_pairs={{0,8},{8,0},{16,24},{24,16},{1,9},{9,1},{17,25},{25,17},{2,10},{10... | collective-permute-start | bytes 2838536 | tf_op jit(solution)/shard_map/ppermute | solution.py:21
  97.4 24.1 %collective-permute-start.16 = (s16[528,896]{1,0:T(8,128)(2,1)S(1)}, s16[528,896]{1,0:T(8,128)(2,1)}, u32[]{:S(2)}, u32[]{:S(2)}) collective-permute-start(s16[528,896]{1,0:T(8,128)(2,1)S(1)} %shard_map.108.refs_2_.refs_3_.refs_4_), channel_id=1, source_target_pairs={{0,16},{8,24},{16,0},{24,8},{1,17},{9,25},{17,1},{25,9},{2,18},{10... | collective-permute-start | bytes 2838536 | tf_op jit(solution)/shard_map/ppermute | solution.py:21
  100.0 24.8 %collective-permute-start.18 = (bf16[2048,128]{1,0:T(8,128)(2,1)}, bf16[2048,128]{1,0:T(8,128)(2,1)}, u32[]{:S(2)}, u32[]{:S(2)}) collective-permute-start(bf16[2048,128]{1,0:T(8,128)(2,1)} %broadcast_select_fusion), channel_id=1, source_target_pairs={{0,1},{2,3},{4,5},{6,7},{8,9},{10,11},{12,13},{14,15},{16,17},{18,... | collective-permute-start | bytes 1572872 | tf_op jit(solution)/shard_map/ppermute | solution.py:30
  104.2 39.4 %collective-permute-start.20 = (s16[784,768]{1,0:T(8,128)(2,1)S(1)}, s16[784,768]{1,0:T(8,128)(2,1)}, u32[]{:S(2)}, u32[]{:S(2)}) collective-permute-start(s16[784,768]{1,0:T(8,128)(2,1)S(1)} %shard_map.106.refs_2_.refs_1_), channel_id=1, source_target_pairs={{0,16},{8,24},{16,0},{24,8},{1,17},{9,25},{17,1},{25,9},{2,18},{10... | collective-permute-start | bytes 3612680 | tf_op jit(solution)/shard_map/ppermute | solution.py:21
  107.4 14.1 %copy-start.3 = (bf16[2048,128]{1,0:T(8,128)(2,1)S(1)}, bf16[2048,128]{1,0:T(8,128)(2,1)}, u32[]{:S(2)}) copy-start(bf16[2048,128]{1,0:T(8,128)(2,1)} %copy-done.2) | copy-start | bytes 1572868
  108.7 12.8 %copy-start.4 = (s16[1040,512]{1,0:T(8,128)(2,1)}, s16[1040,512]{1,0:T(8,128)(2,1)S(1)}, u32[]{:S(2)}) copy-start(s16[1040,512]{1,0:T(8,128)(2,1)S(1)} %shard_map.110.refs_8_) | copy-start | bytes 3194884
  108.7 37.9 %collective-permute-start.21 = (s16[1040,512]{1,0:T(8,128)(2,1)S(1)}, s16[1040,512]{1,0:T(8,128)(2,1)S(1)}, u32[]{:S(2)}, u32[]{:S(2)}) collective-permute-start(s16[1040,512]{1,0:T(8,128)(2,1)S(1)} %shard_map.110.refs_8_), channel_id=1, source_target_pairs={{0,8},{8,0},{16,24},{24,16},{1,9},{9,1},{17,25},{25,17},{2,10},{10... | collective-permute-start | bytes 3194888 | tf_op jit(solution)/shard_map/ppermute | solution.py:21
  123.5 2.4 %collective-permute-start.19 = (bf16[128,1024]{1,0:T(8,128)(2,1)S(1)}, bf16[128,1024]{1,0:T(8,128)(2,1)S(1)}, u32[]{:S(2)}, u32[]{:S(2)}) collective-permute-start(bf16[128,1024]{1,0:T(8,128)(2,1)S(1)} %get-tuple-element.19), channel_id=1, source_target_pairs={{0,4},{1,5},{2,6},{3,7},{8,12},{9,13},{10,14},{11,15},{16,20},{17,... | collective-permute-start | bytes 786440 | tf_op jit(solution)/shard_map/ppermute | solution.py:30
  (2 other events, 3.1 us)

commit v6 on v5

--- a/solution.py
+++ b/solution.py
@@ -493,11 +493,11 @@
     lower_low = lower_stages[-1]
     mid = merge([*[panel]], mid, mid_got, 1)
     mid_got = swapped(mid, 1)
-    a = exchanged([*mid], a, a_got, bits[2:])
+    b = exchanged([*mid], b, b_got, bits[2:])
+    b_got = swapped(b, 1)
+    a = exchanged([*b], a, a_got, bits[2:])
     a_got = swapped(a, 0)
-    b = exchanged([*a], b, b_got, bits[2:])
-    b_got = swapped(b, 1)
-    mid_sums = mid_half([*b], high_bit[None].astype(jnp.int32), mid)
+    mid_sums = mid_half([*a], high_bit[None].astype(jnp.int32), mid)
     low = encode_low([*[mid_sums]], 0, (), 1)
     low_got = swapped(low, 0)
     upper, upper_low = upper_panel([*low, *a_got], flags, order, panel, *b, *b_got, lower_inverse)

time: 150 us -> 148 us (0.987)
  waiting for transfers between devices: 35.9 us -> 31.9 us
    ppermute x13, waiting for transfers between devices: 34 us -> 30 us  [swapped(): lax.ppermute(piece, 'layer', pairs)]
  transfers between devices with their start and end apart: 22 -> 22, of which waited for: 8 -> 7; matrix products, arithmetic and copies ran while one was open for 3% -> 3% of each run, Pallas kernels for 44% -> 45%
where the time goes in v6:
time: 148 us; the launch traced here: 146 us
  Pallas kernels  69.7 us (47%)
  starting transfers between devices  37.8 us (26%)
  waiting for transfers between devices  31.9 us (22%)
  other arithmetic  4.25 us (3%)
  local copies, waits for them, and re-layouts  1.77 us (1%)
    pallas_call x21, Pallas kernels, run(): pl.pallas_call(body, grid_spec=pltpu.PrefetchScalarGridSpec(num_scalar_pr...  69.7 us
    ppermute x13, waiting for transfers between devices, swapped(): lax.ppermute(piece, 'layer', pairs)  30 us
    ppermute x6, starting transfers between devices, broadcast_stages(): lax.ppermute(value, axis, [(i, i + span) for i in range(0, count, 2 * spa...  18.5 us
    ppermute x13, starting transfers between devices, swapped(): lax.ppermute(piece, 'layer', pairs)  14.7 us
    ppermute x3, starting transfers between devices, on_device(): lax.ppermute(corner, 'layer', [(i, i ^ apart) for i in range(count)])  4.6 us
  transfers between devices with their start and end apart: 22, of which 7 were waited for; matrix products, arithmetic and copies ran while one was open for 3% of the time, Pallas kernels for 45%

profile of v6, /device:TPU:0, one launch (start us, length us, event | category | flops | bytes accessed | tf_op | source)
XLA Modules:
  0.0 146.4 jit_solution(6534541778623080477)
XLA Ops:
  2.5 4.0 %collective-permute-start.2 = (f32[128,128]{1,0:T(8,128)S(1)}, f32[128,128]{1,0:T(8,128)S(1)}, u32[]{:S(2)}, u32[]{:S(2)}) collective-permute-start(f32[128,128]{1,0:T(8,128)S(1)} %shard_map.94.refs_3_.refs_0_), channel_id=1, source_target_pairs={{0,24},{8,16},{16,8},{24,0},{1,25},{9,17},{17,9},{25,1},{2,26},{10... | collective-permute-start | bytes 196616 | tf_op jit(solution)/shard_map/ppermute | solution.py:466
  7.2 2.1 %shard_map.95.refs_3_.refs_0_ = s16[2064,128]{1,0:T(8,128)(2,1)S(1)} custom-call(s32[3]{0:T(128)S(1)} %fusion.2.refs_0_, s32[16,8]{1,0:T(8,128)S(1)} %copy.17.refs_1_, f32[1,2048,1024]{2,1,0:T(8,128)} %refs_2_.15, f32[128,128]{1,0:T(8,128)S(1)} %shard_map.94.refs_3_.refs_0_), custom_call_target="tpu_custom_call" | custom-call | bytes 1024 | tf_op jit(solution)/shard_map/pallas_call | solution.py:63
  9.3 2.0 %collective-permute-start.9 = (s16[2064,128]{1,0:T(8,128)(2,1)S(1)}, s16[2064,128]{1,0:T(8,128)(2,1)S(1)}, u32[]{:S(2)}, u32[]{:S(2)}) collective-permute-start(s16[2064,128]{1,0:T(8,128)(2,1)S(1)} %shard_map.95.refs_3_.refs_0_), channel_id=1, source_target_pairs={{0,8},{8,0},{16,24},{24,16},{1,9},{9,1},{17,25},{25,17},{2,10},{10... | collective-permute-start | bytes 1585160 | tf_op jit(solution)/shard_map/ppermute | solution.py:21
  12.2 3.1 %shard_map.96.refs_3_ = s16[784,768]{1,0:T(8,128)(2,1)S(1)} custom-call(s32[3]{0:T(128)S(1)} %add_add_fusion.2.refs_0_, s32[12,6]{1,0:T(8,128)S(1)} %bitcast.17, f32[1,1536,768]{2,1,0:T(8,128)} %refs_2_.13, s16[2064,128]{1,0:T(8,128)(2,1)S(1)} %shard_map.95.refs_3_.refs_0_, f32[128,128]{1,0:T(8,128)S(1)} %collective-permute-done.refs_4_.refs_1_, ...), custom_call_target="tpu_custom_call" | custom-call | bytes 1024 | tf_op jit(solution)/shard_map/pallas_call | solution.py:63
  15.3 1.6 %collective-permute-start.8 = (s16[784,768]{1,0:T(8,128)(2,1)S(1)}, s16[784,768]{1,0:T(8,128)(2,1)}, u32[]{:S(2)}, u32[]{:S(2)}) collective-permute-start(s16[784,768]{1,0:T(8,128)(2,1)S(1)} %shard_map.96.refs_3_), channel_id=1, source_target_pairs={{0,16},{8,24},{16,0},{24,8},{1,17},{9,25},{17,1},{25,9},{2,18},{10... | collective-permute-start | bytes 3612680 | tf_op jit(solution)/shard_map/ppermute | solution.py:21
  17.6 2.9 %shard_map.97.refs_4_ = s16[528,896]{1,0:T(8,128)(2,1)S(1)} custom-call(s32[3]{0:T(128)S(1)} %add_add_fusion.1.refs_0_, s32[16,8]{1,0:T(8,128)S(1)} %copy.17.refs_1_, f32[1,2048,1024]{2,1,0:T(8,128)} %refs_2_.15, s16[784,768]{1,0:T(8,128)(2,1)S(1)} %shard_map.96.refs_3_), custom_call_target="tpu_custom_call" | custom-call | bytes 1024 | tf_op jit(solution)/shard_map/pallas_call | solution.py:63
  22.5 3.8 %shard_map.99.refs_2_ = s16[528,896]{1,0:T(8,128)(2,1)} custom-call(s32[3]{0:T(128)S(1)} %copy-done.7, s32[16,8]{1,0:T(8,128)S(1)} %copy.17.refs_1_, f32[1,2048,1024]{2,1,0:T(8,128)} %refs_2_.15, f32[128,128]{1,0:T(8,128)S(1)} %shard_map.98.refs_3_), custom_call_target="tpu_custom_call" | custom-call | bytes 1024 | tf_op jit(solution)/shard_map/pallas_call | solution.py:63
  26.5 4.9 %collective-permute-start.6 = (f32[128,128]{1,0:T(8,128)S(1)}, f32[128,128]{1,0:T(8,128)S(1)}, u32[]{:S(2)}, u32[]{:S(2)}) collective-permute-start(f32[128,128]{1,0:T(8,128)S(1)} %broadcast_select_fusion.3.refs_3_), channel_id=1, source_target_pairs={{0,2},{4,6},{8,10},{12,14},{16,18},{20,22},{24,26},{28,30}} | collective-permute-start | bytes 196616 | tf_op jit(solution)/shard_map/ppermute | solution.py:30
  31.5 1.9 %collective-permute-done.6 = f32[128,128]{1,0:T(8,128)S(1)} collective-permute-done((f32[128,128]{1,0:T(8,128)S(1)}, f32[128,128]{1,0:T(8,128)S(1)}, u32[]{:S(2)}, u32[]{:S(2)}) %collective-permute-start.6) | collective-permute-done | bytes 65568 | tf_op jit(solution)/shard_map/ppermute | solution.py:30
  35.3 1.6 %collective-permute-start.14 = (s16[2064,128]{1,0:T(8,128)(2,1)S(1)}, s16[2064,128]{1,0:T(8,128)(2,1)S(1)}, u32[]{:S(2)}, u32[]{:S(2)}) collective-permute-start(s16[2064,128]{1,0:T(8,128)(2,1)S(1)} %shard_map.100.refs_4_.refs_2_), channel_id=1, source_target_pairs={{0,16},{8,24},{16,0},{24,8},{1,17},{9,25},{17,1},{25,9},{2,18},{10... | collective-permute-start | bytes 1585160 | tf_op jit(solution)/shard_map/ppermute | solution.py:21
  36.9 8.0 %collective-permute-done.8.refs_3_ = s16[784,768]{1,0:T(8,128)(2,1)} collective-permute-done((s16[784,768]{1,0:T(8,128)(2,1)S(1)}, s16[784,768]{1,0:T(8,128)(2,1)}, u32[]{:S(2)}, u32[]{:S(2)}) %collective-permute-start.8) | collective-permute-done | bytes 1204256 | tf_op jit(solution)/shard_map/ppermute | solution.py:21
  44.9 3.6 %shard_map.101 = (s16[784,384]{1,0:T(8,128)(2,1)S(1)}, s16[784,384]{1,0:T(8,128)(2,1)S(1)}) custom-call(s32[3]{0:T(128)S(1)} %add_add_fusion.5.refs_0_, s32[12,6]{1,0:T(8,128)S(1)} %bitcast.18, f32[1,1536,768]{2,1,0:T(8,128)} %refs_2_.13, s16[784,768]{1,0:T(8,128)(2,1)} %collective-permute-done.8.refs_3_, s16[2064,128]{1,0:T(8,128)(2,1)S(1)} %shard_map.100.refs_4_.refs_2_, ...), custom_call_target="tpu_custom_call" | custom-call | bytes 1024 | tf_op jit(solution)/shard_map/pallas_call | solution.py:63
  48.7 1.9 %collective-permute-start.13 = (s16[784,384]{1,0:T(8,128)(2,1)S(1)}, s16[784,384]{1,0:T(8,128)(2,1)S(1)}, u32[]{:S(2)}, u32[]{:S(2)}) collective-permute-start(s16[784,384]{1,0:T(8,128)(2,1)S(1)} %get-tuple-element.13.refs_2_.refs_1_), channel_id=1, source_target_pairs={{0,8},{8,0},{16,24},{24,16},{1,9},{9,1},{17,25},{25,17},{2,10},{10... | collective-permute-start | bytes 1806344 | tf_op jit(solution)/shard_map/ppermute | solution.py:21
  50.6 15.3 %shard_map.102 = (f32[128,128]{1,0:T(8,128)S(1)}, f32[128,128]{1,0:T(8,128)S(1)}, f32[128,128]{1,0:T(8,128)S(1)}) custom-call(f32[128,128]{1,0:T(8,128)S(1)} %broadcast_select_fusion.5.refs_0_, s16[784,384]{1,0:T(8,128)(2,1)S(1)} %get-tuple-element.12.refs_1_.refs_0_, s16[784,384]{1,0:T(8,128)(2,1)S(1)} %get-tuple-element.13.refs_2_.refs_1_), custom_call_target="tpu_custom_call" | custom-call | bytes 1024 | tf_op jit(solution)/shard_map/pallas_call | solution.py:63
  65.9 3.3 %shard_map.103.refs_4_.refs_0_ = s16[528,896]{1,0:T(8,128)(2,1)S(1)} custom-call(s32[3]{0:T(128)S(1)} %add_add_fusion.3.refs_0_, s32[16,8]{1,0:T(8,128)S(1)} %copy.17.refs_1_, f32[1,2048,1024]{2,1,0:T(8,128)} %refs_2_.15, s16[528,896]{1,0:T(8,128)(2,1)} %collective-permute-done.4.refs_3_, f32[128,128]{1,0:T(8,128)S(1)} %get-tuple-element.14.refs_4_.refs_10_), custom_call_target="tpu_custom_call" | custom-call | bytes 1024 | tf_op jit(solution)/shard_map/pallas_call | solution.py:63
  69.4 3.3 %shard_map.104.refs_5_.refs_0_ = s16[528,896]{1,0:T(8,128)(2,1)S(1)} custom-call(s32[3]{0:T(128)S(1)} %add_add_fusion.refs_0_, s32[16,8]{1,0:T(8,128)S(1)} %copy.17.refs_1_, f32[1,2048,1024]{2,1,0:T(8,128)} %refs_2_.15, s16[528,896]{1,0:T(8,128)(2,1)} %collective-permute-done.3.refs_3_, s16[528,896]{1,0:T(8,128)(2,1)S(1)} %shard_map.103.refs_4_.refs_0_), custom_call_target="tpu_custom_call" | custom-call | bytes 1024 | tf_op jit(solution)/shard_map/pallas_call | solution.py:63
  72.7 2.0 %collective-permute-start.10 = (s16[528,896]{1,0:T(8,128)(2,1)S(1)}, s16[528,896]{1,0:T(8,128)(2,1)S(1)}, u32[]{:S(2)}, u32[]{:S(2)}) collective-permute-start(s16[528,896]{1,0:T(8,128)(2,1)S(1)} %shard_map.104.refs_5_.refs_0_), channel_id=1, source_target_pairs={{0,16},{8,24},{16,0},{24,8},{1,17},{9,25},{17,1},{25,9},{2,18},{10... | collective-permute-start | bytes 2838536 | tf_op jit(solution)/shard_map/ppermute | solution.py:21
  76.4 1.6 %collective-permute-done.13.refs_7_.refs_3_ = s16[784,384]{1,0:T(8,128)(2,1)S(1)} collective-permute-done((s16[784,384]{1,0:T(8,128)(2,1)S(1)}, s16[784,384]{1,0:T(8,128)(2,1)S(1)}, u32[]{:S(2)}, u32[]{:S(2)}) %collective-permute-start.13) | collective-permute-done | bytes 602144 | tf_op jit(solution)/shard_map/ppermute | solution.py:21
  78.0 2.8 %shard_map.105 = (f32[2048,128]{1,0:T(8,128)S(1)}, bf16[2048,128]{1,0:T(8,128)(2,1)S(1)}) custom-call(s32[4]{0:T(128)S(1)} %pad_add_fusion.2.refs_0_, bf16[2048,128]{1,0:T(8,128)(2,1)S(1)} %fusion.refs_1_, s16[2064,128]{1,0:T(8,128)(2,1)S(1)} %shard_map.100.refs_4_.refs_2_, s16[2064,128]{1,0:T(8,128)(2,1)S(1)} %collective-permute-done.14.refs_3_, ...), custom_call_target="tpu_custom_call" | custom-call | bytes 1024 | tf_op jit(solution)/shard_map/pallas_call | solution.py:63
  80.8 4.5 %collective-permute-start.17 = (bf16[2048,128]{1,0:T(8,128)(2,1)S(1)}, bf16[2048,128]{1,0:T(8,128)(2,1)S(1)}, u32[]{:S(2)}, u32[]{:S(2)}) collective-permute-start(bf16[2048,128]{1,0:T(8,128)(2,1)S(1)} %get-tuple-element.17), channel_id=1, source_target_pairs={{0,2},{4,6},{8,10},{12,14},{16,18},{20,22},{24,26},{28,30}} | collective-permute-start | bytes 1572872 | tf_op jit(solution)/shard_map/ppermute | solution.py:30
  86.3 6.3 %collective-permute-done.11.refs_1_ = s16[528,896]{1,0:T(8,128)(2,1)S(1)} collective-permute-done((s16[528,896]{1,0:T(8,128)(2,1)S(1)}, s16[528,896]{1,0:T(8,128)(2,1)S(1)}, u32[]{:S(2)}, u32[]{:S(2)}) %collective-permute-start.11) | collective-permute-done | bytes 946208 | tf_op jit(solution)/shard_map/ppermute | solution.py:21
  93.5 1.6 %collective-permute-start.16 = (s16[528,896]{1,0:T(8,128)(2,1)S(1)}, s16[528,896]{1,0:T(8,128)(2,1)}, u32[]{:S(2)}, u32[]{:S(2)}) collective-permute-start(s16[528,896]{1,0:T(8,128)(2,1)S(1)} %shard_map.107.refs_2_.refs_3_.refs_4_), channel_id=1, source_target_pairs={{0,16},{8,24},{16,0},{24,8},{1,17},{9,25},{17,1},{25,9},{2,18},{10... | collective-permute-start | bytes 2838536 | tf_op jit(solution)/shard_map/ppermute | solution.py:21
  95.1 1.5 %collective-permute-done.10.refs_1_ = s16[528,896]{1,0:T(8,128)(2,1)S(1)} collective-permute-done((s16[528,896]{1,0:T(8,128)(2,1)S(1)}, s16[528,896]{1,0:T(8,128)(2,1)S(1)}, u32[]{:S(2)}, u32[]{:S(2)}) %collective-permute-start.10) | collective-permute-done | bytes 946208 | tf_op jit(solution)/shard_map/ppermute | solution.py:21
  96.7 1.8 %shard_map.108.refs_2_ = s16[528,896]{1,0:T(8,128)(2,1)} custom-call(s16[528,896]{1,0:T(8,128)(2,1)S(1)} %shard_map.104.refs_5_.refs_0_, s16[528,896]{1,0:T(8,128)(2,1)S(1)} %collective-permute-done.10.refs_1_, s16[528,896]{1,0:T(8,128)(2,1)S(1)} %shard_map.107.refs_2_.refs_3_.refs_4_), custom_call_target="tpu_custom_call" | custom-call | bytes 1024 | tf_op jit(solution)/shard_map/pallas_call | solution.py:63
  100.1 5.2 %collective-permute-start.18 = (bf16[2048,128]{1,0:T(8,128)(2,1)}, bf16[2048,128]{1,0:T(8,128)(2,1)}, u32[]{:S(2)}, u32[]{:S(2)}) collective-permute-start(bf16[2048,128]{1,0:T(8,128)(2,1)} %broadcast_select_fusion), channel_id=1, source_target_pairs={{0,1},{2,3},{4,5},{6,7},{8,9},{10,11},{12,13},{14,15},{16,17},{18,... | collective-permute-start | bytes 1572872 | tf_op jit(solution)/shard_map/ppermute | solution.py:30
  105.3 1.5 %collective-permute-start.20 = (s16[784,768]{1,0:T(8,128)(2,1)S(1)}, s16[784,768]{1,0:T(8,128)(2,1)}, u32[]{:S(2)}, u32[]{:S(2)}) collective-permute-start(s16[784,768]{1,0:T(8,128)(2,1)S(1)} %shard_map.106.refs_2_.refs_1_), channel_id=1, source_target_pairs={{0,16},{8,24},{16,0},{24,8},{1,17},{9,25},{17,1},{25,9},{2,18},{10... | collective-permute-start | bytes 3612680 | tf_op jit(solution)/shard_map/ppermute | solution.py:21
  107.0 1.7 %shard_map.109.refs_3_.refs_2_ = f32[1,1536,768]{2,1,0:T(8,128)} custom-call(s32[1]{0:T(128)} %bitcast.1.refs_0_, s16[784,768]{1,0:T(8,128)(2,1)S(1)} %shard_map.106.refs_2_.refs_1_, s16[528,896]{1,0:T(8,128)(2,1)} %shard_map.108.refs_2_), custom_call_target="tpu_custom_call" | custom-call | bytes 1024 | tf_op jit(solution)/shard_map/pallas_call | solution.py:63
  111.5 11.1 %collective-permute-done.15.refs_9_.refs_3_ = s16[528,896]{1,0:T(8,128)(2,1)} collective-permute-done((s16[528,896]{1,0:T(8,128)(2,1)}, s16[528,896]{1,0:T(8,128)(2,1)}, u32[]{:S(2)}, u32[]{:S(2)}) %collective-permute-start.15) | collective-permute-done | bytes 946208 | tf_op jit(solution)/shard_map/ppermute | solution.py:21
  122.7 2.0 %shard_map.111 = (f32[128,1024]{1,0:T(8,128)S(1)}, bf16[128,1024]{1,0:T(8,128)(2,1)S(1)}) custom-call(s32[4]{0:T(128)S(1)} %pad_add_fusion.2.refs_0_, bf16[2048,128]{1,0:T(8,128)(2,1)S(1)} %copy-done.3, f32[2048,128]{1,0:T(8,128)S(1)} %get-tuple-element.16.refs_4_.refs_2_.refs_6_, s16[528,896]{1,0:T(8,128)(2,1)S(1)} %shard_map.107.refs_2_.refs_3_.refs_4_, ...), custom_call_target="tpu_custom_call" | custom-call | bytes 1024 | tf_op jit(solution)/shard_map/pallas_call | solution.py:63
  127.2 13.9 %shard_map.112.refs_3_.refs_4_ = f32[2048,1024]{1,0:T(8,128)} custom-call(s32[4]{0:T(128)S(1)} %pad_add_fusion.2.refs_0_, bf16[2048,128]{1,0:T(8,128)(2,1)S(1)} %copy-done.3, s16[528,896]{1,0:T(8,128)(2,1)} %shard_map.108.refs_2_, s16[528,896]{1,0:T(8,128)(2,1)} %collective-permute-done.15.refs_9_.refs_3_, ...), custom_call_target="tpu_custom_call" | custom-call | bytes 1024 | tf_op jit(solution)/shard_map/pallas_call | solution.py:63
  141.1 2.9 %shard_map.113 = f32[1,1536,768]{2,1,0:T(8,128)} custom-call(s32[1]{0:T(128)} %bitcast.9.refs_0_, s16[784,768]{1,0:T(8,128)(2,1)} %collective-permute-done.20.refs_1_, f32[1,1536,768]{2,1,0:T(8,128)} %shard_map.109.refs_3_.refs_2_, f32[2048,1024]{1,0:T(8,128)} %shard_map.112.refs_3_.refs_4_), custom_call_target="tpu_custom_call", output_to_operand_aliasing={{}: (2, {})} | custom-call | bytes 1024 | tf_op jit(solution)/shard_map/pallas_call | solution.py:63
  144.1 2.4 %shard_map.114 = f32[1,1024,512]{2,1,0:T(8,128)} custom-call(s32[3]{0:T(128)S(1)} %fusion.3.refs_0_, s32[8,4]{1,0:T(8,128)S(1)} %copy.18.refs_1_, f32[1,1024,512]{2,1,0:T(8,128)S(1)} %copy-done.1, s16[1040,512]{1,0:T(8,128)(2,1)S(1)} %collective-permute-done.21.refs_3_, f32[2048,1024]{1,0:T(8,128)} %shard_map.112.refs_3_.refs_4_), custom_call_target="tpu_custom_call" | custom-call | bytes 1024 | tf_op jit(solution)/shard_map/pallas_call | solution.py:63
  (77 shorter events, 19.4 us)
Async XLA Ops:
  1.3 5.7 %copy-start.9 = (s32[1,16,8]{1,2,0:T(8,128)S(1)}, s32[1,16,8]{1,2,0:T(8,128)}, u32[]{:S(2)}) copy-start(s32[1,16,8]{1,2,0:T(8,128)} %param.10) | copy-start | bytes 1540
  2.5 9.7 %collective-permute-start.2 = (f32[128,128]{1,0:T(8,128)S(1)}, f32[128,128]{1,0:T(8,128)S(1)}, u32[]{:S(2)}, u32[]{:S(2)}) collective-permute-start(f32[128,128]{1,0:T(8,128)S(1)} %shard_map.94.refs_3_.refs_0_), channel_id=1, source_target_pairs={{0,24},{8,16},{16,8},{24,0},{1,25},{9,17},{17,9},{25,1},{2,26},{10... | collective-permute-start | bytes 196616 | tf_op jit(solution)/shard_map/ppermute | solution.py:466
  6.4 5.7 %collective-permute-start.1 = (f32[128,128]{1,0:T(8,128)S(1)}, f32[128,128]{1,0:T(8,128)S(1)}, u32[]{:S(2)}, u32[]{:S(2)}) collective-permute-start(f32[128,128]{1,0:T(8,128)S(1)} %shard_map.94.refs_3_.refs_0_), channel_id=1, source_target_pairs={{0,16},{8,24},{16,0},{24,8},{1,17},{9,25},{17,1},{25,9},{2,18},{10... | collective-permute-start | bytes 196616 | tf_op jit(solution)/shard_map/ppermute | solution.py:466
  6.9 5.2 %collective-permute-start = (f32[128,128]{1,0:T(8,128)S(1)}, f32[128,128]{1,0:T(8,128)S(1)}, u32[]{:S(2)}, u32[]{:S(2)}) collective-permute-start(f32[128,128]{1,0:T(8,128)S(1)} %shard_map.94.refs_3_.refs_0_), channel_id=1, source_target_pairs={{0,8},{8,0},{16,24},{24,16},{1,9},{9,1},{17,25},{25,17},{2,10},{10... | collective-permute-start | bytes 196616 | tf_op jit(solution)/shard_map/ppermute | solution.py:466
  7.2 4.8 %copy-start.10 = (s32[1,12,6]{1,0,2:T(1,128)S(1)}, s32[1,12,6]{1,0,2:T(1,128)}, u32[]{:S(2)}) copy-start(s32[1,12,6]{1,0,2:T(1,128)} %param.11) | copy-start | bytes 868
  9.3 25.5 %collective-permute-start.9 = (s16[2064,128]{1,0:T(8,128)(2,1)S(1)}, s16[2064,128]{1,0:T(8,128)(2,1)S(1)}, u32[]{:S(2)}, u32[]{:S(2)}) collective-permute-start(s16[2064,128]{1,0:T(8,128)(2,1)S(1)} %shard_map.95.refs_3_.refs_0_), channel_id=1, source_target_pairs={{0,8},{8,0},{16,24},{24,16},{1,9},{9,1},{17,25},{25,17},{2,10},{10... | collective-permute-start | bytes 1585160 | tf_op jit(solution)/shard_map/ppermute | solution.py:21
  12.1 4.9 %copy-start.6 = (s32[2048]{0:T(1024)S(1)}, s32[2048]{0:T(1024)}, u32[]{:S(2)}) copy-start(s32[2048]{0:T(1024)} %param.13) | copy-start | bytes 24580
  15.3 29.6 %collective-permute-start.8 = (s16[784,768]{1,0:T(8,128)(2,1)S(1)}, s16[784,768]{1,0:T(8,128)(2,1)}, u32[]{:S(2)}, u32[]{:S(2)}) collective-permute-start(s16[784,768]{1,0:T(8,128)(2,1)S(1)} %shard_map.96.refs_3_), channel_id=1, source_target_pairs={{0,16},{8,24},{16,0},{24,8},{1,17},{9,25},{17,1},{25,9},{2,18},{10... | collective-permute-start | bytes 3612680 | tf_op jit(solution)/shard_map/ppermute | solution.py:21
  17.6 4.8 %copy-start.7 = (s32[3]{0:T(128)S(1)}, s32[3]{0:T(128)}, u32[]{:S(2)}) copy-start(s32[3]{0:T(128)} %add_add_fusion.4.refs_0_) | copy-start | bytes 40
  20.6 48.8 %collective-permute-start.3 = (s16[528,896]{1,0:T(8,128)(2,1)S(1)}, s16[528,896]{1,0:T(8,128)(2,1)}, u32[]{:S(2)}, u32[]{:S(2)}) collective-permute-start(s16[528,896]{1,0:T(8,128)(2,1)S(1)} %shard_map.97.refs_4_), channel_id=1, source_target_pairs={{0,8},{8,0},{16,24},{24,16},{1,9},{9,1},{17,25},{25,17},{2,10},{10... | collective-permute-start | bytes 2838536 | tf_op jit(solution)/shard_map/ppermute | solution.py:21
  21.2 5.3 %collective-permute-start.5 = (f32[128,128]{1,0:T(8,128)S(1)}, f32[128,128]{1,0:T(8,128)S(1)}, u32[]{:S(2)}, u32[]{:S(2)}) collective-permute-start(f32[128,128]{1,0:T(8,128)S(1)} %shard_map.98.refs_3_), channel_id=1, source_target_pairs={{0,4},{1,5},{2,6},{3,7},{8,12},{9,13},{10,14},{11,15},{16,20},{17,... | collective-permute-start | bytes 196616 | tf_op jit(solution)/shard_map/ppermute | solution.py:30
  26.3 39.5 %collective-permute-start.4 = (s16[528,896]{1,0:T(8,128)(2,1)}, s16[528,896]{1,0:T(8,128)(2,1)}, u32[]{:S(2)}, u32[]{:S(2)}) collective-permute-start(s16[528,896]{1,0:T(8,128)(2,1)} %shard_map.99.refs_2_), channel_id=1, source_target_pairs={{0,16},{8,24},{16,0},{24,8},{1,17},{9,25},{17,1},{25,9},{2,18},{10... | collective-permute-start | bytes 2838536 | tf_op jit(solution)/shard_map/ppermute | solution.py:21
  26.5 6.9 %collective-permute-start.6 = (f32[128,128]{1,0:T(8,128)S(1)}, f32[128,128]{1,0:T(8,128)S(1)}, u32[]{:S(2)}, u32[]{:S(2)}) collective-permute-start(f32[128,128]{1,0:T(8,128)S(1)} %broadcast_select_fusion.3.refs_3_), channel_id=1, source_target_pairs={{0,2},{4,6},{8,10},{12,14},{16,18},{20,22},{24,26},{28,30}} | collective-permute-start | bytes 196616 | tf_op jit(solution)/shard_map/ppermute | solution.py:30
  33.4 15.2 %collective-permute-start.7 = (f32[128,128]{1,0:T(8,128)S(1)}, f32[128,128]{1,0:T(8,128)S(1)}, u32[]{:S(2)}, u32[]{:S(2)}) collective-permute-start(f32[128,128]{1,0:T(8,128)S(1)} %broadcast_select_fusion.4.refs_5_), channel_id=1, source_target_pairs={{0,1},{2,3},{4,5},{6,7},{8,9},{10,11},{12,13},{14,15},{16,17},{18,... | collective-permute-start | bytes 196616 | tf_op jit(solution)/shard_map/ppermute | solution.py:30
  35.3 41.1 %collective-permute-start.14 = (s16[2064,128]{1,0:T(8,128)(2,1)S(1)}, s16[2064,128]{1,0:T(8,128)(2,1)S(1)}, u32[]{:S(2)}, u32[]{:S(2)}) collective-permute-start(s16[2064,128]{1,0:T(8,128)(2,1)S(1)} %shard_map.100.refs_4_.refs_2_), channel_id=1, source_target_pairs={{0,16},{8,24},{16,0},{24,8},{1,17},{9,25},{17,1},{25,9},{2,18},{10... | collective-permute-start | bytes 1585160 | tf_op jit(solution)/shard_map/ppermute | solution.py:21
  48.5 27.9 %collective-permute-start.12 = (s16[784,384]{1,0:T(8,128)(2,1)S(1)}, s16[784,384]{1,0:T(8,128)(2,1)S(1)}, u32[]{:S(2)}, u32[]{:S(2)}) collective-permute-start(s16[784,384]{1,0:T(8,128)(2,1)S(1)} %get-tuple-element.12.refs_1_.refs_0_), channel_id=1, source_target_pairs={{0,8},{8,0},{16,24},{24,16},{1,9},{9,1},{17,25},{25,17},{2,10},{10... | collective-permute-start | bytes 1806344 | tf_op jit(solution)/shard_map/ppermute | solution.py:21
  48.7 29.3 %collective-permute-start.13 = (s16[784,384]{1,0:T(8,128)(2,1)S(1)}, s16[784,384]{1,0:T(8,128)(2,1)S(1)}, u32[]{:S(2)}, u32[]{:S(2)}) collective-permute-start(s16[784,384]{1,0:T(8,128)(2,1)S(1)} %get-tuple-element.13.refs_2_.refs_1_), channel_id=1, source_target_pairs={{0,8},{8,0},{16,24},{24,16},{1,9},{9,1},{17,25},{25,17},{2,10},{10... | collective-permute-start | bytes 1806344 | tf_op jit(solution)/shard_map/ppermute | solution.py:21
  69.2 5.5 %copy-start.8 = (s32[2048]{0:T(1024)S(1)}, s32[2048]{0:T(1024)}, u32[]{:S(2)}) copy-start(s32[2048]{0:T(1024)} %add_select_fusion) | copy-start | bytes 24580
  69.2 23.5 %collective-permute-start.11 = (s16[528,896]{1,0:T(8,128)(2,1)S(1)}, s16[528,896]{1,0:T(8,128)(2,1)S(1)}, u32[]{:S(2)}, u32[]{:S(2)}) collective-permute-start(s16[528,896]{1,0:T(8,128)(2,1)S(1)} %shard_map.103.refs_4_.refs_0_), channel_id=1, source_target_pairs={{0,8},{8,0},{16,24},{24,16},{1,9},{9,1},{17,25},{25,17},{2,10},{10... | collective-permute-start | bytes 2838536 | tf_op jit(solution)/shard_map/ppermute | solution.py:21
  72.7 24.0 %collective-permute-start.10 = (s16[528,896]{1,0:T(8,128)(2,1)S(1)}, s16[528,896]{1,0:T(8,128)(2,1)S(1)}, u32[]{:S(2)}, u32[]{:S(2)}) collective-permute-start(s16[528,896]{1,0:T(8,128)(2,1)S(1)} %shard_map.104.refs_5_.refs_0_), channel_id=1, source_target_pairs={{0,16},{8,24},{16,0},{24,8},{1,17},{9,25},{17,1},{25,9},{2,18},{10... | collective-permute-start | bytes 2838536 | tf_op jit(solution)/shard_map/ppermute | solution.py:21
  75.0 10.3 %copy-start.2 = (bf16[2048,128]{1,0:T(8,128)(2,1)}, bf16[2048,128]{1,0:T(8,128)(2,1)S(1)}, u32[]{:S(2)}) copy-start(bf16[2048,128]{1,0:T(8,128)(2,1)S(1)} %fusion.refs_1_) | copy-start | bytes 1572868
  80.8 41.9 %copy-start = (f32[2048,128]{1,0:T(8,128)}, f32[2048,128]{1,0:T(8,128)S(1)}, u32[]{:S(2)}) copy-start(f32[2048,128]{1,0:T(8,128)S(1)} %get-tuple-element.16.refs_4_.refs_2_.refs_6_) | copy-start | bytes 3145732
  80.8 18.4 %collective-permute-start.17 = (bf16[2048,128]{1,0:T(8,128)(2,1)S(1)}, bf16[2048,128]{1,0:T(8,128)(2,1)S(1)}, u32[]{:S(2)}, u32[]{:S(2)}) collective-permute-start(bf16[2048,128]{1,0:T(8,128)(2,1)S(1)} %get-tuple-element.17), channel_id=1, source_target_pairs={{0,2},{4,6},{8,10},{12,14},{16,18},{20,22},{24,26},{28,30}} | collective-permute-start | bytes 1572872 | tf_op jit(solution)/shard_map/ppermute | solution.py:30
  93.5 13.3 %copy-start.11 = (s32[1,8,4]{1,2,0:T(4,128)S(1)}, s32[1,8,4]{1,2,0:T(4,128)}, u32[]{:S(2)}) copy-start(s32[1,8,4]{1,2,0:T(4,128)} %param.12) | copy-start | bytes 388
  93.5 29.1 %collective-permute-start.16 = (s16[528,896]{1,0:T(8,128)(2,1)S(1)}, s16[528,896]{1,0:T(8,128)(2,1)}, u32[]{:S(2)}, u32[]{:S(2)}) collective-permute-start(s16[528,896]{1,0:T(8,128)(2,1)S(1)} %shard_map.107.refs_2_.refs_3_.refs_4_), channel_id=1, source_target_pairs={{0,16},{8,24},{16,0},{24,8},{1,17},{9,25},{17,1},{25,9},{2,18},{10... | collective-permute-start | bytes 2838536 | tf_op jit(solution)/shard_map/ppermute | solution.py:21
  98.4 24.2 %collective-permute-start.15 = (s16[528,896]{1,0:T(8,128)(2,1)}, s16[528,896]{1,0:T(8,128)(2,1)}, u32[]{:S(2)}, u32[]{:S(2)}) collective-permute-start(s16[528,896]{1,0:T(8,128)(2,1)} %shard_map.108.refs_2_), channel_id=1, source_target_pairs={{0,8},{8,0},{16,24},{24,16},{1,9},{9,1},{17,25},{25,17},{2,10},{10... | collective-permute-start | bytes 2838536 | tf_op jit(solution)/shard_map/ppermute | solution.py:21
  100.1 25.9 %collective-permute-start.18 = (bf16[2048,128]{1,0:T(8,128)(2,1)}, bf16[2048,128]{1,0:T(8,128)(2,1)}, u32[]{:S(2)}, u32[]{:S(2)}) collective-permute-start(bf16[2048,128]{1,0:T(8,128)(2,1)} %broadcast_select_fusion), channel_id=1, source_target_pairs={{0,1},{2,3},{4,5},{6,7},{8,9},{10,11},{12,13},{14,15},{16,17},{18,... | collective-permute-start | bytes 1572872 | tf_op jit(solution)/shard_map/ppermute | solution.py:30
  105.3 35.8 %collective-permute-start.20 = (s16[784,768]{1,0:T(8,128)(2,1)S(1)}, s16[784,768]{1,0:T(8,128)(2,1)}, u32[]{:S(2)}, u32[]{:S(2)}) collective-permute-start(s16[784,768]{1,0:T(8,128)(2,1)S(1)} %shard_map.106.refs_2_.refs_1_), channel_id=1, source_target_pairs={{0,16},{8,24},{16,0},{24,8},{1,17},{9,25},{17,1},{25,9},{2,18},{10... | collective-permute-start | bytes 3612680 | tf_op jit(solution)/shard_map/ppermute | solution.py:21
  109.5 13.2 %copy-start.3 = (bf16[2048,128]{1,0:T(8,128)(2,1)S(1)}, bf16[2048,128]{1,0:T(8,128)(2,1)}, u32[]{:S(2)}) copy-start(bf16[2048,128]{1,0:T(8,128)(2,1)} %copy-done.2) | copy-start | bytes 1572868
  110.8 11.9 %copy-start.4 = (s16[1040,512]{1,0:T(8,128)(2,1)}, s16[1040,512]{1,0:T(8,128)(2,1)S(1)}, u32[]{:S(2)}) copy-start(s16[1040,512]{1,0:T(8,128)(2,1)S(1)} %shard_map.110.refs_8_) | copy-start | bytes 3194884
  110.8 33.3 %collective-permute-start.21 = (s16[1040,512]{1,0:T(8,128)(2,1)S(1)}, s16[1040,512]{1,0:T(8,128)(2,1)S(1)}, u32[]{:S(2)}, u32[]{:S(2)}) collective-permute-start(s16[1040,512]{1,0:T(8,128)(2,1)S(1)} %shard_map.110.refs_8_), channel_id=1, source_target_pairs={{0,8},{8,0},{16,24},{24,16},{1,9},{9,1},{17,25},{25,17},{2,10},{10... | collective-permute-start | bytes 3194888 | tf_op jit(solution)/shard_map/ppermute | solution.py:21
  124.7 2.4 %collective-permute-start.19 = (bf16[128,1024]{1,0:T(8,128)(2,1)S(1)}, bf16[128,1024]{1,0:T(8,128)(2,1)S(1)}, u32[]{:S(2)}, u32[]{:S(2)}) collective-permute-start(bf16[128,1024]{1,0:T(8,128)(2,1)S(1)} %get-tuple-element.19), channel_id=1, source_target_pairs={{0,4},{1,5},{2,6},{3,7},{8,12},{9,13},{10,14},{11,15},{16,20},{17,... | collective-permute-start | bytes 786440 | tf_op jit(solution)/shard_map/ppermute | solution.py:30
  (2 other events, 3.1 us)

commit v7 on v6

--- a/solution.py
+++ b/solution.py
@@ -318,7 +318,8 @@
     codes = codes.astype(jnp.int32)
     high = (codes >> 8).astype(jnp.float32).astype(jnp.bfloat16)
     low = (codes & 255).astype(jnp.float32).astype(jnp.bfloat16)
-    return (low_dot(order_block, high) * 256.0 + low_dot(order_block, low)) * scale
+    both = jnp.concatenate([high, low], axis=0)
+    return low_dot(jnp.concatenate([order_block * 256.0, order_block], axis=1).astype(jnp.bfloat16), both) * scale
 
 
 def lower_panel(after, flags, order, own, received, upper_inverse):

time: 148 us -> 148 us (level)
  no operation moved by 1% of the time
where the time goes in v7:
time: 148 us; the launch traced here: 146 us
  Pallas kernels  69.5 us (47%)
  starting transfers between devices  37.8 us (26%)
  waiting for transfers between devices  31.9 us (22%)
  other arithmetic  4.25 us (3%)
  local copies, waits for them, and re-layouts  1.77 us (1%)
    pallas_call x21, Pallas kernels, run(): pl.pallas_call(body, grid_spec=pltpu.PrefetchScalarGridSpec(num_scalar_pr...  69.5 us
    ppermute x13, waiting for transfers between devices, swapped(): lax.ppermute(piece, 'layer', pairs)  30 us
    ppermute x6, starting transfers between devices, broadcast_stages(): lax.ppermute(value, axis, [(i, i + span) for i in range(0, count, 2 * spa...  18.5 us
    ppermute x13, starting transfers between devices, swapped(): lax.ppermute(piece, 'layer', pairs)  14.7 us
    ppermute x3, starting transfers between devices, on_device(): lax.ppermute(corner, 'layer', [(i, i ^ apart) for i in range(count)])  4.6 us
  transfers between devices with their start and end apart: 22, of which 7 were waited for; matrix products, arithmetic and copies ran while one was open for 3% of the time, Pallas kernels for 45%

profile of v7, /device:TPU:0, one launch (start us, length us, event | category | flops | bytes accessed | tf_op | source)
XLA Modules:
  0.0 146.2 jit_solution(9451260020215165056)
XLA Ops:
  2.5 4.0 %collective-permute-start.2 = (f32[128,128]{1,0:T(8,128)S(1)}, f32[128,128]{1,0:T(8,128)S(1)}, u32[]{:S(2)}, u32[]{:S(2)}) collective-permute-start(f32[128,128]{1,0:T(8,128)S(1)} %shard_map.94.refs_3_.refs_0_), channel_id=1, source_target_pairs={{0,24},{8,16},{16,8},{24,0},{1,25},{9,17},{17,9},{25,1},{2,26},{10... | collective-permute-start | bytes 196616 | tf_op jit(solution)/shard_map/ppermute | solution.py:467
  7.2 2.1 %shard_map.95.refs_3_.refs_0_ = s16[2064,128]{1,0:T(8,128)(2,1)S(1)} custom-call(s32[3]{0:T(128)S(1)} %fusion.2.refs_0_, s32[16,8]{1,0:T(8,128)S(1)} %copy.17.refs_1_, f32[1,2048,1024]{2,1,0:T(8,128)} %refs_2_.15, f32[128,128]{1,0:T(8,128)S(1)} %shard_map.94.refs_3_.refs_0_), custom_call_target="tpu_custom_call" | custom-call | bytes 1024 | tf_op jit(solution)/shard_map/pallas_call | solution.py:63
  9.3 2.0 %collective-permute-start.9 = (s16[2064,128]{1,0:T(8,128)(2,1)S(1)}, s16[2064,128]{1,0:T(8,128)(2,1)S(1)}, u32[]{:S(2)}, u32[]{:S(2)}) collective-permute-start(s16[2064,128]{1,0:T(8,128)(2,1)S(1)} %shard_map.95.refs_3_.refs_0_), channel_id=1, source_target_pairs={{0,8},{8,0},{16,24},{24,16},{1,9},{9,1},{17,25},{25,17},{2,10},{10... | collective-permute-start | bytes 1585160 | tf_op jit(solution)/shard_map/ppermute | solution.py:21
  12.2 3.1 %shard_map.96.refs_3_ = s16[784,768]{1,0:T(8,128)(2,1)S(1)} custom-call(s32[3]{0:T(128)S(1)} %add_add_fusion.2.refs_0_, s32[12,6]{1,0:T(8,128)S(1)} %bitcast.17, f32[1,1536,768]{2,1,0:T(8,128)} %refs_2_.13, s16[2064,128]{1,0:T(8,128)(2,1)S(1)} %shard_map.95.refs_3_.refs_0_, f32[128,128]{1,0:T(8,128)S(1)} %collective-permute-done.refs_4_.refs_1_, ...), custom_call_target="tpu_custom_call" | custom-call | bytes 1024 | tf_op jit(solution)/shard_map/pallas_call | solution.py:63
  15.3 1.6 %collective-permute-start.8 = (s16[784,768]{1,0:T(8,128)(2,1)S(1)}, s16[784,768]{1,0:T(8,128)(2,1)}, u32[]{:S(2)}, u32[]{:S(2)}) collective-permute-start(s16[784,768]{1,0:T(8,128)(2,1)S(1)} %shard_map.96.refs_3_), channel_id=1, source_target_pairs={{0,16},{8,24},{16,0},{24,8},{1,17},{9,25},{17,1},{25,9},{2,18},{10... | collective-permute-start | bytes 3612680 | tf_op jit(solution)/shard_map/ppermute | solution.py:21
  17.6 2.9 %shard_map.97.refs_4_ = s16[528,896]{1,0:T(8,128)(2,1)S(1)} custom-call(s32[3]{0:T(128)S(1)} %add_add_fusion.1.refs_0_, s32[16,8]{1,0:T(8,128)S(1)} %copy.17.refs_1_, f32[1,2048,1024]{2,1,0:T(8,128)} %refs_2_.15, s16[784,768]{1,0:T(8,128)(2,1)S(1)} %shard_map.96.refs_3_), custom_call_target="tpu_custom_call" | custom-call | bytes 1024 | tf_op jit(solution)/shard_map/pallas_call | solution.py:63
  22.5 3.8 %shard_map.99.refs_2_ = s16[528,896]{1,0:T(8,128)(2,1)} custom-call(s32[3]{0:T(128)S(1)} %copy-done.7, s32[16,8]{1,0:T(8,128)S(1)} %copy.17.refs_1_, f32[1,2048,1024]{2,1,0:T(8,128)} %refs_2_.15, f32[128,128]{1,0:T(8,128)S(1)} %shard_map.98.refs_3_), custom_call_target="tpu_custom_call" | custom-call | bytes 1024 | tf_op jit(solution)/shard_map/pallas_call | solution.py:63
  26.5 4.9 %collective-permute-start.6 = (f32[128,128]{1,0:T(8,128)S(1)}, f32[128,128]{1,0:T(8,128)S(1)}, u32[]{:S(2)}, u32[]{:S(2)}) collective-permute-start(f32[128,128]{1,0:T(8,128)S(1)} %broadcast_select_fusion.3.refs_3_), channel_id=1, source_target_pairs={{0,2},{4,6},{8,10},{12,14},{16,18},{20,22},{24,26},{28,30}} | collective-permute-start | bytes 196616 | tf_op jit(solution)/shard_map/ppermute | solution.py:30
  31.5 1.9 %collective-permute-done.6 = f32[128,128]{1,0:T(8,128)S(1)} collective-permute-done((f32[128,128]{1,0:T(8,128)S(1)}, f32[128,128]{1,0:T(8,128)S(1)}, u32[]{:S(2)}, u32[]{:S(2)}) %collective-permute-start.6) | collective-permute-done | bytes 65568 | tf_op jit(solution)/shard_map/ppermute | solution.py:30
  35.3 1.6 %collective-permute-start.14 = (s16[2064,128]{1,0:T(8,128)(2,1)S(1)}, s16[2064,128]{1,0:T(8,128)(2,1)S(1)}, u32[]{:S(2)}, u32[]{:S(2)}) collective-permute-start(s16[2064,128]{1,0:T(8,128)(2,1)S(1)} %shard_map.100.refs_4_.refs_2_), channel_id=1, source_target_pairs={{0,16},{8,24},{16,0},{24,8},{1,17},{9,25},{17,1},{25,9},{2,18},{10... | collective-permute-start | bytes 1585160 | tf_op jit(solution)/shard_map/ppermute | solution.py:21
  36.9 8.0 %collective-permute-done.8.refs_3_ = s16[784,768]{1,0:T(8,128)(2,1)} collective-permute-done((s16[784,768]{1,0:T(8,128)(2,1)S(1)}, s16[784,768]{1,0:T(8,128)(2,1)}, u32[]{:S(2)}, u32[]{:S(2)}) %collective-permute-start.8) | collective-permute-done | bytes 1204256 | tf_op jit(solution)/shard_map/ppermute | solution.py:21
  44.9 3.6 %shard_map.101 = (s16[784,384]{1,0:T(8,128)(2,1)S(1)}, s16[784,384]{1,0:T(8,128)(2,1)S(1)}) custom-call(s32[3]{0:T(128)S(1)} %add_add_fusion.5.refs_0_, s32[12,6]{1,0:T(8,128)S(1)} %bitcast.18, f32[1,1536,768]{2,1,0:T(8,128)} %refs_2_.13, s16[784,768]{1,0:T(8,128)(2,1)} %collective-permute-done.8.refs_3_, s16[2064,128]{1,0:T(8,128)(2,1)S(1)} %shard_map.100.refs_4_.refs_2_, ...), custom_call_target="tpu_custom_call" | custom-call | bytes 1024 | tf_op jit(solution)/shard_map/pallas_call | solution.py:63
  48.7 1.9 %collective-permute-start.13 = (s16[784,384]{1,0:T(8,128)(2,1)S(1)}, s16[784,384]{1,0:T(8,128)(2,1)S(1)}, u32[]{:S(2)}, u32[]{:S(2)}) collective-permute-start(s16[784,384]{1,0:T(8,128)(2,1)S(1)} %get-tuple-element.13.refs_2_.refs_1_), channel_id=1, source_target_pairs={{0,8},{8,0},{16,24},{24,16},{1,9},{9,1},{17,25},{25,17},{2,10},{10... | collective-permute-start | bytes 1806344 | tf_op jit(solution)/shard_map/ppermute | solution.py:21
  50.6 15.3 %shard_map.102 = (f32[128,128]{1,0:T(8,128)S(1)}, f32[128,128]{1,0:T(8,128)S(1)}, f32[128,128]{1,0:T(8,128)S(1)}) custom-call(f32[128,128]{1,0:T(8,128)S(1)} %broadcast_select_fusion.5.refs_0_, s16[784,384]{1,0:T(8,128)(2,1)S(1)} %get-tuple-element.12.refs_1_.refs_0_, s16[784,384]{1,0:T(8,128)(2,1)S(1)} %get-tuple-element.13.refs_2_.refs_1_), custom_call_target="tpu_custom_call" | custom-call | bytes 1024 | tf_op jit(solution)/shard_map/pallas_call | solution.py:63
  65.9 3.3 %shard_map.103.refs_4_.refs_0_ = s16[528,896]{1,0:T(8,128)(2,1)S(1)} custom-call(s32[3]{0:T(128)S(1)} %add_add_fusion.3.refs_0_, s32[16,8]{1,0:T(8,128)S(1)} %copy.17.refs_1_, f32[1,2048,1024]{2,1,0:T(8,128)} %refs_2_.15, s16[528,896]{1,0:T(8,128)(2,1)} %collective-permute-done.4.refs_3_, f32[128,128]{1,0:T(8,128)S(1)} %get-tuple-element.14.refs_4_.refs_10_), custom_call_target="tpu_custom_call" | custom-call | bytes 1024 | tf_op jit(solution)/shard_map/pallas_call | solution.py:63
  69.4 3.3 %shard_map.104.refs_5_.refs_0_ = s16[528,896]{1,0:T(8,128)(2,1)S(1)} custom-call(s32[3]{0:T(128)S(1)} %add_add_fusion.refs_0_, s32[16,8]{1,0:T(8,128)S(1)} %copy.17.refs_1_, f32[1,2048,1024]{2,1,0:T(8,128)} %refs_2_.15, s16[528,896]{1,0:T(8,128)(2,1)} %collective-permute-done.3.refs_3_, s16[528,896]{1,0:T(8,128)(2,1)S(1)} %shard_map.103.refs_4_.refs_0_), custom_call_target="tpu_custom_call" | custom-call | bytes 1024 | tf_op jit(solution)/shard_map/pallas_call | solution.py:63
  72.7 2.0 %collective-permute-start.10 = (s16[528,896]{1,0:T(8,128)(2,1)S(1)}, s16[528,896]{1,0:T(8,128)(2,1)S(1)}, u32[]{:S(2)}, u32[]{:S(2)}) collective-permute-start(s16[528,896]{1,0:T(8,128)(2,1)S(1)} %shard_map.104.refs_5_.refs_0_), channel_id=1, source_target_pairs={{0,16},{8,24},{16,0},{24,8},{1,17},{9,25},{17,1},{25,9},{2,18},{10... | collective-permute-start | bytes 2838536 | tf_op jit(solution)/shard_map/ppermute | solution.py:21
  76.4 1.6 %collective-permute-done.13.refs_7_.refs_3_ = s16[784,384]{1,0:T(8,128)(2,1)S(1)} collective-permute-done((s16[784,384]{1,0:T(8,128)(2,1)S(1)}, s16[784,384]{1,0:T(8,128)(2,1)S(1)}, u32[]{:S(2)}, u32[]{:S(2)}) %collective-permute-start.13) | collective-permute-done | bytes 602144 | tf_op jit(solution)/shard_map/ppermute | solution.py:21
  78.0 2.8 %shard_map.105 = (f32[2048,128]{1,0:T(8,128)S(1)}, bf16[2048,128]{1,0:T(8,128)(2,1)S(1)}) custom-call(s32[4]{0:T(128)S(1)} %pad_add_fusion.2.refs_0_, bf16[2048,128]{1,0:T(8,128)(2,1)S(1)} %fusion.refs_1_, s16[2064,128]{1,0:T(8,128)(2,1)S(1)} %shard_map.100.refs_4_.refs_2_, s16[2064,128]{1,0:T(8,128)(2,1)S(1)} %collective-permute-done.14.refs_3_, ...), custom_call_target="tpu_custom_call" | custom-call | bytes 1024 | tf_op jit(solution)/shard_map/pallas_call | solution.py:63
  80.8 4.4 %collective-permute-start.17 = (bf16[2048,128]{1,0:T(8,128)(2,1)S(1)}, bf16[2048,128]{1,0:T(8,128)(2,1)S(1)}, u32[]{:S(2)}, u32[]{:S(2)}) collective-permute-start(bf16[2048,128]{1,0:T(8,128)(2,1)S(1)} %get-tuple-element.17), channel_id=1, source_target_pairs={{0,2},{4,6},{8,10},{12,14},{16,18},{20,22},{24,26},{28,30}} | collective-permute-start | bytes 1572872 | tf_op jit(solution)/shard_map/ppermute | solution.py:30
  86.3 6.3 %collective-permute-done.11.refs_1_ = s16[528,896]{1,0:T(8,128)(2,1)S(1)} collective-permute-done((s16[528,896]{1,0:T(8,128)(2,1)S(1)}, s16[528,896]{1,0:T(8,128)(2,1)S(1)}, u32[]{:S(2)}, u32[]{:S(2)}) %collective-permute-start.11) | collective-permute-done | bytes 946208 | tf_op jit(solution)/shard_map/ppermute | solution.py:21
  93.5 1.6 %collective-permute-start.16 = (s16[528,896]{1,0:T(8,128)(2,1)S(1)}, s16[528,896]{1,0:T(8,128)(2,1)}, u32[]{:S(2)}, u32[]{:S(2)}) collective-permute-start(s16[528,896]{1,0:T(8,128)(2,1)S(1)} %shard_map.107.refs_2_.refs_3_.refs_4_), channel_id=1, source_target_pairs={{0,16},{8,24},{16,0},{24,8},{1,17},{9,25},{17,1},{25,9},{2,18},{10... | collective-permute-start | bytes 2838536 | tf_op jit(solution)/shard_map/ppermute | solution.py:21
  95.1 1.5 %collective-permute-done.10.refs_1_ = s16[528,896]{1,0:T(8,128)(2,1)S(1)} collective-permute-done((s16[528,896]{1,0:T(8,128)(2,1)S(1)}, s16[528,896]{1,0:T(8,128)(2,1)S(1)}, u32[]{:S(2)}, u32[]{:S(2)}) %collective-permute-start.10) | collective-permute-done | bytes 946208 | tf_op jit(solution)/shard_map/ppermute | solution.py:21
  96.7 1.8 %shard_map.108.refs_2_ = s16[528,896]{1,0:T(8,128)(2,1)} custom-call(s16[528,896]{1,0:T(8,128)(2,1)S(1)} %shard_map.104.refs_5_.refs_0_, s16[528,896]{1,0:T(8,128)(2,1)S(1)} %collective-permute-done.10.refs_1_, s16[528,896]{1,0:T(8,128)(2,1)S(1)} %shard_map.107.refs_2_.refs_3_.refs_4_), custom_call_target="tpu_custom_call" | custom-call | bytes 1024 | tf_op jit(solution)/shard_map/pallas_call | solution.py:63
  100.1 5.3 %collective-permute-start.18 = (bf16[2048,128]{1,0:T(8,128)(2,1)}, bf16[2048,128]{1,0:T(8,128)(2,1)}, u32[]{:S(2)}, u32[]{:S(2)}) collective-permute-start(bf16[2048,128]{1,0:T(8,128)(2,1)} %broadcast_select_fusion), channel_id=1, source_target_pairs={{0,1},{2,3},{4,5},{6,7},{8,9},{10,11},{12,13},{14,15},{16,17},{18,... | collective-permute-start | bytes 1572872 | tf_op jit(solution)/shard_map/ppermute | solution.py:30
  105.3 1.5 %collective-permute-start.20 = (s16[784,768]{1,0:T(8,128)(2,1)S(1)}, s16[784,768]{1,0:T(8,128)(2,1)}, u32[]{:S(2)}, u32[]{:S(2)}) collective-permute-start(s16[784,768]{1,0:T(8,128)(2,1)S(1)} %shard_map.106.refs_2_.refs_1_), channel_id=1, source_target_pairs={{0,16},{8,24},{16,0},{24,8},{1,17},{9,25},{17,1},{25,9},{2,18},{10... | collective-permute-start | bytes 3612680 | tf_op jit(solution)/shard_map/ppermute | solution.py:21
  107.0 1.7 %shard_map.109.refs_3_.refs_2_ = f32[1,1536,768]{2,1,0:T(8,128)} custom-call(s32[1]{0:T(128)} %bitcast.1.refs_0_, s16[784,768]{1,0:T(8,128)(2,1)S(1)} %shard_map.106.refs_2_.refs_1_, s16[528,896]{1,0:T(8,128)(2,1)} %shard_map.108.refs_2_), custom_call_target="tpu_custom_call" | custom-call | bytes 1024 | tf_op jit(solution)/shard_map/pallas_call | solution.py:63
  111.5 11.1 %collective-permute-done.15.refs_9_.refs_3_ = s16[528,896]{1,0:T(8,128)(2,1)} collective-permute-done((s16[528,896]{1,0:T(8,128)(2,1)}, s16[528,896]{1,0:T(8,128)(2,1)}, u32[]{:S(2)}, u32[]{:S(2)}) %collective-permute-start.15) | collective-permute-done | bytes 946208 | tf_op jit(solution)/shard_map/ppermute | solution.py:21
  122.7 1.9 %shard_map.111 = (f32[128,1024]{1,0:T(8,128)S(1)}, bf16[128,1024]{1,0:T(8,128)(2,1)S(1)}) custom-call(s32[4]{0:T(128)S(1)} %pad_add_fusion.2.refs_0_, bf16[2048,128]{1,0:T(8,128)(2,1)S(1)} %copy-done.3, f32[2048,128]{1,0:T(8,128)S(1)} %get-tuple-element.16.refs_4_.refs_2_.refs_6_, s16[528,896]{1,0:T(8,128)(2,1)S(1)} %shard_map.107.refs_2_.refs_3_.refs_4_, ...), custom_call_target="tpu_custom_call" | custom-call | bytes 1024 | tf_op jit(solution)/shard_map/pallas_call | solution.py:63
  127.1 13.9 %shard_map.112.refs_3_.refs_4_ = f32[2048,1024]{1,0:T(8,128)} custom-call(s32[4]{0:T(128)S(1)} %pad_add_fusion.2.refs_0_, bf16[2048,128]{1,0:T(8,128)(2,1)S(1)} %copy-done.3, s16[528,896]{1,0:T(8,128)(2,1)} %shard_map.108.refs_2_, s16[528,896]{1,0:T(8,128)(2,1)} %collective-permute-done.15.refs_9_.refs_3_, ...), custom_call_target="tpu_custom_call" | custom-call | bytes 1024 | tf_op jit(solution)/shard_map/pallas_call | solution.py:63
  140.9 2.9 %shard_map.113 = f32[1,1536,768]{2,1,0:T(8,128)} custom-call(s32[1]{0:T(128)} %bitcast.9.refs_0_, s16[784,768]{1,0:T(8,128)(2,1)} %collective-permute-done.20.refs_1_, f32[1,1536,768]{2,1,0:T(8,128)} %shard_map.109.refs_3_.refs_2_, f32[2048,1024]{1,0:T(8,128)} %shard_map.112.refs_3_.refs_4_), custom_call_target="tpu_custom_call", output_to_operand_aliasing={{}: (2, {})} | custom-call | bytes 1024 | tf_op jit(solution)/shard_map/pallas_call | solution.py:63
  143.9 2.4 %shard_map.114 = f32[1,1024,512]{2,1,0:T(8,128)} custom-call(s32[3]{0:T(128)S(1)} %fusion.3.refs_0_, s32[8,4]{1,0:T(8,128)S(1)} %copy.18.refs_1_, f32[1,1024,512]{2,1,0:T(8,128)S(1)} %copy-done.1, s16[1040,512]{1,0:T(8,128)(2,1)S(1)} %collective-permute-done.21.refs_3_, f32[2048,1024]{1,0:T(8,128)} %shard_map.112.refs_3_.refs_4_), custom_call_target="tpu_custom_call" | custom-call | bytes 1024 | tf_op jit(solution)/shard_map/pallas_call | solution.py:63
  (77 shorter events, 19.3 us)
Async XLA Ops:
  1.3 5.7 %copy-start.9 = (s32[1,16,8]{1,2,0:T(8,128)S(1)}, s32[1,16,8]{1,2,0:T(8,128)}, u32[]{:S(2)}) copy-start(s32[1,16,8]{1,2,0:T(8,128)} %param.10) | copy-start | bytes 1540
  2.5 9.7 %collective-permute-start.2 = (f32[128,128]{1,0:T(8,128)S(1)}, f32[128,128]{1,0:T(8,128)S(1)}, u32[]{:S(2)}, u32[]{:S(2)}) collective-permute-start(f32[128,128]{1,0:T(8,128)S(1)} %shard_map.94.refs_3_.refs_0_), channel_id=1, source_target_pairs={{0,24},{8,16},{16,8},{24,0},{1,25},{9,17},{17,9},{25,1},{2,26},{10... | collective-permute-start | bytes 196616 | tf_op jit(solution)/shard_map/ppermute | solution.py:467
  6.4 5.7 %collective-permute-start.1 = (f32[128,128]{1,0:T(8,128)S(1)}, f32[128,128]{1,0:T(8,128)S(1)}, u32[]{:S(2)}, u32[]{:S(2)}) collective-permute-start(f32[128,128]{1,0:T(8,128)S(1)} %shard_map.94.refs_3_.refs_0_), channel_id=1, source_target_pairs={{0,16},{8,24},{16,0},{24,8},{1,17},{9,25},{17,1},{25,9},{2,18},{10... | collective-permute-start | bytes 196616 | tf_op jit(solution)/shard_map/ppermute | solution.py:467
  6.9 5.2 %collective-permute-start = (f32[128,128]{1,0:T(8,128)S(1)}, f32[128,128]{1,0:T(8,128)S(1)}, u32[]{:S(2)}, u32[]{:S(2)}) collective-permute-start(f32[128,128]{1,0:T(8,128)S(1)} %shard_map.94.refs_3_.refs_0_), channel_id=1, source_target_pairs={{0,8},{8,0},{16,24},{24,16},{1,9},{9,1},{17,25},{25,17},{2,10},{10... | collective-permute-start | bytes 196616 | tf_op jit(solution)/shard_map/ppermute | solution.py:467
  7.2 4.8 %copy-start.10 = (s32[1,12,6]{1,0,2:T(1,128)S(1)}, s32[1,12,6]{1,0,2:T(1,128)}, u32[]{:S(2)}) copy-start(s32[1,12,6]{1,0,2:T(1,128)} %param.11) | copy-start | bytes 868
  9.3 25.5 %collective-permute-start.9 = (s16[2064,128]{1,0:T(8,128)(2,1)S(1)}, s16[2064,128]{1,0:T(8,128)(2,1)S(1)}, u32[]{:S(2)}, u32[]{:S(2)}) collective-permute-start(s16[2064,128]{1,0:T(8,128)(2,1)S(1)} %shard_map.95.refs_3_.refs_0_), channel_id=1, source_target_pairs={{0,8},{8,0},{16,24},{24,16},{1,9},{9,1},{17,25},{25,17},{2,10},{10... | collective-permute-start | bytes 1585160 | tf_op jit(solution)/shard_map/ppermute | solution.py:21
  12.1 4.9 %copy-start.6 = (s32[2048]{0:T(1024)S(1)}, s32[2048]{0:T(1024)}, u32[]{:S(2)}) copy-start(s32[2048]{0:T(1024)} %param.13) | copy-start | bytes 24580
  15.3 29.6 %collective-permute-start.8 = (s16[784,768]{1,0:T(8,128)(2,1)S(1)}, s16[784,768]{1,0:T(8,128)(2,1)}, u32[]{:S(2)}, u32[]{:S(2)}) collective-permute-start(s16[784,768]{1,0:T(8,128)(2,1)S(1)} %shard_map.96.refs_3_), channel_id=1, source_target_pairs={{0,16},{8,24},{16,0},{24,8},{1,17},{9,25},{17,1},{25,9},{2,18},{10... | collective-permute-start | bytes 3612680 | tf_op jit(solution)/shard_map/ppermute | solution.py:21
  17.6 4.8 %copy-start.7 = (s32[3]{0:T(128)S(1)}, s32[3]{0:T(128)}, u32[]{:S(2)}) copy-start(s32[3]{0:T(128)} %add_add_fusion.4.refs_0_) | copy-start | bytes 40
  20.6 48.8 %collective-permute-start.3 = (s16[528,896]{1,0:T(8,128)(2,1)S(1)}, s16[528,896]{1,0:T(8,128)(2,1)}, u32[]{:S(2)}, u32[]{:S(2)}) collective-permute-start(s16[528,896]{1,0:T(8,128)(2,1)S(1)} %shard_map.97.refs_4_), channel_id=1, source_target_pairs={{0,8},{8,0},{16,24},{24,16},{1,9},{9,1},{17,25},{25,17},{2,10},{10... | collective-permute-start | bytes 2838536 | tf_op jit(solution)/shard_map/ppermute | solution.py:21
  21.2 5.3 %collective-permute-start.5 = (f32[128,128]{1,0:T(8,128)S(1)}, f32[128,128]{1,0:T(8,128)S(1)}, u32[]{:S(2)}, u32[]{:S(2)}) collective-permute-start(f32[128,128]{1,0:T(8,128)S(1)} %shard_map.98.refs_3_), channel_id=1, source_target_pairs={{0,4},{1,5},{2,6},{3,7},{8,12},{9,13},{10,14},{11,15},{16,20},{17,... | collective-permute-start | bytes 196616 | tf_op jit(solution)/shard_map/ppermute | solution.py:30
  26.3 39.5 %collective-permute-start.4 = (s16[528,896]{1,0:T(8,128)(2,1)}, s16[528,896]{1,0:T(8,128)(2,1)}, u32[]{:S(2)}, u32[]{:S(2)}) collective-permute-start(s16[528,896]{1,0:T(8,128)(2,1)} %shard_map.99.refs_2_), channel_id=1, source_target_pairs={{0,16},{8,24},{16,0},{24,8},{1,17},{9,25},{17,1},{25,9},{2,18},{10... | collective-permute-start | bytes 2838536 | tf_op jit(solution)/shard_map/ppermute | solution.py:21
  26.5 6.9 %collective-permute-start.6 = (f32[128,128]{1,0:T(8,128)S(1)}, f32[128,128]{1,0:T(8,128)S(1)}, u32[]{:S(2)}, u32[]{:S(2)}) collective-permute-start(f32[128,128]{1,0:T(8,128)S(1)} %broadcast_select_fusion.3.refs_3_), channel_id=1, source_target_pairs={{0,2},{4,6},{8,10},{12,14},{16,18},{20,22},{24,26},{28,30}} | collective-permute-start | bytes 196616 | tf_op jit(solution)/shard_map/ppermute | solution.py:30
  33.4 15.2 %collective-permute-start.7 = (f32[128,128]{1,0:T(8,128)S(1)}, f32[128,128]{1,0:T(8,128)S(1)}, u32[]{:S(2)}, u32[]{:S(2)}) collective-permute-start(f32[128,128]{1,0:T(8,128)S(1)} %broadcast_select_fusion.4.refs_5_), channel_id=1, source_target_pairs={{0,1},{2,3},{4,5},{6,7},{8,9},{10,11},{12,13},{14,15},{16,17},{18,... | collective-permute-start | bytes 196616 | tf_op jit(solution)/shard_map/ppermute | solution.py:30
  35.3 41.1 %collective-permute-start.14 = (s16[2064,128]{1,0:T(8,128)(2,1)S(1)}, s16[2064,128]{1,0:T(8,128)(2,1)S(1)}, u32[]{:S(2)}, u32[]{:S(2)}) collective-permute-start(s16[2064,128]{1,0:T(8,128)(2,1)S(1)} %shard_map.100.refs_4_.refs_2_), channel_id=1, source_target_pairs={{0,16},{8,24},{16,0},{24,8},{1,17},{9,25},{17,1},{25,9},{2,18},{10... | collective-permute-start | bytes 1585160 | tf_op jit(solution)/shard_map/ppermute | solution.py:21
  48.5 27.9 %collective-permute-start.12 = (s16[784,384]{1,0:T(8,128)(2,1)S(1)}, s16[784,384]{1,0:T(8,128)(2,1)S(1)}, u32[]{:S(2)}, u32[]{:S(2)}) collective-permute-start(s16[784,384]{1,0:T(8,128)(2,1)S(1)} %get-tuple-element.12.refs_1_.refs_0_), channel_id=1, source_target_pairs={{0,8},{8,0},{16,24},{24,16},{1,9},{9,1},{17,25},{25,17},{2,10},{10... | collective-permute-start | bytes 1806344 | tf_op jit(solution)/shard_map/ppermute | solution.py:21
  48.7 29.3 %collective-permute-start.13 = (s16[784,384]{1,0:T(8,128)(2,1)S(1)}, s16[784,384]{1,0:T(8,128)(2,1)S(1)}, u32[]{:S(2)}, u32[]{:S(2)}) collective-permute-start(s16[784,384]{1,0:T(8,128)(2,1)S(1)} %get-tuple-element.13.refs_2_.refs_1_), channel_id=1, source_target_pairs={{0,8},{8,0},{16,24},{24,16},{1,9},{9,1},{17,25},{25,17},{2,10},{10... | collective-permute-start | bytes 1806344 | tf_op jit(solution)/shard_map/ppermute | solution.py:21
  69.2 5.5 %copy-start.8 = (s32[2048]{0:T(1024)S(1)}, s32[2048]{0:T(1024)}, u32[]{:S(2)}) copy-start(s32[2048]{0:T(1024)} %add_select_fusion) | copy-start | bytes 24580
  69.2 23.5 %collective-permute-start.11 = (s16[528,896]{1,0:T(8,128)(2,1)S(1)}, s16[528,896]{1,0:T(8,128)(2,1)S(1)}, u32[]{:S(2)}, u32[]{:S(2)}) collective-permute-start(s16[528,896]{1,0:T(8,128)(2,1)S(1)} %shard_map.103.refs_4_.refs_0_), channel_id=1, source_target_pairs={{0,8},{8,0},{16,24},{24,16},{1,9},{9,1},{17,25},{25,17},{2,10},{10... | collective-permute-start | bytes 2838536 | tf_op jit(solution)/shard_map/ppermute | solution.py:21
  72.7 24.0 %collective-permute-start.10 = (s16[528,896]{1,0:T(8,128)(2,1)S(1)}, s16[528,896]{1,0:T(8,128)(2,1)S(1)}, u32[]{:S(2)}, u32[]{:S(2)}) collective-permute-start(s16[528,896]{1,0:T(8,128)(2,1)S(1)} %shard_map.104.refs_5_.refs_0_), channel_id=1, source_target_pairs={{0,16},{8,24},{16,0},{24,8},{1,17},{9,25},{17,1},{25,9},{2,18},{10... | collective-permute-start | bytes 2838536 | tf_op jit(solution)/shard_map/ppermute | solution.py:21
  75.0 10.3 %copy-start.2 = (bf16[2048,128]{1,0:T(8,128)(2,1)}, bf16[2048,128]{1,0:T(8,128)(2,1)S(1)}, u32[]{:S(2)}) copy-start(bf16[2048,128]{1,0:T(8,128)(2,1)S(1)} %fusion.refs_1_) | copy-start | bytes 1572868
  80.8 41.9 %copy-start = (f32[2048,128]{1,0:T(8,128)}, f32[2048,128]{1,0:T(8,128)S(1)}, u32[]{:S(2)}) copy-start(f32[2048,128]{1,0:T(8,128)S(1)} %get-tuple-element.16.refs_4_.refs_2_.refs_6_) | copy-start | bytes 3145732
  80.8 18.4 %collective-permute-start.17 = (bf16[2048,128]{1,0:T(8,128)(2,1)S(1)}, bf16[2048,128]{1,0:T(8,128)(2,1)S(1)}, u32[]{:S(2)}, u32[]{:S(2)}) collective-permute-start(bf16[2048,128]{1,0:T(8,128)(2,1)S(1)} %get-tuple-element.17), channel_id=1, source_target_pairs={{0,2},{4,6},{8,10},{12,14},{16,18},{20,22},{24,26},{28,30}} | collective-permute-start | bytes 1572872 | tf_op jit(solution)/shard_map/ppermute | solution.py:30
  93.5 13.3 %copy-start.11 = (s32[1,8,4]{1,2,0:T(4,128)S(1)}, s32[1,8,4]{1,2,0:T(4,128)}, u32[]{:S(2)}) copy-start(s32[1,8,4]{1,2,0:T(4,128)} %param.12) | copy-start | bytes 388
  93.5 29.1 %collective-permute-start.16 = (s16[528,896]{1,0:T(8,128)(2,1)S(1)}, s16[528,896]{1,0:T(8,128)(2,1)}, u32[]{:S(2)}, u32[]{:S(2)}) collective-permute-start(s16[528,896]{1,0:T(8,128)(2,1)S(1)} %shard_map.107.refs_2_.refs_3_.refs_4_), channel_id=1, source_target_pairs={{0,16},{8,24},{16,0},{24,8},{1,17},{9,25},{17,1},{25,9},{2,18},{10... | collective-permute-start | bytes 2838536 | tf_op jit(solution)/shard_map/ppermute | solution.py:21
  98.4 24.2 %collective-permute-start.15 = (s16[528,896]{1,0:T(8,128)(2,1)}, s16[528,896]{1,0:T(8,128)(2,1)}, u32[]{:S(2)}, u32[]{:S(2)}) collective-permute-start(s16[528,896]{1,0:T(8,128)(2,1)} %shard_map.108.refs_2_), channel_id=1, source_target_pairs={{0,8},{8,0},{16,24},{24,16},{1,9},{9,1},{17,25},{25,17},{2,10},{10... | collective-permute-start | bytes 2838536 | tf_op jit(solution)/shard_map/ppermute | solution.py:21
  100.1 25.8 %collective-permute-start.18 = (bf16[2048,128]{1,0:T(8,128)(2,1)}, bf16[2048,128]{1,0:T(8,128)(2,1)}, u32[]{:S(2)}, u32[]{:S(2)}) collective-permute-start(bf16[2048,128]{1,0:T(8,128)(2,1)} %broadcast_select_fusion), channel_id=1, source_target_pairs={{0,1},{2,3},{4,5},{6,7},{8,9},{10,11},{12,13},{14,15},{16,17},{18,... | collective-permute-start | bytes 1572872 | tf_op jit(solution)/shard_map/ppermute | solution.py:30
  105.3 35.6 %collective-permute-start.20 = (s16[784,768]{1,0:T(8,128)(2,1)S(1)}, s16[784,768]{1,0:T(8,128)(2,1)}, u32[]{:S(2)}, u32[]{:S(2)}) collective-permute-start(s16[784,768]{1,0:T(8,128)(2,1)S(1)} %shard_map.106.refs_2_.refs_1_), channel_id=1, source_target_pairs={{0,16},{8,24},{16,0},{24,8},{1,17},{9,25},{17,1},{25,9},{2,18},{10... | collective-permute-start | bytes 3612680 | tf_op jit(solution)/shard_map/ppermute | solution.py:21
  109.5 13.2 %copy-start.3 = (bf16[2048,128]{1,0:T(8,128)(2,1)S(1)}, bf16[2048,128]{1,0:T(8,128)(2,1)}, u32[]{:S(2)}) copy-start(bf16[2048,128]{1,0:T(8,128)(2,1)} %copy-done.2) | copy-start | bytes 1572868
  110.8 11.9 %copy-start.4 = (s16[1040,512]{1,0:T(8,128)(2,1)}, s16[1040,512]{1,0:T(8,128)(2,1)S(1)}, u32[]{:S(2)}) copy-start(s16[1040,512]{1,0:T(8,128)(2,1)S(1)} %shard_map.110.refs_8_) | copy-start | bytes 3194884
  110.8 33.1 %collective-permute-start.21 = (s16[1040,512]{1,0:T(8,128)(2,1)S(1)}, s16[1040,512]{1,0:T(8,128)(2,1)S(1)}, u32[]{:S(2)}, u32[]{:S(2)}) collective-permute-start(s16[1040,512]{1,0:T(8,128)(2,1)S(1)} %shard_map.110.refs_8_), channel_id=1, source_target_pairs={{0,8},{8,0},{16,24},{24,16},{1,9},{9,1},{17,25},{25,17},{2,10},{10... | collective-permute-start | bytes 3194888 | tf_op jit(solution)/shard_map/ppermute | solution.py:21
  124.6 2.4 %collective-permute-start.19 = (bf16[128,1024]{1,0:T(8,128)(2,1)S(1)}, bf16[128,1024]{1,0:T(8,128)(2,1)S(1)}, u32[]{:S(2)}, u32[]{:S(2)}) collective-permute-start(bf16[128,1024]{1,0:T(8,128)(2,1)S(1)} %get-tuple-element.19), channel_id=1, source_target_pairs={{0,4},{1,5},{2,6},{3,7},{8,12},{9,13},{10,14},{11,15},{16,20},{17,... | collective-permute-start | bytes 786440 | tf_op jit(solution)/shard_map/ppermute | solution.py:30
  (2 other events, 3.1 us)

commit v8 on v7

--- a/solution.py
+++ b/solution.py
@@ -392,43 +392,48 @@
     part_blocks = rows // BLK
 
     def kernel(flag_ref, order_ref, own_a, got_a, own_b, got_b, slab_ref, low_ref, up_low_ref, up_ref, packed_ref, out_ref):
-        i = pl.program_id(0)
-        part = i // part_blocks
-        row = pl.multiple_of((i % part_blocks) * BLK, BLK)
-        first_row = (flag_ref[2] == 0) & (i == 0)
-        first_col = flag_ref[3] == 0
-        rest_cols = pl.ds(0, rest)
-
-        @pl.when(jnp.logical_not(first_row))
-        def _():
-            low = low_ref[...]
-
-            def write(code_ref):
-                scale = scales(code_ref, rows, rest_cols)
-                value = permuted_codes(order_ref[...], code_ref[pl.ds(row, BLK), :], scale)
-                out_ref[:, PANEL:] = value - low_dot(low, up_low_ref[:, PANEL:])
-
-            owned_b = part == flag_ref[1]
-            owned_a = part == 2 + flag_ref[0]
-            pl.when(owned_b)(lambda: write(own_b))
-            pl.when((part < 2) & jnp.logical_not(owned_b))(lambda: write(got_b))
-            pl.when(owned_a)(lambda: write(own_a))
-            pl.when((part >= 2) & jnp.logical_not(owned_a))(lambda: write(got_a))
-            product = low_dot(low, up_low_ref[:, :PANEL])
-            out_ref[:, :PANEL] = jnp.where(first_col, slab_ref[...], slab_ref[...] - product)
-
-        @pl.when(first_row)
-        def _():
-            out_ref[:, PANEL:] = up_ref[:, PANEL:]
-            out_ref[:, :PANEL] = jnp.where(first_col, packed_ref[...], up_ref[:, :PANEL])
-
-    square = pl.BlockSpec((BLK, BLK), lambda i: (i, 0))
+        def block_rows(sub):
+            i = 2 * pl.program_id(0) + sub
+            here = pl.ds(sub * BLK, BLK)
+            part = i // part_blocks
+            row = pl.multiple_of((i % part_blocks) * BLK, BLK)
+            first_row = (flag_ref[2] == 0) & (i == 0)
+            first_col = flag_ref[3] == 0
+            rest_cols = pl.ds(0, rest)
+
+            @pl.when(jnp.logical_not(first_row))
+            def _():
+                low = low_ref[here, :]
+
+                def write(code_ref):
+                    scale = scales(code_ref, rows, rest_cols)
+                    value = permuted_codes(order_ref[here, :], code_ref[pl.ds(row, BLK), :], scale)
+                    out_ref[here, PANEL:] = value - low_dot(low, up_low_ref[:, PANEL:])
+
+                owned_b = part == flag_ref[1]
+                owned_a = part == 2 + flag_ref[0]
+                pl.when(owned_b)(lambda: write(own_b))
+                pl.when((part < 2) & jnp.logical_not(owned_b))(lambda: write(got_b))
+                pl.when(owned_a)(lambda: write(own_a))
+                pl.when((part >= 2) & jnp.logical_not(owned_a))(lambda: write(got_a))
+                product = low_dot(low, up_low_ref[:, :PANEL])
+                out_ref[here, :PANEL] = jnp.where(first_col, slab_ref[here, :], slab_ref[here, :] - product)
+
+            @pl.when(first_row)
+            def _():
+                out_ref[here, PANEL:] = up_ref[:, PANEL:]
+                out_ref[here, :PANEL] = jnp.where(first_col, packed_ref[...], up_ref[:, :PANEL])
+
+        for sub in range(2):
+            block_rows(sub)
+
+    square = pl.BlockSpec((2 * BLK, BLK), lambda i: (i, 0))
     return run(
         kernel, after, [flags, order, *codes, slab, lower_low, upper_low, upper, packed],
         [SMEM_SPEC, square] + [VMEM_SPEC] * 4 + [square, square] + [VMEM_SPEC] * 3,
-        pl.BlockSpec((BLK, width), lambda i: (i, 0)),
+        pl.BlockSpec((2 * BLK, width), lambda i: (i, 0)),
         jax.ShapeDtypeStruct((total_rows, width), jnp.float32),
-        total_rows * width * 6, total_rows * width * BLK * 6, grid=(total_rows // BLK,),
+        total_rows * width * 6, total_rows * width * BLK * 6, grid=(total_rows // (2 * BLK),),
     )
 
 

time: 148 us -> 147 us (level)
  Pallas kernels: 69.5 us -> 66.5 us
  waiting for transfers between devices: 31.9 us -> 34.6 us
    pallas_call x21, Pallas kernels: 69.5 us -> 66.5 us  [run(): pl.pallas_call(body, grid_spec=pltpu.PrefetchScalarGridSpec(num_scalar_pr...]
    ppermute x13, waiting for transfers between devices: 30 us -> 32.6 us  [swapped(): lax.ppermute(piece, 'layer', pairs)]
  transfers between devices with their start and end apart: 22 -> 22, of which waited for: 7 -> 8; matrix products, arithmetic and copies ran while one was open for 3% -> 3% of each run, Pallas kernels for 45% -> 43%
where the time goes in v8:
time: 147 us; the launch traced here: 146 us
  Pallas kernels  66.5 us (45%)
  starting transfers between devices  37.8 us (26%)
  waiting for transfers between devices  34.6 us (24%)
  other arithmetic  4.25 us (3%)
  local copies, waits for them, and re-layouts  1.77 us (1%)
    pallas_call x21, Pallas kernels, run(): pl.pallas_call(body, grid_spec=pltpu.PrefetchScalarGridSpec(num_scalar_pr...  66.5 us
    ppermute x13, waiting for transfers between devices, swapped(): lax.ppermute(piece, 'layer', pairs)  32.6 us
    ppermute x6, starting transfers between devices, broadcast_stages(): lax.ppermute(value, axis, [(i, i + span) for i in range(0, count, 2 * spa...  18.4 us
    ppermute x13, starting transfers between devices, swapped(): lax.ppermute(piece, 'layer', pairs)  14.7 us
    ppermute x3, starting transfers between devices, on_device(): lax.ppermute(corner, 'layer', [(i, i ^ apart) for i in range(count)])  4.6 us
  transfers between devices with their start and end apart: 22, of which 8 were waited for; matrix products, arithmetic and copies ran while one was open for 3% of the time, Pallas kernels for 43%

profile of v8, /device:TPU:0, one launch (start us, length us, event | category | flops | bytes accessed | tf_op | source)
XLA Modules:
  0.0 145.8 jit_solution(11914543280386844434)
XLA Ops:
  2.5 4.0 %collective-permute-start.2 = (f32[128,128]{1,0:T(8,128)S(1)}, f32[128,128]{1,0:T(8,128)S(1)}, u32[]{:S(2)}, u32[]{:S(2)}) collective-permute-start(f32[128,128]{1,0:T(8,128)S(1)} %shard_map.94.refs_3_.refs_0_), channel_id=1, source_target_pairs={{0,24},{8,16},{16,8},{24,0},{1,25},{9,17},{17,9},{25,1},{2,26},{10... | collective-permute-start | bytes 196616 | tf_op jit(solution)/shard_map/ppermute | solution.py:472
  7.2 2.1 %shard_map.95.refs_3_.refs_0_ = s16[2064,128]{1,0:T(8,128)(2,1)S(1)} custom-call(s32[3]{0:T(128)S(1)} %fusion.2.refs_0_, s32[16,8]{1,0:T(8,128)S(1)} %copy.17.refs_1_, f32[1,2048,1024]{2,1,0:T(8,128)} %refs_2_.15, f32[128,128]{1,0:T(8,128)S(1)} %shard_map.94.refs_3_.refs_0_), custom_call_target="tpu_custom_call" | custom-call | bytes 1024 | tf_op jit(solution)/shard_map/pallas_call | solution.py:63
  9.3 2.0 %collective-permute-start.9 = (s16[2064,128]{1,0:T(8,128)(2,1)S(1)}, s16[2064,128]{1,0:T(8,128)(2,1)S(1)}, u32[]{:S(2)}, u32[]{:S(2)}) collective-permute-start(s16[2064,128]{1,0:T(8,128)(2,1)S(1)} %shard_map.95.refs_3_.refs_0_), channel_id=1, source_target_pairs={{0,8},{8,0},{16,24},{24,16},{1,9},{9,1},{17,25},{25,17},{2,10},{10... | collective-permute-start | bytes 1585160 | tf_op jit(solution)/shard_map/ppermute | solution.py:21
  12.2 3.1 %shard_map.96.refs_3_ = s16[784,768]{1,0:T(8,128)(2,1)S(1)} custom-call(s32[3]{0:T(128)S(1)} %add_add_fusion.2.refs_0_, s32[12,6]{1,0:T(8,128)S(1)} %bitcast.17, f32[1,1536,768]{2,1,0:T(8,128)} %refs_2_.13, s16[2064,128]{1,0:T(8,128)(2,1)S(1)} %shard_map.95.refs_3_.refs_0_, f32[128,128]{1,0:T(8,128)S(1)} %collective-permute-done.refs_4_.refs_1_, ...), custom_call_target="tpu_custom_call" | custom-call | bytes 1024 | tf_op jit(solution)/shard_map/pallas_call | solution.py:63
  15.3 1.6 %collective-permute-start.8 = (s16[784,768]{1,0:T(8,128)(2,1)S(1)}, s16[784,768]{1,0:T(8,128)(2,1)}, u32[]{:S(2)}, u32[]{:S(2)}) collective-permute-start(s16[784,768]{1,0:T(8,128)(2,1)S(1)} %shard_map.96.refs_3_), channel_id=1, source_target_pairs={{0,16},{8,24},{16,0},{24,8},{1,17},{9,25},{17,1},{25,9},{2,18},{10... | collective-permute-start | bytes 3612680 | tf_op jit(solution)/shard_map/ppermute | solution.py:21
  17.6 2.9 %shard_map.97.refs_4_ = s16[528,896]{1,0:T(8,128)(2,1)S(1)} custom-call(s32[3]{0:T(128)S(1)} %add_add_fusion.1.refs_0_, s32[16,8]{1,0:T(8,128)S(1)} %copy.17.refs_1_, f32[1,2048,1024]{2,1,0:T(8,128)} %refs_2_.15, s16[784,768]{1,0:T(8,128)(2,1)S(1)} %shard_map.96.refs_3_), custom_call_target="tpu_custom_call" | custom-call | bytes 1024 | tf_op jit(solution)/shard_map/pallas_call | solution.py:63
  22.5 3.9 %shard_map.99.refs_2_ = s16[528,896]{1,0:T(8,128)(2,1)} custom-call(s32[3]{0:T(128)S(1)} %copy-done.7, s32[16,8]{1,0:T(8,128)S(1)} %copy.17.refs_1_, f32[1,2048,1024]{2,1,0:T(8,128)} %refs_2_.15, f32[128,128]{1,0:T(8,128)S(1)} %shard_map.98.refs_3_), custom_call_target="tpu_custom_call" | custom-call | bytes 1024 | tf_op jit(solution)/shard_map/pallas_call | solution.py:63
  26.5 4.9 %collective-permute-start.6 = (f32[128,128]{1,0:T(8,128)S(1)}, f32[128,128]{1,0:T(8,128)S(1)}, u32[]{:S(2)}, u32[]{:S(2)}) collective-permute-start(f32[128,128]{1,0:T(8,128)S(1)} %broadcast_select_fusion.3.refs_3_), channel_id=1, source_target_pairs={{0,2},{4,6},{8,10},{12,14},{16,18},{20,22},{24,26},{28,30}} | collective-permute-start | bytes 196616 | tf_op jit(solution)/shard_map/ppermute | solution.py:30
  31.5 1.9 %collective-permute-done.6 = f32[128,128]{1,0:T(8,128)S(1)} collective-permute-done((f32[128,128]{1,0:T(8,128)S(1)}, f32[128,128]{1,0:T(8,128)S(1)}, u32[]{:S(2)}, u32[]{:S(2)}) %collective-permute-start.6) | collective-permute-done | bytes 65568 | tf_op jit(solution)/shard_map/ppermute | solution.py:30
  35.3 1.6 %collective-permute-start.14 = (s16[2064,128]{1,0:T(8,128)(2,1)S(1)}, s16[2064,128]{1,0:T(8,128)(2,1)S(1)}, u32[]{:S(2)}, u32[]{:S(2)}) collective-permute-start(s16[2064,128]{1,0:T(8,128)(2,1)S(1)} %shard_map.100.refs_4_.refs_2_), channel_id=1, source_target_pairs={{0,16},{8,24},{16,0},{24,8},{1,17},{9,25},{17,1},{25,9},{2,18},{10... | collective-permute-start | bytes 1585160 | tf_op jit(solution)/shard_map/ppermute | solution.py:21
  36.9 8.0 %collective-permute-done.8.refs_3_ = s16[784,768]{1,0:T(8,128)(2,1)} collective-permute-done((s16[784,768]{1,0:T(8,128)(2,1)S(1)}, s16[784,768]{1,0:T(8,128)(2,1)}, u32[]{:S(2)}, u32[]{:S(2)}) %collective-permute-start.8) | collective-permute-done | bytes 1204256 | tf_op jit(solution)/shard_map/ppermute | solution.py:21
  44.9 3.6 %shard_map.101 = (s16[784,384]{1,0:T(8,128)(2,1)S(1)}, s16[784,384]{1,0:T(8,128)(2,1)S(1)}) custom-call(s32[3]{0:T(128)S(1)} %add_add_fusion.5.refs_0_, s32[12,6]{1,0:T(8,128)S(1)} %bitcast.18, f32[1,1536,768]{2,1,0:T(8,128)} %refs_2_.13, s16[784,768]{1,0:T(8,128)(2,1)} %collective-permute-done.8.refs_3_, s16[2064,128]{1,0:T(8,128)(2,1)S(1)} %shard_map.100.refs_4_.refs_2_, ...), custom_call_target="tpu_custom_call" | custom-call | bytes 1024 | tf_op jit(solution)/shard_map/pallas_call | solution.py:63
  48.7 1.9 %collective-permute-start.13 = (s16[784,384]{1,0:T(8,128)(2,1)S(1)}, s16[784,384]{1,0:T(8,128)(2,1)S(1)}, u32[]{:S(2)}, u32[]{:S(2)}) collective-permute-start(s16[784,384]{1,0:T(8,128)(2,1)S(1)} %get-tuple-element.13.refs_2_.refs_1_), channel_id=1, source_target_pairs={{0,8},{8,0},{16,24},{24,16},{1,9},{9,1},{17,25},{25,17},{2,10},{10... | collective-permute-start | bytes 1806344 | tf_op jit(solution)/shard_map/ppermute | solution.py:21
  50.6 15.3 %shard_map.102 = (f32[128,128]{1,0:T(8,128)S(1)}, f32[128,128]{1,0:T(8,128)S(1)}, f32[128,128]{1,0:T(8,128)S(1)}) custom-call(f32[128,128]{1,0:T(8,128)S(1)} %broadcast_select_fusion.5.refs_0_, s16[784,384]{1,0:T(8,128)(2,1)S(1)} %get-tuple-element.12.refs_1_.refs_0_, s16[784,384]{1,0:T(8,128)(2,1)S(1)} %get-tuple-element.13.refs_2_.refs_1_), custom_call_target="tpu_custom_call" | custom-call | bytes 1024 | tf_op jit(solution)/shard_map/pallas_call | solution.py:63
  65.9 3.3 %shard_map.103.refs_4_.refs_0_ = s16[528,896]{1,0:T(8,128)(2,1)S(1)} custom-call(s32[3]{0:T(128)S(1)} %add_add_fusion.3.refs_0_, s32[16,8]{1,0:T(8,128)S(1)} %copy.17.refs_1_, f32[1,2048,1024]{2,1,0:T(8,128)} %refs_2_.15, s16[528,896]{1,0:T(8,128)(2,1)} %collective-permute-done.4.refs_3_, f32[128,128]{1,0:T(8,128)S(1)} %get-tuple-element.14.refs_4_.refs_10_), custom_call_target="tpu_custom_call" | custom-call | bytes 1024 | tf_op jit(solution)/shard_map/pallas_call | solution.py:63
  69.4 3.3 %shard_map.104.refs_5_.refs_0_ = s16[528,896]{1,0:T(8,128)(2,1)S(1)} custom-call(s32[3]{0:T(128)S(1)} %add_add_fusion.refs_0_, s32[16,8]{1,0:T(8,128)S(1)} %copy.17.refs_1_, f32[1,2048,1024]{2,1,0:T(8,128)} %refs_2_.15, s16[528,896]{1,0:T(8,128)(2,1)} %collective-permute-done.3.refs_3_, s16[528,896]{1,0:T(8,128)(2,1)S(1)} %shard_map.103.refs_4_.refs_0_), custom_call_target="tpu_custom_call" | custom-call | bytes 1024 | tf_op jit(solution)/shard_map/pallas_call | solution.py:63
  72.7 2.0 %collective-permute-start.10 = (s16[528,896]{1,0:T(8,128)(2,1)S(1)}, s16[528,896]{1,0:T(8,128)(2,1)S(1)}, u32[]{:S(2)}, u32[]{:S(2)}) collective-permute-start(s16[528,896]{1,0:T(8,128)(2,1)S(1)} %shard_map.104.refs_5_.refs_0_), channel_id=1, source_target_pairs={{0,16},{8,24},{16,0},{24,8},{1,17},{9,25},{17,1},{25,9},{2,18},{10... | collective-permute-start | bytes 2838536 | tf_op jit(solution)/shard_map/ppermute | solution.py:21
  76.4 1.6 %collective-permute-done.13.refs_7_.refs_3_ = s16[784,384]{1,0:T(8,128)(2,1)S(1)} collective-permute-done((s16[784,384]{1,0:T(8,128)(2,1)S(1)}, s16[784,384]{1,0:T(8,128)(2,1)S(1)}, u32[]{:S(2)}, u32[]{:S(2)}) %collective-permute-start.13) | collective-permute-done | bytes 602144 | tf_op jit(solution)/shard_map/ppermute | solution.py:21
  78.0 2.8 %shard_map.105 = (f32[2048,128]{1,0:T(8,128)S(1)}, bf16[2048,128]{1,0:T(8,128)(2,1)S(1)}) custom-call(s32[4]{0:T(128)S(1)} %pad_add_fusion.2.refs_0_, bf16[2048,128]{1,0:T(8,128)(2,1)S(1)} %fusion.refs_1_, s16[2064,128]{1,0:T(8,128)(2,1)S(1)} %shard_map.100.refs_4_.refs_2_, s16[2064,128]{1,0:T(8,128)(2,1)S(1)} %collective-permute-done.14.refs_3_, ...), custom_call_target="tpu_custom_call" | custom-call | bytes 1024 | tf_op jit(solution)/shard_map/pallas_call | solution.py:63
  80.8 4.4 %collective-permute-start.17 = (bf16[2048,128]{1,0:T(8,128)(2,1)S(1)}, bf16[2048,128]{1,0:T(8,128)(2,1)S(1)}, u32[]{:S(2)}, u32[]{:S(2)}) collective-permute-start(bf16[2048,128]{1,0:T(8,128)(2,1)S(1)} %get-tuple-element.17), channel_id=1, source_target_pairs={{0,2},{4,6},{8,10},{12,14},{16,18},{20,22},{24,26},{28,30}} | collective-permute-start | bytes 1572872 | tf_op jit(solution)/shard_map/ppermute | solution.py:30
  86.3 6.3 %collective-permute-done.11.refs_1_ = s16[528,896]{1,0:T(8,128)(2,1)S(1)} collective-permute-done((s16[528,896]{1,0:T(8,128)(2,1)S(1)}, s16[528,896]{1,0:T(8,128)(2,1)S(1)}, u32[]{:S(2)}, u32[]{:S(2)}) %collective-permute-start.11) | collective-permute-done | bytes 946208 | tf_op jit(solution)/shard_map/ppermute | solution.py:21
  93.5 1.6 %collective-permute-start.16 = (s16[528,896]{1,0:T(8,128)(2,1)S(1)}, s16[528,896]{1,0:T(8,128)(2,1)}, u32[]{:S(2)}, u32[]{:S(2)}) collective-permute-start(s16[528,896]{1,0:T(8,128)(2,1)S(1)} %shard_map.107.refs_2_.refs_3_.refs_4_), channel_id=1, source_target_pairs={{0,16},{8,24},{16,0},{24,8},{1,17},{9,25},{17,1},{25,9},{2,18},{10... | collective-permute-start | bytes 2838536 | tf_op jit(solution)/shard_map/ppermute | solution.py:21
  96.7 1.8 %shard_map.108.refs_2_ = s16[528,896]{1,0:T(8,128)(2,1)} custom-call(s16[528,896]{1,0:T(8,128)(2,1)S(1)} %shard_map.104.refs_5_.refs_0_, s16[528,896]{1,0:T(8,128)(2,1)S(1)} %collective-permute-done.10.refs_1_, s16[528,896]{1,0:T(8,128)(2,1)S(1)} %shard_map.107.refs_2_.refs_3_.refs_4_), custom_call_target="tpu_custom_call" | custom-call | bytes 1024 | tf_op jit(solution)/shard_map/pallas_call | solution.py:63
  100.1 5.2 %collective-permute-start.18 = (bf16[2048,128]{1,0:T(8,128)(2,1)}, bf16[2048,128]{1,0:T(8,128)(2,1)}, u32[]{:S(2)}, u32[]{:S(2)}) collective-permute-start(bf16[2048,128]{1,0:T(8,128)(2,1)} %broadcast_select_fusion), channel_id=1, source_target_pairs={{0,1},{2,3},{4,5},{6,7},{8,9},{10,11},{12,13},{14,15},{16,17},{18,... | collective-permute-start | bytes 1572872 | tf_op jit(solution)/shard_map/ppermute | solution.py:30
  105.3 1.6 %collective-permute-start.20 = (s16[784,768]{1,0:T(8,128)(2,1)S(1)}, s16[784,768]{1,0:T(8,128)(2,1)}, u32[]{:S(2)}, u32[]{:S(2)}) collective-permute-start(s16[784,768]{1,0:T(8,128)(2,1)S(1)} %shard_map.106.refs_2_.refs_1_), channel_id=1, source_target_pairs={{0,16},{8,24},{16,0},{24,8},{1,17},{9,25},{17,1},{25,9},{2,18},{10... | collective-permute-start | bytes 3612680 | tf_op jit(solution)/shard_map/ppermute | solution.py:21
  107.0 1.7 %shard_map.109.refs_3_.refs_2_ = f32[1,1536,768]{2,1,0:T(8,128)} custom-call(s32[1]{0:T(128)} %bitcast.1.refs_0_, s16[784,768]{1,0:T(8,128)(2,1)S(1)} %shard_map.106.refs_2_.refs_1_, s16[528,896]{1,0:T(8,128)(2,1)} %shard_map.108.refs_2_), custom_call_target="tpu_custom_call" | custom-call | bytes 1024 | tf_op jit(solution)/shard_map/pallas_call | solution.py:63
  111.5 11.1 %collective-permute-done.15.refs_9_.refs_3_ = s16[528,896]{1,0:T(8,128)(2,1)} collective-permute-done((s16[528,896]{1,0:T(8,128)(2,1)}, s16[528,896]{1,0:T(8,128)(2,1)}, u32[]{:S(2)}, u32[]{:S(2)}) %collective-permute-start.15) | collective-permute-done | bytes 946208 | tf_op jit(solution)/shard_map/ppermute | solution.py:21
  122.7 1.9 %shard_map.111 = (f32[128,1024]{1,0:T(8,128)S(1)}, bf16[128,1024]{1,0:T(8,128)(2,1)S(1)}) custom-call(s32[4]{0:T(128)S(1)} %pad_add_fusion.2.refs_0_, bf16[2048,128]{1,0:T(8,128)(2,1)S(1)} %copy-done.3, f32[2048,128]{1,0:T(8,128)S(1)} %get-tuple-element.16.refs_4_.refs_2_.refs_6_, s16[528,896]{1,0:T(8,128)(2,1)S(1)} %shard_map.107.refs_2_.refs_3_.refs_4_, ...), custom_call_target="tpu_custom_call" | custom-call | bytes 1024 | tf_op jit(solution)/shard_map/pallas_call | solution.py:63
  127.1 10.8 %shard_map.112.refs_3_.refs_4_ = f32[2048,1024]{1,0:T(8,128)} custom-call(s32[4]{0:T(128)S(1)} %pad_add_fusion.2.refs_0_, bf16[2048,128]{1,0:T(8,128)(2,1)S(1)} %copy-done.3, s16[528,896]{1,0:T(8,128)(2,1)} %shard_map.108.refs_2_, s16[528,896]{1,0:T(8,128)(2,1)} %collective-permute-done.15.refs_9_.refs_3_, ...), custom_call_target="tpu_custom_call" | custom-call | bytes 1024 | tf_op jit(solution)/shard_map/pallas_call | solution.py:63
  137.9 2.6 %collective-permute-done.20.refs_1_ = s16[784,768]{1,0:T(8,128)(2,1)} collective-permute-done((s16[784,768]{1,0:T(8,128)(2,1)S(1)}, s16[784,768]{1,0:T(8,128)(2,1)}, u32[]{:S(2)}, u32[]{:S(2)}) %collective-permute-start.20) | collective-permute-done | bytes 1204256 | tf_op jit(solution)/shard_map/ppermute | solution.py:21
  140.5 2.9 %shard_map.113 = f32[1,1536,768]{2,1,0:T(8,128)} custom-call(s32[1]{0:T(128)} %bitcast.9.refs_0_, s16[784,768]{1,0:T(8,128)(2,1)} %collective-permute-done.20.refs_1_, f32[1,1536,768]{2,1,0:T(8,128)} %shard_map.109.refs_3_.refs_2_, f32[2048,1024]{1,0:T(8,128)} %shard_map.112.refs_3_.refs_4_), custom_call_target="tpu_custom_call", output_to_operand_aliasing={{}: (2, {})} | custom-call | bytes 1024 | tf_op jit(solution)/shard_map/pallas_call | solution.py:63
  143.5 2.4 %shard_map.114 = f32[1,1024,512]{2,1,0:T(8,128)} custom-call(s32[3]{0:T(128)S(1)} %fusion.3.refs_0_, s32[8,4]{1,0:T(8,128)S(1)} %copy.18.refs_1_, f32[1,1024,512]{2,1,0:T(8,128)S(1)} %copy-done.1, s16[1040,512]{1,0:T(8,128)(2,1)S(1)} %collective-permute-done.21.refs_3_, f32[2048,1024]{1,0:T(8,128)} %shard_map.112.refs_3_.refs_4_), custom_call_target="tpu_custom_call" | custom-call | bytes 1024 | tf_op jit(solution)/shard_map/pallas_call | solution.py:63
  (77 shorter events, 20.9 us)
Async XLA Ops:
  1.3 5.7 %copy-start.9 = (s32[1,16,8]{1,2,0:T(8,128)S(1)}, s32[1,16,8]{1,2,0:T(8,128)}, u32[]{:S(2)}) copy-start(s32[1,16,8]{1,2,0:T(8,128)} %param.10) | copy-start | bytes 1540
  2.5 9.7 %collective-permute-start.2 = (f32[128,128]{1,0:T(8,128)S(1)}, f32[128,128]{1,0:T(8,128)S(1)}, u32[]{:S(2)}, u32[]{:S(2)}) collective-permute-start(f32[128,128]{1,0:T(8,128)S(1)} %shard_map.94.refs_3_.refs_0_), channel_id=1, source_target_pairs={{0,24},{8,16},{16,8},{24,0},{1,25},{9,17},{17,9},{25,1},{2,26},{10... | collective-permute-start | bytes 196616 | tf_op jit(solution)/shard_map/ppermute | solution.py:472
  6.4 5.7 %collective-permute-start.1 = (f32[128,128]{1,0:T(8,128)S(1)}, f32[128,128]{1,0:T(8,128)S(1)}, u32[]{:S(2)}, u32[]{:S(2)}) collective-permute-start(f32[128,128]{1,0:T(8,128)S(1)} %shard_map.94.refs_3_.refs_0_), channel_id=1, source_target_pairs={{0,16},{8,24},{16,0},{24,8},{1,17},{9,25},{17,1},{25,9},{2,18},{10... | collective-permute-start | bytes 196616 | tf_op jit(solution)/shard_map/ppermute | solution.py:472
  6.9 5.2 %collective-permute-start = (f32[128,128]{1,0:T(8,128)S(1)}, f32[128,128]{1,0:T(8,128)S(1)}, u32[]{:S(2)}, u32[]{:S(2)}) collective-permute-start(f32[128,128]{1,0:T(8,128)S(1)} %shard_map.94.refs_3_.refs_0_), channel_id=1, source_target_pairs={{0,8},{8,0},{16,24},{24,16},{1,9},{9,1},{17,25},{25,17},{2,10},{10... | collective-permute-start | bytes 196616 | tf_op jit(solution)/shard_map/ppermute | solution.py:472
  7.2 4.8 %copy-start.10 = (s32[1,12,6]{1,0,2:T(1,128)S(1)}, s32[1,12,6]{1,0,2:T(1,128)}, u32[]{:S(2)}) copy-start(s32[1,12,6]{1,0,2:T(1,128)} %param.11) | copy-start | bytes 868
  9.3 25.5 %collective-permute-start.9 = (s16[2064,128]{1,0:T(8,128)(2,1)S(1)}, s16[2064,128]{1,0:T(8,128)(2,1)S(1)}, u32[]{:S(2)}, u32[]{:S(2)}) collective-permute-start(s16[2064,128]{1,0:T(8,128)(2,1)S(1)} %shard_map.95.refs_3_.refs_0_), channel_id=1, source_target_pairs={{0,8},{8,0},{16,24},{24,16},{1,9},{9,1},{17,25},{25,17},{2,10},{10... | collective-permute-start | bytes 1585160 | tf_op jit(solution)/shard_map/ppermute | solution.py:21
  12.1 4.9 %copy-start.6 = (s32[2048]{0:T(1024)S(1)}, s32[2048]{0:T(1024)}, u32[]{:S(2)}) copy-start(s32[2048]{0:T(1024)} %param.13) | copy-start | bytes 24580
  15.3 29.6 %collective-permute-start.8 = (s16[784,768]{1,0:T(8,128)(2,1)S(1)}, s16[784,768]{1,0:T(8,128)(2,1)}, u32[]{:S(2)}, u32[]{:S(2)}) collective-permute-start(s16[784,768]{1,0:T(8,128)(2,1)S(1)} %shard_map.96.refs_3_), channel_id=1, source_target_pairs={{0,16},{8,24},{16,0},{24,8},{1,17},{9,25},{17,1},{25,9},{2,18},{10... | collective-permute-start | bytes 3612680 | tf_op jit(solution)/shard_map/ppermute | solution.py:21
  17.6 4.8 %copy-start.7 = (s32[3]{0:T(128)S(1)}, s32[3]{0:T(128)}, u32[]{:S(2)}) copy-start(s32[3]{0:T(128)} %add_add_fusion.4.refs_0_) | copy-start | bytes 40
  20.6 48.8 %collective-permute-start.3 = (s16[528,896]{1,0:T(8,128)(2,1)S(1)}, s16[528,896]{1,0:T(8,128)(2,1)}, u32[]{:S(2)}, u32[]{:S(2)}) collective-permute-start(s16[528,896]{1,0:T(8,128)(2,1)S(1)} %shard_map.97.refs_4_), channel_id=1, source_target_pairs={{0,8},{8,0},{16,24},{24,16},{1,9},{9,1},{17,25},{25,17},{2,10},{10... | collective-permute-start | bytes 2838536 | tf_op jit(solution)/shard_map/ppermute | solution.py:21
  21.2 5.3 %collective-permute-start.5 = (f32[128,128]{1,0:T(8,128)S(1)}, f32[128,128]{1,0:T(8,128)S(1)}, u32[]{:S(2)}, u32[]{:S(2)}) collective-permute-start(f32[128,128]{1,0:T(8,128)S(1)} %shard_map.98.refs_3_), channel_id=1, source_target_pairs={{0,4},{1,5},{2,6},{3,7},{8,12},{9,13},{10,14},{11,15},{16,20},{17,... | collective-permute-start | bytes 196616 | tf_op jit(solution)/shard_map/ppermute | solution.py:30
  26.3 39.5 %collective-permute-start.4 = (s16[528,896]{1,0:T(8,128)(2,1)}, s16[528,896]{1,0:T(8,128)(2,1)}, u32[]{:S(2)}, u32[]{:S(2)}) collective-permute-start(s16[528,896]{1,0:T(8,128)(2,1)} %shard_map.99.refs_2_), channel_id=1, source_target_pairs={{0,16},{8,24},{16,0},{24,8},{1,17},{9,25},{17,1},{25,9},{2,18},{10... | collective-permute-start | bytes 2838536 | tf_op jit(solution)/shard_map/ppermute | solution.py:21
  26.5 6.9 %collective-permute-start.6 = (f32[128,128]{1,0:T(8,128)S(1)}, f32[128,128]{1,0:T(8,128)S(1)}, u32[]{:S(2)}, u32[]{:S(2)}) collective-permute-start(f32[128,128]{1,0:T(8,128)S(1)} %broadcast_select_fusion.3.refs_3_), channel_id=1, source_target_pairs={{0,2},{4,6},{8,10},{12,14},{16,18},{20,22},{24,26},{28,30}} | collective-permute-start | bytes 196616 | tf_op jit(solution)/shard_map/ppermute | solution.py:30
  33.4 15.2 %collective-permute-start.7 = (f32[128,128]{1,0:T(8,128)S(1)}, f32[128,128]{1,0:T(8,128)S(1)}, u32[]{:S(2)}, u32[]{:S(2)}) collective-permute-start(f32[128,128]{1,0:T(8,128)S(1)} %broadcast_select_fusion.4.refs_5_), channel_id=1, source_target_pairs={{0,1},{2,3},{4,5},{6,7},{8,9},{10,11},{12,13},{14,15},{16,17},{18,... | collective-permute-start | bytes 196616 | tf_op jit(solution)/shard_map/ppermute | solution.py:30
  35.3 41.1 %collective-permute-start.14 = (s16[2064,128]{1,0:T(8,128)(2,1)S(1)}, s16[2064,128]{1,0:T(8,128)(2,1)S(1)}, u32[]{:S(2)}, u32[]{:S(2)}) collective-permute-start(s16[2064,128]{1,0:T(8,128)(2,1)S(1)} %shard_map.100.refs_4_.refs_2_), channel_id=1, source_target_pairs={{0,16},{8,24},{16,0},{24,8},{1,17},{9,25},{17,1},{25,9},{2,18},{10... | collective-permute-start | bytes 1585160 | tf_op jit(solution)/shard_map/ppermute | solution.py:21
  48.5 27.9 %collective-permute-start.12 = (s16[784,384]{1,0:T(8,128)(2,1)S(1)}, s16[784,384]{1,0:T(8,128)(2,1)S(1)}, u32[]{:S(2)}, u32[]{:S(2)}) collective-permute-start(s16[784,384]{1,0:T(8,128)(2,1)S(1)} %get-tuple-element.12.refs_1_.refs_0_), channel_id=1, source_target_pairs={{0,8},{8,0},{16,24},{24,16},{1,9},{9,1},{17,25},{25,17},{2,10},{10... | collective-permute-start | bytes 1806344 | tf_op jit(solution)/shard_map/ppermute | solution.py:21
  48.7 29.3 %collective-permute-start.13 = (s16[784,384]{1,0:T(8,128)(2,1)S(1)}, s16[784,384]{1,0:T(8,128)(2,1)S(1)}, u32[]{:S(2)}, u32[]{:S(2)}) collective-permute-start(s16[784,384]{1,0:T(8,128)(2,1)S(1)} %get-tuple-element.13.refs_2_.refs_1_), channel_id=1, source_target_pairs={{0,8},{8,0},{16,24},{24,16},{1,9},{9,1},{17,25},{25,17},{2,10},{10... | collective-permute-start | bytes 1806344 | tf_op jit(solution)/shard_map/ppermute | solution.py:21
  69.2 5.5 %copy-start.8 = (s32[2048]{0:T(1024)S(1)}, s32[2048]{0:T(1024)}, u32[]{:S(2)}) copy-start(s32[2048]{0:T(1024)} %add_select_fusion) | copy-start | bytes 24580
  69.2 23.5 %collective-permute-start.11 = (s16[528,896]{1,0:T(8,128)(2,1)S(1)}, s16[528,896]{1,0:T(8,128)(2,1)S(1)}, u32[]{:S(2)}, u32[]{:S(2)}) collective-permute-start(s16[528,896]{1,0:T(8,128)(2,1)S(1)} %shard_map.103.refs_4_.refs_0_), channel_id=1, source_target_pairs={{0,8},{8,0},{16,24},{24,16},{1,9},{9,1},{17,25},{25,17},{2,10},{10... | collective-permute-start | bytes 2838536 | tf_op jit(solution)/shard_map/ppermute | solution.py:21
  72.7 24.0 %collective-permute-start.10 = (s16[528,896]{1,0:T(8,128)(2,1)S(1)}, s16[528,896]{1,0:T(8,128)(2,1)S(1)}, u32[]{:S(2)}, u32[]{:S(2)}) collective-permute-start(s16[528,896]{1,0:T(8,128)(2,1)S(1)} %shard_map.104.refs_5_.refs_0_), channel_id=1, source_target_pairs={{0,16},{8,24},{16,0},{24,8},{1,17},{9,25},{17,1},{25,9},{2,18},{10... | collective-permute-start | bytes 2838536 | tf_op jit(solution)/shard_map/ppermute | solution.py:21
  75.0 10.3 %copy-start.2 = (bf16[2048,128]{1,0:T(8,128)(2,1)}, bf16[2048,128]{1,0:T(8,128)(2,1)S(1)}, u32[]{:S(2)}) copy-start(bf16[2048,128]{1,0:T(8,128)(2,1)S(1)} %fusion.refs_1_) | copy-start | bytes 1572868
  80.8 41.9 %copy-start = (f32[2048,128]{1,0:T(8,128)}, f32[2048,128]{1,0:T(8,128)S(1)}, u32[]{:S(2)}) copy-start(f32[2048,128]{1,0:T(8,128)S(1)} %get-tuple-element.16.refs_4_.refs_2_.refs_6_) | copy-start | bytes 3145732
  80.8 18.4 %collective-permute-start.17 = (bf16[2048,128]{1,0:T(8,128)(2,1)S(1)}, bf16[2048,128]{1,0:T(8,128)(2,1)S(1)}, u32[]{:S(2)}, u32[]{:S(2)}) collective-permute-start(bf16[2048,128]{1,0:T(8,128)(2,1)S(1)} %get-tuple-element.17), channel_id=1, source_target_pairs={{0,2},{4,6},{8,10},{12,14},{16,18},{20,22},{24,26},{28,30}} | collective-permute-start | bytes 1572872 | tf_op jit(solution)/shard_map/ppermute | solution.py:30
  93.5 13.3 %copy-start.11 = (s32[1,8,4]{1,2,0:T(4,128)S(1)}, s32[1,8,4]{1,2,0:T(4,128)}, u32[]{:S(2)}) copy-start(s32[1,8,4]{1,2,0:T(4,128)} %param.12) | copy-start | bytes 388
  93.5 29.1 %collective-permute-start.16 = (s16[528,896]{1,0:T(8,128)(2,1)S(1)}, s16[528,896]{1,0:T(8,128)(2,1)}, u32[]{:S(2)}, u32[]{:S(2)}) collective-permute-start(s16[528,896]{1,0:T(8,128)(2,1)S(1)} %shard_map.107.refs_2_.refs_3_.refs_4_), channel_id=1, source_target_pairs={{0,16},{8,24},{16,0},{24,8},{1,17},{9,25},{17,1},{25,9},{2,18},{10... | collective-permute-start | bytes 2838536 | tf_op jit(solution)/shard_map/ppermute | solution.py:21
  98.4 24.2 %collective-permute-start.15 = (s16[528,896]{1,0:T(8,128)(2,1)}, s16[528,896]{1,0:T(8,128)(2,1)}, u32[]{:S(2)}, u32[]{:S(2)}) collective-permute-start(s16[528,896]{1,0:T(8,128)(2,1)} %shard_map.108.refs_2_), channel_id=1, source_target_pairs={{0,8},{8,0},{16,24},{24,16},{1,9},{9,1},{17,25},{25,17},{2,10},{10... | collective-permute-start | bytes 2838536 | tf_op jit(solution)/shard_map/ppermute | solution.py:21
  100.1 25.8 %collective-permute-start.18 = (bf16[2048,128]{1,0:T(8,128)(2,1)}, bf16[2048,128]{1,0:T(8,128)(2,1)}, u32[]{:S(2)}, u32[]{:S(2)}) collective-permute-start(bf16[2048,128]{1,0:T(8,128)(2,1)} %broadcast_select_fusion), channel_id=1, source_target_pairs={{0,1},{2,3},{4,5},{6,7},{8,9},{10,11},{12,13},{14,15},{16,17},{18,... | collective-permute-start | bytes 1572872 | tf_op jit(solution)/shard_map/ppermute | solution.py:30
  105.3 35.2 %collective-permute-start.20 = (s16[784,768]{1,0:T(8,128)(2,1)S(1)}, s16[784,768]{1,0:T(8,128)(2,1)}, u32[]{:S(2)}, u32[]{:S(2)}) collective-permute-start(s16[784,768]{1,0:T(8,128)(2,1)S(1)} %shard_map.106.refs_2_.refs_1_), channel_id=1, source_target_pairs={{0,16},{8,24},{16,0},{24,8},{1,17},{9,25},{17,1},{25,9},{2,18},{10... | collective-permute-start | bytes 3612680 | tf_op jit(solution)/shard_map/ppermute | solution.py:21
  109.5 13.2 %copy-start.3 = (bf16[2048,128]{1,0:T(8,128)(2,1)S(1)}, bf16[2048,128]{1,0:T(8,128)(2,1)}, u32[]{:S(2)}) copy-start(bf16[2048,128]{1,0:T(8,128)(2,1)} %copy-done.2) | copy-start | bytes 1572868
  110.8 11.9 %copy-start.4 = (s16[1040,512]{1,0:T(8,128)(2,1)}, s16[1040,512]{1,0:T(8,128)(2,1)S(1)}, u32[]{:S(2)}) copy-start(s16[1040,512]{1,0:T(8,128)(2,1)S(1)} %shard_map.110.refs_8_) | copy-start | bytes 3194884
  110.8 32.7 %collective-permute-start.21 = (s16[1040,512]{1,0:T(8,128)(2,1)S(1)}, s16[1040,512]{1,0:T(8,128)(2,1)S(1)}, u32[]{:S(2)}, u32[]{:S(2)}) collective-permute-start(s16[1040,512]{1,0:T(8,128)(2,1)S(1)} %shard_map.110.refs_8_), channel_id=1, source_target_pairs={{0,8},{8,0},{16,24},{24,16},{1,9},{9,1},{17,25},{25,17},{2,10},{10... | collective-permute-start | bytes 3194888 | tf_op jit(solution)/shard_map/ppermute | solution.py:21
  124.6 2.4 %collective-permute-start.19 = (bf16[128,1024]{1,0:T(8,128)(2,1)S(1)}, bf16[128,1024]{1,0:T(8,128)(2,1)S(1)}, u32[]{:S(2)}, u32[]{:S(2)}) collective-permute-start(bf16[128,1024]{1,0:T(8,128)(2,1)S(1)} %get-tuple-element.19), channel_id=1, source_target_pairs={{0,4},{1,5},{2,6},{3,7},{8,12},{9,13},{10,14},{11,15},{16,20},{17,... | collective-permute-start | bytes 786440 | tf_op jit(solution)/shard_map/ppermute | solution.py:30
  (2 other events, 3.1 us)

commit v9 on v8

--- a/solution.py
+++ b/solution.py
@@ -393,7 +393,7 @@
 
     def kernel(flag_ref, order_ref, own_a, got_a, own_b, got_b, slab_ref, low_ref, up_low_ref, up_ref, packed_ref, out_ref):
         def block_rows(sub):
-            i = 2 * pl.program_id(0) + sub
+            i = part_blocks * pl.program_id(0) + sub
             here = pl.ds(sub * BLK, BLK)
             part = i // part_blocks
             row = pl.multiple_of((i % part_blocks) * BLK, BLK)
@@ -424,16 +424,16 @@
                 out_ref[here, PANEL:] = up_ref[:, PANEL:]
                 out_ref[here, :PANEL] = jnp.where(first_col, packed_ref[...], up_ref[:, :PANEL])
 
-        for sub in range(2):
+        for sub in range(part_blocks):
             block_rows(sub)
 
-    square = pl.BlockSpec((2 * BLK, BLK), lambda i: (i, 0))
+    square = pl.BlockSpec((rows, BLK), lambda i: (i, 0))
     return run(
         kernel, after, [flags, order, *codes, slab, lower_low, upper_low, upper, packed],
         [SMEM_SPEC, square] + [VMEM_SPEC] * 4 + [square, square] + [VMEM_SPEC] * 3,
-        pl.BlockSpec((2 * BLK, width), lambda i: (i, 0)),
+        pl.BlockSpec((rows, width), lambda i: (i, 0)),
         jax.ShapeDtypeStruct((total_rows, width), jnp.float32),
-        total_rows * width * 6, total_rows * width * BLK * 6, grid=(total_rows // (2 * BLK),),
+        total_rows * width * 6, total_rows * width * BLK * 6, grid=(total_rows // rows,),
     )
 
 

time: 147 us -> 147 us (level)
  no operation moved by 1% of the time
where the time goes in v9:
time: 147 us; the launch traced here: 146 us
  Pallas kernels  66.7 us (45%)
  starting transfers between devices  38 us (26%)
  waiting for transfers between devices  34.2 us (23%)
  other arithmetic  4.25 us (3%)
  local copies, waits for them, and re-layouts  1.77 us (1%)
    pallas_call x21, Pallas kernels, run(): pl.pallas_call(body, grid_spec=pltpu.PrefetchScalarGridSpec(num_scalar_pr...  66.7 us
    ppermute x13, waiting for transfers between devices, swapped(): lax.ppermute(piece, 'layer', pairs)  32.3 us
    ppermute x6, starting transfers between devices, broadcast_stages(): lax.ppermute(value, axis, [(i, i + span) for i in range(0, count, 2 * spa...  18.7 us
    ppermute x13, starting transfers between devices, swapped(): lax.ppermute(piece, 'layer', pairs)  14.7 us
    ppermute x3, starting transfers between devices, on_device(): lax.ppermute(corner, 'layer', [(i, i ^ apart) for i in range(count)])  4.6 us
  transfers between devices with their start and end apart: 22, of which 8 were waited for; matrix products, arithmetic and copies ran while one was open for 3% of the time, Pallas kernels for 43%

profile of v9, /device:TPU:0, one launch (start us, length us, event | category | flops | bytes accessed | tf_op | source)
XLA Modules:
  0.0 145.8 jit_solution(16081556249176512769)
XLA Ops:
  2.5 4.0 %collective-permute-start.2 = (f32[128,128]{1,0:T(8,128)S(1)}, f32[128,128]{1,0:T(8,128)S(1)}, u32[]{:S(2)}, u32[]{:S(2)}) collective-permute-start(f32[128,128]{1,0:T(8,128)S(1)} %shard_map.94.refs_3_.refs_0_), channel_id=1, source_target_pairs={{0,24},{8,16},{16,8},{24,0},{1,25},{9,17},{17,9},{25,1},{2,26},{10... | collective-permute-start | bytes 196616 | tf_op jit(solution)/shard_map/ppermute | solution.py:472
  7.2 2.1 %shard_map.95.refs_3_.refs_0_ = s16[2064,128]{1,0:T(8,128)(2,1)S(1)} custom-call(s32[3]{0:T(128)S(1)} %fusion.2.refs_0_, s32[16,8]{1,0:T(8,128)S(1)} %copy.17.refs_1_, f32[1,2048,1024]{2,1,0:T(8,128)} %refs_2_.15, f32[128,128]{1,0:T(8,128)S(1)} %shard_map.94.refs_3_.refs_0_), custom_call_target="tpu_custom_call" | custom-call | bytes 1024 | tf_op jit(solution)/shard_map/pallas_call | solution.py:63
  9.3 2.0 %collective-permute-start.9 = (s16[2064,128]{1,0:T(8,128)(2,1)S(1)}, s16[2064,128]{1,0:T(8,128)(2,1)S(1)}, u32[]{:S(2)}, u32[]{:S(2)}) collective-permute-start(s16[2064,128]{1,0:T(8,128)(2,1)S(1)} %shard_map.95.refs_3_.refs_0_), channel_id=1, source_target_pairs={{0,8},{8,0},{16,24},{24,16},{1,9},{9,1},{17,25},{25,17},{2,10},{10... | collective-permute-start | bytes 1585160 | tf_op jit(solution)/shard_map/ppermute | solution.py:21
  12.2 3.1 %shard_map.96.refs_3_ = s16[784,768]{1,0:T(8,128)(2,1)S(1)} custom-call(s32[3]{0:T(128)S(1)} %add_add_fusion.2.refs_0_, s32[12,6]{1,0:T(8,128)S(1)} %bitcast.17, f32[1,1536,768]{2,1,0:T(8,128)} %refs_2_.13, s16[2064,128]{1,0:T(8,128)(2,1)S(1)} %shard_map.95.refs_3_.refs_0_, f32[128,128]{1,0:T(8,128)S(1)} %collective-permute-done.refs_4_.refs_1_, ...), custom_call_target="tpu_custom_call" | custom-call | bytes 1024 | tf_op jit(solution)/shard_map/pallas_call | solution.py:63
  15.3 1.6 %collective-permute-start.8 = (s16[784,768]{1,0:T(8,128)(2,1)S(1)}, s16[784,768]{1,0:T(8,128)(2,1)}, u32[]{:S(2)}, u32[]{:S(2)}) collective-permute-start(s16[784,768]{1,0:T(8,128)(2,1)S(1)} %shard_map.96.refs_3_), channel_id=1, source_target_pairs={{0,16},{8,24},{16,0},{24,8},{1,17},{9,25},{17,1},{25,9},{2,18},{10... | collective-permute-start | bytes 3612680 | tf_op jit(solution)/shard_map/ppermute | solution.py:21
  17.6 2.9 %shard_map.97.refs_4_ = s16[528,896]{1,0:T(8,128)(2,1)S(1)} custom-call(s32[3]{0:T(128)S(1)} %add_add_fusion.1.refs_0_, s32[16,8]{1,0:T(8,128)S(1)} %copy.17.refs_1_, f32[1,2048,1024]{2,1,0:T(8,128)} %refs_2_.15, s16[784,768]{1,0:T(8,128)(2,1)S(1)} %shard_map.96.refs_3_), custom_call_target="tpu_custom_call" | custom-call | bytes 1024 | tf_op jit(solution)/shard_map/pallas_call | solution.py:63
  22.5 3.8 %shard_map.99.refs_2_ = s16[528,896]{1,0:T(8,128)(2,1)} custom-call(s32[3]{0:T(128)S(1)} %copy-done.7, s32[16,8]{1,0:T(8,128)S(1)} %copy.17.refs_1_, f32[1,2048,1024]{2,1,0:T(8,128)} %refs_2_.15, f32[128,128]{1,0:T(8,128)S(1)} %shard_map.98.refs_3_), custom_call_target="tpu_custom_call" | custom-call | bytes 1024 | tf_op jit(solution)/shard_map/pallas_call | solution.py:63
  26.5 4.9 %collective-permute-start.6 = (f32[128,128]{1,0:T(8,128)S(1)}, f32[128,128]{1,0:T(8,128)S(1)}, u32[]{:S(2)}, u32[]{:S(2)}) collective-permute-start(f32[128,128]{1,0:T(8,128)S(1)} %broadcast_select_fusion.3.refs_3_), channel_id=1, source_target_pairs={{0,2},{4,6},{8,10},{12,14},{16,18},{20,22},{24,26},{28,30}} | collective-permute-start | bytes 196616 | tf_op jit(solution)/shard_map/ppermute | solution.py:30
  31.5 1.9 %collective-permute-done.6 = f32[128,128]{1,0:T(8,128)S(1)} collective-permute-done((f32[128,128]{1,0:T(8,128)S(1)}, f32[128,128]{1,0:T(8,128)S(1)}, u32[]{:S(2)}, u32[]{:S(2)}) %collective-permute-start.6) | collective-permute-done | bytes 65568 | tf_op jit(solution)/shard_map/ppermute | solution.py:30
  35.3 1.6 %collective-permute-start.14 = (s16[2064,128]{1,0:T(8,128)(2,1)S(1)}, s16[2064,128]{1,0:T(8,128)(2,1)S(1)}, u32[]{:S(2)}, u32[]{:S(2)}) collective-permute-start(s16[2064,128]{1,0:T(8,128)(2,1)S(1)} %shard_map.100.refs_4_.refs_2_), channel_id=1, source_target_pairs={{0,16},{8,24},{16,0},{24,8},{1,17},{9,25},{17,1},{25,9},{2,18},{10... | collective-permute-start | bytes 1585160 | tf_op jit(solution)/shard_map/ppermute | solution.py:21
  36.9 8.0 %collective-permute-done.8.refs_3_ = s16[784,768]{1,0:T(8,128)(2,1)} collective-permute-done((s16[784,768]{1,0:T(8,128)(2,1)S(1)}, s16[784,768]{1,0:T(8,128)(2,1)}, u32[]{:S(2)}, u32[]{:S(2)}) %collective-permute-start.8) | collective-permute-done | bytes 1204256 | tf_op jit(solution)/shard_map/ppermute | solution.py:21
  44.9 3.6 %shard_map.101 = (s16[784,384]{1,0:T(8,128)(2,1)S(1)}, s16[784,384]{1,0:T(8,128)(2,1)S(1)}) custom-call(s32[3]{0:T(128)S(1)} %add_add_fusion.5.refs_0_, s32[12,6]{1,0:T(8,128)S(1)} %bitcast.18, f32[1,1536,768]{2,1,0:T(8,128)} %refs_2_.13, s16[784,768]{1,0:T(8,128)(2,1)} %collective-permute-done.8.refs_3_, s16[2064,128]{1,0:T(8,128)(2,1)S(1)} %shard_map.100.refs_4_.refs_2_, ...), custom_call_target="tpu_custom_call" | custom-call | bytes 1024 | tf_op jit(solution)/shard_map/pallas_call | solution.py:63
  48.7 1.9 %collective-permute-start.13 = (s16[784,384]{1,0:T(8,128)(2,1)S(1)}, s16[784,384]{1,0:T(8,128)(2,1)S(1)}, u32[]{:S(2)}, u32[]{:S(2)}) collective-permute-start(s16[784,384]{1,0:T(8,128)(2,1)S(1)} %get-tuple-element.13.refs_2_.refs_1_), channel_id=1, source_target_pairs={{0,8},{8,0},{16,24},{24,16},{1,9},{9,1},{17,25},{25,17},{2,10},{10... | collective-permute-start | bytes 1806344 | tf_op jit(solution)/shard_map/ppermute | solution.py:21
  50.6 15.3 %shard_map.102 = (f32[128,128]{1,0:T(8,128)S(1)}, f32[128,128]{1,0:T(8,128)S(1)}, f32[128,128]{1,0:T(8,128)S(1)}) custom-call(f32[128,128]{1,0:T(8,128)S(1)} %broadcast_select_fusion.5.refs_0_, s16[784,384]{1,0:T(8,128)(2,1)S(1)} %get-tuple-element.12.refs_1_.refs_0_, s16[784,384]{1,0:T(8,128)(2,1)S(1)} %get-tuple-element.13.refs_2_.refs_1_), custom_call_target="tpu_custom_call" | custom-call | bytes 1024 | tf_op jit(solution)/shard_map/pallas_call | solution.py:63
  65.9 3.3 %shard_map.103.refs_4_.refs_0_ = s16[528,896]{1,0:T(8,128)(2,1)S(1)} custom-call(s32[3]{0:T(128)S(1)} %add_add_fusion.3.refs_0_, s32[16,8]{1,0:T(8,128)S(1)} %copy.17.refs_1_, f32[1,2048,1024]{2,1,0:T(8,128)} %refs_2_.15, s16[528,896]{1,0:T(8,128)(2,1)} %collective-permute-done.4.refs_3_, f32[128,128]{1,0:T(8,128)S(1)} %get-tuple-element.14.refs_4_.refs_10_), custom_call_target="tpu_custom_call" | custom-call | bytes 1024 | tf_op jit(solution)/shard_map/pallas_call | solution.py:63
  69.4 3.3 %shard_map.104.refs_5_.refs_0_ = s16[528,896]{1,0:T(8,128)(2,1)S(1)} custom-call(s32[3]{0:T(128)S(1)} %add_add_fusion.refs_0_, s32[16,8]{1,0:T(8,128)S(1)} %copy.17.refs_1_, f32[1,2048,1024]{2,1,0:T(8,128)} %refs_2_.15, s16[528,896]{1,0:T(8,128)(2,1)} %collective-permute-done.3.refs_3_, s16[528,896]{1,0:T(8,128)(2,1)S(1)} %shard_map.103.refs_4_.refs_0_), custom_call_target="tpu_custom_call" | custom-call | bytes 1024 | tf_op jit(solution)/shard_map/pallas_call | solution.py:63
  72.7 2.0 %collective-permute-start.10 = (s16[528,896]{1,0:T(8,128)(2,1)S(1)}, s16[528,896]{1,0:T(8,128)(2,1)S(1)}, u32[]{:S(2)}, u32[]{:S(2)}) collective-permute-start(s16[528,896]{1,0:T(8,128)(2,1)S(1)} %shard_map.104.refs_5_.refs_0_), channel_id=1, source_target_pairs={{0,16},{8,24},{16,0},{24,8},{1,17},{9,25},{17,1},{25,9},{2,18},{10... | collective-permute-start | bytes 2838536 | tf_op jit(solution)/shard_map/ppermute | solution.py:21
  76.4 1.6 %collective-permute-done.13.refs_7_.refs_3_ = s16[784,384]{1,0:T(8,128)(2,1)S(1)} collective-permute-done((s16[784,384]{1,0:T(8,128)(2,1)S(1)}, s16[784,384]{1,0:T(8,128)(2,1)S(1)}, u32[]{:S(2)}, u32[]{:S(2)}) %collective-permute-start.13) | collective-permute-done | bytes 602144 | tf_op jit(solution)/shard_map/ppermute | solution.py:21
  78.0 2.8 %shard_map.105 = (f32[2048,128]{1,0:T(8,128)S(1)}, bf16[2048,128]{1,0:T(8,128)(2,1)S(1)}) custom-call(s32[4]{0:T(128)S(1)} %pad_add_fusion.2.refs_0_, bf16[2048,128]{1,0:T(8,128)(2,1)S(1)} %fusion.refs_1_, s16[2064,128]{1,0:T(8,128)(2,1)S(1)} %shard_map.100.refs_4_.refs_2_, s16[2064,128]{1,0:T(8,128)(2,1)S(1)} %collective-permute-done.14.refs_3_, ...), custom_call_target="tpu_custom_call" | custom-call | bytes 1024 | tf_op jit(solution)/shard_map/pallas_call | solution.py:63
  80.8 4.4 %collective-permute-start.17 = (bf16[2048,128]{1,0:T(8,128)(2,1)S(1)}, bf16[2048,128]{1,0:T(8,128)(2,1)S(1)}, u32[]{:S(2)}, u32[]{:S(2)}) collective-permute-start(bf16[2048,128]{1,0:T(8,128)(2,1)S(1)} %get-tuple-element.17), channel_id=1, source_target_pairs={{0,2},{4,6},{8,10},{12,14},{16,18},{20,22},{24,26},{28,30}} | collective-permute-start | bytes 1572872 | tf_op jit(solution)/shard_map/ppermute | solution.py:30
  86.3 6.4 %collective-permute-done.11.refs_1_ = s16[528,896]{1,0:T(8,128)(2,1)S(1)} collective-permute-done((s16[528,896]{1,0:T(8,128)(2,1)S(1)}, s16[528,896]{1,0:T(8,128)(2,1)S(1)}, u32[]{:S(2)}, u32[]{:S(2)}) %collective-permute-start.11) | collective-permute-done | bytes 946208 | tf_op jit(solution)/shard_map/ppermute | solution.py:21
  93.5 1.6 %collective-permute-start.16 = (s16[528,896]{1,0:T(8,128)(2,1)S(1)}, s16[528,896]{1,0:T(8,128)(2,1)}, u32[]{:S(2)}, u32[]{:S(2)}) collective-permute-start(s16[528,896]{1,0:T(8,128)(2,1)S(1)} %shard_map.107.refs_2_.refs_3_.refs_4_), channel_id=1, source_target_pairs={{0,16},{8,24},{16,0},{24,8},{1,17},{9,25},{17,1},{25,9},{2,18},{10... | collective-permute-start | bytes 2838536 | tf_op jit(solution)/shard_map/ppermute | solution.py:21
  95.1 1.5 %collective-permute-done.10.refs_1_ = s16[528,896]{1,0:T(8,128)(2,1)S(1)} collective-permute-done((s16[528,896]{1,0:T(8,128)(2,1)S(1)}, s16[528,896]{1,0:T(8,128)(2,1)S(1)}, u32[]{:S(2)}, u32[]{:S(2)}) %collective-permute-start.10) | collective-permute-done | bytes 946208 | tf_op jit(solution)/shard_map/ppermute | solution.py:21
  96.7 1.8 %shard_map.108.refs_2_ = s16[528,896]{1,0:T(8,128)(2,1)} custom-call(s16[528,896]{1,0:T(8,128)(2,1)S(1)} %shard_map.104.refs_5_.refs_0_, s16[528,896]{1,0:T(8,128)(2,1)S(1)} %collective-permute-done.10.refs_1_, s16[528,896]{1,0:T(8,128)(2,1)S(1)} %shard_map.107.refs_2_.refs_3_.refs_4_), custom_call_target="tpu_custom_call" | custom-call | bytes 1024 | tf_op jit(solution)/shard_map/pallas_call | solution.py:63
  100.1 5.3 %collective-permute-start.18 = (bf16[2048,128]{1,0:T(8,128)(2,1)}, bf16[2048,128]{1,0:T(8,128)(2,1)}, u32[]{:S(2)}, u32[]{:S(2)}) collective-permute-start(bf16[2048,128]{1,0:T(8,128)(2,1)} %broadcast_select_fusion), channel_id=1, source_target_pairs={{0,1},{2,3},{4,5},{6,7},{8,9},{10,11},{12,13},{14,15},{16,17},{18,... | collective-permute-start | bytes 1572872 | tf_op jit(solution)/shard_map/ppermute | solution.py:30
  107.0 1.7 %shard_map.109.refs_3_.refs_2_ = f32[1,1536,768]{2,1,0:T(8,128)} custom-call(s32[1]{0:T(128)} %bitcast.1.refs_0_, s16[784,768]{1,0:T(8,128)(2,1)S(1)} %shard_map.106.refs_2_.refs_1_, s16[528,896]{1,0:T(8,128)(2,1)} %shard_map.108.refs_2_), custom_call_target="tpu_custom_call" | custom-call | bytes 1024 | tf_op jit(solution)/shard_map/pallas_call | solution.py:63
  111.5 11.1 %collective-permute-done.15.refs_9_.refs_3_ = s16[528,896]{1,0:T(8,128)(2,1)} collective-permute-done((s16[528,896]{1,0:T(8,128)(2,1)}, s16[528,896]{1,0:T(8,128)(2,1)}, u32[]{:S(2)}, u32[]{:S(2)}) %collective-permute-start.15) | collective-permute-done | bytes 946208 | tf_op jit(solution)/shard_map/ppermute | solution.py:21
  122.7 1.9 %shard_map.111 = (f32[128,1024]{1,0:T(8,128)S(1)}, bf16[128,1024]{1,0:T(8,128)(2,1)S(1)}) custom-call(s32[4]{0:T(128)S(1)} %pad_add_fusion.2.refs_0_, bf16[2048,128]{1,0:T(8,128)(2,1)S(1)} %copy-done.3, f32[2048,128]{1,0:T(8,128)S(1)} %get-tuple-element.16.refs_4_.refs_2_.refs_6_, s16[528,896]{1,0:T(8,128)(2,1)S(1)} %shard_map.107.refs_2_.refs_3_.refs_4_, ...), custom_call_target="tpu_custom_call" | custom-call | bytes 1024 | tf_op jit(solution)/shard_map/pallas_call | solution.py:63
  127.2 11.0 %shard_map.112.refs_3_.refs_4_ = f32[2048,1024]{1,0:T(8,128)} custom-call(s32[4]{0:T(128)S(1)} %pad_add_fusion.2.refs_0_, bf16[2048,128]{1,0:T(8,128)(2,1)S(1)} %copy-done.3, s16[528,896]{1,0:T(8,128)(2,1)} %shard_map.108.refs_2_, s16[528,896]{1,0:T(8,128)(2,1)} %collective-permute-done.15.refs_9_.refs_3_, ...), custom_call_target="tpu_custom_call" | custom-call | bytes 1024 | tf_op jit(solution)/shard_map/pallas_call | solution.py:63
  138.3 2.3 %collective-permute-done.20.refs_1_ = s16[784,768]{1,0:T(8,128)(2,1)} collective-permute-done((s16[784,768]{1,0:T(8,128)(2,1)S(1)}, s16[784,768]{1,0:T(8,128)(2,1)}, u32[]{:S(2)}, u32[]{:S(2)}) %collective-permute-start.20) | collective-permute-done | bytes 1204256 | tf_op jit(solution)/shard_map/ppermute | solution.py:21
  140.5 2.9 %shard_map.113 = f32[1,1536,768]{2,1,0:T(8,128)} custom-call(s32[1]{0:T(128)} %bitcast.9.refs_0_, s16[784,768]{1,0:T(8,128)(2,1)} %collective-permute-done.20.refs_1_, f32[1,1536,768]{2,1,0:T(8,128)} %shard_map.109.refs_3_.refs_2_, f32[2048,1024]{1,0:T(8,128)} %shard_map.112.refs_3_.refs_4_), custom_call_target="tpu_custom_call", output_to_operand_aliasing={{}: (2, {})} | custom-call | bytes 1024 | tf_op jit(solution)/shard_map/pallas_call | solution.py:63
  143.5 2.4 %shard_map.114 = f32[1,1024,512]{2,1,0:T(8,128)} custom-call(s32[3]{0:T(128)S(1)} %fusion.3.refs_0_, s32[8,4]{1,0:T(8,128)S(1)} %copy.18.refs_1_, f32[1,1024,512]{2,1,0:T(8,128)S(1)} %copy-done.1, s16[1040,512]{1,0:T(8,128)(2,1)S(1)} %collective-permute-done.21.refs_3_, f32[2048,1024]{1,0:T(8,128)} %shard_map.112.refs_3_.refs_4_), custom_call_target="tpu_custom_call" | custom-call | bytes 1024 | tf_op jit(solution)/shard_map/pallas_call | solution.py:63
  (77 shorter events, 21.1 us)
Async XLA Ops:
  1.3 5.7 %copy-start.9 = (s32[1,16,8]{1,2,0:T(8,128)S(1)}, s32[1,16,8]{1,2,0:T(8,128)}, u32[]{:S(2)}) copy-start(s32[1,16,8]{1,2,0:T(8,128)} %param.10) | copy-start | bytes 1540
  2.5 9.7 %collective-permute-start.2 = (f32[128,128]{1,0:T(8,128)S(1)}, f32[128,128]{1,0:T(8,128)S(1)}, u32[]{:S(2)}, u32[]{:S(2)}) collective-permute-start(f32[128,128]{1,0:T(8,128)S(1)} %shard_map.94.refs_3_.refs_0_), channel_id=1, source_target_pairs={{0,24},{8,16},{16,8},{24,0},{1,25},{9,17},{17,9},{25,1},{2,26},{10... | collective-permute-start | bytes 196616 | tf_op jit(solution)/shard_map/ppermute | solution.py:472
  6.4 5.7 %collective-permute-start.1 = (f32[128,128]{1,0:T(8,128)S(1)}, f32[128,128]{1,0:T(8,128)S(1)}, u32[]{:S(2)}, u32[]{:S(2)}) collective-permute-start(f32[128,128]{1,0:T(8,128)S(1)} %shard_map.94.refs_3_.refs_0_), channel_id=1, source_target_pairs={{0,16},{8,24},{16,0},{24,8},{1,17},{9,25},{17,1},{25,9},{2,18},{10... | collective-permute-start | bytes 196616 | tf_op jit(solution)/shard_map/ppermute | solution.py:472
  6.9 5.2 %collective-permute-start = (f32[128,128]{1,0:T(8,128)S(1)}, f32[128,128]{1,0:T(8,128)S(1)}, u32[]{:S(2)}, u32[]{:S(2)}) collective-permute-start(f32[128,128]{1,0:T(8,128)S(1)} %shard_map.94.refs_3_.refs_0_), channel_id=1, source_target_pairs={{0,8},{8,0},{16,24},{24,16},{1,9},{9,1},{17,25},{25,17},{2,10},{10... | collective-permute-start | bytes 196616 | tf_op jit(solution)/shard_map/ppermute | solution.py:472
  7.2 4.8 %copy-start.10 = (s32[1,12,6]{1,0,2:T(1,128)S(1)}, s32[1,12,6]{1,0,2:T(1,128)}, u32[]{:S(2)}) copy-start(s32[1,12,6]{1,0,2:T(1,128)} %param.11) | copy-start | bytes 868
  9.3 25.5 %collective-permute-start.9 = (s16[2064,128]{1,0:T(8,128)(2,1)S(1)}, s16[2064,128]{1,0:T(8,128)(2,1)S(1)}, u32[]{:S(2)}, u32[]{:S(2)}) collective-permute-start(s16[2064,128]{1,0:T(8,128)(2,1)S(1)} %shard_map.95.refs_3_.refs_0_), channel_id=1, source_target_pairs={{0,8},{8,0},{16,24},{24,16},{1,9},{9,1},{17,25},{25,17},{2,10},{10... | collective-permute-start | bytes 1585160 | tf_op jit(solution)/shard_map/ppermute | solution.py:21
  12.1 4.9 %copy-start.6 = (s32[2048]{0:T(1024)S(1)}, s32[2048]{0:T(1024)}, u32[]{:S(2)}) copy-start(s32[2048]{0:T(1024)} %param.13) | copy-start | bytes 24580
  15.3 29.6 %collective-permute-start.8 = (s16[784,768]{1,0:T(8,128)(2,1)S(1)}, s16[784,768]{1,0:T(8,128)(2,1)}, u32[]{:S(2)}, u32[]{:S(2)}) collective-permute-start(s16[784,768]{1,0:T(8,128)(2,1)S(1)} %shard_map.96.refs_3_), channel_id=1, source_target_pairs={{0,16},{8,24},{16,0},{24,8},{1,17},{9,25},{17,1},{25,9},{2,18},{10... | collective-permute-start | bytes 3612680 | tf_op jit(solution)/shard_map/ppermute | solution.py:21
  17.6 4.8 %copy-start.7 = (s32[3]{0:T(128)S(1)}, s32[3]{0:T(128)}, u32[]{:S(2)}) copy-start(s32[3]{0:T(128)} %add_add_fusion.4.refs_0_) | copy-start | bytes 40
  20.6 48.8 %collective-permute-start.3 = (s16[528,896]{1,0:T(8,128)(2,1)S(1)}, s16[528,896]{1,0:T(8,128)(2,1)}, u32[]{:S(2)}, u32[]{:S(2)}) collective-permute-start(s16[528,896]{1,0:T(8,128)(2,1)S(1)} %shard_map.97.refs_4_), channel_id=1, source_target_pairs={{0,8},{8,0},{16,24},{24,16},{1,9},{9,1},{17,25},{25,17},{2,10},{10... | collective-permute-start | bytes 2838536 | tf_op jit(solution)/shard_map/ppermute | solution.py:21
  21.2 5.3 %collective-permute-start.5 = (f32[128,128]{1,0:T(8,128)S(1)}, f32[128,128]{1,0:T(8,128)S(1)}, u32[]{:S(2)}, u32[]{:S(2)}) collective-permute-start(f32[128,128]{1,0:T(8,128)S(1)} %shard_map.98.refs_3_), channel_id=1, source_target_pairs={{0,4},{1,5},{2,6},{3,7},{8,12},{9,13},{10,14},{11,15},{16,20},{17,... | collective-permute-start | bytes 196616 | tf_op jit(solution)/shard_map/ppermute | solution.py:30
  26.3 39.5 %collective-permute-start.4 = (s16[528,896]{1,0:T(8,128)(2,1)}, s16[528,896]{1,0:T(8,128)(2,1)}, u32[]{:S(2)}, u32[]{:S(2)}) collective-permute-start(s16[528,896]{1,0:T(8,128)(2,1)} %shard_map.99.refs_2_), channel_id=1, source_target_pairs={{0,16},{8,24},{16,0},{24,8},{1,17},{9,25},{17,1},{25,9},{2,18},{10... | collective-permute-start | bytes 2838536 | tf_op jit(solution)/shard_map/ppermute | solution.py:21
  26.5 6.9 %collective-permute-start.6 = (f32[128,128]{1,0:T(8,128)S(1)}, f32[128,128]{1,0:T(8,128)S(1)}, u32[]{:S(2)}, u32[]{:S(2)}) collective-permute-start(f32[128,128]{1,0:T(8,128)S(1)} %broadcast_select_fusion.3.refs_3_), channel_id=1, source_target_pairs={{0,2},{4,6},{8,10},{12,14},{16,18},{20,22},{24,26},{28,30}} | collective-permute-start | bytes 196616 | tf_op jit(solution)/shard_map/ppermute | solution.py:30
  33.4 15.2 %collective-permute-start.7 = (f32[128,128]{1,0:T(8,128)S(1)}, f32[128,128]{1,0:T(8,128)S(1)}, u32[]{:S(2)}, u32[]{:S(2)}) collective-permute-start(f32[128,128]{1,0:T(8,128)S(1)} %broadcast_select_fusion.4.refs_5_), channel_id=1, source_target_pairs={{0,1},{2,3},{4,5},{6,7},{8,9},{10,11},{12,13},{14,15},{16,17},{18,... | collective-permute-start | bytes 196616 | tf_op jit(solution)/shard_map/ppermute | solution.py:30
  35.3 41.1 %collective-permute-start.14 = (s16[2064,128]{1,0:T(8,128)(2,1)S(1)}, s16[2064,128]{1,0:T(8,128)(2,1)S(1)}, u32[]{:S(2)}, u32[]{:S(2)}) collective-permute-start(s16[2064,128]{1,0:T(8,128)(2,1)S(1)} %shard_map.100.refs_4_.refs_2_), channel_id=1, source_target_pairs={{0,16},{8,24},{16,0},{24,8},{1,17},{9,25},{17,1},{25,9},{2,18},{10... | collective-permute-start | bytes 1585160 | tf_op jit(solution)/shard_map/ppermute | solution.py:21
  48.5 27.9 %collective-permute-start.12 = (s16[784,384]{1,0:T(8,128)(2,1)S(1)}, s16[784,384]{1,0:T(8,128)(2,1)S(1)}, u32[]{:S(2)}, u32[]{:S(2)}) collective-permute-start(s16[784,384]{1,0:T(8,128)(2,1)S(1)} %get-tuple-element.12.refs_1_.refs_0_), channel_id=1, source_target_pairs={{0,8},{8,0},{16,24},{24,16},{1,9},{9,1},{17,25},{25,17},{2,10},{10... | collective-permute-start | bytes 1806344 | tf_op jit(solution)/shard_map/ppermute | solution.py:21
  48.7 29.3 %collective-permute-start.13 = (s16[784,384]{1,0:T(8,128)(2,1)S(1)}, s16[784,384]{1,0:T(8,128)(2,1)S(1)}, u32[]{:S(2)}, u32[]{:S(2)}) collective-permute-start(s16[784,384]{1,0:T(8,128)(2,1)S(1)} %get-tuple-element.13.refs_2_.refs_1_), channel_id=1, source_target_pairs={{0,8},{8,0},{16,24},{24,16},{1,9},{9,1},{17,25},{25,17},{2,10},{10... | collective-permute-start | bytes 1806344 | tf_op jit(solution)/shard_map/ppermute | solution.py:21
  69.2 5.5 %copy-start.8 = (s32[2048]{0:T(1024)S(1)}, s32[2048]{0:T(1024)}, u32[]{:S(2)}) copy-start(s32[2048]{0:T(1024)} %add_select_fusion) | copy-start | bytes 24580
  69.2 23.5 %collective-permute-start.11 = (s16[528,896]{1,0:T(8,128)(2,1)S(1)}, s16[528,896]{1,0:T(8,128)(2,1)S(1)}, u32[]{:S(2)}, u32[]{:S(2)}) collective-permute-start(s16[528,896]{1,0:T(8,128)(2,1)S(1)} %shard_map.103.refs_4_.refs_0_), channel_id=1, source_target_pairs={{0,8},{8,0},{16,24},{24,16},{1,9},{9,1},{17,25},{25,17},{2,10},{10... | collective-permute-start | bytes 2838536 | tf_op jit(solution)/shard_map/ppermute | solution.py:21
  72.7 24.0 %collective-permute-start.10 = (s16[528,896]{1,0:T(8,128)(2,1)S(1)}, s16[528,896]{1,0:T(8,128)(2,1)S(1)}, u32[]{:S(2)}, u32[]{:S(2)}) collective-permute-start(s16[528,896]{1,0:T(8,128)(2,1)S(1)} %shard_map.104.refs_5_.refs_0_), channel_id=1, source_target_pairs={{0,16},{8,24},{16,0},{24,8},{1,17},{9,25},{17,1},{25,9},{2,18},{10... | collective-permute-start | bytes 2838536 | tf_op jit(solution)/shard_map/ppermute | solution.py:21
  75.0 10.3 %copy-start.2 = (bf16[2048,128]{1,0:T(8,128)(2,1)}, bf16[2048,128]{1,0:T(8,128)(2,1)S(1)}, u32[]{:S(2)}) copy-start(bf16[2048,128]{1,0:T(8,128)(2,1)S(1)} %fusion.refs_1_) | copy-start | bytes 1572868
  80.8 41.9 %copy-start = (f32[2048,128]{1,0:T(8,128)}, f32[2048,128]{1,0:T(8,128)S(1)}, u32[]{:S(2)}) copy-start(f32[2048,128]{1,0:T(8,128)S(1)} %get-tuple-element.16.refs_4_.refs_2_.refs_6_) | copy-start | bytes 3145732
  80.8 18.4 %collective-permute-start.17 = (bf16[2048,128]{1,0:T(8,128)(2,1)S(1)}, bf16[2048,128]{1,0:T(8,128)(2,1)S(1)}, u32[]{:S(2)}, u32[]{:S(2)}) collective-permute-start(bf16[2048,128]{1,0:T(8,128)(2,1)S(1)} %get-tuple-element.17), channel_id=1, source_target_pairs={{0,2},{4,6},{8,10},{12,14},{16,18},{20,22},{24,26},{28,30}} | collective-permute-start | bytes 1572872 | tf_op jit(solution)/shard_map/ppermute | solution.py:30
  93.5 13.3 %copy-start.11 = (s32[1,8,4]{1,2,0:T(4,128)S(1)}, s32[1,8,4]{1,2,0:T(4,128)}, u32[]{:S(2)}) copy-start(s32[1,8,4]{1,2,0:T(4,128)} %param.12) | copy-start | bytes 388
  93.5 29.1 %collective-permute-start.16 = (s16[528,896]{1,0:T(8,128)(2,1)S(1)}, s16[528,896]{1,0:T(8,128)(2,1)}, u32[]{:S(2)}, u32[]{:S(2)}) collective-permute-start(s16[528,896]{1,0:T(8,128)(2,1)S(1)} %shard_map.107.refs_2_.refs_3_.refs_4_), channel_id=1, source_target_pairs={{0,16},{8,24},{16,0},{24,8},{1,17},{9,25},{17,1},{25,9},{2,18},{10... | collective-permute-start | bytes 2838536 | tf_op jit(solution)/shard_map/ppermute | solution.py:21
  98.4 24.2 %collective-permute-start.15 = (s16[528,896]{1,0:T(8,128)(2,1)}, s16[528,896]{1,0:T(8,128)(2,1)}, u32[]{:S(2)}, u32[]{:S(2)}) collective-permute-start(s16[528,896]{1,0:T(8,128)(2,1)} %shard_map.108.refs_2_), channel_id=1, source_target_pairs={{0,8},{8,0},{16,24},{24,16},{1,9},{9,1},{17,25},{25,17},{2,10},{10... | collective-permute-start | bytes 2838536 | tf_op jit(solution)/shard_map/ppermute | solution.py:21
  100.1 26.0 %collective-permute-start.18 = (bf16[2048,128]{1,0:T(8,128)(2,1)}, bf16[2048,128]{1,0:T(8,128)(2,1)}, u32[]{:S(2)}, u32[]{:S(2)}) collective-permute-start(bf16[2048,128]{1,0:T(8,128)(2,1)} %broadcast_select_fusion), channel_id=1, source_target_pairs={{0,1},{2,3},{4,5},{6,7},{8,9},{10,11},{12,13},{14,15},{16,17},{18,... | collective-permute-start | bytes 1572872 | tf_op jit(solution)/shard_map/ppermute | solution.py:30
  105.3 35.2 %collective-permute-start.20 = (s16[784,768]{1,0:T(8,128)(2,1)S(1)}, s16[784,768]{1,0:T(8,128)(2,1)}, u32[]{:S(2)}, u32[]{:S(2)}) collective-permute-start(s16[784,768]{1,0:T(8,128)(2,1)S(1)} %shard_map.106.refs_2_.refs_1_), channel_id=1, source_target_pairs={{0,16},{8,24},{16,0},{24,8},{1,17},{9,25},{17,1},{25,9},{2,18},{10... | collective-permute-start | bytes 3612680 | tf_op jit(solution)/shard_map/ppermute | solution.py:21
  109.4 13.2 %copy-start.3 = (bf16[2048,128]{1,0:T(8,128)(2,1)S(1)}, bf16[2048,128]{1,0:T(8,128)(2,1)}, u32[]{:S(2)}) copy-start(bf16[2048,128]{1,0:T(8,128)(2,1)} %copy-done.2) | copy-start | bytes 1572868
  110.8 11.9 %copy-start.4 = (s16[1040,512]{1,0:T(8,128)(2,1)}, s16[1040,512]{1,0:T(8,128)(2,1)S(1)}, u32[]{:S(2)}) copy-start(s16[1040,512]{1,0:T(8,128)(2,1)S(1)} %shard_map.110.refs_8_) | copy-start | bytes 3194884
  110.8 32.7 %collective-permute-start.21 = (s16[1040,512]{1,0:T(8,128)(2,1)S(1)}, s16[1040,512]{1,0:T(8,128)(2,1)S(1)}, u32[]{:S(2)}, u32[]{:S(2)}) collective-permute-start(s16[1040,512]{1,0:T(8,128)(2,1)S(1)} %shard_map.110.refs_8_), channel_id=1, source_target_pairs={{0,8},{8,0},{16,24},{24,16},{1,9},{9,1},{17,25},{25,17},{2,10},{10... | collective-permute-start | bytes 3194888 | tf_op jit(solution)/shard_map/ppermute | solution.py:21
  124.6 2.6 %collective-permute-start.19 = (bf16[128,1024]{1,0:T(8,128)(2,1)S(1)}, bf16[128,1024]{1,0:T(8,128)(2,1)S(1)}, u32[]{:S(2)}, u32[]{:S(2)}) collective-permute-start(bf16[128,1024]{1,0:T(8,128)(2,1)S(1)} %get-tuple-element.19), channel_id=1, source_target_pairs={{0,4},{1,5},{2,6},{3,7},{8,12},{9,13},{10,14},{11,15},{16,20},{17,... | collective-permute-start | bytes 786440 | tf_op jit(solution)/shard_map/ppermute | solution.py:30
  (2 other events, 3.1 us)
